TPU v7x, 32 devices: a whole 2x2x4 slice. The times are simulated.
32 devices in a mesh: seq: 8 (over y, x, core), head: 4 (over z).
Axes of the slice: x: 2, y: 2, z: 4, core: 2. Of those that a mesh axis runs over, the one named last changes fastest.
Arguments:
- tokens: bfloat16 [16384, 1024], P('seq'), may hold values from -6 to 6
- start_flags: int32 [16384], P('seq'), may hold values from 0 to 1, as said below
- in_gain: float32 [1024], replicated, may hold values from 0.5 to 1.5
- proj_zx: bfloat16 [1024, 2, 2048], P(None, None, 'head'), may hold values from -0.1875 to 0.1875
- proj_bc: bfloat16 [1024, 256], P(None, 'head'), may hold values from -0.1875 to 0.1875
- proj_dt: bfloat16 [1024, 32], P(None, 'head'), may hold values from -0.1875 to 0.1875
- conv_x_weight: bfloat16 [4, 2048], P(None, 'head'), may hold values from -3 to 3
- conv_x_bias: float32 [2048], P('head'), may hold values from -3 to 3
- conv_bc_weight: bfloat16 [4, 256], P(None, 'head'), may hold values from -3 to 3
- conv_bc_bias: float32 [256], P('head'), may hold values from -3 to 3
- dt_bias: float32 [32], P('head'), may hold values from -14 to -3
- a_log: float32 [32], P('head'), may hold values from 0 to 1.4
- skip_scale: float32 [32], P('head'), may hold values from 0.5 to 1.5
- norm_gain: float32 [2048], P('head'), may hold values from 0.5 to 1.5
- out_proj: bfloat16 [2048, 1024], P('head'), may hold values from -0.125 to 0.125
- cotangent: bfloat16 [16384, 1024], P('seq'), may hold values from -6 to 6
Outputs:
- mixed_out: bfloat16 [16384, 1024], P('seq')
- grad_tokens: float32 [16384, 1024], P('seq')
- grad_in_gain: float32 [1024], replicated
- grad_proj_zx: float32 [1024, 2, 2048], P(None, None, 'head')
- grad_proj_bc: float32 [1024, 256], P(None, 'head')
- grad_proj_dt: float32 [1024, 32], P(None, 'head')
- grad_conv_x_weight: float32 [4, 2048], P(None, 'head')
- grad_conv_x_bias: float32 [2048], P('head')
- grad_conv_bc_weight: float32 [4, 256], P(None, 'head')
- grad_conv_bc_bias: float32 [256], P('head')
- grad_dt_bias: float32 [32], P('head')
- grad_a_log: float32 [32], P('head')
- grad_skip_scale: float32 [32], P('head')
- grad_norm_gain: float32 [2048], P('head')
- grad_out_proj: float32 [2048, 1024], P('head')
Inputs may be any that keep to these rules, and one draw needn't show every extreme that they name: `start_flags`: position 0 starts a sequence; there are at most two other starts among positions 1 to 2047 and at most two among the last 2047 positions, and none elsewhere, so one sequence runs from the first device of seq to the last.
All inputs are finite; a program needn't handle non-finite values.
Results may differ from a plain program's by a relative error of at most 0.011.
Values may be sent and summed in bfloat16 or wider, within the bound.
A program may use at most 192 MiB of HBM per device.

v0:
```python
import jax
import jax.numpy as jnp
from jax import lax
from jax.sharding import PartitionSpec as P

GROUP = 256


epsilon = 1e-05
highest = lax.Precision.HIGHEST


def shifted(shard, axis, by):
    size = lax.axis_size(axis)
    pairs = [(i, i + by) for i in range(size) if 0 <= i + by < size]
    return lax.ppermute(shard, axis, pairs)


def carried_in(value, axis, join, neutral, backward):
    count, mine = (lax.axis_size(axis), lax.axis_index(axis))
    pieces = jax.tree.map(lambda part: lax.all_gather(part, axis), value)
    if backward:
        pieces = jax.tree.map(lambda part: part[::-1], pieces)
        mine = count - 1 - mine
    running = jax.tree.map(
        lambda part, zero: jnp.full_like(part, 0) + jnp.asarray(zero, part.dtype), value, neutral
    )

    def lap(position, running):
        longer = join(running, jax.tree.map(lambda part: part[position], pieces))
        return jax.tree.map(lambda new, old: jnp.where(position < mine, new, old), longer, running)

    return lax.fori_loop(0, count - 1, lap, running)


def lower_ones(length):
    order = jnp.arange(length)
    return (order[:, None] >= order[None, :]).astype(jnp.float32)


def group_prefix(log_decay, group_flags):
    triangle = lower_ones(group_flags.shape[0])
    running = jnp.dot(triangle, log_decay, precision=highest)
    segment = jnp.dot(triangle, group_flags, precision=highest)
    return (running, segment)


def group_state(x_heads, b_proj, log_decay, step_size, group_flags):
    running, segment = group_prefix(log_decay, group_flags)
    same_seg = (segment == segment[-1]).astype(jnp.float32)
    weights = jnp.exp(running[-1][None, :] - running) * same_seg[:, None] * step_size
    end_state = jnp.einsum("sh,shp,sn->hpn", weights, x_heads, b_proj, precision=highest)
    carry_decay = jnp.exp(running[-1]) * (segment[-1] == 0.0).astype(jnp.float32)
    return (end_state, carry_decay)


def group_output(x_heads, b_proj, c_proj, log_decay, step_size, group_flags, start):
    running, segment = group_prefix(log_decay, group_flags)
    order = jnp.arange(group_flags.shape[0])
    same_seg = (segment[:, None] == segment[None, :]) & (order[:, None] >= order[None, :])
    pair_mask = same_seg[:, :, None]
    log_gap = running[:, None, :] - running[None, :, :]
    decays = jnp.where(pair_mask, jnp.exp(jnp.where(pair_mask, log_gap, 0.0)), 0.0)
    scores = jnp.dot(c_proj, b_proj.T, precision=highest)
    weights = scores[:, :, None] * decays * step_size[None, :, :]
    inner_part = jnp.einsum("tsh,shp->thp", weights, x_heads, precision=highest)
    entry_decay = jnp.exp(running) * (segment == 0.0).astype(jnp.float32)[:, None]
    outer_part = (
        jnp.einsum("tn,hpn->thp", c_proj, start, precision=highest) * entry_decay[:, :, None]
    )
    return inner_part + outer_part


def in_norm(token_rows, gain_vec):
    return (
        token_rows
        * lax.rsqrt(jnp.mean(token_rows * token_rows, axis=1, keepdims=True) + epsilon)
        * gain_vec
    )


def conv_front(
    extended, weight_x, weight_bc, bias_x, bias_bc, step_raw, dt_bias, a_log, keep_masks
):
    conv_weight = jnp.concatenate([weight_x, weight_bc], axis=1)
    conv_bias = jnp.concatenate([bias_x, bias_bc])
    halo_rows = conv_weight.shape[0] - 1
    length = step_raw.shape[0]
    summed = jnp.broadcast_to(conv_bias[None, :], (length, conv_bias.shape[0]))
    for offset in range(conv_weight.shape[0]):
        summed = (
            summed
            + conv_weight[offset]
            * extended[halo_rows - offset : halo_rows - offset + length]
            * keep_masks[offset][:, None]
        )
    step_size = jax.nn.softplus(step_raw + dt_bias)
    log_decay = -step_size * jnp.exp(a_log)
    return (jax.nn.silu(summed), step_size, log_decay)


def mix_gate(ssm_out, x_heads, skip_scale, gate_z):
    mixed = ssm_out + skip_scale[None, :, None] * x_heads
    return mixed.reshape(gate_z.shape) * jax.nn.silu(gate_z)


def group_starts(group_states, group_carries, incoming):
    starts = []
    current = incoming
    for position in range(group_states.shape[0]):
        starts.append(current)
        current = group_carries[position][:, None, None] * current + group_states[position]
    return jnp.stack(starts)


def device_total(group_states, group_carries):
    current = jnp.zeros_like(group_states[0])
    product = jnp.ones_like(group_carries[0])
    for position in range(group_states.shape[0]):
        current = group_carries[position][:, None, None] * current + group_states[position]
        product = product * group_carries[position]
    return (product, current)


def combine_forward(earlier, later):
    return (earlier[0] * later[0], later[0][:, None, None] * earlier[1] + later[1])


def combine_backward(earlier, later):
    return (later[0] * earlier[0], later[1] + later[0][:, None, None] * earlier[1])


def shards(
    tokens,
    start_flags,
    in_gain,
    proj_zx,
    proj_bc,
    proj_dt,
    conv_x_weight,
    conv_x_bias,
    conv_bc_weight,
    conv_bc_bias,
    dt_bias,
    a_log,
    skip_scale,
    norm_gain,
    out_proj,
    cotangent,
):
    length = tokens.shape[0]
    local_heads = a_log.shape[0]
    local_inner = proj_zx.shape[2]
    head_dim = local_inner // local_heads
    halo_rows = conv_x_weight.shape[0] - 1
    group_count = length // GROUP
    head_count = lax.axis_size("head")
    tokens_f = tokens.astype(jnp.float32)
    flag_values = start_flags.astype(jnp.float32)
    normed = in_norm(tokens_f, in_gain)
    normed_low = normed.astype(jnp.bfloat16)
    zx_raw = jnp.einsum("td,dkc->tkc", normed_low, proj_zx, preferred_element_type=jnp.float32)
    gate_z = zx_raw[:, 0]
    bc_raw = jnp.dot(normed_low, proj_bc, preferred_element_type=jnp.float32)
    step_raw = jnp.dot(normed_low, proj_dt, preferred_element_type=jnp.float32)
    conv_in = jnp.concatenate([zx_raw[:, 1], bc_raw], axis=1).astype(jnp.bfloat16)
    tail_rows, tail_flags = shifted(
        (conv_in[length - halo_rows :], flag_values[length - halo_rows :].astype(jnp.bfloat16)),
        "seq",
        1,
    )
    extended = jnp.concatenate([tail_rows, conv_in]).astype(jnp.float32)
    ext_segment = jnp.cumsum(jnp.concatenate([tail_flags.astype(jnp.float32), flag_values]))
    keep_masks = jnp.stack(
        [
            (
                ext_segment[halo_rows - offset : halo_rows - offset + length]
                == ext_segment[halo_rows:]
            ).astype(jnp.float32)
            for offset in range(halo_rows + 1)
        ]
    )
    front_values, front_pull = jax.vjp(
        lambda ext_rows, weight_x, weight_bc, bias_x, bias_bc, raw_steps, bias_steps, log_rates: conv_front(
            ext_rows,
            weight_x,
            weight_bc,
            bias_x,
            bias_bc,
            raw_steps,
            bias_steps,
            log_rates,
            keep_masks,
        ),
        extended,
        conv_x_weight.astype(jnp.float32),
        conv_bc_weight.astype(jnp.float32),
        conv_x_bias,
        conv_bc_bias,
        step_raw,
        dt_bias,
        a_log,
    )
    active, step_size, log_decay = front_values
    bc_full = lax.all_gather(
        active[:, local_inner:].astype(jnp.bfloat16), "head", axis=1, tiled=True
    ).astype(jnp.float32)
    state_dim = bc_full.shape[1] // 2
    x_heads = active[:, :local_inner].reshape(length, local_heads, head_dim)
    x_groups = x_heads.reshape(group_count, GROUP, local_heads, head_dim)
    b_groups = bc_full[:, :state_dim].reshape(group_count, GROUP, state_dim)
    c_groups = bc_full[:, state_dim:].reshape(group_count, GROUP, state_dim)
    decay_groups = log_decay.reshape(group_count, GROUP, local_heads)
    step_groups = step_size.reshape(group_count, GROUP, local_heads)
    flag_groups = flag_values.reshape(group_count, GROUP)

    def states_fn(x_part, b_part, decay_part, step_part):
        return jax.vmap(group_state)(x_part, b_part, decay_part, step_part, flag_groups)

    def outputs_fn(x_part, b_part, c_part, decay_part, step_part, start_part):
        return jax.vmap(group_output)(
            x_part, b_part, c_part, decay_part, step_part, flag_groups, start_part
        )

    (group_states, group_carries), states_pull = jax.vjp(
        states_fn, x_groups, b_groups, decay_groups, step_groups
    )
    (dev_decay, dev_state), total_pull = jax.vjp(device_total, group_states, group_carries)
    _, incoming = carried_in(
        (dev_decay, dev_state),
        "seq",
        combine_forward,
        (jnp.ones_like(dev_decay), jnp.zeros_like(dev_state)),
        False,
    )
    starts, starts_pull = jax.vjp(group_starts, group_states, group_carries, incoming)
    ssm_groups, outputs_pull = jax.vjp(
        outputs_fn, x_groups, b_groups, c_groups, decay_groups, step_groups, starts
    )
    gated_out, gate_pull = jax.vjp(
        mix_gate, ssm_groups.reshape(length, local_heads, head_dim), x_heads, skip_scale, gate_z
    )
    inner_total = local_inner * head_count
    square_sum = lax.psum(jnp.sum(gated_out * gated_out, axis=1), "head")
    inv_rms = lax.rsqrt(square_sum / inner_total + epsilon)[:, None]
    normed_out = (gated_out * inv_rms * norm_gain).astype(jnp.bfloat16)
    partial_out = jnp.dot(normed_out, out_proj, preferred_element_type=jnp.float32)
    mixed_out = (tokens_f + lax.psum(partial_out, "head")).astype(jnp.bfloat16)
    d_normed_out = jnp.einsum("td,cd->tc", cotangent, out_proj, preferred_element_type=jnp.float32)
    grad_out_proj = jnp.einsum(
        "tc,td->cd", normed_out, cotangent, preferred_element_type=jnp.float32
    )
    weighted = d_normed_out * norm_gain
    cross_sum = lax.psum(jnp.sum(weighted * gated_out, axis=1), "head")
    d_gated = weighted * inv_rms - gated_out * inv_rms**3 * (cross_sum / inner_total)[:, None]
    grad_norm_gain = jnp.sum(d_normed_out * gated_out * inv_rms, axis=0)
    d_ssm, d_skip_x, grad_skip_scale, d_gate_z = gate_pull(d_gated)
    d_x_out, d_b_out, d_c_out, d_decay_out, d_step_out, d_starts = outputs_pull(
        d_ssm.reshape(ssm_groups.shape)
    )
    d_states_a, d_carries_a, d_incoming = starts_pull(d_starts)
    _, d_dev_state = carried_in(
        (dev_decay, d_incoming),
        "seq",
        combine_backward,
        (jnp.ones_like(dev_decay), jnp.zeros_like(d_incoming)),
        True,
    )
    d_dev_decay = jnp.sum(d_dev_state * incoming, axis=(1, 2))
    d_states_b, d_carries_b = total_pull((d_dev_decay, d_dev_state))
    d_x_state, d_b_state, d_decay_state, d_step_state = states_pull(
        (d_states_a + d_states_b, d_carries_a + d_carries_b)
    )
    d_b_total = (d_b_out + d_b_state).reshape(length, state_dim)
    d_c_total = d_c_out.reshape(length, state_dim)
    d_bc_slice = lax.psum_scatter(
        jnp.concatenate([d_b_total, d_c_total], axis=1), "head", scatter_dimension=1, tiled=True
    )
    d_x_total = (d_x_out + d_x_state).reshape(length, local_inner) + d_skip_x.reshape(
        length, local_inner
    )
    d_active = jnp.concatenate([d_x_total, d_bc_slice], axis=1)
    d_step_total = (d_step_out + d_step_state).reshape(length, local_heads)
    d_decay_total = (d_decay_out + d_decay_state).reshape(length, local_heads)
    (
        d_ext,
        grad_conv_x_weight,
        grad_conv_bc_weight,
        grad_conv_x_bias,
        grad_conv_bc_bias,
        d_step_raw,
        grad_dt_bias,
        grad_a_log,
    ) = front_pull((d_active, d_step_total, d_decay_total))
    back_rows = shifted(d_ext[:halo_rows], "seq", -1)
    d_conv_in = d_ext[halo_rows:] + jnp.concatenate(
        [jnp.zeros((length - halo_rows, d_ext.shape[1]), jnp.float32), back_rows]
    )
    d_bc_low = d_conv_in[:, local_inner:].astype(jnp.bfloat16)
    d_zx = jnp.stack(
        [d_gate_z.astype(jnp.bfloat16), d_conv_in[:, :local_inner].astype(jnp.bfloat16)], axis=1
    )
    d_step_low = d_step_raw.astype(jnp.bfloat16)
    grad_proj_zx = jnp.einsum("td,tkc->dkc", normed_low, d_zx, preferred_element_type=jnp.float32)
    grad_proj_bc = jnp.einsum("td,tc->dc", normed_low, d_bc_low, preferred_element_type=jnp.float32)
    grad_proj_dt = jnp.einsum(
        "td,th->dh", normed_low, d_step_low, preferred_element_type=jnp.float32
    )
    d_normed_part = jnp.einsum("tkc,dkc->td", d_zx, proj_zx, preferred_element_type=jnp.float32)
    d_normed_part = d_normed_part + jnp.einsum(
        "tc,dc->td", d_bc_low, proj_bc, preferred_element_type=jnp.float32
    )
    d_normed_part = d_normed_part + jnp.einsum(
        "th,dh->td", d_step_low, proj_dt, preferred_element_type=jnp.float32
    )
    d_normed = lax.psum(d_normed_part, "head")
    _, norm_pull = jax.vjp(in_norm, tokens_f, in_gain)
    d_tokens, grad_in_gain = norm_pull(d_normed)
    grad_tokens = cotangent.astype(jnp.float32) + d_tokens
    seq_sums = lax.psum(
        (
            grad_in_gain,
            grad_proj_zx,
            grad_proj_bc,
            grad_proj_dt,
            grad_conv_x_weight,
            grad_conv_x_bias,
            grad_conv_bc_weight,
            grad_conv_bc_bias,
            grad_dt_bias,
            grad_a_log,
            grad_skip_scale,
            grad_norm_gain,
            grad_out_proj,
        ),
        "seq",
    )
    return (
        mixed_out,
        grad_tokens,
        seq_sums[0],
        seq_sums[1],
        seq_sums[2],
        seq_sums[3],
        seq_sums[4],
        seq_sums[5],
        seq_sums[6],
        seq_sums[7],
        seq_sums[8],
        seq_sums[9],
        seq_sums[10],
        seq_sums[11],
        seq_sums[12],
    )


def solution(mesh):
    in_specs = (
        P("seq", None),
        P("seq"),
        P(),
        P(None, None, "head"),
        P(None, "head"),
        P(None, "head"),
        P(None, "head"),
        P("head"),
        P(None, "head"),
        P("head"),
        P("head"),
        P("head"),
        P("head"),
        P("head"),
        P("head", None),
        P("seq", None),
    )
    out_specs = (
        P("seq", None),
        P("seq", None),
        P(),
        P(None, None, "head"),
        P(None, "head"),
        P(None, "head"),
        P(None, "head"),
        P("head"),
        P(None, "head"),
        P("head"),
        P("head"),
        P("head"),
        P("head"),
        P("head"),
        P("head", None),
    )
    return jax.shard_map(shards, mesh=mesh, in_specs=in_specs, out_specs=out_specs, check_vma=False)
```

profile of v0, /device:TPU:0, one launch (start us, length us, event | category | flops | bytes accessed | tf_op | source)
XLA Modules:
  0.0 1124.4 jit_solution(15614918690741895448)
XLA Ops:
  55.7 19.6 %all-gather.5.cloned.1.call-done = bf16[2048,256]{0,1:T(8,128)(2,1)} async-done(((bf16[2048,64]{0,1:T(8,128)(2,1)}), bf16[2048,256]{0,1:T(8,128)(2,1)}) %all-gather.5.cloned.1.call-update) | async-done | bytes 1048592 | tf_op jit(solution)/shard_map/all_gather | solution.py:205
  86.5 9.1 all-gather
  106.3 6.9 all-gather.7.cloned.1.call-done
  113.2 7.6 while.28
  135.3 21.3 %bitcast_add_fusion.4 = f32[8,256,8,64]{1,3,2,0:T(8,128)S(1)} fusion(f32[8,256,8,64]{1,3,2,0:T(8,128)S(1)} %fusion.149, f32[8,256,8]{1,2,0:T(8,128)S(1)} %copy-done.53, f32[8,256,8]{1,2,0:T(8,128)S(1)} %bitcast.417, f32[8,256,8]{1,2,0:T(8,128)S(1)} %bitcast.411, f32[8,256,256]{2,1,0:T(8,128)S(1)} %copy-done.44, pred[8,256,256]{2,1,0:T(8,128)(4,1)S(1)} %copy-done.57, ...), kind=kOutput, calls=%fused_computation.76 | convolution fusion | flops 3244294144 | bytes 15400960 | tf_op jit(solution)/shard_map/jvp(vmap(tsh,shp->thp))/dot_general | solution.py:66
  164.3 12.6 %psum.119 = f32[2048]{0:T(1024)} all-reduce(f32[2048]{0:T(1024)S(1)} %get-tuple-element.397), channel_id=1, replica_groups=mesh['seq'=8,'head'=4] {'head'}, use_global_device_ids=true, to_apply=%region_6.7 | all-reduce | flops 2048 | bytes 16384 | tf_op jit(solution)/shard_map/psum | solution.py:244
  178.1 9.0 multiply_reduce_fusion.6
  187.1 9.2 psum.121
  197.0 11.1 multiply_reduce_fusion.7
  213.8 8.7 fusion.85
  224.1 34.0 %fusion.13 = (f32[8,256,8]{1,2,0:T(8,128)}, f32[8,256,8]{1,2,0:T(8,128)}, f32[8,256,8]{1,2,0:T(8,128)}, f32[8,256,256]{2,1,0:T(8,128)S(1)}) fusion(f32[8,256,8]{1,2,0:T(8,128)S(1)} %bitcast.418, f32[8,256,8]{1,2,0:T(8,128)S(1)} %bitcast.412, f32[8,256,256]{2,1,0:T(8,128)} %fusion.148, pred[8,256,256]{2,1,0:T(8,128)(4,1)} %compare_and_fusion, ...), kind=kOutput, calls=%fused_computation.26 | convolution fusion | flops 3283566592 | bytes 13434880 | tf_op jit(solution)/shard_map/transpose(jvp(vmap(tsh,shp->thp)))/dot_general | solution.py:66
  282.1 16.0 %while.29 = (s32[]{:T(128)}, f32[8,64,128]{2,1,0:T(8,128)S(1)}, s32[]{:T(128)}, f32[8,8,64,128]{3,2,1,0:T(8,128)}, f32[8,8]{1,0:T(8,128)}, /*index=5*/s32[]{:T(128)}, s32[]{:T(128)}) while((s32[]{:T(128)}, f32[8,64,128]{2,1,0:T(8,128)S(1)}, s32[]{:T(128)}, f32[8,8,64,128]{3,2,1,0:T(8,128)}, f32[8,8]{1,0:T(8,128)}, ...), condition=%wide.region_11.12_spmd.clone, body=%wide.region_10.11_spmd.clone.sunk | while | flops 262148 | bytes 786633 | solution.py:33
  304.1 7.6 fusion.82
  320.6 7.4 fusion.137
  331.0 16.7 %bitcast_add_fusion.3 = f32[8,256,8,64]{1,3,2,0:T(8,128)S(1)} fusion(f32[8,256,8,64]{1,3,2,0:T(8,128)S(1)} %fusion.139, f32[8,256,8]{1,2,0:T(8,128)S(1)} %copy-done.62, f32[8,256,8]{1,2,0:T(8,128)S(1)} %bitcast.419, f32[8,256,8]{1,2,0:T(8,128)S(1)} %bitcast.413, f32[8,256,256]{2,1,0:T(8,128)S(1)} %copy-done.45, pred[8,256,256]{2,1,0:T(8,128)(4,1)S(1)} %copy-done.58, ...), kind=kOutput, calls=%fused_computation.72 | convolution fusion | flops 3244294144 | bytes 15400960 | tf_op jit(solution)/shard_map/transpose(jvp(vmap(tsh,shp->thp)))/dot_general | solution.py:66
  354.8 6.1 multiply_add_fusion.1
  363.1 13.8 %multiply_reduce_fusion.4 = (f32[576]{0:T(1024)S(1)}, f32[576]{0:T(1024)S(1)}, f32[576]{0:T(1024)S(1)}, f32[576]{0:T(1024)S(1)}, f32[576]{0:T(1024)S(1)}, /*index=5*/f32[2048,576]{0,1:T(8,128)S(1)}) fusion(f32[2051,576]{0,1:T(8,128)} %copy-done.1, f32[2048]{0:T(1024)S(1)} %copy-done.94, f32[2048]{0:T(1024)S(1)} %copy-done.96, f32[2048]{0:T(1024)S(1)} %copy-done.98, ...), kind=kLoop, calls=%fused_computation.58 | loop fusion | flops 27129024 | bytes 33074432 | tf_op jit(solution)/shard_map/transpose(jvp())/reduce_sum | solution.py:93
  389.6 6.2 fusion.43
  419.6 84.7 %all-reduce.56.cloned.1.call-done = (f32[1024,2,512]{2,0,1:T(8,128)}, f32[1024,64]{0,1:T(8,128)}, f32[512,1024]{1,0:T(8,128)}) async-done(((f32[1024,2,512]{2,0,1:T(8,128)}, f32[1024,64]{0,1:T(8,128)}, f32[512,1024]{1,0:T(8,128)}), (f32[1024,2,512]{2,0,1:T(8,128)}, f32[1024,64]{0,1:T(8,128)}, f32[512,1024]{1,0:T(8,128)})) %all-reduce.56.cloned.1.call-update) | async-done | bytes 6553616 | tf_op jit(solution)/shard_map/psum | solution.py:320
  504.3 7.7 copy.138
  511.9 559.0 %all-reduce.58.cloned.1.call-done = (f32[2048,1024]{1,0:T(8,128)}, f32[2048,1024]{1,0:T(8,128)}) async-done(((f32[2048,1024]{1,0:T(8,128)}, f32[2048,1024]{1,0:T(8,128)}), (f32[2048,1024]{1,0:T(8,128)}, f32[2048,1024]{1,0:T(8,128)})) %all-reduce.58.cloned.1.call-update) | async-done | bytes 16777232 | tf_op jit(solution)/shard_map/psum | solution.py:248
  1070.9 7.1 fusion.15
  1079.3 9.0 fusion.16
  1088.3 25.1 %all-reduce.50 = (f32[1024]{0:T(1024)}, f32[1024,8]{0,1:T(8,128)}, f32[4,512]{1,0:T(4,128)}, f32[512]{0:T(512)}, f32[4,64]{1,0:T(4,128)}, /*index=5*/f32[64]{0:T...) all-reduce(f32[1024]{0:T(1024)S(1)} %get-tuple-element.305, ...), channel_id=1, replica_groups=mesh['seq'=8,'head'=4] {'seq'}, use_global_device_ids=true, to_apply=%region_38.39 | all-reduce | flops 12632 | bytes 101056 | tf_op jit(solution)/shard_map/psum | solution.py:320
  (561 shorter events, 215.2 us)
Async XLA Ops:
  7.2 68.1 %all-gather.5.cloned.1.call-start = ((), (), s32[]{:S(2)}) async-start(), calls=%async_computation.1 | async-start | bytes 1310720 | tf_op jit(solution)/shard_map/all_gather | solution.py:205
  21.7 13.3 %collective-permute-start = (bf16[3,576]{0,1:T(8,128)(2,1)S(1)}, bf16[3,576]{0,1:T(8,128)(2,1)S(1)}, u32[]{:S(2)}, u32[]{:S(2)}) collective-permute-start(bf16[3,576]{0,1:T(8,128)(2,1)S(1)} %pad_maximum_fusion.5), channel_id=1, source_target_pairs={{0,4},{4,8},{8,12},{12,16},{16,20},{20,24},{24,28},{1,5},{5,9},{9,... | collective-permute-start | bytes 10376 | tf_op jit(solution)/shard_map/ppermute | solution.py:16
  24.2 10.0 collective-permute-start.1
  46.9 66.3 %all-gather.7.cloned.1.call-start = ((), (), s32[]{:S(2)}) async-start(), calls=%async_computation.2 | async-start | bytes 2359296 | tf_op jit(solution)/shard_map/all_gather | solution.py:21
  47.9 35.5 %copy-start.153 = (f32[8]{0:T(128)}, f32[8]{0:T(128)S(1)}, u32[]{:S(2)}) copy-start(f32[8]{0:T(128)S(1)} %broadcast_multiply_fusion.1) | copy-start | bytes 100
  48.5 34.9 %copy-start.125 = (f32[8]{0:T(128)}, f32[8]{0:T(128)S(1)}, u32[]{:S(2)}) copy-start(f32[8]{0:T(128)S(1)} %get-tuple-element.456) | copy-start | bytes 100
  48.5 34.9 %copy-start.129 = (f32[8]{0:T(128)}, f32[8]{0:T(128)S(1)}, u32[]{:S(2)}) copy-start(f32[8]{0:T(128)S(1)} %get-tuple-element.457) | copy-start | bytes 100
  48.5 34.9 %copy-start.133 = (f32[8]{0:T(128)}, f32[8]{0:T(128)S(1)}, u32[]{:S(2)}) copy-start(f32[8]{0:T(128)S(1)} %get-tuple-element.458) | copy-start | bytes 100
  48.5 35.0 %copy-start.136 = (f32[8]{0:T(128)}, f32[8]{0:T(128)S(1)}, u32[]{:S(2)}) copy-start(f32[8]{0:T(128)S(1)} %get-tuple-element.465) | copy-start | bytes 100
  48.5 35.0 %copy-start.139 = (f32[8]{0:T(128)}, f32[8]{0:T(128)S(1)}, u32[]{:S(2)}) copy-start(f32[8]{0:T(128)S(1)} %get-tuple-element.459) | copy-start | bytes 100
  48.5 35.0 %copy-start.143 = (f32[8]{0:T(128)}, f32[8]{0:T(128)S(1)}, u32[]{:S(2)}) copy-start(f32[8]{0:T(128)S(1)} %get-tuple-element.460) | copy-start | bytes 100
  48.5 35.0 %copy-start.155 = (f32[8]{0:T(128)}, f32[8]{0:T(128)S(1)}, u32[]{:S(2)}) copy-start(f32[8]{0:T(128)S(1)} %get-tuple-element.461) | copy-start | bytes 100
  85.6 193.3 %all-gather.9.cloned.1.call-start = ((), (), s32[]{:S(2)}) async-start(), calls=%async_computation.3 | async-start | bytes 2359296 | tf_op jit(solution)/shard_map/all_gather | solution.py:21
  224.0 139.0 %reduce-scatter.2.cloned.1.call-start = ((), (), s32[]{:S(2)}) async-start(), calls=%async_computation.4 | async-start | bytes 2621440 | tf_op jit(solution)/shard_map/reduce_scatter | solution.py:276
  224.1 35.3 %copy-start.27 = (bf16[8,256,128]{2,1,0:T(8,128)(2,1)S(1)}, bf16[8,256,128]{2,1,0:T(8,128)(2,1)}, u32[]{:S(2)}) copy-start(bf16[8,256,128]{2,1,0:T(8,128)(2,1)} %copy.114) | copy-start | bytes 1572868
  224.1 35.3 %copy-start.33 = (f32[8,256,128]{2,1,0:T(8,128)S(1)}, f32[8,256,128]{2,1,0:T(8,128)}, u32[]{:S(2)}) copy-start(f32[8,256,128]{2,1,0:T(8,128)} %fusion.85) | copy-start | bytes 3145732
  320.4 183.9 %all-reduce.56.cloned.1.call-start = ((), (), s32[]{:S(2)}) async-start(), calls=%async_computation.5 | async-start | bytes 13107200 | tf_op jit(solution)/shard_map/psum | solution.py:320
  379.4 5.9 collective-permute-start.2
  395.9 675.0 %all-reduce.58.cloned.1.call-start = ((), (), s32[]{:S(2)}) async-start(), calls=%async_computation.6 | async-start | bytes 33554432 | tf_op jit(solution)/shard_map/psum | solution.py:248
  419.5 92.5 %copy-start.149 = (f32[1,576]{1,0:T(1,128)}, f32[1,576]{1,0:T(1,128)S(1)}, u32[]{:S(2)}) copy-start(f32[1,576]{1,0:T(1,128)S(1)} %broadcast_in_dim.182) | copy-start | bytes 6916
  419.6 92.4 %copy-start.122 = (f32[4,576]{1,0:T(4,128)}, f32[4,576]{1,0:T(4,128)S(1)}, u32[]{:S(2)}) copy-start(f32[4,576]{1,0:T(4,128)S(1)} %pad_add_fusion.2) | copy-start | bytes 27652
  504.2 566.7 %copy-start.92 = (f32[2048]{0:T(1024)S(1)}, f32[2048]{0:T(1024)}, u32[]{:S(2)}) copy-start(f32[2048]{0:T(1024)} %copy-done.91) | copy-start | bytes 24580
  504.3 566.7 %copy-start.113 = (f32[1024]{0:T(1024)S(1)}, f32[1024]{0:T(1024)}, u32[]{:S(2)}) copy-start(f32[1024]{0:T(1024)} %param.22) | copy-start | bytes 12292
  1079.2 34.2 %copy-start.89 = (f32[1024,64]{0,1:T(8,128)S(1)}, f32[1024,64]{0,1:T(8,128)}, u32[]{:S(2)}) copy-start(f32[1024,64]{0,1:T(8,128)} %get-tuple-element.590) | copy-start | bytes 786436
  (179 other events, 1184.8 us)
Sparse Core Ops, SparseCore 0:
  47.0 28.2 all-gather.4
  85.8 27.3 all-gather.6
  224.2 26.5 all-gather.8
  320.5 42.5 reduce-scatter.1
  396.0 108.2 all-reduce.55
  507.5 563.3 all-reduce.57
where the time goes:
time: 1130 us; the launch traced here: 1120 us
  waiting for transfers between devices  672 us (59%)
  matrix products  166 us (15%)
  other arithmetic  126 us (11%)
  local copies, waits for them, and re-layouts  78.4 us (7%)
  blocking collectives  56 us (5%)
  between operations  16.9 us (1%)
    psum x1, waiting for transfers between devices, shards(): mixed_out = (tokens_f + lax.psum(partial_out, 'head')).astype(jnp.bfloat16)  559 us
    psum x1, waiting for transfers between devices, shards(): lax.psum((grad_in_gain, grad_proj_zx, grad_proj_bc, grad_proj_dt, grad_co...  84.7 us
    dot_general x3, matrix products, group_output(): inner_part = jnp.einsum('tsh,shp->thp', weights, x_heads, precision=highest)  71.9 us
    unnamed x394, local copies, waits for them, and re-layouts  43.5 us
    psum x1, blocking collectives, shards(): lax.psum((grad_in_gain, grad_proj_zx, grad_proj_bc, grad_proj_dt, grad_co...  25.1 us
  transfers between devices with their start and end apart: 9, of which 5 were waited for; matrix products, arithmetic and copies ran while one was open for 14% of the time, Pallas kernels for 0%

commit v1 on v0

--- a/solution.py
+++ b/solution.py
@@ -1,9 +1,409 @@
+import functools
 import jax
 import jax.numpy as jnp
 from jax import lax
+from jax.experimental import pallas as pl
+from jax.experimental.pallas import tpu as pltpu
 from jax.sharding import PartitionSpec as P
 
 GROUP = 256
+MESH = pl.DeviceIdType.MESH
+f32 = jnp.float32
+bf16 = jnp.bfloat16
+
+
+def rows_of(ref, start, size):
+    return ref.at[pl.ds(pl.multiple_of(start, size), size)]
+
+
+def greet(pairs):
+    barrier = pltpu.get_barrier_semaphore()
+    for live, where in pairs:
+        @pl.when(live)
+        def _():
+            pl.semaphore_signal(barrier, inc=1, device_id=where, device_id_type=MESH)
+    pl.semaphore_wait(barrier, sum(live.astype(jnp.int32) for live, _ in pairs))
+
+
+def greet_axis(axis):
+    barrier = pltpu.get_barrier_semaphore()
+    size, mine = lax.axis_size(axis), lax.axis_index(axis)
+
+    @pl.loop(1, size)
+    def _(k):
+        pl.semaphore_signal(
+            barrier, inc=1, device_id={axis: lax.rem(mine + k, size)}, device_id_type=MESH
+        )
+    pl.semaphore_wait(barrier, size - 1)
+
+
+class LineSum:
+    def __init__(self, own, out, acc, rin, rx, sems, block):
+        self.own, self.out, self.acc, self.rin, self.rx = own, out, acc, rin, rx
+        self.send1, self.got_in, self.got_x, self.got_out, self.send2 = (
+            sems.at[0], sems.at[1], sems.at[2], sems.at[3], sems.at[4])
+        self.block = block
+        size, me = lax.axis_size("head"), lax.axis_index("head")
+        half = size // 2
+        self.size = size
+        left = me < half
+        self.mid = (me == half - 1) | (me == half)
+        self.has_outer = (me > 0) & (me < size - 1)
+        self.inner = jnp.where(left, me + 1, me - 1)
+        outer = jnp.where(left, me - 1, me + 1)
+        self.outer = jnp.clip(outer, 0, size - 1)
+        self.lag = max(1, half - 1)
+
+    def pairs(self):
+        return [(self.inner >= 0, {"head": self.inner}), (self.has_outer, {"head": self.outer})]
+
+    def copy(self, src, dst, b, send, recv, to):
+        return pltpu.make_async_remote_copy(
+            src_ref=rows_of(src, b * self.block, self.block),
+            dst_ref=rows_of(dst, b * self.block, self.block),
+            send_sem=send.at[b], recv_sem=recv.at[b],
+            device_id={"head": to}, device_id_type=MESH)
+
+    def inward(self, b):
+        rows = pl.ds(pl.multiple_of(b * self.block, self.block), self.block)
+
+        @pl.when(self.has_outer)
+        def _():
+            self.copy(self.acc, self.rin, b, self.send1, self.got_in, self.outer).wait_recv()
+            self.acc[rows] = (self.rin[rows].astype(f32) + self.own[rows].astype(f32)).astype(bf16)
+
+        @pl.when(jnp.logical_not(self.has_outer))
+        def _():
+            self.acc[rows] = self.own[rows]
+
+        @pl.when(self.mid)
+        def _():
+            self.copy(self.acc, self.rx, b, self.send1, self.got_x, self.inner).start()
+
+        @pl.when(jnp.logical_not(self.mid))
+        def _():
+            self.copy(self.acc, self.rin, b, self.send1, self.got_in, self.inner).start()
+
+    def outward(self, b, done=None):
+        rows = pl.ds(pl.multiple_of(b * self.block, self.block), self.block)
+
+        @pl.when(self.mid)
+        def _():
+            self.copy(self.acc, self.rx, b, self.send1, self.got_x, self.inner).wait_recv()
+            total = self.acc[rows].astype(f32) + self.rx[rows].astype(f32)
+            if done is not None:
+                total = done(rows, total)
+            self.out[rows] = total.astype(bf16)
+
+        @pl.when(jnp.logical_not(self.mid))
+        def _():
+            self.copy(self.out, self.out, b, self.send2, self.got_out, self.inner).wait_recv()
+
+        @pl.when(self.has_outer)
+        def _():
+            self.copy(self.out, self.out, b, self.send2, self.got_out, self.outer).start()
+
+    def drain(self, count):
+        @pl.loop(0, count)
+        def _(b):
+            self.copy(self.acc, self.rin, b, self.send1, self.got_in, self.inner).wait_send()
+
+            @pl.when(self.has_outer)
+            def _():
+                self.copy(self.out, self.out, b, self.send2, self.got_out, self.outer).wait_send()
+
+    def run(self, first, last, count, done=None):
+        @pl.loop(first, last)
+        def _(b):
+            @pl.when(b < count)
+            def _():
+                self.inward(b)
+
+            @pl.when(b >= self.lag)
+            def _():
+                self.outward(b - self.lag, done)
+
+
+class PlaneSum:
+    def __init__(self, own, slots, res, sems, owners):
+        self.own, self.slots, self.res = own, slots, res
+        self.rs_send, self.rs_got, self.ag_send, self.ag_got = (
+            sems.at[0], sems.at[1], sems.at[2], sems.at[3])
+        self.owners = owners
+        self.size, self.me = lax.axis_size("seq"), lax.axis_index("seq")
+        self.piece = own.shape[0] // owners
+
+    def part(self, ref, k):
+        return rows_of(ref, k * self.piece, self.piece)
+
+    def scatter_copy(self, to, source):
+        return pltpu.make_async_remote_copy(
+            src_ref=self.part(self.own, to), dst_ref=self.slots.at[source],
+            send_sem=self.rs_send.at[to], recv_sem=self.rs_got.at[source],
+            device_id={"seq": to}, device_id_type=MESH)
+
+    def gather_copy(self, owner, to):
+        return pltpu.make_async_remote_copy(
+            src_ref=self.part(self.res, owner), dst_ref=self.part(self.res, owner),
+            send_sem=self.ag_send.at[to], recv_sem=self.ag_got.at[owner],
+            device_id={"seq": to}, device_id_type=MESH)
+
+    def scatter(self):
+        @pl.loop(1, self.size)
+        def _(k):
+            to = lax.rem(self.me + k, self.size)
+
+            @pl.when(to < self.owners)
+            def _():
+                self.scatter_copy(to, self.me).start()
+
+    def reduce(self):
+        @pl.when(self.me < self.owners)
+        def _():
+            @pl.loop(1, self.size)
+            def _(k):
+                source = lax.rem(self.me + k, self.size)
+                self.scatter_copy(self.me, source).wait_recv()
+            mine = pl.ds(pl.multiple_of(self.me * self.piece, self.piece), self.piece)
+            self.slots[self.me] = self.own[mine]
+            total = self.slots[0].astype(f32)
+            for k in range(1, self.size):
+                total = total + self.slots[k].astype(f32)
+            self.res[mine] = total.astype(self.res.dtype)
+
+            @pl.loop(1, self.size)
+            def _(k):
+                self.gather_copy(self.me, lax.rem(self.me + k, self.size)).start()
+
+    def finish(self):
+        @pl.loop(1, self.size)
+        def _(k):
+            other = lax.rem(self.me + k, self.size)
+
+            @pl.when(other < self.owners)
+            def _():
+                self.gather_copy(other, self.me).wait_recv()
+                self.scatter_copy(other, self.me).wait_send()
+
+        @pl.when(self.me < self.owners)
+        def _():
+            @pl.loop(1, self.size)
+            def _(k):
+                self.gather_copy(self.me, lax.rem(self.me + k, self.size)).wait_send()
+
+
+def line_sum_kernel(block, own, out, acc, rin, rx, sems):
+    line = LineSum(own, out, acc, rin, rx, sems, block)
+    greet(line.pairs())
+    count = own.shape[0] // block
+    line.run(0, count + line.lag, count)
+    line.drain(count)
+
+
+VMEM = pl.BlockSpec(memory_space=pltpu.VMEM)
+
+
+def line_sum(part, block=128):
+    rows, width = part.shape
+    slot = pltpu.VMEM((rows, width), bf16)
+    return pl.pallas_call(
+        functools.partial(line_sum_kernel, block),
+        out_shape=jax.ShapeDtypeStruct((rows, width), bf16),
+        in_specs=[VMEM], out_specs=VMEM,
+        scratch_shapes=[slot, slot, slot, pltpu.SemaphoreType.DMA((5, rows // block))],
+        compiler_params=pltpu.CompilerParams(
+            collective_id=1, has_side_effects=True, vmem_limit_bytes=48 * 2**20),
+        name="line_sum",
+    )(part)
+
+
+def tail_kernel(block, owners, part, zx, op, bc, small,
+                out, zx_out, op_out, bc_out, small_out,
+                acc, rin, rx, zx_slots, op_slots, bc_slots, bc_z, small_slots, small_z,
+                line_sems, zx_sems, op_sems, bc_sems, bcz_sems, small_sems, smallz_sems):
+    seq, heads = lax.axis_size("seq"), lax.axis_size("head")
+    me, my_head = lax.axis_index("seq"), lax.axis_index("head")
+    line = LineSum(part, out, acc, rin, rx, line_sems, block)
+    sums = [PlaneSum(zx, zx_slots, zx_out, zx_sems, owners[0]),
+            PlaneSum(op, op_slots, op_out, op_sems, owners[1])]
+    barrier = pltpu.get_barrier_semaphore()
+    for axis, size, mine in (("seq", seq, me), ("head", heads, my_head)):
+        @pl.loop(1, size)
+        def _(k):
+            pl.semaphore_signal(barrier, inc=1, device_id={axis: lax.rem(mine + k, size)},
+                                device_id_type=MESH)
+    pl.semaphore_wait(barrier, seq + heads - 2)
+
+    piece = bc.shape[1] // owners[2]
+
+    def bc_scatter(to, source):
+        return pltpu.make_async_remote_copy(
+            src_ref=bc.at[:, pl.ds(pl.multiple_of(to * piece, piece), piece)],
+            dst_ref=bc_slots.at[source], send_sem=bc_sems.at[0, to], recv_sem=bc_sems.at[1, source],
+            device_id={"seq": to}, device_id_type=MESH)
+
+    def bc_gather(owner, to):
+        rows = pl.ds(pl.multiple_of(owner * piece, piece), piece)
+        return pltpu.make_async_remote_copy(
+            src_ref=bc_out.at[rows], dst_ref=bc_out.at[rows],
+            send_sem=bc_sems.at[2, to], recv_sem=bc_sems.at[3, owner],
+            device_id={"seq": to}, device_id_type=MESH)
+
+    def bc_swap(to, source):
+        return pltpu.make_async_remote_copy(
+            src_ref=bc_slots.at[me, to], dst_ref=bc_z.at[source],
+            send_sem=bcz_sems.at[0, to], recv_sem=bcz_sems.at[1, source],
+            device_id={"head": to}, device_id_type=MESH)
+
+    def small_send(to, source):
+        return pltpu.make_async_remote_copy(
+            src_ref=small, dst_ref=small_slots.at[source],
+            send_sem=small_sems.at[0, to], recv_sem=small_sems.at[1, source],
+            device_id={"seq": to}, device_id_type=MESH)
+
+    both = small_z.shape[1]
+    lone = small.shape[0] - both
+
+    def small_swap(to, source):
+        return pltpu.make_async_remote_copy(
+            src_ref=small_z.at[my_head], dst_ref=small_z.at[source],
+            send_sem=smallz_sems.at[0, to], recv_sem=smallz_sems.at[1, source],
+            device_id={"head": to}, device_id_type=MESH)
+
+    for each in sums:
+        each.scatter()
+
+    @pl.loop(1, seq)
+    def _(k):
+        to = lax.rem(me + k, seq)
+
+        @pl.when(to < owners[2])
+        def _():
+            bc_scatter(to, me).start()
+        small_send(to, me).start()
+
+    count = part.shape[0] // block
+    steps = count + line.lag
+    cut1, cut2 = (steps * 7) // 16, (steps * 10) // 16
+    line.run(0, cut1, count)
+
+    for each in sums:
+        each.reduce()
+
+    @pl.loop(1, seq)
+    def _(k):
+        small_send(me, lax.rem(me + k, seq)).wait_recv()
+    small_slots[me] = small[...]
+    total = small_slots[0]
+    for k in range(1, seq):
+        total = total + small_slots[k]
+    small_out[0:lone] = total[0:lone]
+    small_z[my_head] = total[lone:]
+
+    @pl.when(me < owners[2])
+    def _():
+        @pl.loop(1, seq)
+        def _(k):
+            bc_scatter(me, lax.rem(me + k, seq)).wait_recv()
+        bc_slots[me] = bc[:, pl.ds(pl.multiple_of(me * piece, piece), piece)]
+        total = bc_slots[0]
+        for k in range(1, seq):
+            total = total + bc_slots[k]
+        bc_slots[me] = total
+        bc_z[my_head] = bc_slots[me, my_head]
+
+    @pl.loop(1, heads)
+    def _(k):
+        to = lax.rem(my_head + k, heads)
+        small_swap(to, my_head).start()
+
+        @pl.when(me < owners[2])
+        def _():
+            bc_swap(to, my_head).start()
+
+    line.run(cut1, cut2, count)
+
+    @pl.loop(1, heads)
+    def _(k):
+        source = lax.rem(my_head + k, heads)
+        small_swap(my_head, source).wait_recv()
+
+        @pl.when(me < owners[2])
+        def _():
+            bc_swap(my_head, source).wait_recv()
+    total = small_z[0]
+    for k in range(1, heads):
+        total = total + small_z[k]
+    small_out[lone:] = total
+
+    @pl.when(me < owners[2])
+    def _():
+        total = bc_z[0]
+        for k in range(1, heads):
+            total = total + bc_z[k]
+        bc_out[pl.ds(pl.multiple_of(me * piece, piece), piece)] = total
+
+        @pl.loop(1, seq)
+        def _(k):
+            bc_gather(me, lax.rem(me + k, seq)).start()
+
+    line.run(cut2, steps, count)
+    line.drain(count)
+    for each in sums:
+        each.finish()
+
+    @pl.loop(1, seq)
+    def _(k):
+        other = lax.rem(me + k, seq)
+        small_send(other, me).wait_send()
+
+        @pl.when(other < owners[2])
+        def _():
+            bc_gather(other, me).wait_recv()
+            bc_scatter(other, me).wait_send()
+
+        @pl.when(me < owners[2])
+        def _():
+            bc_gather(me, other).wait_send()
+
+    @pl.loop(1, heads)
+    def _(k):
+        to = lax.rem(my_head + k, heads)
+        small_swap(to, my_head).wait_send()
+
+        @pl.when(me < owners[2])
+        def _():
+            bc_swap(to, my_head).wait_send()
+
+
+def tail(part, zx, op, bc, small, both, block=128):
+    seq, heads = lax.axis_size("seq"), lax.axis_size("head")
+    rows, width = part.shape
+    owners = (min(seq, zx.shape[0] // 16), min(seq, op.shape[0] // 16), min(seq, bc.shape[1] // 8))
+    slot = pltpu.VMEM((rows, width), bf16)
+    dma = pltpu.SemaphoreType.DMA
+    piece = bc.shape[1] // owners[2]
+    return pl.pallas_call(
+        functools.partial(tail_kernel, block, owners),
+        out_shape=(jax.ShapeDtypeStruct((rows, width), bf16),
+                   jax.ShapeDtypeStruct(zx.shape, bf16), jax.ShapeDtypeStruct(op.shape, bf16),
+                   jax.ShapeDtypeStruct(bc.shape[1:], f32), jax.ShapeDtypeStruct(small.shape, f32)),
+        in_specs=[VMEM] * 5, out_specs=(VMEM,) * 5,
+        scratch_shapes=[
+            slot, slot, slot,
+            pltpu.VMEM((seq, zx.shape[0] // owners[0], zx.shape[1]), bf16),
+            pltpu.VMEM((seq, op.shape[0] // owners[1], op.shape[1]), bf16),
+            pltpu.VMEM((seq, heads, piece, bc.shape[2]), f32),
+            pltpu.VMEM((heads, piece, bc.shape[2]), f32),
+            pltpu.VMEM((seq,) + small.shape, f32),
+            pltpu.VMEM((heads, both, small.shape[1]), f32),
+            dma((5, rows // block)), dma((4, seq)), dma((4, seq)), dma((4, seq)),
+            dma((2, heads)), dma((2, seq)), dma((2, heads)),
+        ],
+        compiler_params=pltpu.CompilerParams(
+            collective_id=2, has_side_effects=True, vmem_limit_bytes=56 * 2**20),
+        name="tail",
+    )(part, zx, op, bc, small)
 
 
 epsilon = 1e-05
@@ -245,7 +645,7 @@
     inv_rms = lax.rsqrt(square_sum / inner_total + epsilon)[:, None]
     normed_out = (gated_out * inv_rms * norm_gain).astype(jnp.bfloat16)
     partial_out = jnp.dot(normed_out, out_proj, preferred_element_type=jnp.float32)
-    mixed_out = (tokens_f + lax.psum(partial_out, "head")).astype(jnp.bfloat16)
+    mixed_out = (tokens_f + line_sum(partial_out.astype(jnp.bfloat16)).astype(jnp.float32)).astype(jnp.bfloat16)
     d_normed_out = jnp.einsum("td,cd->tc", cotangent, out_proj, preferred_element_type=jnp.float32)
     grad_out_proj = jnp.einsum(
         "tc,td->cd", normed_out, cotangent, preferred_element_type=jnp.float32
@@ -313,44 +713,53 @@
     d_normed_part = d_normed_part + jnp.einsum(
         "th,dh->td", d_step_low, proj_dt, preferred_element_type=jnp.float32
     )
-    d_normed = lax.psum(d_normed_part, "head")
     _, norm_pull = jax.vjp(in_norm, tokens_f, in_gain)
-    d_tokens, grad_in_gain = norm_pull(d_normed)
+    _, grad_in_gain = norm_pull(d_normed_part)
+    width = tokens.shape[1]
+    small = [grad_conv_x_weight, grad_conv_x_bias, grad_dt_bias, grad_a_log, grad_skip_scale, grad_norm_gain]
+    flat = jnp.concatenate([grad_proj_dt.T.reshape(-1)] + [each.reshape(-1) for each in small])
+    lone = -(-flat.shape[0] // (8 * width)) * 8
+    flat = jnp.pad(flat, (0, lone * width - flat.shape[0])).reshape(lone, width)
+    head_at = lax.axis_index("head")
+    bc_width = conv_bc_bias.shape[0]
+    def spread(piece):
+        return lax.dynamic_update_slice(jnp.zeros(piece.shape[:-1] + (bc_width * head_count,), jnp.float32), piece, (0,) * (piece.ndim - 1) + (head_at * bc_width,))
+    flat_both = jnp.concatenate([grad_in_gain, spread(grad_conv_bc_weight).reshape(-1), spread(grad_conv_bc_bias)])
+    flat_both = jnp.pad(flat_both, (0, 8 * width - flat_both.shape[0])).reshape(8, width)
+    bc_part = lax.dynamic_update_slice(jnp.zeros((head_count, bc_width, width), jnp.float32), grad_proj_bc.T[None], (head_at, 0, 0))
+    d_normed, zx_sum, op_sum, bc_sum, small_sum = tail(
+        d_normed_part.astype(jnp.bfloat16),
+        grad_proj_zx.reshape(width, -1).astype(jnp.bfloat16),
+        grad_out_proj.astype(jnp.bfloat16), bc_part, jnp.concatenate([flat, flat_both]), 8)
+    d_tokens, _ = norm_pull(d_normed.astype(jnp.float32))
     grad_tokens = cotangent.astype(jnp.float32) + d_tokens
-    seq_sums = lax.psum(
-        (
-            grad_in_gain,
-            grad_proj_zx,
-            grad_proj_bc,
-            grad_proj_dt,
-            grad_conv_x_weight,
-            grad_conv_x_bias,
-            grad_conv_bc_weight,
-            grad_conv_bc_bias,
-            grad_dt_bias,
-            grad_a_log,
-            grad_skip_scale,
-            grad_norm_gain,
-            grad_out_proj,
-        ),
-        "seq",
-    )
+    at = 0
+    found = []
+    flat = small_sum[:lone].reshape(-1)
+    for like in [grad_proj_dt.T] + small:
+        found.append(flat[at : at + like.size].reshape(like.shape))
+        at += like.size
+    both = small_sum[lone:].reshape(-1)
+    taps = conv_bc_weight.shape[0]
+    bc_all = bc_width * head_count
+    bc_w = lax.dynamic_slice(both[width : width + taps * bc_all].reshape(taps, bc_all), (0, head_at * bc_width), (taps, bc_width))
+    bc_b = lax.dynamic_slice(both[width + taps * bc_all : width + (taps + 1) * bc_all], (head_at * bc_width,), (bc_width,))
     return (
         mixed_out,
         grad_tokens,
-        seq_sums[0],
-        seq_sums[1],
-        seq_sums[2],
-        seq_sums[3],
-        seq_sums[4],
-        seq_sums[5],
-        seq_sums[6],
-        seq_sums[7],
-        seq_sums[8],
-        seq_sums[9],
-        seq_sums[10],
-        seq_sums[11],
-        seq_sums[12],
+        both[:width],
+        zx_sum.astype(jnp.float32).reshape(grad_proj_zx.shape),
+        bc_sum.T,
+        found[0].T,
+        found[1],
+        found[2],
+        bc_w,
+        bc_b,
+        found[3],
+        found[4],
+        found[5],
+        found[6],
+        op_sum.astype(jnp.float32),
     )
 
 

time: 1130 us -> 895 us (0.79)
  waiting for transfers between devices: 672 us -> 28 us
  Pallas kernels: 0 us -> 421 us
  blocking collectives: 56 us -> 30.8 us
    psum x2 -> x0, waiting for transfers between devices: 644 us -> none  [the longest x1 559 us: shards(): mixed_out = (tokens_f + lax.psum(partial_out, 'head')).astype(jnp.bfloat16)]
    pallas_call x0 -> x2, Pallas kernels: none -> 421 us  [the longest x1 218 us: tail(): pl.pallas_call(functools.partial(tail_kernel, block, owners), out_shape=(...]
    psum x1 -> x0, blocking collectives: 25.1 us -> none  [shards(): lax.psum((grad_in_gain, grad_proj_zx, grad_proj_bc, grad_proj_dt, grad_co...]
    unnamed x394 -> x350, local copies, waits for them, and re-layouts: 43.5 us -> 31.8 us
  transfers between devices with their start and end apart: 9 -> 7, of which waited for: 5 -> 3; matrix products, arithmetic and copies ran while one was open for 14% -> 15% of each run, Pallas kernels for 0% -> 23%
where the time goes in v1:
time: 895 us; the launch traced here: 887 us
  Pallas kernels  421 us (47%)
  matrix products  176 us (20%)
  other arithmetic  122 us (14%)
  local copies, waits for them, and re-layouts  83.5 us (9%)
  blocking collectives  30.8 us (3%)
  waiting for transfers between devices  28 us (3%)
  between operations  16.7 us (2%)
    pallas_call x1, Pallas kernels, tail(): pl.pallas_call(functools.partial(tail_kernel, block, owners), out_shape=(...  218 us
    pallas_call x1, Pallas kernels, line_sum(): pl.pallas_call(functools.partial(line_sum_kernel, block), out_shape=jax.S...  203 us
    dot_general x3, matrix products, group_output(): inner_part = jnp.einsum('tsh,shp->thp', weights, x_heads, precision=highest)  74.7 us
    unnamed x350, local copies, waits for them, and re-layouts  31.8 us
    all_gather x1, waiting for transfers between devices, shards(): lax.all_gather(active[:, local_inner:].astype(jnp.bfloat16), 'head', axis...  19.5 us
  transfers between devices with their start and end apart: 7, of which 3 were waited for; matrix products, arithmetic and copies ran while one was open for 15% of the time, Pallas kernels for 23%

profile of v1, /device:TPU:0, one launch (start us, length us, event | category | flops | bytes accessed | tf_op | source)
XLA Modules:
  0.0 887.4 jit_solution(4055946836613091841)
XLA Ops:
  56.1 19.5 %all-gather.5.cloned.1.call-done = bf16[2048,256]{0,1:T(8,128)(2,1)} async-done(((bf16[2048,64]{0,1:T(8,128)(2,1)}), bf16[2048,256]{0,1:T(8,128)(2,1)}) %all-gather.5.cloned.1.call-update) | async-done | bytes 1048592 | tf_op jit(solution)/shard_map/all_gather | solution.py:605
  86.8 8.9 all-gather
  106.5 7.0 all-gather.7.cloned.1.call-done
  113.5 7.6 while.28
  135.4 21.2 %bitcast_add_fusion.4 = f32[8,256,8,64]{1,3,2,0:T(8,128)S(1)} fusion(f32[8,256,8,64]{1,3,2,0:T(8,128)S(1)} %fusion.151, f32[8,256,8]{1,2,0:T(8,128)S(1)} %copy-done.52, f32[8,256,8]{1,2,0:T(8,128)S(1)} %bitcast.448, f32[8,256,8]{1,2,0:T(8,128)S(1)} %bitcast.442, f32[8,256,256]{2,1,0:T(8,128)S(1)} %copy-done.48, pred[8,256,256]{2,1,0:T(8,128)(4,1)S(1)} %copy-done.57, ...), kind=kOutput, calls=%fused_computation.77 | convolution fusion | flops 3244294144 | bytes 15400960 | tf_op jit(solution)/shard_map/jvp(vmap(tsh,shp->thp))/dot_general | solution.py:466
  165.0 12.7 %psum.14 = f32[2048]{0:T(1024)} all-reduce(f32[2048]{0:T(1024)} %get-tuple-element.330), channel_id=1, replica_groups=mesh['seq'=8,'head'=4] {'head'}, use_global_device_ids=true, to_apply=%region_6.7 | all-reduce | flops 2048 | bytes 16384 | tf_op jit(solution)/shard_map/psum | solution.py:644
  179.1 9.1 %multiply_reduce_fusion.6 = (f32[512]{0:T(512)}, f32[2048]{0:T(1024)}, f32[2048,512]{0,1:T(8,128)}) fusion(f32[2048,512]{0,1:T(8,128)} %get-tuple-element.331, f32[2048]{0:T(1024)S(1)} %get-tuple-element.387, f32[512]{0:T(512)} %param.33, bf16[2048,1024]{1,0:T(8,128)(2,1)} %param.35, bf16[512,1024]{1,0:T(8,128)(2,1)} %param.34), kind=kOutput, calls=%fused_computation.83 | convolution fusion | flops 2153772544 | bytes 13651968 | tf_op jit(solution)/shard_map/td,cd->tc/dot_general | solution.py:649
  188.1 9.2 %psum.15 = f32[2048]{0:T(1024)} all-reduce(f32[2048]{0:T(1024)} %get-tuple-element.260), channel_id=1, replica_groups=mesh['seq'=8,'head'=4] {'head'}, use_global_device_ids=true, to_apply=%region_8.9 | all-reduce | flops 2048 | bytes 16384 | tf_op jit(solution)/shard_map/psum | solution.py:654
  198.0 10.8 %multiply_reduce_fusion.7 = (f32[512]{0:T(512)}, f32[2048,512]{0,1:T(8,128)S(1)}, bf16[2048,1,512]{0,2,1:T(8,128)(2,1)}) fusion(f32[2048,576]{0,1:T(8,128)} %copy-done.11, f32[2048,2,512]{0,2,1:T(8,128)} %copy-done.26, f32[2048]{0:T(1024)S(1)} %broadcast_multiply_fusion, f32[2048,512]{0,1:T(8,128)} %get-tuple-element.331, f32[2048]{0:T(1024)} %get-tuple-element.386, ...), kind=kLoop, calls=%fused_computation.84 | loop fusion | flops 23068160 | bytes 27293696 | tf_op jit(solution)/shard_map/transpose(jvp())/reduce_sum | solution.py:503
  217.3 34.8 %fusion.13 = (f32[8,256,8]{1,2,0:T(8,128)}, f32[8,256,8]{1,2,0:T(8,128)}, f32[8,256,8]{1,2,0:T(8,128)}, f32[8,256,256]{2,1,0:T(8,128)S(1)}) fusion(f32[8,256,8]{1,2,0:T(8,128)S(1)} %bitcast.449, f32[8,256,8]{1,2,0:T(8,128)S(1)} %bitcast.443, f32[8,256,256]{2,1,0:T(8,128)} %fusion.150, pred[8,256,256]{2,1,0:T(8,128)(4,1)} %compare_and_fusion, ...), kind=kOutput, calls=%fused_computation.26 | convolution fusion | flops 3283566592 | bytes 13434880 | tf_op jit(solution)/shard_map/transpose(jvp(vmap(tsh,shp->thp)))/dot_general | solution.py:466
  252.1 7.4 fusion.88
  266.9 7.0 convolution_convert_fusion.own
  273.9 203.3 %line_sum.1 = bf16[2048,1024]{1,0:T(8,128)(2,1)S(1)} custom-call(bf16[2048,1024]{1,0:T(8,128)(2,1)} %convolution_convert_fusion.own), custom_call_target="tpu_custom_call" | custom-call | tf_op jit(solution)/shard_map/line_sum/pallas_call | solution.py:209
  491.1 15.8 %while.29 = (s32[]{:T(128)}, f32[8,64,128]{2,1,0:T(8,128)S(1)}, s32[]{:T(128)}, f32[8,8,64,128]{3,2,1,0:T(8,128)}, f32[8,8]{1,0:T(8,128)}, /*index=5*/s32[]{:T(128)}, s32[]{:T(128)}) while((s32[]{:T(128)}, f32[8,64,128]{2,1,0:T(8,128)S(1)}, s32[]{:T(128)}, f32[8,8,64,128]{3,2,1,0:T(8,128)}, f32[8,8]{1,0:T(8,128)}, ...), condition=%wide.region_10.11_spmd.clone, body=%wide.region_9.10_spmd.clone.sunk | while | flops 262148 | bytes 786633 | solution.py:433
  516.2 7.6 fusion.85
  531.1 18.7 %bitcast_add_fusion.3 = f32[8,256,8,64]{1,3,2,0:T(8,128)S(1)} fusion(f32[8,256,8,64]{1,3,2,0:T(8,128)} %fusion.139, f32[8,256,8]{1,2,0:T(8,128)S(1)} %copy-done.60, f32[8,256,8]{1,2,0:T(8,128)S(1)} %bitcast.450, f32[8,256,8]{1,2,0:T(8,128)S(1)} %bitcast.444, f32[8,256,256]{2,1,0:T(8,128)} %fusion.150, pred[8,256,256]{2,1,0:T(8,128)(4,1)} %compare_and_fusion, ...), kind=kOutput, calls=%fused_computation.73 | convolution fusion | flops 3244294144 | bytes 15400960 | tf_op jit(solution)/shard_map/transpose(jvp(vmap(tsh,shp->thp)))/dot_general | solution.py:466
  556.9 6.1 multiply_reduce_fusion.5
  575.5 13.4 %multiply_reduce_fusion.4 = (f32[576]{0:T(1024)S(1)}, f32[576]{0:T(1024)S(1)}, f32[576]{0:T(1024)S(1)}, f32[576]{0:T(1024)S(1)}, f32[576]{0:T(1024)S(1)}, /*index=5*/f32[2048,576]{0,1:T(8,128)S(1)}) fusion(f32[2051,576]{0,1:T(8,128)} %copy-done.2, f32[2048]{0:T(1024)S(1)} %get-tuple-element.383, f32[2048]{0:T(1024)S(1)} %copy-done.73, ...), kind=kLoop, calls=%fused_computation.59 | loop fusion | flops 27129024 | bytes 33074432 | tf_op jit(solution)/shard_map/transpose(jvp())/reduce_sum | solution.py:493
  591.1 6.0 pad_add_fusion
  604.3 7.2 fusion.64
  617.3 6.1 fusion.15
  632.2 217.8 %tail.1 = (bf16[2048,1024]{1,0:T(8,128)(2,1)}, bf16[1024,1024]{1,0:T(8,128)(2,1)}, bf16[512,1024]{1,0:T(8,128)(2,1)}, f32[64,1024]{1,0:T(8,128)}, f32[24,1024]{1,0:T(8,128)}) custom-call(bf16[2048,1024]{1,0:T(8,128)(2,1)} %get-tuple-element.351.part, bf16[1024,1024]{1,0:T(8,128)(2,1)} %copy.154.zx, bf16[512,1024]{1,0:T(8,128)(2,1)} %convolution_convert_fusion.2.op, ...), custom_call_target="tpu_custom_call" | custom-call | tf_op jit(solution)/shard_map/tail/pallas_call | solution.py:386
  859.4 6.6 reshape.356
  869.5 10.1 %fusion.16 = (f32[2048,1024]{1,0:T(8,128)}, bf16[2048,1024]{1,0:T(8,128)(2,1)}) fusion(bf16[2048,1024]{1,0:T(8,128)(2,1)} %param.20, bf16[2048,1024]{1,0:T(8,128)(2,1)} %get-tuple-element.210, bf16[2048,1024]{1,0:T(8,128)(2,1)} %param.35, f32[2048]{0:T(1024)S(1)} %multiply_multiply_fusion.10, f32[1024]{0:T(1024)S(1)} %copy-done.88, f32[2048]{0:T(1024)S(1)} %copy-done.71, ...), kind=kLoop, calls=%fused_computation.29 | loop fusion | flops 25165824 | bytes 29380608 | tf_op jit(solution)/shard_map/add | solution.py:735
  (532 shorter events, 219.7 us)
Async XLA Ops:
  7.2 68.4 %all-gather.5.cloned.1.call-start = ((), (), s32[]{:S(2)}) async-start(), calls=%async_computation.1 | async-start | bytes 1310720 | tf_op jit(solution)/shard_map/all_gather | solution.py:605
  21.7 13.7 %collective-permute-start = (bf16[3,576]{0,1:T(8,128)(2,1)S(1)}, bf16[3,576]{0,1:T(8,128)(2,1)S(1)}, u32[]{:S(2)}, u32[]{:S(2)}) collective-permute-start(bf16[3,576]{0,1:T(8,128)(2,1)S(1)} %pad_maximum_fusion.7), channel_id=1, source_target_pairs={{0,4},{4,8},{8,12},{12,16},{16,20},{20,24},{24,28},{1,5},{5,9},{9,... | collective-permute-start | bytes 10376 | tf_op jit(solution)/shard_map/ppermute | solution.py:416
  24.2 10.4 %collective-permute-start.1 = (bf16[3]{0:T(256)(128)(2,1)S(1)}, bf16[3]{0:T(256)(128)(2,1)S(1)}, u32[]{:S(2)}, u32[]{:S(2)}) collective-permute-start(bf16[3]{0:T(256)(128)(2,1)S(1)} %slice.481), channel_id=1, source_target_pairs={{0,4},{4,8},{8,12},{12,16},{16,20},{20,24},{24,28},{1,5},{5,9},{9,... | collective-permute-start | bytes 26 | tf_op jit(solution)/shard_map/ppermute | solution.py:416
  47.2 66.3 %all-gather.7.cloned.1.call-start = ((), (), s32[]{:S(2)}) async-start(), calls=%async_computation.2 | async-start | bytes 2359296 | tf_op jit(solution)/shard_map/all_gather | solution.py:421
  48.3 35.4 %copy-start.124 = (f32[8]{0:T(128)}, f32[8]{0:T(128)S(1)}, u32[]{:S(2)}) copy-start(f32[8]{0:T(128)S(1)} %broadcast_multiply_fusion.1) | copy-start | bytes 100
  48.8 34.9 %copy-start.101 = (f32[8]{0:T(128)}, f32[8]{0:T(128)S(1)}, u32[]{:S(2)}) copy-start(f32[8]{0:T(128)S(1)} %get-tuple-element.400) | copy-start | bytes 100
  48.8 34.9 %copy-start.104 = (f32[8]{0:T(128)}, f32[8]{0:T(128)S(1)}, u32[]{:S(2)}) copy-start(f32[8]{0:T(128)S(1)} %get-tuple-element.401) | copy-start | bytes 100
  48.8 34.9 %copy-start.108 = (f32[8]{0:T(128)}, f32[8]{0:T(128)S(1)}, u32[]{:S(2)}) copy-start(f32[8]{0:T(128)S(1)} %get-tuple-element.402) | copy-start | bytes 100
  48.8 34.9 %copy-start.111 = (f32[8]{0:T(128)}, f32[8]{0:T(128)S(1)}, u32[]{:S(2)}) copy-start(f32[8]{0:T(128)S(1)} %get-tuple-element.409) | copy-start | bytes 100
  48.8 34.9 %copy-start.114 = (f32[8]{0:T(128)}, f32[8]{0:T(128)S(1)}, u32[]{:S(2)}) copy-start(f32[8]{0:T(128)S(1)} %get-tuple-element.403) | copy-start | bytes 100
  48.9 34.9 %copy-start.118 = (f32[8]{0:T(128)}, f32[8]{0:T(128)S(1)}, u32[]{:S(2)}) copy-start(f32[8]{0:T(128)S(1)} %get-tuple-element.404) | copy-start | bytes 100
  48.9 34.9 %copy-start.126 = (f32[8]{0:T(128)}, f32[8]{0:T(128)S(1)}, u32[]{:S(2)}) copy-start(f32[8]{0:T(128)S(1)} %get-tuple-element.405) | copy-start | bytes 100
  86.0 402.0 %all-gather.9.cloned.1.call-start = ((), (), s32[]{:S(2)}) async-start(), calls=%async_computation.3 | async-start | bytes 2359296 | tf_op jit(solution)/shard_map/all_gather | solution.py:421
  217.3 358.2 %reduce-scatter.2.cloned.1.call-start = ((), (), s32[]{:S(2)}) async-start(), calls=%async_computation.4 | async-start | bytes 2621440 | tf_op jit(solution)/shard_map/reduce_scatter | solution.py:676
  217.3 34.8 %copy-start.9 = (f32[64,8,8,256]{3,2,1,0:T(8,128)S(1)}, f32[64,8,8,256]{3,2,1,0:T(8,128)}, u32[]{:S(2)}) copy-start(f32[64,8,8,256]{3,2,1,0:T(8,128)} %copy-done.8) | copy-start | bytes 12582916
  217.3 34.8 %copy-start.28 = (f32[8,8,64,128]{3,2,1,0:T(8,128)S(1)}, f32[8,8,64,128]{3,2,1,0:T(8,128)}, u32[]{:S(2)}) copy-start(f32[8,8,64,128]{3,2,1,0:T(8,128)} %copy-done.27) | copy-start | bytes 6291460
  273.9 203.3 %copy-start.10 = (f32[64,8,8,256]{3,2,1,0:T(8,128)S(1)}, f32[64,8,8,256]{3,2,1,0:T(8,128)}, u32[]{:S(2)}) copy-start(f32[64,8,8,256]{3,2,1,0:T(8,128)} %copy-done.8) | copy-start | bytes 12582916
  273.9 203.4 %copy-start.25 = (f32[8,256,8,64]{1,3,2,0:T(8,128)S(1)}, f32[8,256,8,64]{1,3,2,0:T(8,128)}, u32[]{:S(2)}) copy-start(f32[8,256,8,64]{1,3,2,0:T(8,128)} %copy-done.24) | copy-start | bytes 12582916
  273.9 205.5 %copy-start.123 = (f32[256,8]{0,1:T(8,128)S(1)}, f32[256,8]{0,1:T(8,128)}, u32[]{:S(2)}) copy-start(f32[256,8]{0,1:T(8,128)} %get-tuple-element.421) | copy-start | bytes 24580
  273.9 208.1 %copy-start.117 = (f32[8]{0:T(128)S(1)}, f32[8]{0:T(128)}, u32[]{:S(2)}) copy-start(f32[8]{0:T(128)} %copy-done.114) | copy-start | bytes 100
  273.9 208.1 %copy-start.121 = (f32[8]{0:T(128)S(1)}, f32[8]{0:T(128)}, u32[]{:S(2)}) copy-start(f32[8]{0:T(128)} %copy-done.118) | copy-start | bytes 100
  597.2 3.5 collective-permute-start.2
  632.2 223.5 %copy-start.7 = (bf16[2048,1024]{1,0:T(8,128)(2,1)S(1)}, bf16[2048,1024]{1,0:T(8,128)(2,1)}, u32[]{:S(2)}) copy-start(bf16[2048,1024]{1,0:T(8,128)(2,1)} %param.20) | copy-start | bytes 12582916
  632.2 223.5 %copy-start.88 = (f32[1024]{0:T(1024)S(1)}, f32[1024]{0:T(1024)}, u32[]{:S(2)}) copy-start(f32[1024]{0:T(1024)} %param.22) | copy-start | bytes 12292
  (150 other events, 933.0 us)
Sparse Core Ops, SparseCore 0:
  47.3 28.2 all-gather.4
  86.1 27.3 all-gather.6
  217.4 26.5 all-gather.8
  531.2 43.1 reduce-scatter.1

commit v2 on v1

v2 whole, which is shorter than its diff:
```python
import functools

import jax
import jax.numpy as jnp
from jax import lax
from jax.experimental import pallas as pl
from jax.experimental.pallas import tpu as pltpu
from jax.sharding import PartitionSpec as P

MESH = pl.DeviceIdType.MESH
f32 = jnp.float32
bf16 = jnp.bfloat16


def rows_of(ref, start, size):
    return ref.at[pl.ds(pl.multiple_of(start, size), size)]


def greet(pairs):
    barrier = pltpu.get_barrier_semaphore()
    for live, where in pairs:
        @pl.when(live)
        def _():
            pl.semaphore_signal(barrier, inc=1, device_id=where, device_id_type=MESH)
    pl.semaphore_wait(barrier, sum(live.astype(jnp.int32) for live, _ in pairs))


def greet_axis(axis):
    barrier = pltpu.get_barrier_semaphore()
    size, mine = lax.axis_size(axis), lax.axis_index(axis)

    @pl.loop(1, size)
    def _(k):
        pl.semaphore_signal(
            barrier, inc=1, device_id={axis: lax.rem(mine + k, size)}, device_id_type=MESH
        )
    pl.semaphore_wait(barrier, size - 1)


class LineSum:
    def __init__(self, own, out, acc, rin, rx, sems, block):
        self.own, self.out, self.acc, self.rin, self.rx = own, out, acc, rin, rx
        self.send1, self.got_in, self.got_x, self.got_out, self.send2 = (
            sems.at[0], sems.at[1], sems.at[2], sems.at[3], sems.at[4])
        self.block = block
        size, me = lax.axis_size("head"), lax.axis_index("head")
        half = size // 2
        self.size = size
        left = me < half
        self.mid = (me == half - 1) | (me == half)
        self.has_outer = (me > 0) & (me < size - 1)
        self.inner = jnp.where(left, me + 1, me - 1)
        outer = jnp.where(left, me - 1, me + 1)
        self.outer = jnp.clip(outer, 0, size - 1)
        self.lag = max(2, half)

    def pairs(self):
        return [(self.inner >= 0, {"head": self.inner}), (self.has_outer, {"head": self.outer})]

    def copy(self, src, dst, b, send, recv, to):
        return pltpu.make_async_remote_copy(
            src_ref=rows_of(src, b * self.block, self.block),
            dst_ref=rows_of(dst, b * self.block, self.block),
            send_sem=send.at[b], recv_sem=recv.at[b],
            device_id={"head": to}, device_id_type=MESH)

    def inward(self, b):
        rows = pl.ds(pl.multiple_of(b * self.block, self.block), self.block)

        @pl.when(self.has_outer)
        def _():
            self.copy(self.acc, self.rin, b, self.send1, self.got_in, self.outer).wait_recv()
            self.acc[rows] = (self.rin[rows].astype(f32) + self.own[rows].astype(f32)).astype(bf16)

        @pl.when(jnp.logical_not(self.has_outer))
        def _():
            self.acc[rows] = self.own[rows]

        @pl.when(self.mid)
        def _():
            self.copy(self.acc, self.rx, b, self.send1, self.got_x, self.inner).start()

        @pl.when(jnp.logical_not(self.mid))
        def _():
            self.copy(self.acc, self.rin, b, self.send1, self.got_in, self.inner).start()

    def outward(self, b, done=None):
        rows = pl.ds(pl.multiple_of(b * self.block, self.block), self.block)

        @pl.when(self.mid)
        def _():
            self.copy(self.acc, self.rx, b, self.send1, self.got_x, self.inner).wait_recv()
            total = self.acc[rows].astype(f32) + self.rx[rows].astype(f32)
            if done is not None:
                total = done(rows, total)
            self.out[rows] = total.astype(bf16)

        @pl.when(jnp.logical_not(self.mid))
        def _():
            self.copy(self.out, self.out, b, self.send2, self.got_out, self.inner).wait_recv()

        @pl.when(self.has_outer)
        def _():
            self.copy(self.out, self.out, b, self.send2, self.got_out, self.outer).start()

    def drain(self, count):
        @pl.loop(0, count)
        def _(b):
            self.copy(self.acc, self.rin, b, self.send1, self.got_in, self.inner).wait_send()

            @pl.when(self.has_outer)
            def _():
                self.copy(self.out, self.out, b, self.send2, self.got_out, self.outer).wait_send()

    def run(self, first, last, count, done=None):
        if first == 0:
            @pl.when(jnp.logical_not(self.has_outer))
            def _():
                @pl.loop(0, count)
                def _(b):
                    self.inward(b)

        @pl.loop(first, last)
        def _(b):
            @pl.when((b < count) & self.has_outer)
            def _():
                self.inward(b)

            @pl.when(b >= self.lag)
            def _():
                self.outward(b - self.lag, done)


class PlaneSum:
    def __init__(self, own, slots, res, sems, owners):
        self.own, self.slots, self.res = own, slots, res
        self.rs_send, self.rs_got, self.ag_send, self.ag_got = (
            sems.at[0], sems.at[1], sems.at[2], sems.at[3])
        self.owners = owners
        self.size, self.me = lax.axis_size("seq"), lax.axis_index("seq")
        self.piece = own.shape[0] // owners

    def part(self, ref, k):
        return rows_of(ref, k * self.piece, self.piece)

    def scatter_copy(self, to, source):
        return pltpu.make_async_remote_copy(
            src_ref=self.part(self.own, to), dst_ref=self.slots.at[source],
            send_sem=self.rs_send.at[to], recv_sem=self.rs_got.at[source],
            device_id={"seq": to}, device_id_type=MESH)

    def gather_copy(self, owner, to):
        return pltpu.make_async_remote_copy(
            src_ref=self.part(self.res, owner), dst_ref=self.part(self.res, owner),
            send_sem=self.ag_send.at[to], recv_sem=self.ag_got.at[owner],
            device_id={"seq": to}, device_id_type=MESH)

    def scatter(self):
        @pl.loop(1, self.size)
        def _(k):
            to = lax.rem(self.me + k, self.size)

            @pl.when(to < self.owners)
            def _():
                self.scatter_copy(to, self.me).start()

    def reduce(self):
        @pl.when(self.me < self.owners)
        def _():
            @pl.loop(1, self.size)
            def _(k):
                source = lax.rem(self.me + k, self.size)
                self.scatter_copy(self.me, source).wait_recv()
            mine = pl.ds(pl.multiple_of(self.me * self.piece, self.piece), self.piece)
            self.slots[self.me] = self.own[mine]
            total = self.slots[0].astype(f32)
            for k in range(1, self.size):
                total = total + self.slots[k].astype(f32)
            self.res[mine] = total.astype(self.res.dtype)

            @pl.loop(1, self.size)
            def _(k):
                self.gather_copy(self.me, lax.rem(self.me + k, self.size)).start()

    def finish(self):
        @pl.loop(1, self.size)
        def _(k):
            other = lax.rem(self.me + k, self.size)

            @pl.when(other < self.owners)
            def _():
                self.gather_copy(other, self.me).wait_recv()
                self.scatter_copy(other, self.me).wait_send()

        @pl.when(self.me < self.owners)
        def _():
            @pl.loop(1, self.size)
            def _(k):
                self.gather_copy(self.me, lax.rem(self.me + k, self.size)).wait_send()


def line_sum_kernel(block, own, out, acc, rin, rx, sems):
    line = LineSum(own, out, acc, rin, rx, sems, block)
    greet(line.pairs())
    count = own.shape[0] // block
    line.run(0, count + line.lag, count)
    line.drain(count)


VMEM = pl.BlockSpec(memory_space=pltpu.VMEM)


def line_sum(part, block=128):
    rows, width = part.shape
    slot = pltpu.VMEM((rows, width), bf16)
    return pl.pallas_call(
        functools.partial(line_sum_kernel, block),
        out_shape=jax.ShapeDtypeStruct((rows, width), bf16),
        in_specs=[VMEM], out_specs=VMEM,
        scratch_shapes=[slot, slot, slot, pltpu.SemaphoreType.DMA((5, rows // block))],
        compiler_params=pltpu.CompilerParams(
            collective_id=1, has_side_effects=True, vmem_limit_bytes=48 * 2**20),
        name="line_sum",
    )(part)


def tail_kernel(block, owners, part, zx, op, bc, small,
                out, zx_out, op_out, bc_out, small_out,
                acc, rin, rx, zx_slots, op_slots, bc_slots, bc_z, small_slots, small_z,
                line_sems, zx_sems, op_sems, bc_sems, bcz_sems, small_sems, smallz_sems):
    seq, heads = lax.axis_size("seq"), lax.axis_size("head")
    me, my_head = lax.axis_index("seq"), lax.axis_index("head")
    line = LineSum(part, out, acc, rin, rx, line_sems, block)
    sums = [PlaneSum(zx, zx_slots, zx_out, zx_sems, owners[0]),
            PlaneSum(op, op_slots, op_out, op_sems, owners[1])]
    barrier = pltpu.get_barrier_semaphore()
    for axis, size, mine in (("seq", seq, me), ("head", heads, my_head)):
        @pl.loop(1, size)
        def _(k):
            pl.semaphore_signal(barrier, inc=1, device_id={axis: lax.rem(mine + k, size)},
                                device_id_type=MESH)
    pl.semaphore_wait(barrier, seq + heads - 2)

    piece = bc.shape[1] // owners[2]

    def bc_scatter(to, source):
        return pltpu.make_async_remote_copy(
            src_ref=bc.at[:, pl.ds(pl.multiple_of(to * piece, piece), piece)],
            dst_ref=bc_slots.at[source], send_sem=bc_sems.at[0, to], recv_sem=bc_sems.at[1, source],
            device_id={"seq": to}, device_id_type=MESH)

    def bc_gather(owner, to):
        rows = pl.ds(pl.multiple_of(owner * piece, piece), piece)
        return pltpu.make_async_remote_copy(
            src_ref=bc_out.at[rows], dst_ref=bc_out.at[rows],
            send_sem=bc_sems.at[2, to], recv_sem=bc_sems.at[3, owner],
            device_id={"seq": to}, device_id_type=MESH)

    def bc_swap(to, source):
        return pltpu.make_async_remote_copy(
            src_ref=bc_slots.at[me, to], dst_ref=bc_z.at[source],
            send_sem=bcz_sems.at[0, to], recv_sem=bcz_sems.at[1, source],
            device_id={"head": to}, device_id_type=MESH)

    def small_send(to, source):
        return pltpu.make_async_remote_copy(
            src_ref=small, dst_ref=small_slots.at[source],
            send_sem=small_sems.at[0, to], recv_sem=small_sems.at[1, source],
            device_id={"seq": to}, device_id_type=MESH)

    both = small_z.shape[1]
    lone = small.shape[0] - both

    def small_swap(to, source):
        return pltpu.make_async_remote_copy(
            src_ref=small_z.at[my_head], dst_ref=small_z.at[source],
            send_sem=smallz_sems.at[0, to], recv_sem=smallz_sems.at[1, source],
            device_id={"head": to}, device_id_type=MESH)

    for each in sums:
        each.scatter()

    @pl.loop(1, seq)
    def _(k):
        to = lax.rem(me + k, seq)

        @pl.when(to < owners[2])
        def _():
            bc_scatter(to, me).start()
        small_send(to, me).start()

    count = part.shape[0] // block
    steps = count + line.lag
    cut1, cut2 = (steps * 7) // 16, (steps * 10) // 16
    line.run(0, cut1, count)

    for each in sums:
        each.reduce()

    @pl.loop(1, seq)
    def _(k):
        small_send(me, lax.rem(me + k, seq)).wait_recv()
    small_slots[me] = small[...]
    total = small_slots[0]
    for k in range(1, seq):
        total = total + small_slots[k]
    small_out[0:lone] = total[0:lone]
    small_z[my_head] = total[lone:]

    @pl.when(me < owners[2])
    def _():
        @pl.loop(1, seq)
        def _(k):
            bc_scatter(me, lax.rem(me + k, seq)).wait_recv()
        bc_slots[me] = bc[:, pl.ds(pl.multiple_of(me * piece, piece), piece)]
        total = bc_slots[0]
        for k in range(1, seq):
            total = total + bc_slots[k]
        bc_slots[me] = total
        bc_z[my_head] = bc_slots[me, my_head]

    @pl.loop(1, heads)
    def _(k):
        to = lax.rem(my_head + k, heads)
        small_swap(to, my_head).start()

        @pl.when(me < owners[2])
        def _():
            bc_swap(to, my_head).start()

    line.run(cut1, cut2, count)

    @pl.loop(1, heads)
    def _(k):
        source = lax.rem(my_head + k, heads)
        small_swap(my_head, source).wait_recv()

        @pl.when(me < owners[2])
        def _():
            bc_swap(my_head, source).wait_recv()
    total = small_z[0]
    for k in range(1, heads):
        total = total + small_z[k]
    small_out[lone:] = total

    @pl.when(me < owners[2])
    def _():
        total = bc_z[0]
        for k in range(1, heads):
            total = total + bc_z[k]
        bc_out[pl.ds(pl.multiple_of(me * piece, piece), piece)] = total

        @pl.loop(1, seq)
        def _(k):
            bc_gather(me, lax.rem(me + k, seq)).start()

    line.run(cut2, steps, count)
    line.drain(count)
    for each in sums:
        each.finish()

    @pl.loop(1, seq)
    def _(k):
        other = lax.rem(me + k, seq)
        small_send(other, me).wait_send()

        @pl.when(other < owners[2])
        def _():
            bc_gather(other, me).wait_recv()
            bc_scatter(other, me).wait_send()

        @pl.when(me < owners[2])
        def _():
            bc_gather(me, other).wait_send()

    @pl.loop(1, heads)
    def _(k):
        to = lax.rem(my_head + k, heads)
        small_swap(to, my_head).wait_send()

        @pl.when(me < owners[2])
        def _():
            bc_swap(to, my_head).wait_send()


def tail(part, zx, op, bc, small, both, block=128):
    seq, heads = lax.axis_size("seq"), lax.axis_size("head")
    rows, width = part.shape
    owners = (min(seq, zx.shape[0] // 16), min(seq, op.shape[0] // 16), min(seq, bc.shape[1] // 8))
    slot = pltpu.VMEM((rows, width), bf16)
    dma = pltpu.SemaphoreType.DMA
    piece = bc.shape[1] // owners[2]
    return pl.pallas_call(
        functools.partial(tail_kernel, block, owners),
        out_shape=(jax.ShapeDtypeStruct((rows, width), bf16),
                   jax.ShapeDtypeStruct(zx.shape, bf16), jax.ShapeDtypeStruct(op.shape, bf16),
                   jax.ShapeDtypeStruct(bc.shape[1:], f32), jax.ShapeDtypeStruct(small.shape, f32)),
        in_specs=[VMEM] * 5, out_specs=(VMEM,) * 5,
        scratch_shapes=[
            slot, slot, slot,
            pltpu.VMEM((seq, zx.shape[0] // owners[0], zx.shape[1]), bf16),
            pltpu.VMEM((seq, op.shape[0] // owners[1], op.shape[1]), bf16),
            pltpu.VMEM((seq, heads, piece, bc.shape[2]), f32),
            pltpu.VMEM((heads, piece, bc.shape[2]), f32),
            pltpu.VMEM((seq,) + small.shape, f32),
            pltpu.VMEM((heads, both, small.shape[1]), f32),
            dma((5, rows // block)), dma((4, seq)), dma((4, seq)), dma((4, seq)),
            dma((2, heads)), dma((2, seq)), dma((2, heads)),
        ],
        compiler_params=pltpu.CompilerParams(
            collective_id=2, has_side_effects=True, vmem_limit_bytes=56 * 2**20),
        name="tail",
    )(part, zx, op, bc, small)


GROUP = 256
STRIP = 128
GAP = 200.0
epsilon = 1e-05
LIMIT = 56 * 2**20


def dot(a, b):
    return jnp.dot(a, b, preferred_element_type=f32)


def dot_nt(a, b):
    return lax.dot_general(a, b, (((1,), (1,)), ((), ())), preferred_element_type=f32)


def dot_tn(a, b):
    return lax.dot_general(a, b, (((0,), (0,)), ((), ())), preferred_element_type=f32)


def split3(v):
    one = v.astype(bf16)
    rest = v - one.astype(f32)
    two = rest.astype(bf16)
    return one, two, (rest - two.astype(f32)).astype(bf16)


def exact_left(ones, v):
    width = v.shape[1]
    out = dot(ones, jnp.concatenate(split3(v), axis=1))
    return out[:, :width] + out[:, width : 2 * width] + out[:, 2 * width :]


def head_sum(v, group_ones):
    high = v.astype(bf16)
    low = (v - high.astype(f32)).astype(bf16)
    return dot(high, group_ones) + dot(low, group_ones)


def sigmoid(v):
    return 1.0 / (1.0 + jnp.exp(-v))


def softplus(v):
    return jnp.maximum(v, 0.0) + jnp.log1p(jnp.exp(-jnp.abs(v)))


def spread(cols, first, heads, head_dim):
    rows = cols.shape[0]
    per = 128 // head_dim
    lane = lax.broadcasted_iota(jnp.int32, (rows, 128), 1)
    tiles = []
    for at in range(0, heads, per):
        tile = cols[:, first + at : first + at + 1]
        for k in range(1, per):
            tile = jnp.where(lane < k * head_dim, tile, cols[:, first + at + k : first + at + k + 1])
        tiles.append(jnp.broadcast_to(tile, (rows, 128)))
    return jnp.concatenate(tiles, axis=1)


def norm_rows(block, gain):
    value = block.astype(f32)
    inv = lax.rsqrt(jnp.mean(value * value, axis=1, keepdims=True) + epsilon)
    return (value * inv * gain).astype(bf16)


def lane_groups(rows, *parts):
    lane = lax.broadcasted_iota(jnp.int32, (rows, 128), 1)
    out = parts[-1]
    for k in range(len(parts) - 2, -1, -1):
        out = jnp.where(lane < 8 * (k + 1), parts[k], out)
    return out


RAW, STEP, CUM, DEV = 0, 8, 16, 24


def front_kernel(heads, head_dim, state_dim,
                 normed, halo, weights, flags, conv_w, params,
                 gate_out, conv_in_out, conv_out_out, heads_out, state_out, decay_out, halo_out,
                 carry, ext, state, running):
    at = pl.program_id(0)
    rows = normed.shape[0]
    inner = heads * head_dim
    width = inner + 2 * state_dim

    @pl.when(at == 0)
    def _():
        ahead = dot(halo[...], weights[:, inner : inner + width]).astype(bf16)
        halo_out[...] = ahead
        carry[...] = ahead[8:].astype(f32)
        state[...] = jnp.zeros_like(state)
        running[...] = jnp.zeros_like(running)

    raw = dot(normed[...], weights[...])
    gate_out[...] = raw[:, :inner]
    conv_in = raw[:, inner : inner + width].astype(bf16)
    conv_in_out[...] = conv_in
    current = conv_in.astype(f32)
    ext[0:8] = carry[...]
    ext[8:] = current
    carry[...] = ext[rows:]
    keep = 1.0 - flags[...]
    total = conv_w[4:5] + conv_w[0:1] * current
    for j in range(1, 4):
        total = total + conv_w[j : j + 1] * ext[pl.ds(8 - j, rows)] * keep[:, j : j + 1]
    conv_out_out[...] = total
    active = total * sigmoid(total)

    step_raw = raw[:, inner + width :]
    step = softplus(step_raw + params[0:1])
    log_decay = step * params[1:2] - GAP * flags[:, 1:2]
    order_r = lax.broadcasted_iota(jnp.int32, (rows, rows), 0)
    order_c = lax.broadcasted_iota(jnp.int32, (rows, rows), 1)
    cum = exact_left((order_r >= order_c).astype(bf16), log_decay)
    heads_out[...] = lane_groups(rows, step_raw, step, cum, cum + running[0:1])
    end = cum[rows - 1 : rows]
    running[...] = running[...] + end
    weight = step * jnp.exp(end - cum)
    scaled = (active[:, :inner] * spread(weight, 0, heads, head_dim)).astype(bf16)
    b_proj = active[:, inner : inner + state_dim].astype(bf16)
    state[...] = state[...] * spread(jnp.exp(end), 0, heads, head_dim) + dot_tn(b_proj, scaled)

    @pl.when(at == pl.num_programs(0) - 1)
    def _():
        state_out[...] = state[...]
        decay_out[...] = spread(jnp.exp(running[...]), 0, heads, head_dim)


def params_of(name, grid=1):
    return pltpu.CompilerParams(dimension_semantics=("arbitrary",) * grid, vmem_limit_bytes=LIMIT)


def whole(shape):
    return pl.BlockSpec(shape, lambda g: (0,) * len(shape))


def front(normed, halo, weights, flags, conv_w, params, heads, head_dim, state_dim):
    length, width = normed.shape
    count = length // GROUP
    inner = heads * head_dim
    conv = inner + 2 * state_dim

    def by(cols):
        return pl.BlockSpec((GROUP, cols), lambda g: (g, 0))
    shape = jax.ShapeDtypeStruct
    return pl.pallas_call(
        functools.partial(front_kernel, heads, head_dim, state_dim),
        grid=(count,),
        out_shape=(shape((length, inner), f32), shape((length, conv), bf16), shape((length, conv), f32),
                   shape((length, 128), f32), shape((state_dim, inner), f32), shape((8, inner), f32),
                   shape((16, conv), bf16)),
        in_specs=[by(width), whole(halo.shape), whole(weights.shape), by(8), whole(conv_w.shape),
                  whole(params.shape)],
        out_specs=(by(inner), by(conv), by(conv), by(128), whole((state_dim, inner)),
                   whole((8, inner)), whole((16, conv))),
        scratch_shapes=[pltpu.VMEM((8, conv), f32), pltpu.VMEM((GROUP + 8, conv), f32),
                        pltpu.VMEM((state_dim, inner), f32), pltpu.VMEM((8, 128), f32)],
        compiler_params=params_of("front"), name="front",
    )(normed, halo, weights, flags, conv_w, params)


def scan_kernel(backward, own, decay, out, total, fade, lead, got, got_fade, sent, sent_fade, sems):
    size, me = lax.axis_size("seq"), lax.axis_index("seq")
    barrier = pltpu.get_barrier_semaphore()
    rounds = size.bit_length() - 1
    for k in range(rounds):
        pl.semaphore_signal(barrier, inc=1, device_id={"seq": jnp.bitwise_xor(me, 1 << k)},
                            device_id_type=MESH)
    pl.semaphore_wait(barrier, rounds)
    total[...] = own[...]
    fade[...] = decay[...]
    out[...] = jnp.zeros_like(out)
    lead[...] = jnp.ones_like(lead)
    for k in range(rounds):
        sent[k] = total[...].astype(bf16)
        sent_fade[k] = fade[...]
        copies = [
            pltpu.make_async_remote_copy(
                src_ref=src.at[k], dst_ref=dst.at[k], send_sem=sems.at[i, k], recv_sem=sems.at[i + 1, k],
                device_id={"seq": jnp.bitwise_xor(me, 1 << k)}, device_id_type=MESH)
            for src, dst, i in ((sent, got, 0), (sent_fade, got_fade, 2))]
        for copy in copies:
            copy.start()
        for copy in copies:
            copy.wait()
        later = lax.rem(me // (1 << k), 2) == (0 if backward else 1)

        @pl.when(later)
        def _():
            theirs = got[k].astype(f32)
            out[...] = out[...] + lead[0:1] * theirs
            total[...] = total[...] + fade[0:1] * theirs

        @pl.when(jnp.logical_not(later))
        def _():
            total[...] = got[k].astype(f32) + got_fade[k, 0:1] * total[...]

        @pl.when(later)
        def _():
            lead[...] = lead[...] * got_fade[k]
        fade[...] = fade[...] * got_fade[k]


def device_scan(state, decay, backward):
    rounds = lax.axis_size("seq").bit_length() - 1
    return pl.pallas_call(
        functools.partial(scan_kernel, backward),
        out_shape=jax.ShapeDtypeStruct(state.shape, f32),
        in_specs=[VMEM, VMEM], out_specs=VMEM,
        scratch_shapes=[
            pltpu.VMEM(state.shape, f32), pltpu.VMEM(decay.shape, f32), pltpu.VMEM(decay.shape, f32),
            pltpu.VMEM((rounds,) + state.shape, bf16), pltpu.VMEM((rounds,) + decay.shape, f32),
            pltpu.VMEM((rounds,) + state.shape, bf16), pltpu.VMEM((rounds,) + decay.shape, f32),
            pltpu.SemaphoreType.DMA((4, rounds))],
        compiler_params=pltpu.CompilerParams(
            collective_id=4 if backward else 3, has_side_effects=True, vmem_limit_bytes=16 * 2**20),
        name="scan_back" if backward else "scan_ahead",
    )(state, decay)


def strips(rows):
    return [(lo, lo + STRIP) for lo in range(0, rows, STRIP)]


def mix_kernel(heads, head_dim, state_dim,
               conv_out, heads_in, gate, cot, out_proj, gains, entering,
               ssm_out, d_normed_out, partial_out, sums_out, starts_out,
               state):
    at = pl.program_id(0)
    rows = conv_out.shape[0]
    inner = heads * head_dim
    per = 128 // head_dim

    @pl.when(at == 0)
    def _():
        state[...] = entering[...]

    values = conv_out[...]
    active = values * sigmoid(values)
    x = active[:, :inner]
    b_proj = active[:, inner : inner + state_dim].astype(bf16)
    c_proj = active[:, inner + state_dim :].astype(bf16)
    info = heads_in[...]
    flipped = info.T
    stepped = x * spread(info, STEP, heads, head_dim)
    low = stepped.astype(bf16)
    scores = dot_nt(c_proj, b_proj)
    lane = lax.broadcasted_iota(jnp.int32, (rows, 128), 1)
    tiles = []
    for pair in range(heads // per):
        tile = low[:, pair * 128 : (pair + 1) * 128]
        parts = [None] * (rows // STRIP)
        for k in range(per):
            head = pair * per + k
            masked = jnp.where((lane >= k * head_dim) & (lane < (k + 1) * head_dim), tile, jnp.zeros_like(tile))
            for n, (lo, hi) in enumerate(strips(rows)):
                gap = info[lo:hi, CUM + head : CUM + head + 1] - flipped[CUM + head : CUM + head + 1, :hi]
                ok = (lax.broadcasted_iota(jnp.int32, (STRIP, hi), 0) + lo
                      >= lax.broadcasted_iota(jnp.int32, (STRIP, hi), 1))
                weight = jnp.exp(jnp.where(ok, gap, -1e30)) * scores[lo:hi, :hi]
                part = dot(weight.astype(bf16), masked[:hi])
                parts[n] = part if parts[n] is None else parts[n] + part
        tiles.append(jnp.concatenate(parts, axis=0))
    inside = jnp.concatenate(tiles, axis=1)
    cum = info[:, CUM : CUM + 8]
    end = info[rows - 1 : rows]
    start = state[...]
    starts_out[0] = start.astype(bf16)
    grown = spread(jnp.exp(info), CUM, heads, head_dim)
    result = inside + grown * dot(c_proj, start.astype(bf16)) + gains[1:2] * x
    fade = spread(jnp.exp(end - info), CUM, heads, head_dim)
    state[...] = start * spread(jnp.exp(end), CUM, heads, head_dim) + dot_tn(b_proj, (stepped * fade).astype(bf16))
    ssm_out[...] = result
    z = gate[...]
    gated = result * (z * sigmoid(z))
    d_normed = dot_nt(cot[...], out_proj[...])
    d_normed_out[...] = d_normed
    scaled = gated * gains[0:1]
    partial_out[...] = dot(scaled.astype(bf16), out_proj[...]).astype(bf16)
    squares = jnp.sum(gated * gated, axis=1, keepdims=True)
    cross = jnp.sum(d_normed * scaled, axis=1, keepdims=True)
    turned = jnp.where(lane == 0, squares, cross).T
    sums_out[0, pl.ds(at, 1)] = turned[0:1]
    sums_out[1, pl.ds(at, 1)] = turned[1:2]


def mix(conv_out, heads_in, gate, cot, out_proj, gains, entering, heads, head_dim, state_dim):
    length = conv_out.shape[0]
    count = length // GROUP
    inner = heads * head_dim
    width = cot.shape[1]

    def by(cols):
        return pl.BlockSpec((GROUP, cols), lambda g: (g, 0))
    shape = jax.ShapeDtypeStruct
    return pl.pallas_call(
        functools.partial(mix_kernel, heads, head_dim, state_dim),
        grid=(count,),
        out_shape=(shape((length, inner), f32), shape((length, inner), f32), shape((length, width), bf16),
                   shape((2, count, GROUP), f32), shape((count, state_dim, inner), bf16)),
        in_specs=[by(conv_out.shape[1]), by(128), by(inner), by(width), whole(out_proj.shape),
                  whole(gains.shape), whole(entering.shape)],
        out_specs=(by(inner), by(inner), by(width), whole((2, count, GROUP)),
                   pl.BlockSpec((1, state_dim, inner), lambda g: (g, 0, 0))),
        scratch_shapes=[pltpu.VMEM((state_dim, inner), f32)],
        compiler_params=params_of("mix"), name="mix",
    )(conv_out, heads_in, gate, cot, out_proj, gains, entering)


def gate_kernel(heads, head_dim, state_dim, all_channels,
                ssm, gate, d_normed, sums, conv_out, heads_in, cot, gains,
                d_ssm_out, d_gate_out, grad_out, rows_out, total_out):
    at = pl.program_id(0)
    rows = ssm.shape[0]
    inner = heads * head_dim

    @pl.when(at == 0)
    def _():
        grad_out[...] = jnp.zeros_like(grad_out)
        rows_out[...] = jnp.zeros_like(rows_out)
        total_out[...] = jnp.zeros_like(total_out)

    tall = jnp.concatenate([sums[0, pl.ds(at, 1)], sums[1, pl.ds(at, 1)], jnp.zeros((126, rows), f32)], axis=0).T
    inv = lax.rsqrt(tall[:, 0:1] / all_channels + epsilon)
    cross = tall[:, 1:2] / all_channels
    z = gate[...]
    s = sigmoid(z)
    y = ssm[...]
    gated = y * (z * s)
    gain = gains[0:1]
    back = d_normed[...]
    unit = gated * inv
    d_gated = inv * (back * gain - unit * (inv * cross))
    grad_out[...] += dot_tn((unit * gain).astype(bf16), cot[...])
    d_ssm = d_gated * (z * s)
    d_ssm_out[...] = d_ssm
    d_gate_out[...] = (d_gated * y * (s * (1.0 + z * (1.0 - s)))).astype(bf16)
    values = conv_out[...]
    active = values * sigmoid(values)
    rows_out[0:1] += jnp.sum(back * unit, axis=0, keepdims=True)
    rows_out[1:2] += jnp.sum(d_ssm * active[:, :inner], axis=0, keepdims=True)
    c_proj = active[:, inner + state_dim :].astype(bf16)
    grown = spread(jnp.exp(heads_in[...]), DEV, heads, head_dim)
    total_out[...] += dot_tn(c_proj, (grown * d_ssm).astype(bf16))


def gate_back(ssm, gate, d_normed, sums, conv_out, heads_in, cot, gains, heads, head_dim, state_dim, all_channels):
    length, inner = ssm.shape
    width = cot.shape[1]

    def by(cols):
        return pl.BlockSpec((GROUP, cols), lambda g: (g, 0))
    shape = jax.ShapeDtypeStruct
    return pl.pallas_call(
        functools.partial(gate_kernel, heads, head_dim, state_dim, all_channels),
        grid=(length // GROUP,),
        out_shape=(shape((length, inner), f32), shape((length, inner), bf16), shape((inner, width), f32),
                   shape((8, inner), f32), shape((state_dim, inner), f32)),
        in_specs=[by(inner), by(inner), by(inner), whole(sums.shape), by(conv_out.shape[1]), by(128),
                  by(width), whole(gains.shape)],
        out_specs=(by(inner), by(inner), whole((inner, width)), whole((8, inner)),
                   whole((state_dim, inner))),
        compiler_params=params_of("gate_back"), name="gate_back",
    )(ssm, gate, d_normed, sums, conv_out, heads_in, cot, gains)


def back_kernel(heads, head_dim, state_dim,
                d_ssm, conv_out, conv_in, heads_in, starts, entering, flags, conv_w, params, skip, conv_halo,
                d_conv_in_out, d_step_out, conv_grads, head_grads, halo_out,
                lam, shift1, shift2, shift3):
    at = pl.program_id(0)
    rows = d_ssm.shape[0]
    inner = heads * head_dim
    per = 128 // head_dim
    shifts = (shift1, shift2, shift3)

    @pl.when(at == 0)
    def _():
        lam[...] = entering[...]
        conv_grads[...] = jnp.zeros_like(conv_grads)
        head_grads[...] = jnp.zeros_like(head_grads)
        for each in shifts:
            each[rows:] = jnp.zeros((8, each.shape[1]), f32)

    values = conv_out[...]
    gates = sigmoid(values)
    active = values * gates
    x = active[:, :inner]
    b_proj = active[:, inner : inner + state_dim].astype(bf16)
    c_proj = active[:, inner + state_dim :].astype(bf16)
    info = heads_in[...]
    flipped = info.T
    step = spread(info, STEP, heads, head_dim)
    stepped = x * step
    low = stepped.astype(bf16)
    dy = d_ssm[...]
    dy_low = dy.astype(bf16)
    scores = dot_nt(b_proj, c_proj)
    lane = lax.broadcasted_iota(jnp.int32, (rows, 128), 1)
    lane_one = lax.broadcasted_iota(jnp.int32, (STRIP, 128), 1)
    cuts = strips(rows)
    d_scores = [jnp.zeros((STRIP, rows - lo), f32) for lo, _ in cuts]
    d_rows = []
    d_cols = [jnp.zeros((STRIP, 128), f32) for _ in cuts]
    tiles = []
    for pair in range(heads // per):
        tile = low[:, pair * 128 : (pair + 1) * 128]
        dy_tile = dy_low[:, pair * 128 : (pair + 1) * 128]
        parts = [None] * len(cuts)
        for k in range(per):
            head = pair * per + k
            own = (lane >= k * head_dim) & (lane < (k + 1) * head_dim)
            masked = jnp.where(own, tile, jnp.zeros_like(tile))
            dy_masked = jnp.where(own, dy_tile, jnp.zeros_like(dy_tile))
            row_total = jnp.zeros((1, rows), f32)
            for n, (lo, hi) in enumerate(cuts):
                gap = flipped[CUM + head : CUM + head + 1, lo:] - info[lo:hi, CUM + head : CUM + head + 1]
                ok = (lax.broadcasted_iota(jnp.int32, (STRIP, rows - lo), 1)
                      >= lax.broadcasted_iota(jnp.int32, (STRIP, rows - lo), 0))
                decay = jnp.exp(jnp.where(ok, gap, -1e30))
                weight = decay * scores[lo:hi, lo:]
                part = dot(weight.astype(bf16), dy_masked[lo:])
                parts[n] = part if parts[n] is None else parts[n] + part
                pairs = dot_nt(masked[lo:hi], dy_tile[lo:])
                d_scores[n] = d_scores[n] + pairs * decay
                moved = pairs * weight
                d_cols[n] = d_cols[n] - jnp.where(lane_one == head, jnp.sum(moved, axis=1, keepdims=True), 0.0)
                col = jnp.sum(moved, axis=0, keepdims=True)
                if lo:
                    col = jnp.concatenate([jnp.zeros((1, lo), f32), col], axis=1)
                row_total = row_total + col
            d_rows.append(row_total)
        tiles.append(jnp.concatenate(parts, axis=0))
    d_stepped = jnp.concatenate(tiles, axis=1)
    d_cum = jnp.concatenate(d_cols, axis=0)
    d_cum = d_cum + jnp.concatenate(d_rows + [jnp.zeros((128 - heads, rows), f32)], axis=0).T
    full = jnp.concatenate(
        [jnp.concatenate([jnp.zeros((STRIP, lo), f32), part], axis=1) if lo else part
         for part, (lo, _) in zip(d_scores, cuts)], axis=0).astype(bf16)
    d_b = dot(full, c_proj)
    d_c = dot_tn(full, b_proj)

    group_ones = (lax.broadcasted_iota(jnp.int32, (inner, 128), 0) // head_dim
                  == lax.broadcasted_iota(jnp.int32, (inner, 128), 1)).astype(bf16)
    start = starts[0]
    after = lam[...]
    after_low = after.astype(bf16)
    end = info[rows - 1 : rows]
    grown = spread(jnp.exp(info), CUM, heads, head_dim)
    fade = spread(jnp.exp(end - info), CUM, heads, head_dim)
    end_grown = spread(jnp.exp(end), CUM, heads, head_dim)
    from_after = fade * dot(b_proj, after_low)
    d_stepped = d_stepped + from_after
    grown_dy = grown * dy
    grown_low = grown_dy.astype(bf16)
    to_cum = head_sum(grown_dy * dot(c_proj, start), group_ones)
    left = head_sum(stepped * from_after, group_ones)
    kept = jnp.sum(after * start.astype(f32), axis=0, keepdims=True) * end_grown
    kept = head_sum(jnp.broadcast_to(kept, (8, inner)), group_ones)[0:1]
    last = kept + jnp.sum(left, axis=0, keepdims=True)
    row_id = lax.broadcasted_iota(jnp.int32, (rows, 128), 0)
    d_cum = d_cum + to_cum - left + jnp.where(row_id == rows - 1, last, 0.0)
    d_c = d_c + dot_nt(grown_low, start)
    d_b = d_b + dot_nt((fade * stepped).astype(bf16), after_low)
    lam[...] = end_grown * after + dot_tn(c_proj, grown_low)
    d_step = head_sum(d_stepped * x, group_ones)
    d_x = step * d_stepped + skip[0:1] * dy

    order_r = lax.broadcasted_iota(jnp.int32, (rows, rows), 0)
    order_c = lax.broadcasted_iota(jnp.int32, (rows, rows), 1)
    free = 1.0 - flags[...]
    d_decay = exact_left((order_r <= order_c).astype(bf16), d_cum) * free[:, 1:2]
    rate = params[1:2]
    real = lane < heads
    step_raw = jnp.where(real, info, 0.0) + params[0:1]
    slope = sigmoid(step_raw)
    d_pre = jnp.where(real, (d_step + d_decay * rate) * slope, 0.0)
    d_step_out[...] = d_pre.astype(bf16)
    head_grads[0:1] += jnp.sum(d_pre, axis=0, keepdims=True)
    head_grads[1:2] += jnp.sum(jnp.where(real, d_decay * softplus(step_raw) * rate, 0.0), axis=0, keepdims=True)

    d_active = jnp.concatenate([d_x, d_b, d_c], axis=1)
    d_conv = d_active * (gates * (1.0 + values * (1.0 - gates)))
    taken = conv_in[...].astype(f32)
    total = d_conv * conv_w[0:1]
    conv_grads[0:1] += jnp.sum(d_conv * taken, axis=0, keepdims=True)
    conv_grads[4:5] += jnp.sum(d_conv, axis=0, keepdims=True)
    for j in range(1, 4):
        ref = shifts[j - 1]
        ref[0:rows] = d_conv * free[:, j : j + 1]
        moved = ref[pl.ds(j, rows)]
        total = total + moved * conv_w[j : j + 1]
        conv_grads[j : j + 1] += jnp.sum(moved * taken, axis=0, keepdims=True)
    d_conv_in_out[...] = total.astype(bf16)

    @pl.when(at == pl.num_programs(0) - 1)
    def _():
        ahead = conv_halo[...].astype(f32)
        halo_out[...] = jnp.zeros_like(halo_out)
        for j in range(1, 4):
            first = shifts[j - 1][0:8]
            for t in range(j):
                row = 16 + t - j
                conv_grads[j : j + 1] += first[t : t + 1] * ahead[row : row + 1]
                halo_out[row - 8 : row - 7] += first[t : t + 1] * conv_w[j : j + 1]
    for each in shifts:
        each[rows:] = each[0:8]


def back(d_ssm, conv_out, conv_in, heads_in, starts, entering, flags, conv_w, params, skip, conv_halo,
         heads, head_dim, state_dim):
    length, inner = d_ssm.shape
    count = length // GROUP
    conv = conv_out.shape[1]

    def by(cols):
        return pl.BlockSpec((GROUP, cols), lambda g: (count - 1 - g, 0))
    shape = jax.ShapeDtypeStruct
    return pl.pallas_call(
        functools.partial(back_kernel, heads, head_dim, state_dim),
        grid=(count,),
        out_shape=(shape((length, conv), bf16), shape((length, 128), bf16), shape((8, conv), f32),
                   shape((8, 128), f32), shape((8, conv), f32)),
        in_specs=[by(inner), by(conv), by(conv), by(128),
                  pl.BlockSpec((1, state_dim, inner), lambda g: (count - 1 - g, 0, 0)),
                  whole(entering.shape), by(8), whole(conv_w.shape), whole(params.shape),
                  whole(skip.shape), whole(conv_halo.shape)],
        out_specs=(by(conv), by(128), whole((8, conv)), whole((8, 128)), whole((8, conv))),
        scratch_shapes=[pltpu.VMEM((state_dim, inner), f32)] + [pltpu.VMEM((GROUP + 8, conv), f32)] * 3,
        compiler_params=params_of("back"), name="back",
    )(d_ssm, conv_out, conv_in, heads_in, starts, entering, flags, conv_w, params, skip, conv_halo)


def project_kernel(count, normed, tokens, d_gate, d_conv, d_step, d_back, weights,
                   partial_out, grad_zx, grad_bc, grad_gain):
    at = pl.program_id(0)
    inner = d_gate.shape[1]

    @pl.when(at == 0)
    def _():
        grad_zx[...] = jnp.zeros_like(grad_zx)
        grad_bc[...] = jnp.zeros_like(grad_bc)
        grad_gain[...] = jnp.zeros_like(grad_gain)

    def add(block, source, d_rows, skipped):
        d_normed = dot_nt(d_rows, weights[:, skipped:])
        grad_zx[:, skipped:] += dot_tn(block, d_rows[:, : 2 * inner - skipped])
        grad_bc[...] += dot_tn(d_rows[:, 2 * inner - skipped :], block)
        value = source.astype(f32)
        inv = lax.rsqrt(jnp.mean(value * value, axis=1, keepdims=True) + epsilon)
        grad_gain[0:1] += jnp.sum(d_normed * (value * inv), axis=0, keepdims=True)
        return d_normed
    d_rows = jnp.concatenate([d_gate[...], d_conv[...], d_step[...]], axis=1)
    partial_out[...] = add(normed[...], tokens[...], d_rows, 0).astype(bf16)

    @pl.when(at == count - 1)
    def _():
        extra = add(normed[GROUP - 16 :], tokens[GROUP - 16 :], d_back[...], inner)
        partial_out[GROUP - 16 :] = (partial_out[GROUP - 16 :].astype(f32) + extra).astype(bf16)


def project_back(normed, tokens, d_gate, d_conv, d_step, d_back, weights):
    length, width = normed.shape
    inner, conv = d_gate.shape[1], d_conv.shape[1]
    count = length // GROUP
    rest = weights.shape[1] - 2 * inner

    def by(cols):
        return pl.BlockSpec((GROUP, cols), lambda g: (g, 0))
    shape = jax.ShapeDtypeStruct
    return pl.pallas_call(
        functools.partial(project_kernel, count),
        grid=(count,),
        out_shape=(shape((length, width), bf16), shape((width, 2 * inner), f32), shape((rest, width), f32),
                   shape((8, width), f32)),
        in_specs=[by(width), by(width), by(inner), by(conv), by(128), whole(d_back.shape),
                  whole(weights.shape)],
        out_specs=(by(width), whole((width, 2 * inner)), whole((rest, width)), whole((8, width))),
        compiler_params=params_of("project_back"), name="project_back",
    )(normed, tokens, d_gate, d_conv, d_step, d_back, weights)


def swap_kernel(own, out, slots, sems):
    size, me = lax.axis_size("head"), lax.axis_index("head")
    greet_axis("head")

    def copy(to, source):
        return pltpu.make_async_remote_copy(
            src_ref=own, dst_ref=slots.at[source], send_sem=sems.at[0, to], recv_sem=sems.at[1, source],
            device_id={"head": to}, device_id_type=MESH)

    @pl.loop(1, size)
    def _(k):
        copy(lax.rem(me + k, size), me).start()
    slots[me] = own[...]

    @pl.loop(1, size)
    def _(k):
        copy(me, lax.rem(me + k, size)).wait_recv()
    total = slots[0]
    for k in range(1, size):
        total = total + slots[k]
    out[...] = total

    @pl.loop(1, size)
    def _(k):
        copy(lax.rem(me + k, size), me).wait_send()


def head_total(sums):
    size = lax.axis_size("head")
    return pl.pallas_call(
        swap_kernel, out_shape=jax.ShapeDtypeStruct(sums.shape, f32),
        in_specs=[VMEM], out_specs=VMEM,
        scratch_shapes=[pltpu.VMEM((size,) + sums.shape, f32), pltpu.SemaphoreType.DMA((2, size))],
        compiler_params=pltpu.CompilerParams(collective_id=5, has_side_effects=True),
        name="head_total",
    )(sums)


def begin_kernel(tokens, gain, tail_rows, proj_bc, conv_bc,
                 normed, halo, proj_all, conv_all, landed, sems, seq_sems):
    heads, my_head = lax.axis_size("head"), lax.axis_index("head")
    seq, me = lax.axis_size("seq"), lax.axis_index("seq")
    before, after = lax.rem(me + seq - 1, seq), lax.rem(me + 1, seq)
    barrier = pltpu.get_barrier_semaphore()

    @pl.loop(1, heads)
    def _(k):
        pl.semaphore_signal(barrier, inc=1, device_id={"head": lax.rem(my_head + k, heads)},
                            device_id_type=MESH)
    for to in (before, after):
        pl.semaphore_signal(barrier, inc=1, device_id={"seq": to}, device_id_type=MESH)
    pl.semaphore_wait(barrier, heads + 1)

    def copies(to, source):
        return [pltpu.make_async_remote_copy(
            src_ref=src, dst_ref=dst.at[source], send_sem=sems.at[i, to], recv_sem=sems.at[i + 1, source],
            device_id={"head": to}, device_id_type=MESH)
            for src, dst, i in ((proj_bc, proj_all, 0), (conv_bc, conv_all, 2))]
    row_copy = pltpu.make_async_remote_copy(
        src_ref=tail_rows, dst_ref=landed, send_sem=seq_sems.at[0], recv_sem=seq_sems.at[1],
        device_id={"seq": after}, device_id_type=MESH)
    row_copy.start()

    @pl.loop(1, heads)
    def _(k):
        for copy in copies(lax.rem(my_head + k, heads), my_head):
            copy.start()
    proj_all[my_head] = proj_bc[...]
    conv_all[my_head] = conv_bc[...]
    count = tokens.shape[0] // 128

    @pl.loop(0, count)
    def _(b):
        rows = pl.ds(pl.multiple_of(b * 128, 128), 128)
        normed[rows] = norm_rows(tokens[rows], gain[0:1])
    row_copy.wait()
    halo[...] = jnp.where(me > 0, norm_rows(landed[...], gain[0:1]), jnp.zeros(halo.shape, bf16))

    @pl.loop(1, heads)
    def _(k):
        other = lax.rem(my_head + k, heads)
        for copy in copies(my_head, other):
            copy.wait_recv()
        for copy in copies(other, my_head):
            copy.wait_send()


def begin(tokens, gain, tail_rows, proj_bc, conv_bc):
    heads = lax.axis_size("head")
    shape = jax.ShapeDtypeStruct
    return pl.pallas_call(
        begin_kernel,
        out_shape=(shape(tokens.shape, bf16), shape(tail_rows.shape, bf16),
                   shape((heads,) + proj_bc.shape, bf16), shape((heads,) + conv_bc.shape, f32)),
        in_specs=[VMEM] * 5, out_specs=(VMEM,) * 4,
        scratch_shapes=[pltpu.VMEM(tail_rows.shape, bf16), pltpu.SemaphoreType.DMA((4, heads)),
                        pltpu.SemaphoreType.DMA((2,))],
        compiler_params=pltpu.CompilerParams(
            collective_id=6, has_side_effects=True, vmem_limit_bytes=32 * 2**20),
        name="begin",
    )(tokens, gain, tail_rows, proj_bc, conv_bc)


def halo_kernel(own, out, sems):
    seq, me = lax.axis_size("seq"), lax.axis_index("seq")
    before, after = lax.rem(me + seq - 1, seq), lax.rem(me + 1, seq)
    barrier = pltpu.get_barrier_semaphore()
    for to in (before, after):
        pl.semaphore_signal(barrier, inc=1, device_id={"seq": to}, device_id_type=MESH)
    pl.semaphore_wait(barrier, 2)
    copy = pltpu.make_async_remote_copy(
        src_ref=own, dst_ref=out, send_sem=sems.at[0], recv_sem=sems.at[1],
        device_id={"seq": before}, device_id_type=MESH)
    copy.start()
    copy.wait()


def to_before(rows):
    return pl.pallas_call(
        halo_kernel, out_shape=jax.ShapeDtypeStruct(rows.shape, rows.dtype),
        in_specs=[VMEM], out_specs=VMEM, scratch_shapes=[pltpu.SemaphoreType.DMA((2,))],
        compiler_params=pltpu.CompilerParams(collective_id=7, has_side_effects=True),
        name="to_before",
    )(rows)


def padded(block, rows, cols):
    return jnp.pad(block, ((0, rows - block.shape[0]), (0, cols - block.shape[1])))


def shards(
    tokens, start_flags, in_gain, proj_zx, proj_bc, proj_dt, conv_x_weight, conv_x_bias,
    conv_bc_weight, conv_bc_bias, dt_bias, a_log, skip_scale, norm_gain, out_proj, cotangent,
):
    length, width = tokens.shape
    heads = a_log.shape[0]
    inner = proj_zx.shape[2]
    head_dim = inner // heads
    taps = conv_x_weight.shape[0]
    head_count = lax.axis_size("head")
    bc_part = conv_bc_bias.shape[0]
    bc_width = bc_part * head_count
    state_dim = bc_width // 2
    my_head = lax.axis_index("head")

    flag = start_flags.astype(f32)
    free = 1.0 - flag
    free1 = jnp.pad(free, (1, 0), constant_values=1.0)[:length]
    free2 = jnp.pad(free, (2, 0), constant_values=1.0)[:length]
    flags = jnp.pad(jnp.stack([flag, 1.0 - free * free1, 1.0 - free * free1 * free2], axis=1), ((0, 0), (1, 4)))
    last = jnp.stack([free[length - 1] * free[length - 2], free[length - 1], jnp.ones((), f32)])
    tail_mask = jnp.pad(last, (13, 0))[:, None]
    tail_rows = (tokens[length - 16 :].astype(f32) * tail_mask).astype(bf16)
    gain8 = jnp.broadcast_to(in_gain[None], (8, width))
    conv_bc = padded(jnp.concatenate([conv_bc_weight.astype(f32), conv_bc_bias[None]]), 8, bc_part)

    normed, halo, proj_all, conv_all = begin(tokens, gain8, tail_rows, proj_bc, conv_bc)

    eight = jnp.pad(proj_dt, ((0, 0), (0, 8 - heads)))
    weights = jnp.concatenate(
        [proj_zx[:, 0], proj_zx[:, 1], jnp.moveaxis(proj_all, 0, 1).reshape(width, bc_width)]
        + [eight] * 16, axis=1)
    conv_x = padded(jnp.concatenate([conv_x_weight.astype(f32), conv_x_bias[None]]), 8, inner)
    conv_w = jnp.concatenate([conv_x, jnp.moveaxis(conv_all, 0, 1).reshape(8, bc_width)], axis=1)
    head_rows = jnp.pad(jnp.stack([dt_bias, -jnp.exp(a_log)]), ((0, 6), (0, 8 - heads)))
    params = jnp.tile(head_rows, (1, 16))
    skip = jnp.repeat(skip_scale, head_dim)
    gains = jnp.pad(jnp.stack([norm_gain, skip]), ((0, 6), (0, 0)))
    skip8 = jnp.broadcast_to(skip[None], (8, inner))

    gate, conv_in, conv_out, info, state, decay, conv_halo = front(
        normed, halo, weights, flags, conv_w, params, heads, head_dim, state_dim)
    entering = device_scan(state, decay, False)
    ssm, d_normed_out, partial, sums, starts = mix(
        conv_out, info, gate, cotangent, out_proj, gains, entering, heads, head_dim, state_dim)
    sums = head_total(sums)
    mixed = line_sum(partial, 64)
    all_channels = inner * head_count
    inv_rms = lax.rsqrt(sums[0].reshape(length, 1) / all_channels + epsilon)
    mixed_out = (tokens.astype(f32) + mixed.astype(f32) * inv_rms).astype(bf16)
    d_ssm, d_gate, grad_out, gate_rows, d_total = gate_back(
        ssm, gate, d_normed_out, sums, conv_out, info, cotangent, gains, heads, head_dim, state_dim,
        all_channels)
    leaving = device_scan(d_total, decay, True)
    d_conv, d_step, conv_grads, head_grads, back_rows = back(
        d_ssm, conv_out, conv_in, info, starts, leaving, flags, conv_w, params, skip8, conv_halo,
        heads, head_dim, state_dim)
    landed = to_before(back_rows)
    last_device = lax.axis_index("seq") == lax.axis_size("seq") - 1
    landed = jnp.where(last_device, 0.0, landed * tail_mask[8:])
    d_back = jnp.pad(landed.astype(bf16), ((8, 0), (0, 128)))
    part, grad_zx, grad_bc, grad_gain = project_back(
        normed, tokens, d_gate, d_conv, d_step, d_back, weights)

    right = jnp.concatenate([gate_rows[:2], padded(head_grads[:2], 6, inner)])
    small = jnp.concatenate([
        grad_bc[bc_width : bc_width + 8],
        padded(jnp.concatenate([conv_grads[:, :inner], right], axis=1), 8, width),
        grad_gain[:1], padded(conv_grads[: taps + 1, inner:], 7, width)])
    d_normed, zx_sum, op_sum, bc_sum, small_sum = tail(
        part, grad_zx.astype(bf16), grad_out.astype(bf16),
        grad_bc[:bc_width].reshape(head_count, bc_part, width), small, 8, 64)

    tokens_f = tokens.astype(f32)
    inv = lax.rsqrt(jnp.mean(tokens_f * tokens_f, axis=1, keepdims=True) + epsilon)
    xhat = tokens_f * inv
    scaled = d_normed.astype(f32) * in_gain
    grad_tokens = cotangent.astype(f32) + inv * (
        scaled - xhat * jnp.mean(scaled * xhat, axis=1, keepdims=True))
    conv_bc_sum = lax.dynamic_slice(small_sum, (17, my_head * bc_part), (taps + 1, bc_part))
    return (
        mixed_out,
        grad_tokens,
        small_sum[16],
        zx_sum.astype(f32).reshape(width, 2, inner),
        bc_sum.T,
        small_sum[:heads].T,
        small_sum[8 : 8 + taps, :inner],
        small_sum[8 + taps, :inner],
        conv_bc_sum[:taps],
        conv_bc_sum[taps],
        small_sum[10, inner : inner + heads],
        small_sum[11, inner : inner + heads],
        small_sum[9, inner : 2 * inner].reshape(heads, head_dim).sum(axis=1),
        small_sum[8, inner : 2 * inner],
        op_sum.astype(f32),
    )


def solution(mesh):
    in_specs = (
        P("seq", None),
        P("seq"),
        P(),
        P(None, None, "head"),
        P(None, "head"),
        P(None, "head"),
        P(None, "head"),
        P("head"),
        P(None, "head"),
        P("head"),
        P("head"),
        P("head"),
        P("head"),
        P("head"),
        P("head", None),
        P("seq", None),
    )
    out_specs = (
        P("seq", None),
        P("seq", None),
        P(),
        P(None, None, "head"),
        P(None, "head"),
        P(None, "head"),
        P(None, "head"),
        P("head"),
        P(None, "head"),
        P("head"),
        P("head"),
        P("head"),
        P("head"),
        P("head"),
        P("head", None),
    )
    return jax.shard_map(shards, mesh=mesh, in_specs=in_specs, out_specs=out_specs, check_vma=False)
```

time: 895 us -> 524 us (0.59)
  matrix products: 176 us -> 0 us
  other arithmetic: 122 us -> 24.7 us
  local copies, waits for them, and re-layouts: 83.5 us -> 46.3 us
  blocking collectives: 30.8 us -> 0 us
  Pallas kernels: 421 us -> 449 us
  waiting for transfers between devices: 28 us -> 0 us
  between operations: 16.7 us -> 2.35 us
    pallas_call x0 -> x10, Pallas kernels: none -> 197 us  [the longest x1 52.9 us: back(): pl.pallas_call(functools.partial(back_kernel, heads, head_dim, state_dim)...]
    dot_general x27 -> x0, matrix products: 176 us -> none  [the longest x3 74.7 us: group_output(): inner_part = jnp.einsum('tsh,shp->thp', weights, x_heads, precision=highest)]
    pallas_call x1, Pallas kernels: 203 us -> 105 us  [line_sum(): pl.pallas_call(functools.partial(line_sum_kernel, block), out_shape=jax.S...]
    pallas_call x1, Pallas kernels: 218 us -> 148 us  [tail(): pl.pallas_call(functools.partial(tail_kernel, block, owners), out_shape=(...]
    reduce_sum x12 -> x3, other arithmetic: 43.6 us -> 3.48 us  [the longest x1 1.97 us: shards(): jnp.mean(scaled * xhat, axis=1, keepdims=True)]
    all_gather x3 -> x0, waiting for transfers between devices: 26.5 us -> none  [the longest x1 19.5 us: shards(): lax.all_gather(active[:, local_inner:].astype(jnp.bfloat16), 'head', axis...]
    psum x2 -> x0, blocking collectives: 21.9 us -> none  [the longest x1 12.7 us: shards(): square_sum = lax.psum(jnp.sum(gated_out * gated_out, axis=1), 'head')]
    unnamed x350 -> x66, local copies, waits for them, and re-layouts: 31.8 us -> 12.4 us
  transfers between devices with their start and end apart: 7 -> 0, of which waited for: 3 -> 0; matrix products, arithmetic and copies ran while one was open for 15% -> 0% of each run, Pallas kernels for 23% -> 0%
where the time goes in v2:
time: 524 us; the launch traced here: 523 us
  Pallas kernels  449 us (86%)
  local copies, waits for them, and re-layouts  46.3 us (9%)
  other arithmetic  24.7 us (5%)
    pallas_call x1, Pallas kernels, tail(): pl.pallas_call(functools.partial(tail_kernel, block, owners), out_shape=(...  148 us
    pallas_call x1, Pallas kernels, line_sum(): pl.pallas_call(functools.partial(line_sum_kernel, block), out_shape=jax.S...  105 us
    pallas_call x1, Pallas kernels, back(): pl.pallas_call(functools.partial(back_kernel, heads, head_dim, state_dim)...  52.9 us
    pallas_call x2, Pallas kernels, device_scan(): pl.pallas_call(functools.partial(scan_kernel, backward), out_shape=jax.Sh...  25.8 us
    pallas_call x1, Pallas kernels, begin(): pl.pallas_call(begin_kernel, out_shape=(shape(tokens.shape, bf16), shape(...  24.8 us
    pallas_call x1, Pallas kernels, project_back(): pl.pallas_call(functools.partial(project_kernel, count), grid=(count,), o...  21.4 us
    pallas_call x1, Pallas kernels, mix(): pl.pallas_call(functools.partial(mix_kernel, heads, head_dim, state_dim),...  21 us
    pallas_call x1, Pallas kernels, front(): pl.pallas_call(functools.partial(front_kernel, heads, head_dim, state_dim...  20.5 us

profile of v2, /device:TPU:0, one launch (start us, length us, event | category | flops | bytes accessed | tf_op | source)
XLA Modules:
  0.0 522.8 jit_solution(596212526644522384)
XLA Ops:
  7.9 2.2 copy-done
  10.1 24.8 %begin.1 = (bf16[2048,1024]{1,0:T(8,128)(2,1)S(1)}, bf16[16,1024]{1,0:T(8,128)(2,1)S(1)}, bf16[4,1024,64]{2,1,0:T(8,128)(2,1)S(1)}, f32[4,8,64]{2,1,0:T(8,128)S(1)}) custom-call(bf16[2048,1024]{1,0:T(8,128)(2,1)S(1)} %copy-done, f32[8,1024]{1,0:T(8,128)S(1)} %broadcast_in_dim.30.gain, bf16[16,1024]{1,0:T(8,128)(2,1)S(1)} %multiply_convert_fusion.tail_rows, ...), custom_call_target="tpu_custom_call" | custom-call | tf_op jit(solution)/shard_map/begin/pallas_call | solution.py:1088
  34.9 2.0 copy-done.2
  38.6 2.0 copy.81
  40.7 3.0 fusion.16
  44.7 8.5 %concatenate.22.weights = bf16[1024,1408]{1,0:T(8,128)(2,1)} concatenate(bf16[1024,512]{1,0:T(8,128)(2,1)S(1)} %get-tuple-element.99, bf16[1024,512]{1,0:T(8,128)(2,1)S(1)} %get-tuple-element.98, bf16[1024,256]{1,0:T(8,128)(2,1)S(1)} %copy-done.14, bf16[1024,8]{1,0:T(8,128)(2,1)S(1)} %copy.82, bf16[1024,8]{1,0:T(8,128)(2,1)S(1)} %copy.82, bf16[1024,8]{1,0:T(8,128)(2,1)S(1)} %copy.82, ...), dimensions={1} | concatenate | bytes 5767168 | tf_op jit(solution)/shard_map/concatenate | solution.py:1157
  54.4 1.4 pad.48.flags
  56.5 20.5 %front.1 = (f32[2048,512]{1,0:T(8,128)}, bf16[2048,768]{1,0:T(8,128)(2,1)}, f32[2048,768]{1,0:T(8,128)}, f32[2048,128]{1,0:T(8,128)}, f32[128,512]{1,0:T(8,128)}...) custom-call(bf16[2048,1024]{1,0:T(8,128)(2,1)} %copy-done.2, bf16[16,1024]{1,0:T(8,128)(2,1)} %copy-done.9, ...), custom_call_target="tpu_custom_call" | custom-call | tf_op jit(solution)/shard_map/front/pallas_call | solution.py:561
  78.7 12.7 %scan_ahead.1.entering = f32[128,512]{1,0:T(8,128)S(1)} custom-call(f32[128,512]{1,0:T(8,128)S(1)} %copy-done.6, f32[8,512]{1,0:T(8,128)S(1)} %copy-done.7), custom_call_target="tpu_custom_call" | custom-call | tf_op jit(solution)/shard_map/scan_ahead/pallas_call | solution.py:621
  92.8 21.0 %mix.1 = (f32[2048,512]{1,0:T(8,128)}, f32[2048,512]{1,0:T(8,128)}, bf16[2048,1024]{1,0:T(8,128)(2,1)}, f32[2,8,256]{2,1,0:T(8,128)}, bf16[8,128,512]{2,1,0:T(8,128)(2,1)}) custom-call(f32[2048,768]{1,0:T(8,128)} %get-tuple-element.54.conv_out, f32[2048,128]{1,0:T(8,128)} %get-tuple-element.55.heads_in, f32[2048,512]{1,0:T(8,128)} %get-tuple-element.56.gate, ...), custom_call_target="tpu_custom_call" | custom-call | tf_op jit(solution)/shard_map/mix/pallas_call | solution.py:711
  113.9 11.2 %head_total.1.sums = f32[2,8,256]{2,1,0:T(8,128)} custom-call(f32[2,8,256]{2,1,0:T(8,128)} %get-tuple-element.60.own), custom_call_target="tpu_custom_call" | custom-call | tf_op jit(solution)/shard_map/head_total/pallas_call | solution.py:1027
  125.0 16.3 %gate_back.1 = (f32[2048,512]{1,0:T(8,128)}, bf16[2048,512]{1,0:T(8,128)(2,1)}, f32[512,1024]{1,0:T(8,128)}, f32[8,512]{1,0:T(8,128)}, f32[128,512]{1,0:T(8,128)}) custom-call(f32[2048,512]{1,0:T(8,128)} %get-tuple-element.61.ssm, f32[2048,512]{1,0:T(8,128)} %get-tuple-element.56.gate, f32[2048,512]{1,0:T(8,128)} %get-tuple-element.62.d_normed, ...), custom_call_target="tpu_custom_call" | custom-call | tf_op jit(solution)/shard_map/gate_back/pallas_call | solution.py:769
  142.3 13.1 %scan_back.1.entering = f32[128,512]{1,0:T(8,128)S(1)} custom-call(f32[128,512]{1,0:T(8,128)S(1)} %copy-done.5, f32[8,512]{1,0:T(8,128)S(1)} %copy-done.8), custom_call_target="tpu_custom_call" | custom-call | tf_op jit(solution)/shard_map/scan_back/pallas_call | solution.py:621
  156.8 52.9 %back.1 = (bf16[2048,768]{1,0:T(8,128)(2,1)}, bf16[2048,128]{1,0:T(8,128)(2,1)}, f32[8,768]{1,0:T(8,128)}, f32[8,128]{1,0:T(8,128)}, f32[8,768]{1,0:T(8,128)}) custom-call(f32[2048,512]{1,0:T(8,128)} %get-tuple-element.64.d_ssm, f32[2048,768]{1,0:T(8,128)} %get-tuple-element.54.conv_out, bf16[2048,768]{1,0:T(8,128)(2,1)} %get-tuple-element.65.conv_in, ...), custom_call_target="tpu_custom_call" | custom-call | tf_op jit(solution)/shard_map/back/pallas_call | solution.py:934
  209.7 3.2 to_before.1
  214.4 21.4 %project_back.1 = (bf16[2048,1024]{1,0:T(8,128)(2,1)}, f32[1024,1024]{1,0:T(8,128)}, f32[384,1024]{1,0:T(8,128)}, f32[8,1024]{1,0:T(8,128)}) custom-call(bf16[2048,1024]{1,0:T(8,128)(2,1)} %copy-done.2, bf16[2048,1024]{1,0:T(8,128)(2,1)} %tokens.3, bf16[2048,512]{1,0:T(8,128)(2,1)} %get-tuple-element.63.d_gate, bf16[2048,768]{1,0:T(8,128)(2,1)} %get-tuple-element.69.d_conv, ...), custom_call_target="tpu_custom_call" | custom-call | tf_op jit(solution)/shard_map/project_back/pallas_call | solution.py:986
  239.5 4.0 convert_element_type.72.zx
  245.7 147.7 %tail.1 = (bf16[2048,1024]{1,0:T(8,128)(2,1)}, bf16[1024,1024]{1,0:T(8,128)(2,1)}, bf16[512,1024]{1,0:T(8,128)(2,1)}, f32[64,1024]{1,0:T(8,128)}, f32[24,1024]{1,0:T(8,128)}) custom-call(bf16[2048,1024]{1,0:T(8,128)(2,1)} %get-tuple-element.72.part, bf16[1024,1024]{1,0:T(8,128)(2,1)} %convert_element_type.72.zx, bf16[512,1024]{1,0:T(8,128)(2,1)} %convert_element_type.73.op, ...), custom_call_target="tpu_custom_call" | custom-call | tf_op jit(solution)/shard_map/tail/pallas_call | solution.py:393
  394.4 1.3 copy-done.11
  395.6 2.0 fusion.2
  397.7 104.7 %line_sum.1 = bf16[2048,1024]{1,0:T(8,128)(2,1)S(1)} custom-call(bf16[2048,1024]{1,0:T(8,128)(2,1)} %get-tuple-element.59.own), custom_call_target="tpu_custom_call" | custom-call | tf_op jit(solution)/shard_map/line_sum/pallas_call | solution.py:216
  502.5 8.1 %fusion.5 = (f32[2048,1024]{1,0:T(8,128)}, bf16[2048,1024]{1,0:T(8,128)(2,1)}) fusion(bf16[2048,1024]{1,0:T(8,128)(2,1)S(1)} %copy-done.1, bf16[2048,1024]{1,0:T(8,128)(2,1)} %get-tuple-element.80, bf16[2048,1024]{1,0:T(8,128)(2,1)S(1)} %copy-done.10, f32[2048]{0:T(1024)S(1)} %broadcast_multiply_fusion, f32[1024]{0:T(1024)S(1)} %copy-done.20, ...), kind=kLoop, calls=%fused_computation.8 | loop fusion | flops 27262976 | bytes 29388800 | tf_op jit(solution)/shard_map/add | solution.py:1205
  510.6 5.1 reshape.90
  515.7 1.6 convert_element_type.75
  (116 shorter events, 29.9 us)
Async XLA Ops:
  7.9 2.2 copy-start
  10.1 30.6 %copy-start.12 = (bf16[1024,2,512]{2,1,0:T(2,128)(2,1)S(1)}, bf16[1024,2,512]{2,1,0:T(2,128)(2,1)}, u32[]{:S(2)}) copy-start(bf16[1024,2,512]{2,1,0:T(2,128)(2,1)} %param.19) | copy-start | bytes 6291460
  34.9 2.0 copy-start.2
  43.7 1.0 copy-start.14
  44.7 8.6 %copy-start.25 = (bf16[4,512]{1,0:T(4,128)(2,1)S(1)}, bf16[4,512]{1,0:T(4,128)(2,1)}, u32[]{:S(2)}) copy-start(bf16[4,512]{1,0:T(4,128)(2,1)} %param.22) | copy-start | bytes 12292
  44.7 8.6 %copy-start.27 = (f32[512]{0:T(512)S(1)}, f32[512]{0:T(512)}, u32[]{:S(2)}) copy-start(f32[512]{0:T(512)} %param.23) | copy-start | bytes 6148
  44.7 9.3 %copy-start.21 = (s32[2048]{0:T(1024)S(1)}, s32[2048]{0:T(1024)}, u32[]{:S(2)}) copy-start(s32[2048]{0:T(1024)} %param.17) | copy-start | bytes 24580
  44.7 11.1 %copy-start.30 = (f32[8]{0:T(128)S(1)}, f32[8]{0:T(128)}, u32[]{:S(2)}) copy-start(f32[8]{0:T(128)} %param.27) | copy-start | bytes 100
  44.7 11.1 %copy-start.28 = (f32[8]{0:T(128)S(1)}, f32[8]{0:T(128)}, u32[]{:S(2)}) copy-start(f32[8]{0:T(128)} %param.26) | copy-start | bytes 100
  56.5 35.6 %copy-start.29 = (f32[8]{0:T(128)S(1)}, f32[8]{0:T(128)}, u32[]{:S(2)}) copy-start(f32[8]{0:T(128)} %param.28) | copy-start | bytes 100
  56.5 35.7 %copy-start.26 = (f32[512]{0:T(512)S(1)}, f32[512]{0:T(512)}, u32[]{:S(2)}) copy-start(f32[512]{0:T(512)} %param.29) | copy-start | bytes 6148
  125.0 16.3 %copy-start.8 = (f32[8,512]{1,0:T(8,128)S(1)}, f32[8,512]{1,0:T(8,128)}, u32[]{:S(2)}) copy-start(f32[8,512]{1,0:T(8,128)} %get-tuple-element.58.decay) | copy-start | bytes 49156
  214.4 23.1 %copy-start.23 = (f32[8,768]{1,0:T(8,128)S(1)}, f32[8,768]{1,0:T(8,128)}, u32[]{:S(2)}) copy-start(f32[8,768]{1,0:T(8,128)} %get-tuple-element.76) | copy-start | bytes 73732
  235.8 7.7 %copy-start.17 = (f32[384,1024]{1,0:T(8,128)S(1)}, f32[384,1024]{1,0:T(8,128)}, u32[]{:S(2)}) copy-start(f32[384,1024]{1,0:T(8,128)} %get-tuple-element.75) | copy-start | bytes 4718596
  239.5 5.0 copy-start.15
  245.7 147.8 %copy-start.1 = (bf16[2048,1024]{1,0:T(8,128)(2,1)S(1)}, bf16[2048,1024]{1,0:T(8,128)(2,1)}, u32[]{:S(2)}) copy-start(bf16[2048,1024]{1,0:T(8,128)(2,1)} %tokens.3) | copy-start | bytes 12582916
  393.5 2.2 copy-start.11
  393.5 2.2 copy-start.20
  397.6 104.8 %copy-start.19 = (f32[2,8,256]{2,1,0:T(8,128)S(1)}, f32[2,8,256]{2,1,0:T(8,128)}, u32[]{:S(2)}) copy-start(f32[2,8,256]{2,1,0:T(8,128)} %head_total.1.sums) | copy-start | bytes 49156
  397.6 104.8 %copy-start.10 = (bf16[2048,1024]{1,0:T(8,128)(2,1)S(1)}, bf16[2048,1024]{1,0:T(8,128)(2,1)}, u32[]{:S(2)}) copy-start(bf16[2048,1024]{1,0:T(8,128)(2,1)} %cot.3) | copy-start | bytes 12582916
  502.5 8.1 %copy-start.13 = (bf16[1024,1024]{1,0:T(8,128)(2,1)S(1)}, bf16[1024,1024]{1,0:T(8,128)(2,1)}, u32[]{:S(2)}) copy-start(bf16[1024,1024]{1,0:T(8,128)(2,1)} %get-tuple-element.82) | copy-start | bytes 6291460
  510.6 5.2 copy-start.16
  510.6 6.7 %copy-start.22 = (f32[24,1024]{1,0:T(8,128)S(1)}, f32[24,1024]{1,0:T(8,128)}, u32[]{:S(2)}) copy-start(f32[24,1024]{1,0:T(8,128)} %get-tuple-element.81) | copy-start | bytes 294916
  510.6 11.5 %copy-start.18 = (f32[64,1024]{1,0:T(8,128)S(1)}, f32[64,1024]{1,0:T(8,128)}, u32[]{:S(2)}) copy-start(f32[64,1024]{1,0:T(8,128)} %get-tuple-element.83) | copy-start | bytes 786436
  (7 other events, 5.4 us)

commit v3 on v2

v3 whole, which is shorter than its diff:
```python
import functools

import jax
import jax.numpy as jnp
from jax import lax
from jax.experimental import pallas as pl
from jax.experimental.pallas import tpu as pltpu
from jax.sharding import PartitionSpec as P

MESH = pl.DeviceIdType.MESH
f32 = jnp.float32
bf16 = jnp.bfloat16
VMEM = pl.BlockSpec(memory_space=pltpu.VMEM)
HBM = pl.BlockSpec(memory_space=pl.ANY)
DMA = pltpu.SemaphoreType.DMA


def rows_of(ref, start, size):
    return ref.at[pl.ds(pl.multiple_of(start, size), size)]


def other_of(axis, k):
    size = lax.axis_size(axis)
    return lax.rem(lax.axis_index(axis) + k, size)


def greet(*axes):
    barrier = pltpu.get_barrier_semaphore()
    count = 0
    for axis in axes:
        size = lax.axis_size(axis)
        count += size - 1

        @pl.loop(1, size)
        def _(k):
            pl.semaphore_signal(barrier, inc=1, device_id={axis: other_of(axis, k)}, device_id_type=MESH)
    pl.semaphore_wait(barrier, count)


class LineSum:
    AHEAD = 3

    def __init__(self, own, got, total, out, sems, block):
        self.own, self.got, self.total, self.out = own, got, total, out
        self.send1, self.got_in, self.got_total, self.send2, self.stored = (sems.at[i] for i in range(5))
        self.block = block
        self.count = own.shape[0] // block
        size, me = lax.axis_size("head"), lax.axis_index("head")
        half = size // 2
        left = me < half
        self.mid = (me == half - 1) | (me == half)
        self.has_outer = (me > 0) & (me < size - 1)
        self.inner = jnp.where(left, me + 1, me - 1)
        self.outer = jnp.clip(jnp.where(left, me - 1, me + 1), 0, size - 1)

    @staticmethod
    def sems(rows, block):
        return DMA((5, rows // block))

    def rows(self, b):
        return pl.ds(pl.multiple_of(b * self.block, self.block), self.block)

    def copy(self, src, dst, b, send, recv, to):
        return pltpu.make_async_remote_copy(
            src_ref=src.at[self.rows(b)], dst_ref=dst.at[self.rows(b)],
            send_sem=send.at[b], recv_sem=recv.at[b], device_id={"head": to}, device_id_type=MESH)

    def store(self, b):
        return pltpu.make_async_copy(
            self.total.at[self.rows(b)], self.out.at[self.rows(b)], self.stored.at[b])

    def inward(self, b):
        rows = self.rows(b)

        @pl.when(self.has_outer)
        def _():
            self.copy(self.own, self.got, b, self.send1, self.got_in, self.outer).wait_recv()
            self.own[rows] = (self.got[rows].astype(f32) + self.own[rows].astype(f32)).astype(bf16)

        @pl.when(self.mid)
        def _():
            self.copy(self.own, self.total, b, self.send1, self.got_total, self.inner).start()

        @pl.when(jnp.logical_not(self.mid))
        def _():
            self.copy(self.own, self.got, b, self.send1, self.got_in, self.inner).start()

    def outward(self, b):
        rows = self.rows(b)
        self.copy(self.own, self.total, b, self.send1, self.got_total, self.inner).wait_recv()

        @pl.when(self.mid)
        def _():
            self.total[rows] = (self.own[rows].astype(f32) + self.total[rows].astype(f32)).astype(bf16)

        @pl.when(self.has_outer)
        def _():
            self.copy(self.total, self.total, b, self.send2, self.got_total, self.outer).start()
        self.store(b).start()

    def serve(self, first, last, lag):
        @pl.when(self.has_outer)
        def _():
            @pl.loop(first, last)
            def _(b):
                @pl.when(b < self.count)
                def _():
                    self.inward(b)

                @pl.when(b >= lag)
                def _():
                    self.outward(b - lag)

    def send(self, first, last):
        @pl.when(jnp.logical_not(self.has_outer))
        def _():
            @pl.loop(first, last)
            def _(b):
                @pl.when(b >= self.AHEAD)
                def _():
                    self.copy(self.own, self.got, b - self.AHEAD, self.send1, self.got_in, self.inner).wait_send()
                self.inward(b)

    def finish(self):
        @pl.when(jnp.logical_not(self.has_outer))
        def _():
            pl.loop(0, self.count)(self.outward)

        @pl.loop(0, self.count)
        def _(b):
            @pl.when(self.has_outer | (b >= self.count - self.AHEAD))
            def _():
                self.copy(self.own, self.got, b, self.send1, self.got_in, self.inner).wait_send()
            self.store(b).wait()

            @pl.when(self.has_outer)
            def _():
                self.copy(self.total, self.total, b, self.send2, self.got_total, self.outer).wait_send()


class PlaneSum:
    def __init__(self, own, slots, res, sems, owners):
        self.own, self.slots, self.res = own, slots, res
        self.rs_send, self.rs_got, self.ag_send, self.ag_got = (sems.at[i] for i in range(4))
        self.owners = owners
        self.size, self.me = lax.axis_size("seq"), lax.axis_index("seq")
        self.piece = own.shape[0] // owners

    def part(self, ref, k):
        return rows_of(ref, k * self.piece, self.piece)

    def scatter_copy(self, to, source):
        return pltpu.make_async_remote_copy(
            src_ref=self.part(self.own, to), dst_ref=self.slots.at[source],
            send_sem=self.rs_send.at[to], recv_sem=self.rs_got.at[source],
            device_id={"seq": to}, device_id_type=MESH)

    def gather_copy(self, owner, to):
        return pltpu.make_async_remote_copy(
            src_ref=self.part(self.res, owner), dst_ref=self.part(self.res, owner),
            send_sem=self.ag_send.at[to], recv_sem=self.ag_got.at[owner],
            device_id={"seq": to}, device_id_type=MESH)

    def scatter(self):
        @pl.loop(1, self.size)
        def _(k):
            to = other_of("seq", k)

            @pl.when(to < self.owners)
            def _():
                self.scatter_copy(to, self.me).start()

    def reduce(self):
        @pl.when(self.me < self.owners)
        def _():
            @pl.loop(1, self.size)
            def _(k):
                self.scatter_copy(self.me, other_of("seq", k)).wait_recv()
            mine = pl.ds(pl.multiple_of(self.me * self.piece, self.piece), self.piece)
            self.slots[self.me] = self.own[mine]
            total = self.slots[0].astype(f32)
            for k in range(1, self.size):
                total = total + self.slots[k].astype(f32)
            self.res[mine] = total.astype(self.res.dtype)

            @pl.loop(1, self.size)
            def _(k):
                self.gather_copy(self.me, other_of("seq", k)).start()

    def finish(self):
        @pl.loop(1, self.size)
        def _(k):
            other = other_of("seq", k)

            @pl.when(other < self.owners)
            def _():
                self.gather_copy(other, self.me).wait_recv()
                self.scatter_copy(other, self.me).wait_send()

        @pl.when(self.me < self.owners)
        def _():
            @pl.loop(1, self.size)
            def _(k):
                self.gather_copy(self.me, other_of("seq", k)).wait_send()


class Swap:
    def __init__(self, axis, own, slots, sems):
        self.axis, self.own, self.slots = axis, own, slots
        self.send, self.got = sems.at[0], sems.at[1]
        self.size, self.me = lax.axis_size(axis), lax.axis_index(axis)

    def copy(self, to, source):
        return pltpu.make_async_remote_copy(
            src_ref=self.own, dst_ref=self.slots.at[source],
            send_sem=self.send.at[to], recv_sem=self.got.at[source],
            device_id={self.axis: to}, device_id_type=MESH)

    def start(self):
        @pl.loop(1, self.size)
        def _(k):
            self.copy(other_of(self.axis, k), self.me).start()
        self.slots[self.me] = self.own[...]

    def wait(self):
        @pl.loop(1, self.size)
        def _(k):
            self.copy(self.me, other_of(self.axis, k)).wait_recv()

    def total(self):
        out = self.slots[0]
        for k in range(1, self.size):
            out = out + self.slots[k]
        return out

    def finish(self):
        @pl.loop(1, self.size)
        def _(k):
            self.copy(other_of(self.axis, k), self.me).wait_send()


class DeviceScan:
    def __init__(self, backward, total, fade, lead, out, got, got_fade, sent, sent_fade, sems):
        self.backward, self.total, self.fade, self.lead, self.out = backward, total, fade, lead, out
        self.got, self.got_fade, self.sent, self.sent_fade, self.sems = got, got_fade, sent, sent_fade, sems
        self.me = lax.axis_index("seq")
        self.rounds = lax.axis_size("seq").bit_length() - 1

    @staticmethod
    def scratch(state, fade):
        rounds = lax.axis_size("seq").bit_length() - 1
        return [pltpu.VMEM(fade, f32), pltpu.VMEM(fade, f32)] + [
            pltpu.VMEM((rounds,) + state, bf16), pltpu.VMEM((rounds,) + fade, f32)] * 2 + [DMA((4, rounds))]

    def copies(self, k):
        return [
            pltpu.make_async_remote_copy(
                src_ref=src.at[k], dst_ref=dst.at[k],
                send_sem=self.sems.at[i, k], recv_sem=self.sems.at[i + 1, k],
                device_id={"seq": jnp.bitwise_xor(self.me, 1 << k)}, device_id_type=MESH)
            for src, dst, i in ((self.sent, self.got, 0), (self.sent_fade, self.got_fade, 2))]

    def begin(self, decay):
        self.fade[...] = decay
        self.out[...] = jnp.zeros_like(self.out)
        self.lead[...] = jnp.ones_like(self.lead)

    def start(self, k):
        self.sent[k] = self.total[...].astype(bf16)
        self.sent_fade[k] = self.fade[...]
        for copy in self.copies(k):
            copy.start()

    def finish(self, k):
        for copy in self.copies(k):
            copy.wait()
        later = lax.rem(self.me // (1 << k), 2) == (0 if self.backward else 1)

        @pl.when(later)
        def _():
            theirs = self.got[k].astype(f32)
            self.out[...] = self.out[...] + self.lead[0:1] * theirs
            self.total[...] = self.total[...] + self.fade[0:1] * theirs
            self.lead[...] = self.lead[...] * self.got_fade[k]

        @pl.when(jnp.logical_not(later))
        def _():
            self.total[...] = self.got[k].astype(f32) + self.got_fade[k, 0:1] * self.total[...]
        self.fade[...] = self.fade[...] * self.got_fade[k]

    def run(self, between=None):
        for k in range(self.rounds):
            self.start(k)
            if between is not None:
                between(k)
            self.finish(k)


GROUP = 256
STRIP = 128
GAP = 200.0
epsilon = 1e-05
LIMIT = 56 * 2**20


def dot(a, b):
    return jnp.dot(a, b, preferred_element_type=f32)


def dot_nt(a, b):
    return lax.dot_general(a, b, (((1,), (1,)), ((), ())), preferred_element_type=f32)


def dot_tn(a, b):
    return lax.dot_general(a, b, (((0,), (0,)), ((), ())), preferred_element_type=f32)


def split3(v):
    one = v.astype(bf16)
    rest = v - one.astype(f32)
    two = rest.astype(bf16)
    return one, two, (rest - two.astype(f32)).astype(bf16)


def exact_left(ones, v):
    width = v.shape[1]
    out = dot(ones, jnp.concatenate(split3(v), axis=1))
    return out[:, :width] + out[:, width : 2 * width] + out[:, 2 * width :]


def head_sum(v, group_ones):
    high = v.astype(bf16)
    low = (v - high.astype(f32)).astype(bf16)
    return dot(high, group_ones) + dot(low, group_ones)


def sigmoid(v):
    return 1.0 / (1.0 + jnp.exp(-v))


def softplus(v):
    return jnp.maximum(v, 0.0) + jnp.log1p(jnp.exp(-jnp.abs(v)))


def spread(cols, first, heads, head_dim):
    rows = cols.shape[0]
    per = 128 // head_dim
    lane = lax.broadcasted_iota(jnp.int32, (rows, 128), 1)
    tiles = []
    for at in range(0, heads, per):
        tile = cols[:, first + at : first + at + 1]
        for k in range(1, per):
            tile = jnp.where(lane < k * head_dim, tile, cols[:, first + at + k : first + at + k + 1])
        tiles.append(jnp.broadcast_to(tile, (rows, 128)))
    return jnp.concatenate(tiles, axis=1)


def norm_rows(block, gain):
    value = block.astype(f32)
    inv = lax.rsqrt(jnp.mean(value * value, axis=1, keepdims=True) + epsilon)
    return (value * inv * gain).astype(bf16)


def whole(shape):
    return pl.BlockSpec(shape, lambda g: (0,) * len(shape))


def lane_groups(rows, *parts):
    lane = lax.broadcasted_iota(jnp.int32, (rows, 128), 1)
    out = parts[-1]
    for k in range(len(parts) - 2, -1, -1):
        out = jnp.where(lane < 8 * (k + 1), parts[k], out)
    return out


RAW, STEP, CUM, DEV = 0, 8, 16, 24


def front_kernel(heads, head_dim, state_dim, count,
                 tokens, zx, dt, flags, gain, tail_rows, proj_bc, conv_bc, conv_x, params,
                 normed_out, gate_out, conv_in_out, conv_out_out, heads_out, entering, decay_out,
                 halo_out, weights_out, conv_w_out,
                 normed, taken, landed, proj_all, conv_all, carry, ext, state, running, lead, fade,
                 scan_got, scan_got_fade, scan_sent, scan_sent_fade, scan_sems, proj_sems, conv_sems, row_sems):
    at = pl.program_id(0)
    rows = tokens.shape[0]
    inner = heads * head_dim
    bc_width = 2 * state_dim
    seq, me = lax.axis_size("seq"), lax.axis_index("seq")
    block = lax.rem(at, count)
    mine = pl.ds(pl.multiple_of(block * rows, rows), rows)
    swaps = [Swap("head", proj_bc, proj_all, proj_sems), Swap("head", conv_bc, conv_all, conv_sems)]
    row_copy = pltpu.make_async_remote_copy(
        src_ref=tail_rows, dst_ref=landed, send_sem=row_sems.at[0], recv_sem=row_sems.at[1],
        device_id={"seq": lax.rem(me + 1, seq)}, device_id_type=MESH)

    @pl.when(at == 0)
    def _():
        greet("head", "seq")
        row_copy.start()
        for each in swaps:
            each.start()

    @pl.when(at < count)
    def _():
        low = norm_rows(tokens[...], gain[0:1])
        normed[mine] = low
        normed_out[...] = low
        raw = dot(low, zx[...])
        gate_out[...] = raw[:, :inner]
        taken[mine] = raw[:, inner:].astype(bf16)

    @pl.when(at == count)
    def _():
        row_copy.wait()
        for each in swaps:
            each.wait()
            each.finish()
        heads_there = proj_all.shape[0]
        weights_out[:, :bc_width] = jnp.concatenate([proj_all[k] for k in range(heads_there)], axis=1)
        weights_out[:, bc_width:] = dt[...]
        conv_w_out[...] = jnp.concatenate([conv_x[...]] + [conv_all[k] for k in range(heads_there)], axis=1)
        head_rows = norm_rows(landed[...], gain[0:1])
        ahead = jnp.concatenate([dot(head_rows, zx[:, inner:]), dot(head_rows, weights_out[:, :bc_width])], axis=1)
        ahead = jnp.where(me > 0, ahead, 0.0).astype(bf16)
        halo_out[...] = ahead
        carry[...] = ahead[8:].astype(f32)
        state[...] = jnp.zeros_like(state)
        running[...] = jnp.zeros_like(running)

    @pl.when(at >= count)
    def _():
        raw = dot(normed[mine], weights_out[...])
        conv_in = jnp.concatenate([taken[mine], raw[:, :bc_width].astype(bf16)], axis=1)
        conv_in_out[...] = conv_in
        current = conv_in.astype(f32)
        ext[0:8] = carry[...]
        ext[8:] = current
        carry[...] = ext[rows:]
        keep = 1.0 - flags[...]
        total = conv_w_out[4:5] + conv_w_out[0:1] * current
        for j in range(1, 4):
            total = total + conv_w_out[j : j + 1] * ext[pl.ds(8 - j, rows)] * keep[:, j : j + 1]
        conv_out_out[...] = total
        active = total * sigmoid(total)

        step_raw = raw[:, bc_width:]
        step = softplus(step_raw + params[0:1])
        log_decay = step * params[1:2] - GAP * flags[:, 1:2]
        order_r = lax.broadcasted_iota(jnp.int32, (rows, rows), 0)
        order_c = lax.broadcasted_iota(jnp.int32, (rows, rows), 1)
        cum = exact_left((order_r >= order_c).astype(bf16), log_decay)
        heads_out[...] = lane_groups(rows, step_raw, step, cum, cum + running[0:1])
        end = cum[rows - 1 : rows]
        running[...] = running[...] + end
        weight = step * jnp.exp(end - cum)
        scaled = (active[:, :inner] * spread(weight, 0, heads, head_dim)).astype(bf16)
        b_proj = active[:, inner : inner + state_dim].astype(bf16)
        state[...] = state[...] * spread(jnp.exp(end), 0, heads, head_dim) + dot_tn(b_proj, scaled)

    @pl.when(at == 2 * count - 1)
    def _():
        decay = spread(jnp.exp(running[...]), 0, heads, head_dim)
        decay_out[...] = decay
        scan = DeviceScan(False, state, fade, lead, entering, scan_got, scan_got_fade, scan_sent,
                          scan_sent_fade, scan_sems)
        scan.begin(decay)
        scan.run()


def front(tokens, zx, dt, flags, gain, tail_rows, proj_bc, conv_bc, conv_x, params, heads, head_dim, state_dim):
    length, width = tokens.shape
    count = length // GROUP
    inner = heads * head_dim
    conv = inner + 2 * state_dim
    head_count = lax.axis_size("head")

    def early(cols):
        return pl.BlockSpec((GROUP, cols), lambda g: (jnp.minimum(g, count - 1), 0))

    def late(cols):
        return pl.BlockSpec((GROUP, cols), lambda g: (jnp.maximum(g - count, 0), 0))
    shape = jax.ShapeDtypeStruct
    state, fade = (state_dim, inner), (8, inner)
    return pl.pallas_call(
        functools.partial(front_kernel, heads, head_dim, state_dim, count),
        grid=(2 * count,),
        out_shape=(shape((length, width), bf16), shape((length, inner), f32), shape((length, conv), bf16),
                   shape((length, conv), f32), shape((length, 128), f32), shape(state, f32),
                   shape(fade, f32), shape((16, conv), bf16), shape((width, 2 * state_dim + 128), bf16),
                   shape((8, conv), f32)),
        in_specs=[early(width), whole(zx.shape), whole(dt.shape), late(8), VMEM, VMEM, VMEM, VMEM, VMEM, VMEM],
        out_specs=(early(width), early(inner), late(conv), late(conv), late(128), whole(state), whole(fade),
                   whole((16, conv)), whole((width, 2 * state_dim + 128)), whole((8, conv))),
        scratch_shapes=[
            pltpu.VMEM((length, width), bf16), pltpu.VMEM((length, inner), bf16),
            pltpu.VMEM(tail_rows.shape, bf16), pltpu.VMEM((head_count,) + proj_bc.shape, bf16),
            pltpu.VMEM((head_count,) + conv_bc.shape, f32), pltpu.VMEM((8, conv), f32),
            pltpu.VMEM((GROUP + 8, conv), f32), pltpu.VMEM(state, f32), pltpu.VMEM((8, 128), f32)]
        + DeviceScan.scratch(state, fade) + [DMA((2, head_count)), DMA((2, head_count)), DMA((2,))],
        compiler_params=pltpu.CompilerParams(
            dimension_semantics=("arbitrary",), collective_id=3, has_side_effects=True,
            vmem_limit_bytes=LIMIT),
        name="front",
    )(tokens, zx, dt, flags, gain, tail_rows, proj_bc, conv_bc, conv_x, params)


def strips(rows):
    return [(lo, lo + STRIP) for lo in range(0, rows, STRIP)]


def mix_step(heads, head_dim, state_dim, at,
             conv_out, heads_in, gate, cot, out_proj, gains, entering,
             ssm_out, d_normed_out, partial_out, sums_out, starts_out, state):
    rows = conv_out.shape[0]
    inner = heads * head_dim
    per = 128 // head_dim

    @pl.when(at == 0)
    def _():
        state[...] = entering[...]

    values = conv_out[...]
    active = values * sigmoid(values)
    x = active[:, :inner]
    b_proj = active[:, inner : inner + state_dim].astype(bf16)
    c_proj = active[:, inner + state_dim :].astype(bf16)
    info = heads_in[...]
    flipped = info.T
    stepped = x * spread(info, STEP, heads, head_dim)
    low = stepped.astype(bf16)
    scores = dot_nt(c_proj, b_proj)
    lane = lax.broadcasted_iota(jnp.int32, (rows, 128), 1)
    tiles = []
    for pair in range(heads // per):
        tile = low[:, pair * 128 : (pair + 1) * 128]
        parts = [None] * (rows // STRIP)
        for k in range(per):
            head = pair * per + k
            masked = jnp.where((lane >= k * head_dim) & (lane < (k + 1) * head_dim), tile, jnp.zeros_like(tile))
            for n, (lo, hi) in enumerate(strips(rows)):
                gap = info[lo:hi, CUM + head : CUM + head + 1] - flipped[CUM + head : CUM + head + 1, :hi]
                ok = (lax.broadcasted_iota(jnp.int32, (STRIP, hi), 0) + lo
                      >= lax.broadcasted_iota(jnp.int32, (STRIP, hi), 1))
                weight = jnp.exp(jnp.where(ok, gap, -1e30)) * scores[lo:hi, :hi]
                part = dot(weight.astype(bf16), masked[:hi])
                parts[n] = part if parts[n] is None else parts[n] + part
        tiles.append(jnp.concatenate(parts, axis=0))
    inside = jnp.concatenate(tiles, axis=1)
    cum = info[:, CUM : CUM + 8]
    end = info[rows - 1 : rows]
    start = state[...]
    starts_out[at] = start.astype(bf16)
    grown = spread(jnp.exp(info), CUM, heads, head_dim)
    result = inside + grown * dot(c_proj, start.astype(bf16)) + gains[1:2] * x
    fade = spread(jnp.exp(end - info), CUM, heads, head_dim)
    state[...] = start * spread(jnp.exp(end), CUM, heads, head_dim) + dot_tn(b_proj, (stepped * fade).astype(bf16))
    ssm_out[...] = result
    z = gate[...]
    gated = result * (z * sigmoid(z))
    d_normed = dot_nt(cot[...], out_proj[...])
    d_normed_out[...] = d_normed
    scaled = gated * gains[0:1]
    partial_out[...] = dot(scaled.astype(bf16), out_proj[...]).astype(bf16)
    squares = jnp.sum(gated * gated, axis=1, keepdims=True)
    cross = jnp.sum(d_normed * scaled, axis=1, keepdims=True)
    turned = jnp.where(lane == 0, squares, cross).T
    sums_out[0, pl.ds(at, 1)] = turned[0:1]
    sums_out[1, pl.ds(at, 1)] = turned[1:2]


def gate_step(heads, head_dim, state_dim, all_channels, at,
              ssm, gate, d_normed, sums, conv_out, heads_in, cot, gains,
              d_ssm_out, d_gate_out, grad_out, rows_out, total_out):
    rows = ssm.shape[0]
    inner = heads * head_dim

    @pl.when(at == 0)
    def _():
        grad_out[...] = jnp.zeros_like(grad_out)
        rows_out[...] = jnp.zeros_like(rows_out)
        total_out[...] = jnp.zeros_like(total_out)

    tall = jnp.concatenate([sums[0, pl.ds(at, 1)], sums[1, pl.ds(at, 1)], jnp.zeros((126, rows), f32)], axis=0).T
    inv = lax.rsqrt(tall[:, 0:1] / all_channels + epsilon)
    cross = tall[:, 1:2] / all_channels
    z = gate[...]
    s = sigmoid(z)
    y = ssm[...]
    gated = y * (z * s)
    gain = gains[0:1]
    back = d_normed[...]
    unit = gated * inv
    d_gated = inv * (back * gain - unit * (inv * cross))
    grad_out[...] += dot_tn((unit * gain).astype(bf16), cot[...])
    d_ssm = d_gated * (z * s)
    d_ssm_out[...] = d_ssm
    d_gate_out[...] = (d_gated * y * (s * (1.0 + z * (1.0 - s)))).astype(bf16)
    values = conv_out[...]
    active = values * sigmoid(values)
    rows_out[0:1] += jnp.sum(back * unit, axis=0, keepdims=True)
    rows_out[1:2] += jnp.sum(d_ssm * active[:, :inner], axis=0, keepdims=True)
    c_proj = active[:, inner + state_dim :].astype(bf16)
    grown = spread(jnp.exp(heads_in[...]), DEV, heads, head_dim)
    total_out[...] += dot_tn(c_proj, (grown * d_ssm).astype(bf16))


def back_step(heads, head_dim, state_dim, first_step, last_step,
              d_ssm, conv_out, conv_in, heads_in, start, entering, flags, conv_w, params, skip, conv_halo,
              d_conv_in_out, d_step_out, conv_grads, head_grads, halo_out,
              lam, shift1, shift2, shift3, between):
    rows = d_ssm.shape[0]
    inner = heads * head_dim
    per = 128 // head_dim
    shifts = (shift1, shift2, shift3)

    @pl.when(first_step)
    def _():
        lam[...] = entering[...]
        conv_grads[...] = jnp.zeros_like(conv_grads)
        head_grads[...] = jnp.zeros_like(head_grads)
        for each in shifts:
            each[rows:] = jnp.zeros((8, each.shape[1]), f32)

    values = conv_out[...]
    gates = sigmoid(values)
    active = values * gates
    x = active[:, :inner]
    b_proj = active[:, inner : inner + state_dim].astype(bf16)
    c_proj = active[:, inner + state_dim :].astype(bf16)
    info = heads_in[...]
    flipped = info.T
    step = spread(info, STEP, heads, head_dim)
    stepped = x * step
    low = stepped.astype(bf16)
    dy = d_ssm[...]
    dy_low = dy.astype(bf16)
    scores = dot_nt(b_proj, c_proj)
    lane = lax.broadcasted_iota(jnp.int32, (rows, 128), 1)
    lane_one = lax.broadcasted_iota(jnp.int32, (STRIP, 128), 1)
    cuts = strips(rows)
    d_scores = [jnp.zeros((STRIP, rows - lo), f32) for lo, _ in cuts]
    d_rows = []
    d_cols = [jnp.zeros((STRIP, 128), f32) for _ in cuts]
    tiles = []
    for pair in range(heads // per):
        tile = low[:, pair * 128 : (pair + 1) * 128]
        dy_tile = dy_low[:, pair * 128 : (pair + 1) * 128]
        parts = [None] * len(cuts)
        for k in range(per):
            head = pair * per + k
            own = (lane >= k * head_dim) & (lane < (k + 1) * head_dim)
            masked = jnp.where(own, tile, jnp.zeros_like(tile))
            dy_masked = jnp.where(own, dy_tile, jnp.zeros_like(dy_tile))
            row_total = jnp.zeros((1, rows), f32)
            for n, (lo, hi) in enumerate(cuts):
                gap = flipped[CUM + head : CUM + head + 1, lo:] - info[lo:hi, CUM + head : CUM + head + 1]
                ok = (lax.broadcasted_iota(jnp.int32, (STRIP, rows - lo), 1)
                      >= lax.broadcasted_iota(jnp.int32, (STRIP, rows - lo), 0))
                decay = jnp.exp(jnp.where(ok, gap, -1e30))
                weight = decay * scores[lo:hi, lo:]
                part = dot(weight.astype(bf16), dy_masked[lo:])
                parts[n] = part if parts[n] is None else parts[n] + part
                pairs = dot_nt(masked[lo:hi], dy_tile[lo:])
                d_scores[n] = d_scores[n] + pairs * decay
                moved = pairs * weight
                d_cols[n] = d_cols[n] - jnp.where(lane_one == head, jnp.sum(moved, axis=1, keepdims=True), 0.0)
                col = jnp.sum(moved, axis=0, keepdims=True)
                if lo:
                    col = jnp.concatenate([jnp.zeros((1, lo), f32), col], axis=1)
                row_total = row_total + col
            d_rows.append(row_total)
        tiles.append(jnp.concatenate(parts, axis=0))
    between()
    d_stepped = jnp.concatenate(tiles, axis=1)
    d_cum = jnp.concatenate(d_cols, axis=0)
    d_cum = d_cum + jnp.concatenate(d_rows + [jnp.zeros((128 - heads, rows), f32)], axis=0).T
    full = jnp.concatenate(
        [jnp.concatenate([jnp.zeros((STRIP, lo), f32), part], axis=1) if lo else part
         for part, (lo, _) in zip(d_scores, cuts)], axis=0).astype(bf16)
    d_b = dot(full, c_proj)
    d_c = dot_tn(full, b_proj)

    group_ones = (lax.broadcasted_iota(jnp.int32, (inner, 128), 0) // head_dim
                  == lax.broadcasted_iota(jnp.int32, (inner, 128), 1)).astype(bf16)
    after = lam[...]
    after_low = after.astype(bf16)
    end = info[rows - 1 : rows]
    grown = spread(jnp.exp(info), CUM, heads, head_dim)
    fade = spread(jnp.exp(end - info), CUM, heads, head_dim)
    end_grown = spread(jnp.exp(end), CUM, heads, head_dim)
    from_after = fade * dot(b_proj, after_low)
    d_stepped = d_stepped + from_after
    grown_dy = grown * dy
    grown_low = grown_dy.astype(bf16)
    to_cum = head_sum(grown_dy * dot(c_proj, start), group_ones)
    left = head_sum(stepped * from_after, group_ones)
    kept = jnp.sum(after * start.astype(f32), axis=0, keepdims=True) * end_grown
    kept = head_sum(jnp.broadcast_to(kept, (8, inner)), group_ones)[0:1]
    last = kept + jnp.sum(left, axis=0, keepdims=True)
    row_id = lax.broadcasted_iota(jnp.int32, (rows, 128), 0)
    d_cum = d_cum + to_cum - left + jnp.where(row_id == rows - 1, last, 0.0)
    d_c = d_c + dot_nt(grown_low, start)
    d_b = d_b + dot_nt((fade * stepped).astype(bf16), after_low)
    lam[...] = end_grown * after + dot_tn(c_proj, grown_low)
    d_step = head_sum(d_stepped * x, group_ones)
    d_x = step * d_stepped + skip[0:1] * dy

    order_r = lax.broadcasted_iota(jnp.int32, (rows, rows), 0)
    order_c = lax.broadcasted_iota(jnp.int32, (rows, rows), 1)
    free = 1.0 - flags[...]
    d_decay = exact_left((order_r <= order_c).astype(bf16), d_cum) * free[:, 1:2]
    rate = params[1:2]
    real = lane < heads
    step_raw = jnp.where(real, info, 0.0) + params[0:1]
    slope = sigmoid(step_raw)
    d_pre = jnp.where(real, (d_step + d_decay * rate) * slope, 0.0)
    d_step_out[...] = d_pre.astype(bf16)
    head_grads[0:1] += jnp.sum(d_pre, axis=0, keepdims=True)
    head_grads[1:2] += jnp.sum(jnp.where(real, d_decay * softplus(step_raw) * rate, 0.0), axis=0, keepdims=True)

    d_active = jnp.concatenate([d_x, d_b, d_c], axis=1)
    d_conv = d_active * (gates * (1.0 + values * (1.0 - gates)))
    taken = conv_in[...].astype(f32)
    total = d_conv * conv_w[0:1]
    conv_grads[0:1] += jnp.sum(d_conv * taken, axis=0, keepdims=True)
    conv_grads[4:5] += jnp.sum(d_conv, axis=0, keepdims=True)
    for j in range(1, 4):
        ref = shifts[j - 1]
        ref[0:rows] = d_conv * free[:, j : j + 1]
        moved = ref[pl.ds(j, rows)]
        total = total + moved * conv_w[j : j + 1]
        conv_grads[j : j + 1] += jnp.sum(moved * taken, axis=0, keepdims=True)
    d_conv_in_out[...] = total.astype(bf16)

    @pl.when(last_step)
    def _():
        ahead = conv_halo[...].astype(f32)
        halo_out[...] = jnp.zeros_like(halo_out)
        for j in range(1, 4):
            first = shifts[j - 1][0:8]
            for t in range(j):
                row = 16 + t - j
                conv_grads[j : j + 1] += first[t : t + 1] * ahead[row : row + 1]
                halo_out[row - 8 : row - 7] += first[t : t + 1] * conv_w[j : j + 1]
    for each in shifts:
        each[rows:] = each[0:8]


def paced(times, pace, behind, most):
    return [max(0, min(most, int((time - behind) / pace))) for time in times]


def at_point(counts):
    def count(point):
        if isinstance(point, int):
            return counts[point] if point >= 0 else 0
        out = jnp.int32(0)
        for k, value in enumerate(counts):
            more = value - (counts[k - 1] if k else 0)
            if more:
                out = out + more * (point >= k).astype(jnp.int32)
        return out
    return count


def layer_kernel(heads, head_dim, state_dim, all_channels, count, block, lag, plans,
                 conv_out, conv_in, heads_in, gate, cot, flags, out_proj, gains, entering, decay, conv_w,
                 params, conv_halo,
                 line_out, d_gate_out, d_conv_out, d_step_out, grad_out_out, gate_rows, conv_grads, head_grads,
                 halo_out, sums_out,
                 own, got, total, ssm, d_normed, starts, state, leaving, shift1, shift2, shift3, sums, sum_slots,
                 grad_out, grad_low, grad_slots, grad_res, lead, fade,
                 scan_got, scan_got_fade, scan_sent, scan_sent_fade, scan_sems, line_sems, sum_sems, grad_sems):
    at = pl.program_id(0)
    rows = conv_out.shape[0]
    seq = lax.axis_size("seq")
    line = LineSum(own, got, total, line_out, line_sems, block)
    swap = Swap("head", sums, sum_slots, sum_sems)
    scan = DeviceScan(True, state, fade, lead, leaving, scan_got, scan_got_fade, scan_sent, scan_sent_fade,
                      scan_sems)
    grad_sum = PlaneSum(grad_low, grad_slots, grad_res, grad_sems, min(seq, grad_low.shape[0] // 16))
    served, sent = at_point(plans[0]), at_point(plans[1])

    def serve(point):
        line.send(sent(point - 1), sent(point))
        line.serve(served(point - 1), served(point), lag)

    @pl.when(at == 0)
    def _():
        greet("head", "seq")
        state[...] = entering[...]

    serve(2 * at)

    @pl.when(at < count)
    def _():
        mine = pl.ds(pl.multiple_of(at * rows, rows), rows)
        mix_step(heads, head_dim, state_dim, at, conv_out, heads_in, gate, cot, out_proj, gains, entering,
                 ssm.at[mine], d_normed.at[mine], own.at[mine], sums, starts, state)

    @pl.when(at == count - 1)
    def _():
        swap.start()

    @pl.when(at == count)
    def _():
        swap.wait()
        sums_out[...] = swap.total()
        swap.finish()
        grad_out[...] = jnp.zeros_like(grad_out)
        gate_rows[...] = jnp.zeros_like(gate_rows)
        state[...] = jnp.zeros_like(state)

    @pl.when((at >= count) & (at < 2 * count))
    def _():
        here = at - count
        mine = pl.ds(pl.multiple_of(here * rows, rows), rows)
        gate_step(heads, head_dim, state_dim, all_channels, here,
                  ssm.at[mine], gate, d_normed.at[mine], sums_out, conv_out, heads_in, cot, gains,
                  ssm.at[mine], d_gate_out, grad_out, gate_rows, state)

    @pl.when(at == 2 * count)
    def _():
        grad_low[...] = grad_out[...].astype(bf16)
        scan.begin(decay[...])
        scan.run()
        grad_sum.scatter()

    @pl.when(at >= 2 * count)
    def _():
        here = 3 * count - 1 - at
        mine = pl.ds(pl.multiple_of(here * rows, rows), rows)
        back_step(heads, head_dim, state_dim, at == 2 * count, at == 3 * count - 1,
                  ssm.at[mine], conv_out, conv_in, heads_in, starts[here], leaving, flags, conv_w, params,
                  gains[1:2], conv_halo, d_conv_out, d_step_out, conv_grads, head_grads, halo_out,
                  state, shift1, shift2, shift3, lambda: serve(2 * at + 1))

    @pl.when(at == 2 * count + count // 2)
    def _():
        grad_sum.reduce()

    @pl.when(at == 3 * count - 1)
    def _():
        grad_sum.finish()
        grad_out_out[...] = grad_res[...]
        serve(6 * count)
        line.finish()


def layer(conv_out, conv_in, heads_in, gate, cot, flags, out_proj, gains, entering, decay, conv_w, params,
          conv_halo, heads, head_dim, state_dim, all_channels):
    length, conv = conv_out.shape
    count = length // GROUP
    inner = heads * head_dim
    width = cot.shape[1]
    seq, head_count = lax.axis_size("seq"), lax.axis_size("head")
    block = 64
    blocks = length // block
    lag = max(2, head_count // 2)
    steps = [MIX] * count + [GATE] * count + [BACK] * count
    times, now = [], 0.0
    for k, step in enumerate(steps):
        now += SWAP if k == count else 0.0
        half = SCAN + step / 2 if k == 2 * count else step / 2 if k > 2 * count else 0.0
        times += [now, now + half]
        now += step + (SCAN if k == 2 * count else 0.0)
    made = [min(blocks, (k // 2) * (GROUP // block)) for k in range(6 * count)]
    plans = (paced(times, PACE, LATE, blocks) + [blocks + lag],
             [min(a, b) for a, b in zip(made, paced(times, PACE, EARLY, blocks))] + [blocks])

    def by(cols, first, step):
        def index(g):
            ahead = jnp.where(g < count, g, jnp.where(g < 2 * count, g - count, 3 * count - 1 - g))
            if first == 2:
                ahead = jnp.where(g < 2 * count, count - 1, ahead)
            if first == 1:
                ahead = jnp.where(g < count, 0, ahead)
            if step == 1:
                ahead = jnp.where(g < 2 * count, ahead, count - 1)
            return (ahead, 0)
        return pl.BlockSpec((GROUP, cols), index)
    shape = jax.ShapeDtypeStruct
    state, fade = (state_dim, inner), (8, inner)
    owners = min(seq, inner // 16)
    return pl.pallas_call(
        functools.partial(layer_kernel, heads, head_dim, state_dim, all_channels, count, block, lag, plans),
        grid=(3 * count,),
        out_shape=(shape((length, width), bf16), shape((length, inner), bf16), shape((length, conv), bf16),
                   shape((length, 128), bf16), shape((inner, width), bf16), shape((8, inner), f32),
                   shape((8, conv), f32), shape((8, 128), f32), shape((8, conv), f32),
                   shape((2, count, GROUP), f32)),
        in_specs=[by(conv, 0, 2), by(conv, 2, 2), by(128, 0, 2), by(inner, 0, 1), by(width, 0, 1), by(8, 2, 2)]
        + [VMEM] * 7,
        out_specs=(HBM, by(inner, 1, 1), by(conv, 2, 2), by(128, 2, 2)) + (VMEM,) * 6,
        scratch_shapes=[pltpu.VMEM((length, width), bf16)] * 3 + [pltpu.VMEM((length, inner), f32)] * 2 + [
            pltpu.VMEM((count,) + state, bf16), pltpu.VMEM(state, f32), pltpu.VMEM(state, f32)]
        + [pltpu.VMEM((GROUP + 8, conv), f32)] * 3 + [
            pltpu.VMEM((2, count, GROUP), f32), pltpu.VMEM((head_count, 2, count, GROUP), f32),
            pltpu.VMEM((inner, width), f32), pltpu.VMEM((inner, width), bf16),
            pltpu.VMEM((seq, inner // owners, width), bf16), pltpu.VMEM((inner, width), bf16)]
        + DeviceScan.scratch(state, fade) + [LineSum.sems(length, block), DMA((2, head_count)), DMA((4, seq))],
        compiler_params=pltpu.CompilerParams(
            dimension_semantics=("arbitrary",), collective_id=4, has_side_effects=True,
            vmem_limit_bytes=LIMIT),
        name="layer",
    )(conv_out, conv_in, heads_in, gate, cot, flags, out_proj, gains, entering, decay, conv_w, params, conv_halo)


PACE = 2.9
MIX, SWAP, GATE, SCAN, BACK = 2.7, 3.0, 2.0, 10.0, 6.6
EARLY, LATE = -2.0, 5.0
PROJECT, CUTS = 2.6, (17, 21)


def tail_kernel(count, block, lag, plans, cuts, owners, last_rows,
                normed, d_gate, d_conv, d_step, zx, weights, gain, back_rows, tail_mask, small_in,
                line_out, zx_out, bc_out, small_out,
                own, got, total, grad_zx, grad_low, zx_slots, zx_res, grad_bc, bc_part, bc_slots, bc_z, bc_res, small, small_slots,
                small_own, small_z, landed,
                line_sems, zx_sems, bc_sems, bcz_sems, small_sems, smallz_sems, row_sems):
    at = pl.program_id(0)
    rows, width = normed.shape
    inner = d_gate.shape[1]
    seq, heads = lax.axis_size("seq"), lax.axis_size("head")
    me, my_head = lax.axis_index("seq"), lax.axis_index("head")
    bc_width = bc_part.shape[0] * bc_part.shape[1]
    line = LineSum(own, got, total, line_out, line_sems, block)
    zx_sum = PlaneSum(grad_low, zx_slots, zx_res, zx_sems, owners[0])
    small_swap = Swap("seq", small, small_slots, small_sems)
    both_swap = Swap("head", small_own, small_z, smallz_sems)
    row_copy = pltpu.make_async_remote_copy(
        src_ref=back_rows, dst_ref=landed, send_sem=row_sems.at[0], recv_sem=row_sems.at[1],
        device_id={"seq": lax.rem(me + seq - 1, seq)}, device_id_type=MESH)
    served, sent = at_point(plans[0]), at_point(plans[1])

    @pl.when(at == 0)
    def _():
        greet("head", "seq")
        row_copy.start()
        grad_zx[...] = jnp.zeros_like(grad_zx)
        grad_bc[...] = jnp.zeros_like(grad_bc)
        small[...] = small_in[...]

    line.send(sent(at - 1), sent(at))
    line.serve(served(at - 1), served(at), lag)

    block_low = normed[...]
    gate_low, conv_low, step_low = d_gate[...], d_conv[...], d_step[...]
    rest_low = jnp.concatenate([conv_low[:, inner:], step_low], axis=1)
    d_normed = (dot_nt(gate_low, zx[:, :inner]) + dot_nt(conv_low[:, :inner], zx[:, inner:])
                + dot_nt(rest_low, weights[...]))
    grad_zx[:, :inner] += dot_tn(block_low, gate_low)
    grad_zx[:, inner:] += dot_tn(block_low, conv_low[:, :inner])
    grad_bc[...] += dot_tn(rest_low, block_low)
    small[16:17] += jnp.sum(d_normed * block_low.astype(f32), axis=0, keepdims=True) / gain[0:1]
    mine = pl.ds(pl.multiple_of(at * rows, rows), rows)
    own[mine] = d_normed.astype(bf16)

    @pl.when(at == count - 1)
    def _():
        row_copy.wait()
        extra = jnp.where(me < seq - 1, landed[...] * tail_mask[...], 0.0)
        extra = jnp.concatenate([jnp.zeros_like(extra), extra], axis=0).astype(bf16)
        tail_low = normed[rows - 16 :]
        more = dot_nt(extra[:, :inner], zx[:, inner:]) + dot_nt(extra[:, inner:], weights[:, :bc_width])
        grad_zx[:, inner:] += dot_tn(tail_low, extra[:, :inner])
        grad_bc[:bc_width] += dot_tn(extra[:, inner:], tail_low)
        small[16:17] += jnp.sum(more * tail_low.astype(f32), axis=0, keepdims=True) / gain[0:1]
        own[last_rows:] = (own[last_rows:].astype(f32) + more).astype(bf16)

    piece = bc_part.shape[1] // owners[1]

    def bc_scatter(to, source):
        return pltpu.make_async_remote_copy(
            src_ref=bc_part.at[:, pl.ds(pl.multiple_of(to * piece, piece), piece)],
            dst_ref=bc_slots.at[source], send_sem=bc_sems.at[0, to], recv_sem=bc_sems.at[1, source],
            device_id={"seq": to}, device_id_type=MESH)

    def bc_gather(owner, to):
        rows = pl.ds(pl.multiple_of(owner * piece, piece), piece)
        return pltpu.make_async_remote_copy(
            src_ref=bc_res.at[rows], dst_ref=bc_res.at[rows],
            send_sem=bc_sems.at[2, to], recv_sem=bc_sems.at[3, owner],
            device_id={"seq": to}, device_id_type=MESH)

    def bc_swap(to, source):
        return pltpu.make_async_remote_copy(
            src_ref=bc_slots.at[me, to], dst_ref=bc_z.at[source],
            send_sem=bcz_sems.at[0, to], recv_sem=bcz_sems.at[1, source],
            device_id={"head": to}, device_id_type=MESH)

    @pl.when(at == count - 1)
    def _():
        grad_low[...] = grad_zx[...].astype(bf16)
        zx_sum.scatter()
        small[0:8] += grad_bc[bc_width : bc_width + 8]
        small_swap.start()
        for k in range(heads):
            bc_part[k] = grad_bc[k * bc_part.shape[1] : (k + 1) * bc_part.shape[1]]

        @pl.loop(1, seq)
        def _(k):
            to = other_of("seq", k)

            @pl.when(to < owners[1])
            def _():
                bc_scatter(to, me).start()

        last = count - 1

        def go(first, until, sent_first, sent_until):
            line.send(sent_first, sent_until)
            line.serve(first, until, lag)
        go(served(last), cuts[0], sent(last), cuts[0] + 2)
        zx_sum.reduce()
        small_swap.wait()
        sums = small_swap.total()
        lone = small.shape[0] - small_own.shape[0]
        small_out[:lone] = sums[:lone]
        small_own[...] = sums[lone:]
        both_swap.start()

        @pl.when(me < owners[1])
        def _():
            @pl.loop(1, seq)
            def _(k):
                bc_scatter(me, other_of("seq", k)).wait_recv()
            bc_slots[me] = bc_part[:, pl.ds(pl.multiple_of(me * piece, piece), piece)]
            sums = bc_slots[0]
            for k in range(1, seq):
                sums = sums + bc_slots[k]
            bc_slots[me] = sums
            bc_z[my_head] = bc_slots[me, my_head]

            @pl.loop(1, heads)
            def _(k):
                bc_swap(other_of("head", k), my_head).start()

        go(cuts[0], cuts[1], cuts[0] + 2, cuts[1] + 2)
        both_swap.wait()
        small_out[lone:] = both_swap.total()

        @pl.when(me < owners[1])
        def _():
            @pl.loop(1, heads)
            def _(k):
                bc_swap(my_head, other_of("head", k)).wait_recv()
            sums = bc_z[0]
            for k in range(1, heads):
                sums = sums + bc_z[k]
            bc_res[pl.ds(pl.multiple_of(me * piece, piece), piece)] = sums

            @pl.loop(1, seq)
            def _(k):
                bc_gather(me, other_of("seq", k)).start()

        go(cuts[1], line.count + lag, cuts[1] + 2, line.count)
        line.finish()
        zx_sum.finish()
        zx_out[...] = zx_res[...]
        small_swap.finish()
        both_swap.finish()

        @pl.loop(1, seq)
        def _(k):
            other = other_of("seq", k)

            @pl.when(other < owners[1])
            def _():
                bc_gather(other, me).wait_recv()
                bc_scatter(other, me).wait_send()

            @pl.when(me < owners[1])
            def _():
                bc_gather(me, other).wait_send()
        bc_out[...] = bc_res[...]

        @pl.when(me < owners[1])
        def _():
            @pl.loop(1, heads)
            def _(k):
                bc_swap(other_of("head", k), my_head).wait_send()


def tail(normed, d_gate, d_conv, d_step, zx, weights, gain, back_rows, tail_mask, small_in, both):
    length, width = normed.shape
    inner, conv = d_gate.shape[1], d_conv.shape[1]
    count = length // GROUP
    seq, heads = lax.axis_size("seq"), lax.axis_size("head")
    bc_rows = (conv - inner) // heads
    owners = (min(seq, width // 16), min(seq, bc_rows // 8))
    piece = bc_rows // owners[1]
    block = 64
    blocks = length // block
    lag = max(2, heads // 2)
    made = [k * (GROUP // block) for k in range(count)]
    times = [PROJECT * k for k in range(count)]
    plans = (paced(times, PACE, LATE, blocks), [min(a, b) for a, b in zip(made, paced(times, PACE, EARLY, blocks))])
    cuts = ((blocks * CUTS[0]) // 32, (blocks * CUTS[1]) // 32)

    def by(cols):
        return pl.BlockSpec((GROUP, cols), lambda g: (g, 0))
    shape = jax.ShapeDtypeStruct
    return pl.pallas_call(
        functools.partial(tail_kernel, count, block, lag, plans, cuts, owners, length - 16),
        grid=(count,),
        out_shape=(shape((length, width), bf16), shape((width, 2 * inner), bf16), shape((bc_rows, width), f32),
                   shape(small_in.shape, f32)),
        in_specs=[by(width), by(inner), by(conv), by(128)] + [VMEM] * 6,
        out_specs=(HBM, VMEM, VMEM, VMEM),
        scratch_shapes=[pltpu.VMEM((length, width), bf16)] * 3 + [
            pltpu.VMEM((width, 2 * inner), f32), pltpu.VMEM((width, 2 * inner), bf16),
            pltpu.VMEM((seq, width // owners[0], 2 * inner), bf16), pltpu.VMEM((width, 2 * inner), bf16),
            pltpu.VMEM((conv - inner + 128, width), f32), pltpu.VMEM((heads, bc_rows, width), f32),
            pltpu.VMEM((seq, heads, piece, width), f32), pltpu.VMEM((heads, piece, width), f32),
            pltpu.VMEM((bc_rows, width), f32), pltpu.VMEM(small_in.shape, f32), pltpu.VMEM((seq,) + small_in.shape, f32),
            pltpu.VMEM((both, width), f32), pltpu.VMEM((heads, both, width), f32),
            pltpu.VMEM(back_rows.shape, f32),
            LineSum.sems(length, block), DMA((4, seq)), DMA((4, seq)), DMA((2, heads)), DMA((2, seq)),
            DMA((2, heads)), DMA((2,))],
        compiler_params=pltpu.CompilerParams(
            dimension_semantics=("arbitrary",), collective_id=5, has_side_effects=True,
            vmem_limit_bytes=LIMIT),
        name="tail",
    )(normed, d_gate, d_conv, d_step, zx, weights, gain, back_rows, tail_mask, small_in)


def padded(block, rows, cols):
    return jnp.pad(block, ((0, rows - block.shape[0]), (0, cols - block.shape[1])))


def shards(
    tokens, start_flags, in_gain, proj_zx, proj_bc, proj_dt, conv_x_weight, conv_x_bias,
    conv_bc_weight, conv_bc_bias, dt_bias, a_log, skip_scale, norm_gain, out_proj, cotangent,
):
    length, width = tokens.shape
    heads = a_log.shape[0]
    inner = proj_zx.shape[2]
    head_dim = inner // heads
    taps = conv_x_weight.shape[0]
    head_count = lax.axis_size("head")
    bc_part = conv_bc_bias.shape[0]
    bc_width = bc_part * head_count
    state_dim = bc_width // 2
    my_head = lax.axis_index("head")

    flag = start_flags.astype(f32)
    free = 1.0 - flag
    free1 = jnp.pad(free, (1, 0), constant_values=1.0)[:length]
    free2 = jnp.pad(free, (2, 0), constant_values=1.0)[:length]
    flags = jnp.pad(jnp.stack([flag, 1.0 - free * free1, 1.0 - free * free1 * free2], axis=1), ((0, 0), (1, 4)))
    last = jnp.stack([free[length - 1] * free[length - 2], free[length - 1], jnp.ones((), f32)])
    tail_mask = jnp.pad(last, (13, 0))[:, None]
    tail_rows = (tokens[length - 16 :].astype(f32) * tail_mask).astype(bf16)
    gain8 = jnp.broadcast_to(in_gain[None], (8, width))
    conv_bc = padded(jnp.concatenate([conv_bc_weight.astype(f32), conv_bc_bias[None]]), 8, bc_part)

    conv_x = padded(jnp.concatenate([conv_x_weight.astype(f32), conv_x_bias[None]]), 8, inner)
    head_rows = jnp.pad(jnp.stack([dt_bias, -jnp.exp(a_log)]), ((0, 6), (0, 8 - heads)))
    params = jnp.tile(head_rows, (1, 16))
    gains = jnp.pad(jnp.stack([norm_gain, jnp.repeat(skip_scale, head_dim)]), ((0, 6), (0, 0)))
    zx = proj_zx.reshape(width, 2 * inner)
    dt = jnp.tile(jnp.pad(proj_dt, ((0, 0), (0, 8 - heads))), (1, 16))

    normed, gate, conv_in, conv_out, info, entering, decay, conv_halo, weights, conv_w = front(
        tokens, zx, dt, flags, gain8, tail_rows, proj_bc, conv_bc, conv_x, params, heads, head_dim, state_dim)
    all_channels = inner * head_count
    mixed, d_gate, d_conv, d_step, op_sum, gate_rows, conv_grads, head_grads, back_rows, sums = layer(
        conv_out, conv_in, info, gate, cotangent, flags, out_proj, gains, entering, decay, conv_w, params,
        conv_halo, heads, head_dim, state_dim, all_channels)
    inv_rms = lax.rsqrt(sums[0].reshape(length, 1) / all_channels + epsilon)
    mixed_out = (tokens.astype(f32) + mixed.astype(f32) * inv_rms).astype(bf16)

    right = jnp.concatenate([gate_rows[:2], padded(head_grads[:2], 6, inner)])
    small = jnp.concatenate([
        jnp.zeros((8, width), f32),
        padded(jnp.concatenate([conv_grads[:, :inner], right], axis=1), 8, width),
        jnp.zeros((1, width), f32), padded(conv_grads[: taps + 1, inner:], 7, width)])
    d_normed, zx_sum, bc_sum, small_sum = tail(
        normed, d_gate, d_conv, d_step, zx, weights, gain8, back_rows, tail_mask[8:], small, 8)

    tokens_f = tokens.astype(f32)
    inv = lax.rsqrt(jnp.mean(tokens_f * tokens_f, axis=1, keepdims=True) + epsilon)
    xhat = tokens_f * inv
    scaled = d_normed.astype(f32) * in_gain
    grad_tokens = cotangent.astype(f32) + inv * (
        scaled - xhat * jnp.mean(scaled * xhat, axis=1, keepdims=True))
    conv_bc_sum = lax.dynamic_slice(small_sum, (17, my_head * bc_part), (taps + 1, bc_part))
    return (
        mixed_out,
        grad_tokens,
        small_sum[16],
        zx_sum.astype(f32).reshape(width, 2, inner),
        bc_sum.T,
        small_sum[:heads].T,
        small_sum[8 : 8 + taps, :inner],
        small_sum[8 + taps, :inner],
        conv_bc_sum[:taps],
        conv_bc_sum[taps],
        small_sum[10, inner : inner + heads],
        small_sum[11, inner : inner + heads],
        small_sum[9, inner : 2 * inner].reshape(heads, head_dim).sum(axis=1),
        small_sum[8, inner : 2 * inner],
        op_sum.astype(f32),
    )


def solution(mesh):
    in_specs = (
        P("seq", None),
        P("seq"),
        P(),
        P(None, None, "head"),
        P(None, "head"),
        P(None, "head"),
        P(None, "head"),
        P("head"),
        P(None, "head"),
        P("head"),
        P("head"),
        P("head"),
        P("head"),
        P("head"),
        P("head", None),
        P("seq", None),
    )
    out_specs = (
        P("seq", None),
        P("seq", None),
        P(),
        P(None, None, "head"),
        P(None, "head"),
        P(None, "head"),
        P(None, "head"),
        P("head"),
        P(None, "head"),
        P("head"),
        P("head"),
        P("head"),
        P("head"),
        P("head"),
        P("head", None),
    )
    return jax.shard_map(shards, mesh=mesh, in_specs=in_specs, out_specs=out_specs, check_vma=False)
```

time: 524 us -> 363 us (0.69)
  Pallas kernels: 449 us -> 311 us
  local copies, waits for them, and re-layouts: 46.3 us -> 24.2 us
    pallas_call x11 -> x2, Pallas kernels: 429 us -> 252 us  [the longest x1 131 us: layer(): pl.pallas_call(functools.partial(layer_kernel, heads, head_dim, state_dim...]
    pallas_call x1, Pallas kernels: 20.5 us -> 59 us  [front(): pl.pallas_call(functools.partial(front_kernel, heads, head_dim, state_dim...]
    concatenate x1 -> x2, local copies, waits for them, and re-layouts: 8.46 us -> 0.08 us  [shards(): jnp.concatenate([jnp.zeros((8, width), f32), padded(jnp.concatenate([conv...]
    unnamed x66 -> x42, local copies, waits for them, and re-layouts: 12.4 us -> 6.01 us
    convert_element_type x3 -> x0, other arithmetic: 5.93 us -> none  [the longest x1 3.98 us: shards(): grad_zx.astype(bf16)]
where the time goes in v3:
time: 363 us; the launch traced here: 358 us
  Pallas kernels  311 us (86%)
  local copies, waits for them, and re-layouts  24.2 us (7%)
  other arithmetic  21.3 us (6%)
    pallas_call x1, Pallas kernels, layer(): pl.pallas_call(functools.partial(layer_kernel, heads, head_dim, state_dim...  131 us
    pallas_call x1, Pallas kernels, tail(): pl.pallas_call(functools.partial(tail_kernel, count, block, lag, plans, c...  120 us
    pallas_call x1, Pallas kernels, front(): pl.pallas_call(functools.partial(front_kernel, heads, head_dim, state_dim...  59 us

profile of v3, /device:TPU:0, one launch (start us, length us, event | category | flops | bytes accessed | tf_op | source)
XLA Modules:
  0.0 358.3 jit_solution(3929435810912914835)
XLA Ops:
  0.7 0.8 broadcast_subtract_fusion.1
  3.4 0.7 select_maximum_fusion.6
  4.1 1.4 multiply_convert_fusion.tail_rows
  5.6 0.7 convert_element_type.52
  6.8 1.3 pad.42.flags
  8.1 3.5 copy.44
  12.9 0.7 tile.21.params
  13.6 1.3 broadcast_in_dim.12.gain
  14.9 0.8 copy.41.dt
  15.7 0.8 copy.42.proj_bc
  17.8 59.0 %front.1 = (bf16[2048,1024]{1,0:T(8,128)(2,1)}, f32[2048,512]{1,0:T(8,128)}, bf16[2048,768]{1,0:T(8,128)(2,1)}, f32[2048,768]{1,0:T(8,128)}, f32[2048,128]{1,0:T...) custom-call(bf16[2048,1024]{1,0:T(8,128)(2,1)} %tokens.1, ...), custom_call_target="tpu_custom_call" | custom-call | tf_op jit(solution)/shard_map/front/pallas_call | solution.py:485
  77.6 131.3 %layer.1 = (bf16[2048,1024]{1,0:T(8,128)(2,1)}, bf16[2048,512]{1,0:T(8,128)(2,1)}, bf16[2048,768]{1,0:T(8,128)(2,1)}, bf16[2048,128]{1,0:T(8,128)(2,1)}, bf16[51...) custom-call(f32[2048,768]{1,0:T(8,128)} %get-tuple-element.39.conv_o, ...), custom_call_target="tpu_custom_call" | custom-call | tf_op jit(solution)/shard_map/layer/pallas_call | solution.py:886
  208.8 0.7 slice.75
  209.5 0.7 slice.78
  210.2 0.7 slice.76
  211.7 0.7 select_maximum_fusion.small_in
  213.2 120.4 %tail.1 = (bf16[2048,1024]{1,0:T(8,128)(2,1)}, bf16[1024,1024]{1,0:T(8,128)(2,1)}, f32[64,1024]{1,0:T(8,128)}, f32[24,1024]{1,0:T(8,128)}) custom-call(bf16[2048,1024]{1,0:T(8,128)(2,1)} %get-tuple-element.49.normed, bf16[2048,512]{1,0:T(8,128)(2,1)} %get-tuple-element.50.d_gate, bf16[2048,768]{1,0:T(8,128)(2,1)} %get-tuple-element.51.d_conv, ...), custom_call_target="tpu_custom_call" | custom-call | tf_op jit(solution)/shard_map/tail/pallas_call | solution.py:1105
  333.7 0.9 fusion.7
  334.6 4.0 %fusion.2 = f32[2048]{0:T(1024)S(1)} fusion(bf16[2048,1024]{1,0:T(8,128)(2,1)S(1)} %copy-done.2, bf16[2048,1024]{1,0:T(8,128)(2,1)} %get-tuple-element.58, f32[1024]{0:T(1024)S(1)} %copy-done.10, f32[2048]{0:T(1024)S(1)} %add_rsqrt_fusion), kind=kLoop, calls=%fused_computation.5 | loop fusion | flops 12580864 | bytes 8409088 | tf_op jit(solution)/shard_map/reduce_sum | solution.py:1188
  338.7 0.9 copy-done.5
  339.6 6.6 %fusion.5 = (f32[2048,1024]{1,0:T(8,128)}, bf16[2048,1024]{1,0:T(8,128)(2,1)}) fusion(bf16[2048,1024]{1,0:T(8,128)(2,1)S(1)} %copy-done.2, bf16[2048,1024]{1,0:T(8,128)(2,1)S(1)} %copy-done.4, bf16[2048,1024]{1,0:T(8,128)(2,1)S(1)} %copy-done.3, f32[2048]{0:T(1024)S(1)} %broadcast_multiply_fusion, f32[1024]{0:T(1024)S(1)} %copy-done.10, ...), kind=kLoop, calls=%fused_computation.8 | loop fusion | flops 27262976 | bytes 29388800 | tf_op jit(solution)/shard_map/add | solution.py:1187
  346.1 5.1 %reshape.84 = f32[1024,2,512]{2,1,0:T(2,128)} reshape(bf16[1024,1024]{1,0:T(8,128)(2,1)S(1)} %copy-done.6) | data formatting | bytes 6291456 | tf_op jit(solution)/shard_map/reshape | solution.py:1194
  356.0 1.6 convert_element_type.61
  357.6 0.7 copy.47
  (72 shorter events, 10.8 us)
Async XLA Ops:
  0.6 14.2 %copy-start = (bf16[1024,8]{0,1:T(8,128)(2,1)S(1)}, bf16[1024,8]{0,1:T(8,128)(2,1)}, u32[]{:S(2)}) copy-start(bf16[1024,8]{0,1:T(8,128)(2,1)} %param.21) | copy-start | bytes 49156
  0.7 15.1 %copy-start.9 = (bf16[1024,64]{0,1:T(8,128)(2,1)S(1)}, bf16[1024,64]{0,1:T(8,128)(2,1)}, u32[]{:S(2)}) copy-start(bf16[1024,64]{0,1:T(8,128)(2,1)} %param.20) | copy-start | bytes 393220
  0.7 15.9 %copy-start.12 = (bf16[4,512]{1,0:T(4,128)(2,1)S(1)}, bf16[4,512]{1,0:T(4,128)(2,1)}, u32[]{:S(2)}) copy-start(bf16[4,512]{1,0:T(4,128)(2,1)} %param.22) | copy-start | bytes 12292
  0.7 15.9 %copy-start.15 = (f32[512]{0:T(512)S(1)}, f32[512]{0:T(512)}, u32[]{:S(2)}) copy-start(f32[512]{0:T(512)} %param.23) | copy-start | bytes 6148
  0.7 16.5 %copy-start.16 = (bf16[4,64]{1,0:T(4,128)(2,1)S(1)}, bf16[4,64]{1,0:T(4,128)(2,1)}, u32[]{:S(2)}) copy-start(bf16[4,64]{1,0:T(4,128)(2,1)} %param.24) | copy-start | bytes 1540
  0.7 16.5 %copy-start.18 = (f32[64]{0:T(128)S(1)}, f32[64]{0:T(128)}, u32[]{:S(2)}) copy-start(f32[64]{0:T(128)} %param.25) | copy-start | bytes 772
  6.4 70.4 %copy-start.17 = (f32[8]{0:T(128)S(1)}, f32[8]{0:T(128)}, u32[]{:S(2)}) copy-start(f32[8]{0:T(128)} %param.28) | copy-start | bytes 100
  6.4 70.6 %copy-start.14 = (f32[512]{0:T(512)S(1)}, f32[512]{0:T(512)}, u32[]{:S(2)}) copy-start(f32[512]{0:T(512)} %param.29) | copy-start | bytes 6148
  213.2 120.5 %copy-start.2 = (bf16[2048,1024]{1,0:T(8,128)(2,1)S(1)}, bf16[2048,1024]{1,0:T(8,128)(2,1)}, u32[]{:S(2)}) copy-start(bf16[2048,1024]{1,0:T(8,128)(2,1)} %tokens.1) | copy-start | bytes 12582916
  213.2 121.4 %copy-start.10 = (f32[1024]{0:T(1024)S(1)}, f32[1024]{0:T(1024)}, u32[]{:S(2)}) copy-start(f32[1024]{0:T(1024)} %param.18) | copy-start | bytes 12292
  333.6 5.0 %copy-start.13 = (f32[2,8,256]{2,1,0:T(8,128)S(1)}, f32[2,8,256]{2,1,0:T(8,128)}, u32[]{:S(2)}) copy-start(f32[2,8,256]{2,1,0:T(8,128)} %get-tuple-element.48) | copy-start | bytes 49156
  333.6 5.0 %copy-start.3 = (bf16[2048,1024]{1,0:T(8,128)(2,1)S(1)}, bf16[2048,1024]{1,0:T(8,128)(2,1)}, u32[]{:S(2)}) copy-start(bf16[2048,1024]{1,0:T(8,128)(2,1)} %cot.1) | copy-start | bytes 12582916
  333.6 5.0 %copy-start.4 = (bf16[2048,1024]{1,0:T(8,128)(2,1)S(1)}, bf16[2048,1024]{1,0:T(8,128)(2,1)}, u32[]{:S(2)}) copy-start(bf16[2048,1024]{1,0:T(8,128)(2,1)} %get-tuple-element.58) | copy-start | bytes 12582916
  333.6 5.9 %copy-start.5 = (bf16[2048,1024]{1,0:T(8,128)(2,1)S(1)}, bf16[2048,1024]{1,0:T(8,128)(2,1)}, u32[]{:S(2)}) copy-start(bf16[2048,1024]{1,0:T(8,128)(2,1)} %get-tuple-element.47) | copy-start | bytes 12582916
  339.5 6.6 %copy-start.6 = (bf16[1024,1024]{1,0:T(8,128)(2,1)S(1)}, bf16[1024,1024]{1,0:T(8,128)(2,1)}, u32[]{:S(2)}) copy-start(bf16[1024,1024]{1,0:T(8,128)(2,1)} %get-tuple-element.60) | copy-start | bytes 6291460
  339.5 11.7 %copy-start.11 = (f32[24,1024]{1,0:T(8,128)S(1)}, f32[24,1024]{1,0:T(8,128)}, u32[]{:S(2)}) copy-start(f32[24,1024]{1,0:T(8,128)} %get-tuple-element.59) | copy-start | bytes 294916
  339.5 16.5 %copy-start.7 = (bf16[512,1024]{1,0:T(8,128)(2,1)S(1)}, bf16[512,1024]{1,0:T(8,128)(2,1)}, u32[]{:S(2)}) copy-start(bf16[512,1024]{1,0:T(8,128)(2,1)} %get-tuple-element.62) | copy-start | bytes 3145732
  339.5 18.8 %copy-start.1 = (bf16[1024,8]{0,1:T(8,128)(2,1)S(1)}, bf16[1024,8]{0,1:T(8,128)(2,1)}, u32[]{:S(2)}) copy-start(bf16[1024,8]{0,1:T(8,128)(2,1)} %param.21) | copy-start | bytes 49156
  346.1 11.5 %copy-start.8 = (f32[64,1024]{1,0:T(8,128)S(1)}, f32[64,1024]{1,0:T(8,128)}, u32[]{:S(2)}) copy-start(f32[64,1024]{1,0:T(8,128)} %get-tuple-element.61) | copy-start | bytes 786436

commit v4 on v3

--- a/solution.py
+++ b/solution.py
@@ -373,19 +373,29 @@
     return out
 
 
-RAW, STEP, CUM, DEV = 0, 8, 16, 24
+RAW, STEP, CUM, DEV, KEEP = 0, 8, 16, 24, 32
+
+
+def head_lanes(row, heads, lane):
+    out = jnp.zeros(lane.shape, f32)
+    for k in range(heads):
+        out = jnp.where(lane % 8 == k, row[:, k : k + 1], out)
+    return out
 
 
 def front_kernel(heads, head_dim, state_dim, count,
-                 tokens, zx, dt, flags, gain, tail_rows, proj_bc, conv_bc, conv_x, params,
+                 tokens, last_tokens, zx, flags, gain, proj_bc, proj_dt, conv_x_weight, conv_x_bias,
+                 conv_bc_weight, conv_bc_bias, dt_bias, a_log, skip, norm_gain,
                  normed_out, gate_out, conv_in_out, conv_out_out, heads_out, entering, decay_out,
-                 halo_out, weights_out, conv_w_out,
-                 normed, taken, landed, proj_all, conv_all, carry, ext, state, running, lead, fade,
+                 halo_out, weights_out, conv_w_out, params, gains_out, mask_out,
+                 normed, taken, tail_rows, landed, proj_all, conv_bc, conv_all, flag_cols, flag_ext,
+                 carry, ext, state, running, lead, fade,
                  scan_got, scan_got_fade, scan_sent, scan_sent_fade, scan_sems, proj_sems, conv_sems, row_sems):
     at = pl.program_id(0)
     rows = tokens.shape[0]
     inner = heads * head_dim
     bc_width = 2 * state_dim
+    bc_part = proj_bc.shape[0]
     seq, me = lax.axis_size("seq"), lax.axis_index("seq")
     block = lax.rem(at, count)
     mine = pl.ds(pl.multiple_of(block * rows, rows), rows)
@@ -393,17 +403,37 @@
     row_copy = pltpu.make_async_remote_copy(
         src_ref=tail_rows, dst_ref=landed, send_sem=row_sems.at[0], recv_sem=row_sems.at[1],
         device_id={"seq": lax.rem(me + 1, seq)}, device_id_type=MESH)
+    lane_row = lax.broadcasted_iota(jnp.int32, (1, 128), 1)
 
     @pl.when(at == 0)
     def _():
+        final = 1.0 - flags[flags.shape[0] - 1 :].astype(f32)
+        one, two = final[:, 127:128], final[:, 126:127]
+        row = lax.broadcasted_iota(jnp.int32, (16, 128), 0)
+        mask = jnp.where(row == 15, 1.0, jnp.where(row == 14, one, jnp.where(row == 13, one * two, 0.0)))
+        mask_out[...] = mask
+        tail_rows[...] = (last_tokens[...].astype(f32) * mask[:, 0:1]).astype(bf16)
+        conv_bc[...] = jnp.zeros_like(conv_bc)
+        conv_bc[0:4, :bc_part] = conv_bc_weight[...].astype(f32)
+        conv_bc[4:5, :bc_part] = conv_bc_bias[...]
         greet("head", "seq")
         row_copy.start()
         for each in swaps:
             each.start()
+        params[...] = jnp.zeros_like(params)
+        params[0:1] = head_lanes(dt_bias[...], heads, lane_row)
+        params[1:2] = -jnp.exp(head_lanes(a_log[...], heads, lane_row))
+        gains_out[...] = jnp.zeros_like(gains_out)
+        gains_out[0:1] = norm_gain[...]
+        gains_out[1:2] = spread(head_lanes(skip[...], heads, lane_row), 0, heads, head_dim)
+        flat = flags[...].astype(f32)
+        turned = jnp.concatenate([flat, jnp.zeros((128 - flat.shape[0], 128), f32)], axis=0).T
+        for k in range(flat.shape[0]):
+            flag_cols[k * 128 : (k + 1) * 128] = jnp.broadcast_to(turned[:, k : k + 1], (128, 128))
 
     @pl.when(at < count)
     def _():
-        low = norm_rows(tokens[...], gain[0:1])
+        low = norm_rows(tokens[...], gain[...])
         normed[mine] = low
         normed_out[...] = low
         raw = dot(low, zx[...])
@@ -417,40 +447,55 @@
             each.wait()
             each.finish()
         heads_there = proj_all.shape[0]
-        weights_out[:, :bc_width] = jnp.concatenate([proj_all[k] for k in range(heads_there)], axis=1)
-        weights_out[:, bc_width:] = dt[...]
-        conv_w_out[...] = jnp.concatenate([conv_x[...]] + [conv_all[k] for k in range(heads_there)], axis=1)
-        head_rows = norm_rows(landed[...], gain[0:1])
-        ahead = jnp.concatenate([dot(head_rows, zx[:, inner:]), dot(head_rows, weights_out[:, :bc_width])], axis=1)
+        for k in range(heads_there):
+            weights_out[k * bc_part : (k + 1) * bc_part] = proj_all[k]
+        eight = jnp.concatenate([proj_dt[...].astype(f32)] + (
+            [jnp.zeros((8 - heads, proj_dt.shape[1]), f32)] if heads < 8 else []), axis=0)
+        weights_out[bc_width:] = jnp.concatenate([eight] * 16, axis=0).astype(bf16)
+        conv_w_out[...] = jnp.zeros_like(conv_w_out)
+        conv_w_out[0:4, :inner] = conv_x_weight[...].astype(f32)
+        conv_w_out[4:5, :inner] = conv_x_bias[...]
+        conv_w_out[:, inner:] = jnp.concatenate([conv_all[k, :, :bc_part] for k in range(heads_there)], axis=1)
+        head_rows = norm_rows(landed[...], gain[...])
+        ahead = jnp.concatenate([dot(head_rows, zx[:, inner:]), dot_nt(head_rows, weights_out[:bc_width])], axis=1)
         ahead = jnp.where(me > 0, ahead, 0.0).astype(bf16)
         halo_out[...] = ahead
         carry[...] = ahead[8:].astype(f32)
         state[...] = jnp.zeros_like(state)
         running[...] = jnp.zeros_like(running)
+        flag_ext[0:8] = jnp.zeros((8, 128), f32)
 
     @pl.when(at >= count)
     def _():
-        raw = dot(normed[mine], weights_out[...])
+        raw = dot_nt(normed[mine], weights_out[...])
         conv_in = jnp.concatenate([taken[mine], raw[:, :bc_width].astype(bf16)], axis=1)
         conv_in_out[...] = conv_in
         current = conv_in.astype(f32)
         ext[0:8] = carry[...]
         ext[8:] = current
         carry[...] = ext[rows:]
-        keep = 1.0 - flags[...]
+        flag = flag_cols[mine]
+        flag_ext[8:] = flag
+        keep1 = 1.0 - flag
+        keep2 = keep1 * (1.0 - flag_ext[7 : 7 + rows])
+        keep3 = keep2 * (1.0 - flag_ext[6 : 6 + rows])
+        flag_ext[0:8] = flag_ext[rows:]
+        keep = (None, keep1, keep2, keep3)
         total = conv_w_out[4:5] + conv_w_out[0:1] * current
         for j in range(1, 4):
-            total = total + conv_w_out[j : j + 1] * ext[pl.ds(8 - j, rows)] * keep[:, j : j + 1]
+            total = total + conv_w_out[j : j + 1] * ext[pl.ds(8 - j, rows)] * keep[j][:, 0:1]
         conv_out_out[...] = total
         active = total * sigmoid(total)
 
         step_raw = raw[:, bc_width:]
         step = softplus(step_raw + params[0:1])
-        log_decay = step * params[1:2] - GAP * flags[:, 1:2]
+        log_decay = step * params[1:2] - GAP * flag
         order_r = lax.broadcasted_iota(jnp.int32, (rows, rows), 0)
         order_c = lax.broadcasted_iota(jnp.int32, (rows, rows), 1)
         cum = exact_left((order_r >= order_c).astype(bf16), log_decay)
-        heads_out[...] = lane_groups(rows, step_raw, step, cum, cum + running[0:1])
+        lane = lax.broadcasted_iota(jnp.int32, (rows, 128), 1)
+        keeps = jnp.where(lane < KEEP + 1, keep1, jnp.where(lane < KEEP + 2, keep2, keep3))
+        heads_out[...] = lane_groups(rows, step_raw, step, cum, cum + running[0:1], keeps)
         end = cum[rows - 1 : rows]
         running[...] = running[...] + end
         weight = step * jnp.exp(end - cum)
@@ -468,7 +513,8 @@
         scan.run()
 
 
-def front(tokens, zx, dt, flags, gain, tail_rows, proj_bc, conv_bc, conv_x, params, heads, head_dim, state_dim):
+def front(tokens, zx, flags, gain, proj_bc, proj_dt, conv_x_weight, conv_x_bias, conv_bc_weight, conv_bc_bias,
+          dt_bias, a_log, skip, norm_gain, heads, head_dim, state_dim):
     length, width = tokens.shape
     count = length // GROUP
     inner = heads * head_dim
@@ -482,27 +528,30 @@
         return pl.BlockSpec((GROUP, cols), lambda g: (jnp.maximum(g - count, 0), 0))
     shape = jax.ShapeDtypeStruct
     state, fade = (state_dim, inner), (8, inner)
+    rest = 2 * state_dim + 128
     return pl.pallas_call(
         functools.partial(front_kernel, heads, head_dim, state_dim, count),
         grid=(2 * count,),
         out_shape=(shape((length, width), bf16), shape((length, inner), f32), shape((length, conv), bf16),
                    shape((length, conv), f32), shape((length, 128), f32), shape(state, f32),
-                   shape(fade, f32), shape((16, conv), bf16), shape((width, 2 * state_dim + 128), bf16),
-                   shape((8, conv), f32)),
-        in_specs=[early(width), whole(zx.shape), whole(dt.shape), late(8), VMEM, VMEM, VMEM, VMEM, VMEM, VMEM],
-        out_specs=(early(width), early(inner), late(conv), late(conv), late(128), whole(state), whole(fade),
-                   whole((16, conv)), whole((width, 2 * state_dim + 128)), whole((8, conv))),
+                   shape(fade, f32), shape((16, conv), bf16), shape((rest, width), bf16),
+                   shape((8, conv), f32), shape((8, 128), f32), shape((8, inner), f32), shape((16, 128), f32)),
+        in_specs=[early(width), pl.BlockSpec((16, width), lambda g: (length // 16 - 1, 0))] + [VMEM] * 13,
+        out_specs=(early(width), early(inner), late(conv), late(conv), late(128)) + (VMEM,) * 8,
         scratch_shapes=[
             pltpu.VMEM((length, width), bf16), pltpu.VMEM((length, inner), bf16),
-            pltpu.VMEM(tail_rows.shape, bf16), pltpu.VMEM((head_count,) + proj_bc.shape, bf16),
-            pltpu.VMEM((head_count,) + conv_bc.shape, f32), pltpu.VMEM((8, conv), f32),
+            pltpu.VMEM((16, width), bf16), pltpu.VMEM((16, width), bf16),
+            pltpu.VMEM((head_count,) + proj_bc.shape, bf16), pltpu.VMEM((8, 128), f32),
+            pltpu.VMEM((head_count, 8, 128), f32), pltpu.VMEM((length, 128), f32),
+            pltpu.VMEM((GROUP + 8, 128), f32), pltpu.VMEM((8, conv), f32),
             pltpu.VMEM((GROUP + 8, conv), f32), pltpu.VMEM(state, f32), pltpu.VMEM((8, 128), f32)]
         + DeviceScan.scratch(state, fade) + [DMA((2, head_count)), DMA((2, head_count)), DMA((2,))],
         compiler_params=pltpu.CompilerParams(
             dimension_semantics=("arbitrary",), collective_id=3, has_side_effects=True,
             vmem_limit_bytes=LIMIT),
         name="front",
-    )(tokens, zx, dt, flags, gain, tail_rows, proj_bc, conv_bc, conv_x, params)
+    )(tokens, tokens, zx, flags, gain, proj_bc, proj_dt, conv_x_weight, conv_x_bias, conv_bc_weight,
+      conv_bc_bias, dt_bias, a_log, skip, norm_gain)
 
 
 def strips(rows):
@@ -606,7 +655,7 @@
 
 
 def back_step(heads, head_dim, state_dim, first_step, last_step,
-              d_ssm, conv_out, conv_in, heads_in, start, entering, flags, conv_w, params, skip, conv_halo,
+              d_ssm, conv_out, conv_in, heads_in, start, entering, conv_w, params, skip, conv_halo,
               d_conv_in_out, d_step_out, conv_grads, head_grads, halo_out,
               lam, shift1, shift2, shift3, between):
     rows = d_ssm.shape[0]
@@ -708,8 +757,7 @@
 
     order_r = lax.broadcasted_iota(jnp.int32, (rows, rows), 0)
     order_c = lax.broadcasted_iota(jnp.int32, (rows, rows), 1)
-    free = 1.0 - flags[...]
-    d_decay = exact_left((order_r <= order_c).astype(bf16), d_cum) * free[:, 1:2]
+    d_decay = exact_left((order_r <= order_c).astype(bf16), d_cum) * info[:, KEEP : KEEP + 1]
     rate = params[1:2]
     real = lane < heads
     step_raw = jnp.where(real, info, 0.0) + params[0:1]
@@ -727,7 +775,7 @@
     conv_grads[4:5] += jnp.sum(d_conv, axis=0, keepdims=True)
     for j in range(1, 4):
         ref = shifts[j - 1]
-        ref[0:rows] = d_conv * free[:, j : j + 1]
+        ref[0:rows] = d_conv * info[:, KEEP + j - 1 : KEEP + j]
         moved = ref[pl.ds(j, rows)]
         total = total + moved * conv_w[j : j + 1]
         conv_grads[j : j + 1] += jnp.sum(moved * taken, axis=0, keepdims=True)
@@ -765,7 +813,7 @@
 
 
 def layer_kernel(heads, head_dim, state_dim, all_channels, count, block, lag, plans,
-                 conv_out, conv_in, heads_in, gate, cot, flags, out_proj, gains, entering, decay, conv_w,
+                 conv_out, conv_in, heads_in, gate, cot, out_proj, gains, entering, decay, conv_w,
                  params, conv_halo,
                  line_out, d_gate_out, d_conv_out, d_step_out, grad_out_out, gate_rows, conv_grads, head_grads,
                  halo_out, sums_out,
@@ -832,7 +880,7 @@
         here = 3 * count - 1 - at
         mine = pl.ds(pl.multiple_of(here * rows, rows), rows)
         back_step(heads, head_dim, state_dim, at == 2 * count, at == 3 * count - 1,
-                  ssm.at[mine], conv_out, conv_in, heads_in, starts[here], leaving, flags, conv_w, params,
+                  ssm.at[mine], conv_out, conv_in, heads_in, starts[here], leaving, conv_w, params,
                   gains[1:2], conv_halo, d_conv_out, d_step_out, conv_grads, head_grads, halo_out,
                   state, shift1, shift2, shift3, lambda: serve(2 * at + 1))
 
@@ -848,7 +896,7 @@
         line.finish()
 
 
-def layer(conv_out, conv_in, heads_in, gate, cot, flags, out_proj, gains, entering, decay, conv_w, params,
+def layer(conv_out, conv_in, heads_in, gate, cot, out_proj, gains, entering, decay, conv_w, params,
           conv_halo, heads, head_dim, state_dim, all_channels):
     length, conv = conv_out.shape
     count = length // GROUP
@@ -890,7 +938,7 @@
                    shape((length, 128), bf16), shape((inner, width), bf16), shape((8, inner), f32),
                    shape((8, conv), f32), shape((8, 128), f32), shape((8, conv), f32),
                    shape((2, count, GROUP), f32)),
-        in_specs=[by(conv, 0, 2), by(conv, 2, 2), by(128, 0, 2), by(inner, 0, 1), by(width, 0, 1), by(8, 2, 2)]
+        in_specs=[by(conv, 0, 2), by(conv, 2, 2), by(128, 0, 2), by(inner, 0, 1), by(width, 0, 1)]
         + [VMEM] * 7,
         out_specs=(HBM, by(inner, 1, 1), by(conv, 2, 2), by(128, 2, 2)) + (VMEM,) * 6,
         scratch_shapes=[pltpu.VMEM((length, width), bf16)] * 3 + [pltpu.VMEM((length, inner), f32)] * 2 + [
@@ -904,7 +952,7 @@
             dimension_semantics=("arbitrary",), collective_id=4, has_side_effects=True,
             vmem_limit_bytes=LIMIT),
         name="layer",
-    )(conv_out, conv_in, heads_in, gate, cot, flags, out_proj, gains, entering, decay, conv_w, params, conv_halo)
+    )(conv_out, conv_in, heads_in, gate, cot, out_proj, gains, entering, decay, conv_w, params, conv_halo)
 
 
 PACE = 2.9
@@ -913,9 +961,9 @@
 PROJECT, CUTS = 2.6, (17, 21)
 
 
-def tail_kernel(count, block, lag, plans, cuts, owners, last_rows,
-                normed, d_gate, d_conv, d_step, zx, weights, gain, back_rows, tail_mask, small_in,
-                line_out, zx_out, bc_out, small_out,
+def tail_kernel(count, block, lag, plans, cuts, owners, last_rows, taps,
+                normed, d_gate, d_conv, d_step, zx, weights, gain, back_rows, tail_mask, gate_rows, conv_grads,
+                head_grads, line_out, zx_out, bc_out, small_out,
                 own, got, total, grad_zx, grad_low, zx_slots, zx_res, grad_bc, bc_part, bc_slots, bc_z, bc_res, small, small_slots,
                 small_own, small_z, landed,
                 line_sems, zx_sems, bc_sems, bcz_sems, small_sems, smallz_sems, row_sems):
@@ -940,7 +988,11 @@
         row_copy.start()
         grad_zx[...] = jnp.zeros_like(grad_zx)
         grad_bc[...] = jnp.zeros_like(grad_bc)
-        small[...] = small_in[...]
+        small[...] = jnp.zeros_like(small)
+        small[8 : 9 + taps, :inner] = conv_grads[: taps + 1, :inner]
+        small[8:10, inner : 2 * inner] = gate_rows[0:2]
+        small[10:12, inner : inner + 128] = head_grads[0:2]
+        small[17 : 18 + taps, :bc_width] = conv_grads[: taps + 1, inner:]
 
     line.send(sent(at - 1), sent(at))
     line.serve(served(at - 1), served(at), lag)
@@ -949,24 +1001,24 @@
     gate_low, conv_low, step_low = d_gate[...], d_conv[...], d_step[...]
     rest_low = jnp.concatenate([conv_low[:, inner:], step_low], axis=1)
     d_normed = (dot_nt(gate_low, zx[:, :inner]) + dot_nt(conv_low[:, :inner], zx[:, inner:])
-                + dot_nt(rest_low, weights[...]))
+                + dot(rest_low, weights[...]))
     grad_zx[:, :inner] += dot_tn(block_low, gate_low)
     grad_zx[:, inner:] += dot_tn(block_low, conv_low[:, :inner])
     grad_bc[...] += dot_tn(rest_low, block_low)
-    small[16:17] += jnp.sum(d_normed * block_low.astype(f32), axis=0, keepdims=True) / gain[0:1]
+    small[16:17] += jnp.sum(d_normed * block_low.astype(f32), axis=0, keepdims=True) / gain[...]
     mine = pl.ds(pl.multiple_of(at * rows, rows), rows)
     own[mine] = d_normed.astype(bf16)
 
     @pl.when(at == count - 1)
     def _():
         row_copy.wait()
-        extra = jnp.where(me < seq - 1, landed[...] * tail_mask[...], 0.0)
+        extra = jnp.where(me < seq - 1, landed[...] * tail_mask[8:, 0:1], 0.0)
         extra = jnp.concatenate([jnp.zeros_like(extra), extra], axis=0).astype(bf16)
         tail_low = normed[rows - 16 :]
-        more = dot_nt(extra[:, :inner], zx[:, inner:]) + dot_nt(extra[:, inner:], weights[:, :bc_width])
+        more = dot_nt(extra[:, :inner], zx[:, inner:]) + dot(extra[:, inner:], weights[:bc_width])
         grad_zx[:, inner:] += dot_tn(tail_low, extra[:, :inner])
         grad_bc[:bc_width] += dot_tn(extra[:, inner:], tail_low)
-        small[16:17] += jnp.sum(more * tail_low.astype(f32), axis=0, keepdims=True) / gain[0:1]
+        small[16:17] += jnp.sum(more * tail_low.astype(f32), axis=0, keepdims=True) / gain[...]
         own[last_rows:] = (own[last_rows:].astype(f32) + more).astype(bf16)
 
     piece = bc_part.shape[1] // owners[1]
@@ -1083,7 +1135,8 @@
                 bc_swap(other_of("head", k), my_head).wait_send()
 
 
-def tail(normed, d_gate, d_conv, d_step, zx, weights, gain, back_rows, tail_mask, small_in, both):
+def tail(normed, d_gate, d_conv, d_step, zx, weights, gain, back_rows, tail_mask, gate_rows, conv_grads,
+         head_grads, taps):
     length, width = normed.shape
     inner, conv = d_gate.shape[1], d_conv.shape[1]
     count = length // GROUP
@@ -1103,19 +1156,19 @@
         return pl.BlockSpec((GROUP, cols), lambda g: (g, 0))
     shape = jax.ShapeDtypeStruct
     return pl.pallas_call(
-        functools.partial(tail_kernel, count, block, lag, plans, cuts, owners, length - 16),
+        functools.partial(tail_kernel, count, block, lag, plans, cuts, owners, length - 16, taps),
         grid=(count,),
         out_shape=(shape((length, width), bf16), shape((width, 2 * inner), bf16), shape((bc_rows, width), f32),
-                   shape(small_in.shape, f32)),
-        in_specs=[by(width), by(inner), by(conv), by(128)] + [VMEM] * 6,
+                   shape((24, width), f32)),
+        in_specs=[by(width), by(inner), by(conv), by(128)] + [VMEM] * 8,
         out_specs=(HBM, VMEM, VMEM, VMEM),
         scratch_shapes=[pltpu.VMEM((length, width), bf16)] * 3 + [
             pltpu.VMEM((width, 2 * inner), f32), pltpu.VMEM((width, 2 * inner), bf16),
             pltpu.VMEM((seq, width // owners[0], 2 * inner), bf16), pltpu.VMEM((width, 2 * inner), bf16),
             pltpu.VMEM((conv - inner + 128, width), f32), pltpu.VMEM((heads, bc_rows, width), f32),
             pltpu.VMEM((seq, heads, piece, width), f32), pltpu.VMEM((heads, piece, width), f32),
-            pltpu.VMEM((bc_rows, width), f32), pltpu.VMEM(small_in.shape, f32), pltpu.VMEM((seq,) + small_in.shape, f32),
-            pltpu.VMEM((both, width), f32), pltpu.VMEM((heads, both, width), f32),
+            pltpu.VMEM((bc_rows, width), f32), pltpu.VMEM((24, width), f32), pltpu.VMEM((seq, 24, width), f32),
+            pltpu.VMEM((8, width), f32), pltpu.VMEM((heads, 8, width), f32),
             pltpu.VMEM(back_rows.shape, f32),
             LineSum.sems(length, block), DMA((4, seq)), DMA((4, seq)), DMA((2, heads)), DMA((2, seq)),
             DMA((2, heads)), DMA((2,))],
@@ -1123,11 +1176,82 @@
             dimension_semantics=("arbitrary",), collective_id=5, has_side_effects=True,
             vmem_limit_bytes=LIMIT),
         name="tail",
-    )(normed, d_gate, d_conv, d_step, zx, weights, gain, back_rows, tail_mask, small_in)
-
-
-def padded(block, rows, cols):
-    return jnp.pad(block, ((0, rows - block.shape[0]), (0, cols - block.shape[1])))
+    )(normed, d_gate, d_conv, d_step, zx, weights, gain, back_rows, tail_mask, gate_rows, conv_grads, head_grads)
+
+
+def finish_kernel(heads, head_dim, all_channels, taps,
+                  tokens, cot, mixed, d_normed, sums, gain, zx, op, bc, small,
+                  mixed_out, tokens_out, zx_out, op_out, bc_out, dt_out, gain_out, conv_w_out, conv_b_out,
+                  bc_w_out, bc_b_out, bias_out, rate_out, skip_out, norm_out):
+    at = pl.program_id(0)
+    rows = tokens.shape[0]
+    inner = heads * head_dim
+    value = tokens[...].astype(f32)
+    tall = jnp.concatenate([sums[0, pl.ds(at, 1)], jnp.zeros((127, rows), f32)], axis=0).T
+    inv_rms = lax.rsqrt(tall[:, 0:1] / all_channels + epsilon)
+    mixed_out[...] = (value + mixed[...].astype(f32) * inv_rms).astype(bf16)
+    inv = lax.rsqrt(jnp.mean(value * value, axis=1, keepdims=True) + epsilon)
+    xhat = value * inv
+    scaled = d_normed[...].astype(f32) * gain[...]
+    tokens_out[...] = cot[...].astype(f32) + inv * (
+        scaled - xhat * jnp.mean(scaled * xhat, axis=1, keepdims=True))
+    sums_zx = zx[...].astype(f32)
+    zx_out[:, 0, :] = sums_zx[:, :inner]
+    zx_out[:, 1, :] = sums_zx[:, inner:]
+    op_out[...] = op[...].astype(f32)
+    cols = bc.shape[1]
+    mine = pl.ds(pl.multiple_of(at * cols, cols), cols)
+    bc_out[...] = bc[...].T
+    dt_out[...] = small[0:8, mine].T[:, :heads]
+
+    @pl.when(at == 0)
+    def _():
+        gain_out[...] = small[16:17]
+        conv_w_out[...] = small[8 : 8 + taps, :inner]
+        conv_b_out[...] = small[8 + taps : 9 + taps, :inner]
+        bias_out[...] = small[10:11, inner : inner + heads]
+        rate_out[...] = small[11:12, inner : inner + heads]
+        norm_out[...] = small[8:9, inner : 2 * inner]
+        group_ones = (lax.broadcasted_iota(jnp.int32, (inner, 128), 0) // head_dim
+                      == lax.broadcasted_iota(jnp.int32, (inner, 128), 1)).astype(bf16)
+        skips = jnp.broadcast_to(small[9:10, inner : 2 * inner], (8, inner))
+        total = sum(dot(part, group_ones) for part in split3(skips))
+        skip_out[...] = total[0:1, :heads]
+        part = bc_w_out.shape[1]
+        mine_bc = small[17 : 18 + taps, : part * lax.axis_size("head")]
+        chosen = mine_bc[:, :part]
+        for k in range(1, lax.axis_size("head")):
+            chosen = jnp.where(lax.axis_index("head") == k, mine_bc[:, k * part : (k + 1) * part], chosen)
+        bc_w_out[...] = chosen[:taps]
+        bc_b_out[...] = chosen[taps : taps + 1]
+
+
+def finish(tokens, cot, mixed, d_normed, sums, gain, zx, op, bc, small, heads, head_dim, taps):
+    length, width = tokens.shape
+    count = length // GROUP
+    inner = heads * head_dim
+    part = bc.shape[0]
+
+    def by(rows, cols):
+        return pl.BlockSpec((rows, cols), lambda g: (g, 0))
+    shape = jax.ShapeDtypeStruct
+    tall = by(GROUP, width)
+    lone = [(1, width), (taps, inner), (1, inner), (taps, part), (1, part), (1, heads), (1, heads), (1, heads),
+            (1, inner)]
+    cols = width // count
+    return pl.pallas_call(
+        functools.partial(finish_kernel, heads, head_dim, inner * lax.axis_size("head"), taps),
+        grid=(count,),
+        out_shape=(shape((length, width), bf16), shape((length, width), f32), shape((width, 2, inner), f32),
+                   shape((inner, width), f32), shape((width, part), f32), shape((width, heads), f32))
+        + tuple(shape(each, f32) for each in lone),
+        in_specs=[tall] * 4 + [VMEM, VMEM, by(cols, 2 * inner), by(inner // count, width),
+                               pl.BlockSpec((part, cols), lambda g: (0, g)), VMEM],
+        out_specs=(tall, tall, pl.BlockSpec((cols, 2, inner), lambda g: (g, 0, 0)), by(inner // count, width),
+                   by(cols, part), by(cols, heads)) + (VMEM,) * len(lone),
+        compiler_params=pltpu.CompilerParams(dimension_semantics=("arbitrary",), vmem_limit_bytes=LIMIT),
+        name="finish",
+    )(tokens, cot, mixed, d_normed, sums, gain, zx, op, bc, small)
 
 
 def shards(
@@ -1143,66 +1267,26 @@
     bc_part = conv_bc_bias.shape[0]
     bc_width = bc_part * head_count
     state_dim = bc_width // 2
-    my_head = lax.axis_index("head")
-
-    flag = start_flags.astype(f32)
-    free = 1.0 - flag
-    free1 = jnp.pad(free, (1, 0), constant_values=1.0)[:length]
-    free2 = jnp.pad(free, (2, 0), constant_values=1.0)[:length]
-    flags = jnp.pad(jnp.stack([flag, 1.0 - free * free1, 1.0 - free * free1 * free2], axis=1), ((0, 0), (1, 4)))
-    last = jnp.stack([free[length - 1] * free[length - 2], free[length - 1], jnp.ones((), f32)])
-    tail_mask = jnp.pad(last, (13, 0))[:, None]
-    tail_rows = (tokens[length - 16 :].astype(f32) * tail_mask).astype(bf16)
-    gain8 = jnp.broadcast_to(in_gain[None], (8, width))
-    conv_bc = padded(jnp.concatenate([conv_bc_weight.astype(f32), conv_bc_bias[None]]), 8, bc_part)
-
-    conv_x = padded(jnp.concatenate([conv_x_weight.astype(f32), conv_x_bias[None]]), 8, inner)
-    head_rows = jnp.pad(jnp.stack([dt_bias, -jnp.exp(a_log)]), ((0, 6), (0, 8 - heads)))
-    params = jnp.tile(head_rows, (1, 16))
-    gains = jnp.pad(jnp.stack([norm_gain, jnp.repeat(skip_scale, head_dim)]), ((0, 6), (0, 0)))
     zx = proj_zx.reshape(width, 2 * inner)
-    dt = jnp.tile(jnp.pad(proj_dt, ((0, 0), (0, 8 - heads))), (1, 16))
-
-    normed, gate, conv_in, conv_out, info, entering, decay, conv_halo, weights, conv_w = front(
-        tokens, zx, dt, flags, gain8, tail_rows, proj_bc, conv_bc, conv_x, params, heads, head_dim, state_dim)
+    gain = in_gain[None]
+    (normed, gate, conv_in, conv_out, info, entering, decay, conv_halo, weights, conv_w, params, gains,
+     tail_mask) = front(
+        tokens, zx, start_flags.reshape(length // 128, 128), gain, proj_bc.T, proj_dt.T, conv_x_weight,
+        conv_x_bias[None], conv_bc_weight, conv_bc_bias[None], dt_bias[None], a_log[None], skip_scale[None],
+        norm_gain[None], heads, head_dim, state_dim)
     all_channels = inner * head_count
     mixed, d_gate, d_conv, d_step, op_sum, gate_rows, conv_grads, head_grads, back_rows, sums = layer(
-        conv_out, conv_in, info, gate, cotangent, flags, out_proj, gains, entering, decay, conv_w, params,
+        conv_out, conv_in, info, gate, cotangent, out_proj, gains, entering, decay, conv_w, params,
         conv_halo, heads, head_dim, state_dim, all_channels)
-    inv_rms = lax.rsqrt(sums[0].reshape(length, 1) / all_channels + epsilon)
-    mixed_out = (tokens.astype(f32) + mixed.astype(f32) * inv_rms).astype(bf16)
-
-    right = jnp.concatenate([gate_rows[:2], padded(head_grads[:2], 6, inner)])
-    small = jnp.concatenate([
-        jnp.zeros((8, width), f32),
-        padded(jnp.concatenate([conv_grads[:, :inner], right], axis=1), 8, width),
-        jnp.zeros((1, width), f32), padded(conv_grads[: taps + 1, inner:], 7, width)])
     d_normed, zx_sum, bc_sum, small_sum = tail(
-        normed, d_gate, d_conv, d_step, zx, weights, gain8, back_rows, tail_mask[8:], small, 8)
-
-    tokens_f = tokens.astype(f32)
-    inv = lax.rsqrt(jnp.mean(tokens_f * tokens_f, axis=1, keepdims=True) + epsilon)
-    xhat = tokens_f * inv
-    scaled = d_normed.astype(f32) * in_gain
-    grad_tokens = cotangent.astype(f32) + inv * (
-        scaled - xhat * jnp.mean(scaled * xhat, axis=1, keepdims=True))
-    conv_bc_sum = lax.dynamic_slice(small_sum, (17, my_head * bc_part), (taps + 1, bc_part))
+        normed, d_gate, d_conv, d_step, zx, weights, gain, back_rows, tail_mask, gate_rows, conv_grads,
+        head_grads, taps)
+    (mixed_out, grad_tokens, grad_zx, grad_op, grad_bc, grad_dt, grad_gain, grad_conv_w, grad_conv_b,
+     grad_bc_w, grad_bc_b, grad_bias, grad_rate, grad_skip, grad_norm) = finish(
+        tokens, cotangent, mixed, d_normed, sums, gain, zx_sum, op_sum, bc_sum, small_sum, heads, head_dim, taps)
     return (
-        mixed_out,
-        grad_tokens,
-        small_sum[16],
-        zx_sum.astype(f32).reshape(width, 2, inner),
-        bc_sum.T,
-        small_sum[:heads].T,
-        small_sum[8 : 8 + taps, :inner],
-        small_sum[8 + taps, :inner],
-        conv_bc_sum[:taps],
-        conv_bc_sum[taps],
-        small_sum[10, inner : inner + heads],
-        small_sum[11, inner : inner + heads],
-        small_sum[9, inner : 2 * inner].reshape(heads, head_dim).sum(axis=1),
-        small_sum[8, inner : 2 * inner],
-        op_sum.astype(f32),
+        mixed_out, grad_tokens, grad_gain[0], grad_zx, grad_bc, grad_dt, grad_conv_w, grad_conv_b[0],
+        grad_bc_w, grad_bc_b[0], grad_bias[0], grad_rate[0], grad_skip[0], grad_norm[0], grad_op,
     )
 
 

time: 363 us -> 331 us (0.912)
  other arithmetic: 21.3 us -> 0 us
  local copies, waits for them, and re-layouts: 24.2 us -> 7.23 us
  Pallas kernels: 311 us -> 318 us
    pallas_call x0 -> x1, Pallas kernels: none -> 18.5 us  [finish(): pl.pallas_call(functools.partial(finish_kernel, heads, head_dim, inner *...]
    pallas_call x1, Pallas kernels: 59 us -> 47.9 us  [front(): pl.pallas_call(functools.partial(front_kernel, heads, head_dim, state_dim...]
    add x1 -> x0, other arithmetic: 6.57 us -> none  [shards(): cotangent.astype(f32)]
    slice x11 -> x0, local copies, waits for them, and re-layouts: 6.5 us -> none  [the longest x2 1.39 us: shards(): right = jnp.concatenate([gate_rows[:2], padded(head_grads[:2], 6, inner)])]
    reduce_sum x3 -> x0, other arithmetic: 5.53 us -> none  [the longest x1 4.02 us: shards(): jnp.mean(scaled * xhat, axis=1, keepdims=True)]
    reshape x1 -> x0, local copies, waits for them, and re-layouts: 5.11 us -> none  [shards(): zx_sum.astype(f32).reshape(width, 2, inner)]
    convert_element_type x5 -> x0, other arithmetic: 3.72 us -> none  [the longest x1 1.57 us: shards(): op_sum.astype(f32)]
where the time goes in v4:
time: 331 us; the launch traced here: 326 us
  Pallas kernels  318 us (96%)
  local copies, waits for them, and re-layouts  7.23 us (2%)
    pallas_call x1, Pallas kernels, layer(): pl.pallas_call(functools.partial(layer_kernel, heads, head_dim, state_dim...  131 us
    pallas_call x1, Pallas kernels, tail(): pl.pallas_call(functools.partial(tail_kernel, count, block, lag, plans, c...  120 us
    pallas_call x1, Pallas kernels, front(): pl.pallas_call(functools.partial(front_kernel, heads, head_dim, state_dim...  47.9 us
    pallas_call x1, Pallas kernels, finish(): pl.pallas_call(functools.partial(finish_kernel, heads, head_dim, inner *...  18.5 us
    unnamed x3, local copies, waits for them, and re-layouts  7.23 us

profile of v4, /device:TPU:0, one launch (start us, length us, event | category | flops | bytes accessed | tf_op | source)
XLA Modules:
  0.0 325.8 jit_solution(9659290821865614625)
XLA Ops:
  0.6 3.5 %copy.33 = bf16[128,8,2,512]{3,1,2,0:T(8,128)(2,1)} copy(bf16[128,8,2,512]{3,2,1,0:T(2,128)(2,1)} %bitcast.21) | data formatting | bytes 4194304
  4.1 47.9 %front.1 = (bf16[2048,1024]{1,0:T(8,128)(2,1)}, f32[2048,512]{1,0:T(8,128)}, bf16[2048,768]{1,0:T(8,128)(2,1)}, f32[2048,768]{1,0:T(8,128)}, f32[2048,128]{1,0:T...) custom-call(bf16[2048,1024]{1,0:T(8,128)(2,1)} %tokens.3, ...), custom_call_target="tpu_custom_call" | custom-call | tf_op jit(solution)/shard_map/front/pallas_call | solution.py:532
  52.0 131.2 %layer.1 = (bf16[2048,1024]{1,0:T(8,128)(2,1)}, bf16[2048,512]{1,0:T(8,128)(2,1)}, bf16[2048,768]{1,0:T(8,128)(2,1)}, bf16[2048,128]{1,0:T(8,128)(2,1)}, bf16[51...) custom-call(f32[2048,768]{1,0:T(8,128)} %get-tuple-element.57.conv_o, ...), custom_call_target="tpu_custom_call" | custom-call | tf_op jit(solution)/shard_map/layer/pallas_call | solution.py:934
  183.2 120.3 %tail.1 = (bf16[2048,1024]{1,0:T(8,128)(2,1)}, bf16[1024,1024]{1,0:T(8,128)(2,1)}, f32[64,1024]{1,0:T(8,128)}, f32[24,1024]{1,0:T(8,128)}) custom-call(bf16[2048,1024]{1,0:T(8,128)(2,1)} %get-tuple-element.68.normed, bf16[2048,512]{1,0:T(8,128)(2,1)} %get-tuple-element.69.d_gate, bf16[2048,768]{1,0:T(8,128)(2,1)} %get-tuple-element.70.d_conv, ...), custom_call_target="tpu_custom_call" | custom-call | tf_op jit(solution)/shard_map/tail/pallas_call | solution.py:1158
  303.5 18.5 %finish.1 = (bf16[2048,1024]{1,0:T(8,128)(2,1)}, f32[2048,1024]{1,0:T(8,128)}, f32[1024,2,512]{2,1,0:T(2,128)}, f32[512,1024]{1,0:T(8,128)}, f32[1024,64]{1,0:T(...) custom-call(bf16[2048,1024]{1,0:T(8,128)(2,1)} %tokens.3, ...), custom_call_target="tpu_custom_call" | custom-call | tf_op jit(solution)/shard_map/finish/pallas_call | solution.py:1242
  322.1 1.8 copy.32
  323.9 1.9 copy.31

commit v5 on v4

--- a/solution.py
+++ b/solution.py
@@ -37,66 +37,107 @@
     pl.semaphore_wait(barrier, count)
 
 
+class Pace:
+    def __init__(self, phases, pace, behind, most):
+        self.phases, self.pace, self.behind, self.most = phases, pace, behind, most
+        self.before = [0]
+        for n, (points, _, _) in enumerate(phases):
+            self.before.append(self.count(n, points - 1) if points else self.before[-1])
+
+    def count(self, phase, k):
+        _, start, step = self.phases[phase]
+        low, top = self.before[phase], self.most
+        value = (start + k * step - self.behind) // self.pace
+        if isinstance(value, int):
+            return max(low, min(top, value))
+        return jnp.clip(value, low, top)
+
+    def span(self, phase, k):
+        if isinstance(k, int):
+            return (self.count(phase, k - 1) if k else self.before[phase]), self.count(phase, k)
+        return jnp.where(k == 0, self.before[phase], self.count(phase, k - 1)), self.count(phase, k)
+
+
 class LineSum:
     AHEAD = 3
 
-    def __init__(self, own, got, total, out, sems, block):
-        self.own, self.got, self.total, self.out = own, got, total, out
+    def __init__(self, own, got, total, outs, place, sems, block):
+        self.own, self.got, self.total, self.outs, self.place = own, got, total, outs, place
         self.send1, self.got_in, self.got_total, self.send2, self.stored = (sems.at[i] for i in range(5))
         self.block = block
-        self.count = own.shape[0] // block
+        self.half = own.shape[0] // block
+        self.count = 2 * self.half
         size, me = lax.axis_size("head"), lax.axis_index("head")
-        half = size // 2
-        left = me < half
-        self.mid = (me == half - 1) | (me == half)
+        left = me < size // 2
+        self.mid = (me == size // 2 - 1) | (me == size // 2)
         self.has_outer = (me > 0) & (me < size - 1)
         self.inner = jnp.where(left, me + 1, me - 1)
         self.outer = jnp.clip(jnp.where(left, me - 1, me + 1), 0, size - 1)
 
     @staticmethod
     def sems(rows, block):
-        return DMA((5, rows // block))
+        return DMA((5, 2 * rows // block))
 
     def rows(self, b):
         return pl.ds(pl.multiple_of(b * self.block, self.block), self.block)
 
-    def copy(self, src, dst, b, send, recv, to):
+    def slot(self, b):
+        return self.rows(lax.rem(b, self.half))
+
+    def in_copy(self, b, to):
         return pltpu.make_async_remote_copy(
-            src_ref=src.at[self.rows(b)], dst_ref=dst.at[self.rows(b)],
-            send_sem=send.at[b], recv_sem=recv.at[b], device_id={"head": to}, device_id_type=MESH)
-
-    def store(self, b):
-        return pltpu.make_async_copy(
-            self.total.at[self.rows(b)], self.out.at[self.rows(b)], self.stored.at[b])
+            src_ref=self.own.at[self.slot(b)], dst_ref=self.got.at[self.slot(b)],
+            send_sem=self.send1.at[b], recv_sem=self.got_in.at[b], device_id={"head": to}, device_id_type=MESH)
+
+    def cross_copy(self, b):
+        return pltpu.make_async_remote_copy(
+            src_ref=self.own.at[self.slot(b)], dst_ref=self.total.at[self.rows(b)],
+            send_sem=self.send1.at[b], recv_sem=self.got_total.at[b],
+            device_id={"head": self.inner}, device_id_type=MESH)
+
+    def out_copy(self, b, to):
+        return pltpu.make_async_remote_copy(
+            src_ref=self.total.at[self.rows(b)], dst_ref=self.total.at[self.rows(b)],
+            send_sem=self.send2.at[b], recv_sem=self.got_total.at[b],
+            device_id={"head": to}, device_id_type=MESH)
+
+    def store(self, b, do):
+        for n, out in enumerate(self.outs):
+            @pl.when(b // self.half == n)
+            def _():
+                do(pltpu.make_async_copy(self.total.at[self.rows(b)],
+                                         out.at[self.rows(self.place(n, lax.rem(b, self.half)))],
+                                         self.stored.at[b]))
 
     def inward(self, b):
-        rows = self.rows(b)
-
-        @pl.when(self.has_outer)
-        def _():
-            self.copy(self.own, self.got, b, self.send1, self.got_in, self.outer).wait_recv()
-            self.own[rows] = (self.got[rows].astype(f32) + self.own[rows].astype(f32)).astype(bf16)
+        rows = self.slot(b)
+        self.in_copy(b, self.outer).wait_recv()
+        self.own[rows] = (self.got[rows].astype(f32) + self.own[rows].astype(f32)).astype(bf16)
 
         @pl.when(self.mid)
         def _():
-            self.copy(self.own, self.total, b, self.send1, self.got_total, self.inner).start()
+            self.cross_copy(b).start()
 
         @pl.when(jnp.logical_not(self.mid))
         def _():
-            self.copy(self.own, self.got, b, self.send1, self.got_in, self.inner).start()
+            self.in_copy(b, self.inner).start()
 
     def outward(self, b):
         rows = self.rows(b)
-        self.copy(self.own, self.total, b, self.send1, self.got_total, self.inner).wait_recv()
+        self.cross_copy(b).wait_recv()
+
+        @pl.when(self.has_outer)
+        def _():
+            self.cross_copy(b).wait_send()
 
         @pl.when(self.mid)
         def _():
-            self.total[rows] = (self.own[rows].astype(f32) + self.total[rows].astype(f32)).astype(bf16)
+            self.total[rows] = (self.own[self.slot(b)].astype(f32) + self.total[rows].astype(f32)).astype(bf16)
 
         @pl.when(self.has_outer)
         def _():
-            self.copy(self.total, self.total, b, self.send2, self.got_total, self.outer).start()
-        self.store(b).start()
+            self.out_copy(b, self.outer).start()
+        self.store(b, lambda copy: copy.start())
 
     def serve(self, first, last, lag):
         @pl.when(self.has_outer)
@@ -118,90 +159,111 @@
             def _(b):
                 @pl.when(b >= self.AHEAD)
                 def _():
-                    self.copy(self.own, self.got, b - self.AHEAD, self.send1, self.got_in, self.inner).wait_send()
-                self.inward(b)
+                    self.in_copy(b - self.AHEAD, self.inner).wait_send()
+
+                @pl.when(b >= self.half)
+                def _():
+                    self.outward(b - self.half)
+                self.in_copy(b, self.inner).start()
 
     def finish(self):
         @pl.when(jnp.logical_not(self.has_outer))
         def _():
-            pl.loop(0, self.count)(self.outward)
+            pl.loop(self.half, self.count)(self.outward)
+
+            @pl.loop(self.count - self.AHEAD, self.count)
+            def _(b):
+                self.in_copy(b, self.inner).wait_send()
 
         @pl.loop(0, self.count)
         def _(b):
-            @pl.when(self.has_outer | (b >= self.count - self.AHEAD))
-            def _():
-                self.copy(self.own, self.got, b, self.send1, self.got_in, self.inner).wait_send()
-            self.store(b).wait()
+            self.store(b, lambda copy: copy.wait())
 
             @pl.when(self.has_outer)
             def _():
-                self.copy(self.total, self.total, b, self.send2, self.got_total, self.outer).wait_send()
-
-
-class PlaneSum:
-    def __init__(self, own, slots, res, sems, owners):
-        self.own, self.slots, self.res = own, slots, res
-        self.rs_send, self.rs_got, self.ag_send, self.ag_got = (sems.at[i] for i in range(4))
-        self.owners = owners
-        self.size, self.me = lax.axis_size("seq"), lax.axis_index("seq")
-        self.piece = own.shape[0] // owners
-
-    def part(self, ref, k):
-        return rows_of(ref, k * self.piece, self.piece)
+                self.out_copy(b, self.outer).wait_send()
+
+
+class PairedSum:
+    def __init__(self, own, pair, mine, slots, theirs, sems):
+        self.own, self.pair, self.mine, self.slots, self.theirs = own, pair, mine, slots, theirs
+        self.sems = sems
+        self.me = lax.axis_index("seq")
+        self.chip, self.odd = self.me // 2, lax.rem(self.me, 2)
+        self.partner = self.me + 1 - 2 * self.odd
+        self.chips, self.piece = own.shape[0], own.shape[1] // 2
+
+    @staticmethod
+    def scratch(rows, width):
+        seq = lax.axis_size("seq")
+        piece = max(16, rows // seq)
+        part = pltpu.VMEM((seq // 2, piece, width), bf16)
+        return [pltpu.VMEM((seq // 2, 2 * piece, width), bf16)] + [part] * 4 + [DMA((6, seq // 2))]
+
+    def half(self, odd):
+        return pl.ds(pl.multiple_of(odd * self.piece, self.piece), self.piece)
+
+    def swap_copy(self):
+        return pltpu.make_async_remote_copy(
+            src_ref=self.own.at[:, self.half(1 - self.odd)], dst_ref=self.pair,
+            send_sem=self.sems.at[0, 0], recv_sem=self.sems.at[1, 0],
+            device_id={"seq": self.partner}, device_id_type=MESH)
+
+    def back_copy(self):
+        return pltpu.make_async_remote_copy(
+            src_ref=self.pair, dst_ref=self.theirs,
+            send_sem=self.sems.at[0, 1], recv_sem=self.sems.at[1, 1],
+            device_id={"seq": self.partner}, device_id_type=MESH)
 
     def scatter_copy(self, to, source):
         return pltpu.make_async_remote_copy(
-            src_ref=self.part(self.own, to), dst_ref=self.slots.at[source],
-            send_sem=self.rs_send.at[to], recv_sem=self.rs_got.at[source],
-            device_id={"seq": to}, device_id_type=MESH)
+            src_ref=self.mine.at[to], dst_ref=self.slots.at[source],
+            send_sem=self.sems.at[2, to], recv_sem=self.sems.at[3, source],
+            device_id={"seq": 2 * to + self.odd}, device_id_type=MESH)
 
     def gather_copy(self, owner, to):
         return pltpu.make_async_remote_copy(
-            src_ref=self.part(self.res, owner), dst_ref=self.part(self.res, owner),
-            send_sem=self.ag_send.at[to], recv_sem=self.ag_got.at[owner],
-            device_id={"seq": to}, device_id_type=MESH)
+            src_ref=self.pair.at[owner], dst_ref=self.pair.at[owner],
+            send_sem=self.sems.at[4, to], recv_sem=self.sems.at[5, owner],
+            device_id={"seq": 2 * to + self.odd}, device_id_type=MESH)
+
+    def release(self, free):
+        pl.semaphore_signal(free, inc=1, device_id={"seq": self.partner}, device_id_type=MESH)
+
+    def others(self, do):
+        @pl.loop(1, self.chips)
+        def _(k):
+            do(lax.rem(self.chip + k, self.chips))
+
+    def swap(self):
+        self.swap_copy().start()
 
     def scatter(self):
-        @pl.loop(1, self.size)
-        def _(k):
-            to = other_of("seq", k)
-
-            @pl.when(to < self.owners)
-            def _():
-                self.scatter_copy(to, self.me).start()
-
-    def reduce(self):
-        @pl.when(self.me < self.owners)
-        def _():
-            @pl.loop(1, self.size)
-            def _(k):
-                self.scatter_copy(self.me, other_of("seq", k)).wait_recv()
-            mine = pl.ds(pl.multiple_of(self.me * self.piece, self.piece), self.piece)
-            self.slots[self.me] = self.own[mine]
-            total = self.slots[0].astype(f32)
-            for k in range(1, self.size):
-                total = total + self.slots[k].astype(f32)
-            self.res[mine] = total.astype(self.res.dtype)
-
-            @pl.loop(1, self.size)
-            def _(k):
-                self.gather_copy(self.me, other_of("seq", k)).start()
-
-    def finish(self):
-        @pl.loop(1, self.size)
-        def _(k):
-            other = other_of("seq", k)
-
-            @pl.when(other < self.owners)
-            def _():
-                self.gather_copy(other, self.me).wait_recv()
-                self.scatter_copy(other, self.me).wait_send()
-
-        @pl.when(self.me < self.owners)
-        def _():
-            @pl.loop(1, self.size)
-            def _(k):
-                self.gather_copy(self.me, other_of("seq", k)).wait_send()
+        self.swap_copy().wait()
+        self.mine[...] = (self.own[:, self.half(self.odd)].astype(f32) + self.pair[...].astype(f32)).astype(bf16)
+        self.others(lambda other: self.scatter_copy(other, self.chip).start())
+
+    def gather(self):
+        self.others(lambda other: self.scatter_copy(self.chip, other).wait_recv())
+        self.others(lambda other: self.scatter_copy(other, self.chip).wait_send())
+        self.slots[self.chip] = self.mine[self.chip]
+        total = self.slots[0].astype(f32)
+        for k in range(1, self.chips):
+            total = total + self.slots[k].astype(f32)
+        self.pair[self.chip] = total.astype(bf16)
+        self.others(lambda other: self.gather_copy(self.chip, other).start())
+
+    def back(self):
+        self.others(lambda other: self.gather_copy(other, self.chip).wait_recv())
+        self.back_copy().start()
+
+    def finish(self, out):
+        self.back_copy().wait()
+        self.others(lambda other: self.gather_copy(self.chip, other).wait_send())
+        for k in range(min(self.chips, out.shape[0] // (2 * self.piece))):
+            for odd, ref in ((self.odd, self.pair), (1 - self.odd, self.theirs)):
+                start = pl.multiple_of((2 * k + odd) * self.piece, self.piece)
+                out[pl.ds(start, self.piece)] = ref[k]
 
 
 class Swap:
@@ -560,7 +622,7 @@
 
 def mix_step(heads, head_dim, state_dim, at,
              conv_out, heads_in, gate, cot, out_proj, gains, entering,
-             ssm_out, d_normed_out, partial_out, sums_out, starts_out, state):
+             ssm_out, d_normed_out, partial_out, sums_out, starts_out, state, between):
     rows = conv_out.shape[0]
     inner = heads * head_dim
     per = 128 // head_dim
@@ -583,18 +645,24 @@
     tiles = []
     for pair in range(heads // per):
         tile = low[:, pair * 128 : (pair + 1) * 128]
-        parts = [None] * (rows // STRIP)
+        weights, masked = [], []
         for k in range(per):
             head = pair * per + k
-            masked = jnp.where((lane >= k * head_dim) & (lane < (k + 1) * head_dim), tile, jnp.zeros_like(tile))
-            for n, (lo, hi) in enumerate(strips(rows)):
+            masked.append(jnp.where((lane >= k * head_dim) & (lane < (k + 1) * head_dim), tile,
+                                    jnp.zeros_like(tile)))
+            parts = []
+            for lo, hi in strips(rows):
                 gap = info[lo:hi, CUM + head : CUM + head + 1] - flipped[CUM + head : CUM + head + 1, :hi]
                 ok = (lax.broadcasted_iota(jnp.int32, (STRIP, hi), 0) + lo
                       >= lax.broadcasted_iota(jnp.int32, (STRIP, hi), 1))
-                weight = jnp.exp(jnp.where(ok, gap, -1e30)) * scores[lo:hi, :hi]
-                part = dot(weight.astype(bf16), masked[:hi])
-                parts[n] = part if parts[n] is None else parts[n] + part
-        tiles.append(jnp.concatenate(parts, axis=0))
+                part = (jnp.exp(jnp.where(ok, gap, -1e30)) * scores[lo:hi, :hi]).astype(bf16)
+                if hi < rows:
+                    part = jnp.concatenate([part, jnp.zeros((STRIP, rows - hi), bf16)], axis=1)
+                parts.append(part)
+            weights.append(jnp.concatenate(parts, axis=0))
+        tiles.append(dot(jnp.concatenate(weights, axis=1), jnp.concatenate(masked, axis=0)))
+        if pair == heads // per // 2 - 1:
+            between()
     inside = jnp.concatenate(tiles, axis=1)
     cum = info[:, CUM : CUM + 8]
     end = info[rows - 1 : rows]
@@ -608,7 +676,7 @@
     z = gate[...]
     gated = result * (z * sigmoid(z))
     d_normed = dot_nt(cot[...], out_proj[...])
-    d_normed_out[...] = d_normed
+    d_normed_out[...] = d_normed.astype(bf16)
     scaled = gated * gains[0:1]
     partial_out[...] = dot(scaled.astype(bf16), out_proj[...]).astype(bf16)
     squares = jnp.sum(gated * gated, axis=1, keepdims=True)
@@ -638,10 +706,10 @@
     y = ssm[...]
     gated = y * (z * s)
     gain = gains[0:1]
-    back = d_normed[...]
+    back = d_normed[...].astype(f32)
     unit = gated * inv
     d_gated = inv * (back * gain - unit * (inv * cross))
-    grad_out[...] += dot_tn((unit * gain).astype(bf16), cot[...])
+    grad_out[:, : cot.shape[1]] += dot_tn((unit * gain).astype(bf16), cot[...])
     d_ssm = d_gated * (z * s)
     d_ssm_out[...] = d_ssm
     d_gate_out[...] = (d_gated * y * (s * (1.0 + z * (1.0 - s)))).astype(bf16)
@@ -657,18 +725,17 @@
 def back_step(heads, head_dim, state_dim, first_step, last_step,
               d_ssm, conv_out, conv_in, heads_in, start, entering, conv_w, params, skip, conv_halo,
               d_conv_in_out, d_step_out, conv_grads, head_grads, halo_out,
-              lam, shift1, shift2, shift3, between):
+              lam, later, later_info, between):
     rows = d_ssm.shape[0]
     inner = heads * head_dim
     per = 128 // head_dim
-    shifts = (shift1, shift2, shift3)
 
     @pl.when(first_step)
     def _():
         lam[...] = entering[...]
         conv_grads[...] = jnp.zeros_like(conv_grads)
         head_grads[...] = jnp.zeros_like(head_grads)
-        for each in shifts:
+        for each in (later, later_info):
             each[rows:] = jnp.zeros((8, each.shape[1]), f32)
 
     values = conv_out[...]
@@ -695,22 +762,25 @@
     for pair in range(heads // per):
         tile = low[:, pair * 128 : (pair + 1) * 128]
         dy_tile = dy_low[:, pair * 128 : (pair + 1) * 128]
-        parts = [None] * len(cuts)
+        owns = [(lane >= k * head_dim) & (lane < (k + 1) * head_dim) for k in range(per)]
+        stacked = jnp.concatenate([jnp.where(own, tile, jnp.zeros_like(tile)) for own in owns], axis=0)
+        all_pairs = dot_nt(stacked, dy_tile)
+        weights = []
         for k in range(per):
             head = pair * per + k
-            own = (lane >= k * head_dim) & (lane < (k + 1) * head_dim)
-            masked = jnp.where(own, tile, jnp.zeros_like(tile))
-            dy_masked = jnp.where(own, dy_tile, jnp.zeros_like(dy_tile))
             row_total = jnp.zeros((1, rows), f32)
+            parts = []
             for n, (lo, hi) in enumerate(cuts):
                 gap = flipped[CUM + head : CUM + head + 1, lo:] - info[lo:hi, CUM + head : CUM + head + 1]
                 ok = (lax.broadcasted_iota(jnp.int32, (STRIP, rows - lo), 1)
                       >= lax.broadcasted_iota(jnp.int32, (STRIP, rows - lo), 0))
                 decay = jnp.exp(jnp.where(ok, gap, -1e30))
                 weight = decay * scores[lo:hi, lo:]
-                part = dot(weight.astype(bf16), dy_masked[lo:])
-                parts[n] = part if parts[n] is None else parts[n] + part
-                pairs = dot_nt(masked[lo:hi], dy_tile[lo:])
+                part = weight.astype(bf16)
+                if lo:
+                    part = jnp.concatenate([jnp.zeros((STRIP, lo), bf16), part], axis=1)
+                parts.append(part)
+                pairs = all_pairs[k * rows + lo : k * rows + hi, lo:]
                 d_scores[n] = d_scores[n] + pairs * decay
                 moved = pairs * weight
                 d_cols[n] = d_cols[n] - jnp.where(lane_one == head, jnp.sum(moved, axis=1, keepdims=True), 0.0)
@@ -718,9 +788,12 @@
                 if lo:
                     col = jnp.concatenate([jnp.zeros((1, lo), f32), col], axis=1)
                 row_total = row_total + col
+            weights.append(jnp.concatenate(parts, axis=0))
             d_rows.append(row_total)
-        tiles.append(jnp.concatenate(parts, axis=0))
-    between()
+        dy_stack = jnp.concatenate([jnp.where(own, dy_tile, jnp.zeros_like(dy_tile)) for own in owns], axis=0)
+        tiles.append(dot(jnp.concatenate(weights, axis=1), dy_stack))
+        if pair < BACK_POINTS - 1:
+            between(pair + 1)
     d_stepped = jnp.concatenate(tiles, axis=1)
     d_cum = jnp.concatenate(d_cols, axis=0)
     d_cum = d_cum + jnp.concatenate(d_rows + [jnp.zeros((128 - heads, rows), f32)], axis=0).T
@@ -742,17 +815,17 @@
     d_stepped = d_stepped + from_after
     grown_dy = grown * dy
     grown_low = grown_dy.astype(bf16)
-    to_cum = head_sum(grown_dy * dot(c_proj, start), group_ones)
-    left = head_sum(stepped * from_after, group_ones)
+    left = stepped * from_after
+    to_cum = head_sum(grown_dy * dot(c_proj, start) - left, group_ones)
     kept = jnp.sum(after * start.astype(f32), axis=0, keepdims=True) * end_grown
-    kept = head_sum(jnp.broadcast_to(kept, (8, inner)), group_ones)[0:1]
-    last = kept + jnp.sum(left, axis=0, keepdims=True)
+    kept = kept + jnp.sum(left, axis=0, keepdims=True)
+    last = head_sum(jnp.broadcast_to(kept, (8, inner)), group_ones)[0:1]
     row_id = lax.broadcasted_iota(jnp.int32, (rows, 128), 0)
-    d_cum = d_cum + to_cum - left + jnp.where(row_id == rows - 1, last, 0.0)
+    d_cum = d_cum + to_cum + jnp.where(row_id == rows - 1, last, 0.0)
     d_c = d_c + dot_nt(grown_low, start)
     d_b = d_b + dot_nt((fade * stepped).astype(bf16), after_low)
     lam[...] = end_grown * after + dot_tn(c_proj, grown_low)
-    d_step = head_sum(d_stepped * x, group_ones)
+    d_step = dot((d_stepped * x).astype(bf16), group_ones)
     d_x = step * d_stepped + skip[0:1] * dy
 
     order_r = lax.broadcasted_iota(jnp.int32, (rows, rows), 0)
@@ -773,10 +846,10 @@
     total = d_conv * conv_w[0:1]
     conv_grads[0:1] += jnp.sum(d_conv * taken, axis=0, keepdims=True)
     conv_grads[4:5] += jnp.sum(d_conv, axis=0, keepdims=True)
+    later[0:rows] = d_conv
+    later_info[0:rows] = info
     for j in range(1, 4):
-        ref = shifts[j - 1]
-        ref[0:rows] = d_conv * info[:, KEEP + j - 1 : KEEP + j]
-        moved = ref[pl.ds(j, rows)]
+        moved = later[pl.ds(j, rows)] * later_info[pl.ds(j, rows)][:, KEEP + j - 1 : KEEP + j]
         total = total + moved * conv_w[j : j + 1]
         conv_grads[j : j + 1] += jnp.sum(moved * taken, axis=0, keepdims=True)
     d_conv_in_out[...] = total.astype(bf16)
@@ -786,77 +859,93 @@
         ahead = conv_halo[...].astype(f32)
         halo_out[...] = jnp.zeros_like(halo_out)
         for j in range(1, 4):
-            first = shifts[j - 1][0:8]
+            first = later[0:8] * later_info[0:8, KEEP + j - 1 : KEEP + j]
             for t in range(j):
                 row = 16 + t - j
                 conv_grads[j : j + 1] += first[t : t + 1] * ahead[row : row + 1]
                 halo_out[row - 8 : row - 7] += first[t : t + 1] * conv_w[j : j + 1]
-    for each in shifts:
+    for each in (later, later_info):
         each[rows:] = each[0:8]
 
 
-def paced(times, pace, behind, most):
-    return [max(0, min(most, int((time - behind) / pace))) for time in times]
-
-
-def at_point(counts):
-    def count(point):
-        if isinstance(point, int):
-            return counts[point] if point >= 0 else 0
-        out = jnp.int32(0)
-        for k, value in enumerate(counts):
-            more = value - (counts[k - 1] if k else 0)
-            if more:
-                out = out + more * (point >= k).astype(jnp.int32)
-        return out
-    return count
-
-
-def layer_kernel(heads, head_dim, state_dim, all_channels, count, block, lag, plans,
-                 conv_out, conv_in, heads_in, gate, cot, out_proj, gains, entering, decay, conv_w,
-                 params, conv_halo,
-                 line_out, d_gate_out, d_conv_out, d_step_out, grad_out_out, gate_rows, conv_grads, head_grads,
-                 halo_out, sums_out,
-                 own, got, total, ssm, d_normed, starts, state, leaving, shift1, shift2, shift3, sums, sum_slots,
-                 grad_out, grad_low, grad_slots, grad_res, lead, fade,
-                 scan_got, scan_got_fade, scan_sent, scan_sent_fade, scan_sems, line_sems, sum_sems, grad_sems):
+def block_place(per, blocks):
+    def place(n, b):
+        if n == 0:
+            return b
+        late = b - (per - 1)
+        group = blocks // per - 2 - late // per
+        rest = jnp.where(b == blocks - 1, blocks - 1, group * per + lax.rem(late, per))
+        return jnp.where(b < per - 1, blocks - per + b, rest)
+    return place
+
+
+def layer_kernel(heads, head_dim, state_dim, all_channels, count, block, lag, plans, cuts, owners, taps,
+                 conv_out, conv_in, heads_in, gate, cot, normed, last_normed, out_proj, gains, entering, decay,
+                 conv_w, params, conv_halo, zx, weights, gain, tail_mask,
+                 mixed_out, d_normed_out, sums_out, zx_out, op_out, bc_out, small_out,
+                 own, got, total, held, ssm, d_normed, starts, state, leaving, later, later_info,
+                 sums, sum_slots, lead, fade,
+                 scan_got, scan_got_fade, scan_sent, scan_sent_fade, scan_sems,
+                 grad, sum_own, sum_pair, sum_mine, sum_slot, sum_theirs, sum_sems, grad_bc,
+                 bc_slots, bc_z, bc_res, small, small_slots, small_own, small_z,
+                 d_conv, d_step, gate_rows, conv_grads, head_grads, halo_rows, landed,
+                 line_sems, swap_sems, bc_sems, bcz_sems, small_sems, smallz_sems, row_sems, free_sem):
     at = pl.program_id(0)
-    rows = conv_out.shape[0]
-    seq = lax.axis_size("seq")
-    line = LineSum(own, got, total, line_out, line_sems, block)
-    swap = Swap("head", sums, sum_slots, sum_sems)
+    rows, width = cot.shape
+    inner = heads * head_dim
+    bc_width = 2 * state_dim
+    seq, head_count = lax.axis_size("seq"), lax.axis_size("head")
+    me, my_head = lax.axis_index("seq"), lax.axis_index("head")
+    per = rows // block
+    line = LineSum(own, got, total, (mixed_out, d_normed_out), block_place(per, count * per), line_sems, block)
+    swap = Swap("head", sums, sum_slots, swap_sems)
     scan = DeviceScan(True, state, fade, lead, leaving, scan_got, scan_got_fade, scan_sent, scan_sent_fade,
                       scan_sems)
-    grad_sum = PlaneSum(grad_low, grad_slots, grad_res, grad_sems, min(seq, grad_low.shape[0] // 16))
-    served, sent = at_point(plans[0]), at_point(plans[1])
-
-    def serve(point):
-        line.send(sent(point - 1), sent(point))
-        line.serve(served(point - 1), served(point), lag)
+    op_rows = max(16, inner // seq)
+    sum_refs = (sum_own, sum_pair, sum_mine, sum_slot, sum_theirs)
+    op_sum = PairedSum(*(ref.at[:, : op_rows * (2 if ref is sum_own else 1), :width] for ref in sum_refs),
+                       sum_sems.at[0])
+    zx_sum = PairedSum(*(ref.at[:, :, : 2 * inner] for ref in sum_refs), sum_sems.at[1])
+    small_swap = Swap("seq", small, small_slots, small_sems)
+    both_swap = Swap("head", small_own, small_z, smallz_sems)
+    row_copy = pltpu.make_async_remote_copy(
+        src_ref=halo_rows, dst_ref=landed, send_sem=row_sems.at[0], recv_sem=row_sems.at[1],
+        device_id={"seq": lax.rem(me + seq - 1, seq)}, device_id_type=MESH)
+    served, sent = plans
+    back_at = at - 2 * count - 1
+    last_step = back_at == count - 1
+
+    def serve(phase, k):
+        line.send(*sent.span(phase, k))
+        line.serve(*served.span(phase, k), lag)
 
     @pl.when(at == 0)
     def _():
         greet("head", "seq")
         state[...] = entering[...]
 
-    serve(2 * at)
-
     @pl.when(at < count)
     def _():
         mine = pl.ds(pl.multiple_of(at * rows, rows), rows)
+        serve(0, MIX_POINTS * at)
         mix_step(heads, head_dim, state_dim, at, conv_out, heads_in, gate, cot, out_proj, gains, entering,
-                 ssm.at[mine], d_normed.at[mine], own.at[mine], sums, starts, state)
+                 ssm.at[mine], d_normed.at[mine], own.at[mine], sums, starts, state,
+                 lambda: serve(0, MIX_POINTS * at + 1))
 
     @pl.when(at == count - 1)
     def _():
         swap.start()
+
+    @pl.when((at >= count) & (at < 2 * count))
+    def _():
+        serve(1, at - count)
 
     @pl.when(at == count)
     def _():
         swap.wait()
         sums_out[...] = swap.total()
         swap.finish()
-        grad_out[...] = jnp.zeros_like(grad_out)
+        grad[...] = jnp.zeros_like(grad)
         gate_rows[...] = jnp.zeros_like(gate_rows)
         state[...] = jnp.zeros_like(state)
 
@@ -866,317 +955,292 @@
         mine = pl.ds(pl.multiple_of(here * rows, rows), rows)
         gate_step(heads, head_dim, state_dim, all_channels, here,
                   ssm.at[mine], gate, d_normed.at[mine], sums_out, conv_out, heads_in, cot, gains,
-                  ssm.at[mine], d_gate_out, grad_out, gate_rows, state)
+                  ssm.at[mine], d_normed.at[mine], grad.at[:inner], gate_rows, state)
 
     @pl.when(at == 2 * count)
     def _():
-        grad_low[...] = grad_out[...].astype(bf16)
+        for k in range(seq // 2):
+            lo, hi = min(inner, k * 2 * op_rows), min(inner, (k + 1) * 2 * op_rows)
+            if hi > lo:
+                sum_own[k, : hi - lo, :width] = grad[lo:hi, :width].astype(bf16)
         scan.begin(decay[...])
-        scan.run()
-        grad_sum.scatter()
-
-    @pl.when(at >= 2 * count)
-    def _():
-        here = 3 * count - 1 - at
+        scan.run(lambda k: serve(2, k))
+        op_sum.swap()
+        grad[...] = jnp.zeros_like(grad)
+        grad_bc[...] = jnp.zeros_like(grad_bc)
+        small[...] = jnp.zeros_like(small)
+
+    def project(block_low, gate_low, conv_low, rest_low):
+        d_rows = dot_nt(conv_low, zx[:, inner:]) + dot(rest_low, weights[...])
+        grad[:, inner : 2 * inner] += dot_tn(block_low, conv_low)
+        if gate_low is not None:
+            d_rows = d_rows + dot_nt(gate_low, zx[:, :inner])
+            grad[:, :inner] += dot_tn(block_low, gate_low)
+        grad_bc[...] += dot_tn(rest_low, block_low).reshape(grad_bc.shape)
+        small[16:17] += jnp.sum(d_rows * block_low.astype(f32), axis=0, keepdims=True) / gain[...]
+        return d_rows
+
+    @pl.when(at > 2 * count)
+    def _():
+        here = 3 * count - at
         mine = pl.ds(pl.multiple_of(here * rows, rows), rows)
-        back_step(heads, head_dim, state_dim, at == 2 * count, at == 3 * count - 1,
+        serve(3, BACK_POINTS * back_at)
+        back_step(heads, head_dim, state_dim, back_at == 0, last_step,
                   ssm.at[mine], conv_out, conv_in, heads_in, starts[here], leaving, conv_w, params,
-                  gains[1:2], conv_halo, d_conv_out, d_step_out, conv_grads, head_grads, halo_out,
-                  state, shift1, shift2, shift3, lambda: serve(2 * at + 1))
-
-    @pl.when(at == 2 * count + count // 2)
-    def _():
-        grad_sum.reduce()
-
-    @pl.when(at == 3 * count - 1)
-    def _():
-        grad_sum.finish()
-        grad_out_out[...] = grad_res[...]
-        serve(6 * count)
+                  gains[1:2], conv_halo, d_conv, d_step, conv_grads, head_grads, halo_rows,
+                  state, later, later_info, lambda k: serve(3, BACK_POINTS * back_at + k))
+
+        @pl.when(last_step)
+        def _():
+            row_copy.start()
+        rest_low = jnp.concatenate([d_conv[:, inner:], d_step[...]], axis=1)
+        d_rows = project(normed[...], d_normed[mine], d_conv[:, :inner], rest_low).astype(bf16)
+
+        @pl.when(back_at == 0)
+        def _():
+            own[: rows - block] = d_rows[: rows - block]
+            held[...] = d_rows[rows - block :]
+
+        @pl.when(back_at > 0)
+        def _():
+            start = pl.multiple_of(back_at * rows - block, block)
+            own[pl.ds(start, rows)] = d_rows
+
+    @pl.when(back_at == 1)
+    def _():
+        op_sum.scatter()
+
+    @pl.when(back_at == 3)
+    def _():
+        op_sum.gather()
+
+    @pl.when(back_at == 5)
+    def _():
+        op_sum.back()
+
+    piece = grad_bc.shape[1] // owners
+
+    def bc_scatter(to, source):
+        return pltpu.make_async_remote_copy(
+            src_ref=grad_bc.at[:head_count, pl.ds(pl.multiple_of(to * piece, piece), piece)],
+            dst_ref=bc_slots.at[source], send_sem=bc_sems.at[0, to], recv_sem=bc_sems.at[1, source],
+            device_id={"seq": to}, device_id_type=MESH)
+
+    def bc_gather(owner, to):
+        rows = pl.ds(pl.multiple_of(owner * piece, piece), piece)
+        return pltpu.make_async_remote_copy(
+            src_ref=bc_res.at[rows], dst_ref=bc_res.at[rows],
+            send_sem=bc_sems.at[2, to], recv_sem=bc_sems.at[3, owner],
+            device_id={"seq": to}, device_id_type=MESH)
+
+    def bc_swap(to, source):
+        return pltpu.make_async_remote_copy(
+            src_ref=bc_slots.at[me, to], dst_ref=bc_z.at[source],
+            send_sem=bcz_sems.at[0, to], recv_sem=bcz_sems.at[1, source],
+            device_id={"head": to}, device_id_type=MESH)
+
+    @pl.when(last_step)
+    def _():
+        op_sum.finish(op_out)
+        op_sum.release(free_sem)
+        at_block = [served.count(3, plans[0].phases[3][0] - 1), sent.count(3, plans[0].phases[3][0] - 1)]
+
+        def go(until):
+            ahead = max(at_block[1], min(line.count, until + 2))
+            line.send(at_block[1], ahead)
+            line.serve(at_block[0], until, lag)
+            at_block[:] = [until, ahead]
+        go(cuts[0])
+        row_copy.wait()
+        extra = jnp.where(me < seq - 1, landed[...] * tail_mask[8:, 0:1], 0.0)
+        extra = jnp.concatenate([jnp.zeros_like(extra), extra], axis=0).astype(bf16)
+        extra_rest = jnp.concatenate([extra[:, inner:], jnp.zeros((16, 128), bf16)], axis=1)
+        more = project(last_normed[...], None, extra[:, :inner], extra_rest)
+        final = held[...].astype(f32) + jnp.concatenate([jnp.zeros((block - 16, width), f32), more], axis=0)
+        own[count * rows - block :] = final.astype(bf16)
+
+        pair_rows = sum_own.shape[1]
+        for k in range(sum_own.shape[0]):
+            sum_own[k, :, : 2 * inner] = grad[k * pair_rows : (k + 1) * pair_rows, : 2 * inner].astype(bf16)
+        pl.semaphore_wait(free_sem, 1)
+        zx_sum.swap()
+        small[0:8] += grad_bc[head_count, 0:8]
+        small[8 : 9 + taps, :inner] = conv_grads[: taps + 1, :inner]
+        small[8:10, inner : 2 * inner] = gate_rows[0:2]
+        small[10:12, inner : inner + 128] = head_grads[0:2]
+        small[17 : 18 + taps, :bc_width] = conv_grads[: taps + 1, inner:]
+        small_swap.start()
+
+        @pl.loop(1, seq)
+        def _(k):
+            to = other_of("seq", k)
+
+            @pl.when(to < owners)
+            def _():
+                bc_scatter(to, me).start()
+
+        go(cuts[1])
+        zx_sum.scatter()
+        go(cuts[2])
+        small_swap.wait()
+        sums_small = small_swap.total()
+        lone = small.shape[0] - small_own.shape[0]
+        small_out[:lone] = sums_small[:lone]
+        small_own[...] = sums_small[lone:]
+        both_swap.start()
+
+        @pl.when(me < owners)
+        def _():
+            @pl.loop(1, seq)
+            def _(k):
+                bc_scatter(me, other_of("seq", k)).wait_recv()
+            bc_slots[me] = grad_bc[:head_count, pl.ds(pl.multiple_of(me * piece, piece), piece)]
+            sums_bc = bc_slots[0]
+            for k in range(1, seq):
+                sums_bc = sums_bc + bc_slots[k]
+            bc_slots[me] = sums_bc
+            bc_z[my_head] = bc_slots[me, my_head]
+
+            @pl.loop(1, head_count)
+            def _(k):
+                bc_swap(other_of("head", k), my_head).start()
+
+        go(cuts[3])
+        zx_sum.gather()
+        both_swap.wait()
+        small_out[lone:] = both_swap.total()
+
+        @pl.when(me < owners)
+        def _():
+            @pl.loop(1, head_count)
+            def _(k):
+                bc_swap(my_head, other_of("head", k)).wait_recv()
+            sums_bc = bc_z[0]
+            for k in range(1, head_count):
+                sums_bc = sums_bc + bc_z[k]
+            bc_res[pl.ds(pl.multiple_of(me * piece, piece), piece)] = sums_bc
+
+            @pl.loop(1, seq)
+            def _(k):
+                bc_gather(me, other_of("seq", k)).start()
+
+        go(cuts[4])
+        zx_sum.back()
+        go(cuts[5])
+        zx_sum.finish(zx_out)
+        go(line.count + lag)
         line.finish()
-
-
-def layer(conv_out, conv_in, heads_in, gate, cot, out_proj, gains, entering, decay, conv_w, params,
-          conv_halo, heads, head_dim, state_dim, all_channels):
+        small_swap.finish()
+        both_swap.finish()
+
+        @pl.loop(1, seq)
+        def _(k):
+            other = other_of("seq", k)
+
+            @pl.when(other < owners)
+            def _():
+                bc_gather(other, me).wait_recv()
+                bc_scatter(other, me).wait_send()
+
+            @pl.when(me < owners)
+            def _():
+                bc_gather(me, other).wait_send()
+        bc_out[...] = bc_res[...]
+
+        @pl.when(me < owners)
+        def _():
+            @pl.loop(1, head_count)
+            def _(k):
+                bc_swap(other_of("head", k), my_head).wait_send()
+
+
+def layer(conv_out, conv_in, heads_in, gate, cot, normed, out_proj, gains, entering, decay, conv_w, params,
+          conv_halo, zx, weights, gain, tail_mask, heads, head_dim, state_dim, all_channels, taps):
     length, conv = conv_out.shape
     count = length // GROUP
     inner = heads * head_dim
     width = cot.shape[1]
     seq, head_count = lax.axis_size("seq"), lax.axis_size("head")
-    block = 64
+    block = BLOCK
+    pace = PACE * block // 64
     blocks = length // block
+    per = GROUP // block
     lag = max(2, head_count // 2)
-    steps = [MIX] * count + [GATE] * count + [BACK] * count
-    times, now = [], 0.0
-    for k, step in enumerate(steps):
-        now += SWAP if k == count else 0.0
-        half = SCAN + step / 2 if k == 2 * count else step / 2 if k > 2 * count else 0.0
-        times += [now, now + half]
-        now += step + (SCAN if k == 2 * count else 0.0)
-    made = [min(blocks, (k // 2) * (GROUP // block)) for k in range(6 * count)]
-    plans = (paced(times, PACE, LATE, blocks) + [blocks + lag],
-             [min(a, b) for a, b in zip(made, paced(times, PACE, EARLY, blocks))] + [blocks])
+    back_points = min(BACK_POINTS, inner // 128)
+    gate_at = MIX * count + SWAP
+    scan_at = gate_at + GATE * count
+    back_start = scan_at + SCAN
+    rounds = seq.bit_length() - 1
+    phases = [(MIX_POINTS * count, 0, MIX // MIX_POINTS), (count, gate_at, GATE),
+              (rounds, scan_at, SCAN // rounds), (back_points * count, back_start, BACK // back_points)]
+    served = Pace(phases, pace, LATE, 2 * blocks + lag)
+    sent = Pace(phases, pace, EARLY, 2 * blocks)
+    for k in range(count):
+        point = (k + 1) * back_points - 1
+        assert served.count(3, point) >= min(blocks, (k + 1) * per) + lag
+        assert sent.count(3, point) >= min(blocks, (k + 1) * per) + LineSum.AHEAD
+        for each in (served, sent):
+            assert each.count(3, point) <= blocks + max(0, k * per - 1)
+    cuts = [2 * blocks - (blocks * (32 - cut)) // 32 for cut in CUTS]
 
     def by(cols, first, step):
         def index(g):
-            ahead = jnp.where(g < count, g, jnp.where(g < 2 * count, g - count, 3 * count - 1 - g))
+            ahead = jnp.where(g < count, g, jnp.where(g < 2 * count, g - count, jnp.minimum(3 * count - g, count - 1)))
             if first == 2:
                 ahead = jnp.where(g < 2 * count, count - 1, ahead)
-            if first == 1:
-                ahead = jnp.where(g < count, 0, ahead)
             if step == 1:
                 ahead = jnp.where(g < 2 * count, ahead, count - 1)
             return (ahead, 0)
         return pl.BlockSpec((GROUP, cols), index)
     shape = jax.ShapeDtypeStruct
     state, fade = (state_dim, inner), (8, inner)
-    owners = min(seq, inner // 16)
+    bc_rows = (conv - inner) // head_count
+    owners = min(seq, bc_rows // 8)
+    piece = bc_rows // owners
+    vm = pltpu.VMEM
+    grad_rows = max(width, inner)
+    paired = PairedSum.scratch(width, max(width, 2 * inner))
     return pl.pallas_call(
-        functools.partial(layer_kernel, heads, head_dim, state_dim, all_channels, count, block, lag, plans),
-        grid=(3 * count,),
-        out_shape=(shape((length, width), bf16), shape((length, inner), bf16), shape((length, conv), bf16),
-                   shape((length, 128), bf16), shape((inner, width), bf16), shape((8, inner), f32),
-                   shape((8, conv), f32), shape((8, 128), f32), shape((8, conv), f32),
-                   shape((2, count, GROUP), f32)),
-        in_specs=[by(conv, 0, 2), by(conv, 2, 2), by(128, 0, 2), by(inner, 0, 1), by(width, 0, 1)]
-        + [VMEM] * 7,
-        out_specs=(HBM, by(inner, 1, 1), by(conv, 2, 2), by(128, 2, 2)) + (VMEM,) * 6,
-        scratch_shapes=[pltpu.VMEM((length, width), bf16)] * 3 + [pltpu.VMEM((length, inner), f32)] * 2 + [
-            pltpu.VMEM((count,) + state, bf16), pltpu.VMEM(state, f32), pltpu.VMEM(state, f32)]
-        + [pltpu.VMEM((GROUP + 8, conv), f32)] * 3 + [
-            pltpu.VMEM((2, count, GROUP), f32), pltpu.VMEM((head_count, 2, count, GROUP), f32),
-            pltpu.VMEM((inner, width), f32), pltpu.VMEM((inner, width), bf16),
-            pltpu.VMEM((seq, inner // owners, width), bf16), pltpu.VMEM((inner, width), bf16)]
-        + DeviceScan.scratch(state, fade) + [LineSum.sems(length, block), DMA((2, head_count)), DMA((4, seq))],
+        functools.partial(layer_kernel, heads, head_dim, state_dim, all_channels, count, block, lag,
+                          (served, sent), cuts, owners, taps),
+        grid=(3 * count + 1,),
+        out_shape=(shape((length, width), bf16), shape((length, width), bf16), shape((2, count, GROUP), f32),
+                   shape((width, 2 * inner), bf16), shape((inner, width), bf16), shape((bc_rows, width), f32),
+                   shape((24, width), f32)),
+        in_specs=[by(conv, 0, 2), by(conv, 2, 2), by(128, 0, 2), by(inner, 0, 1), by(width, 0, 1),
+                  by(width, 2, 2), pl.BlockSpec((16, width), lambda g: (length // 16 - 1, 0))] + [VMEM] * 11,
+        out_specs=(HBM, HBM) + (VMEM,) * 5,
+        scratch_shapes=[
+            vm((length, width), bf16), vm((length, width), bf16), vm((2 * length, width), bf16),
+            vm((block, width), bf16), vm((length, inner), f32), vm((length, inner), bf16),
+            vm((count,) + state, bf16), vm(state, f32), vm(state, f32)]
+        + [vm((GROUP + 8, conv), f32), vm((GROUP + 8, 128), f32)]
+        + [vm((2, count, GROUP), f32), vm((head_count, 2, count, GROUP), f32)]
+        + DeviceScan.scratch(state, fade)
+        + [vm((grad_rows, max(width, 2 * inner)), f32)] + paired[:-1] + [DMA((2,) + (6, seq // 2))]
+        + [vm(((conv - inner + 128) // bc_rows, bc_rows, width), f32),
+           vm((seq, head_count, piece, width), f32), vm((head_count, piece, width), f32),
+           vm((bc_rows, width), f32), vm((24, width), f32), vm((seq, 24, width), f32),
+           vm((8, width), f32), vm((head_count, 8, width), f32),
+           vm((GROUP, conv), bf16), vm((GROUP, 128), bf16), vm((8, inner), f32), vm((8, conv), f32),
+           vm((8, 128), f32), vm((8, conv), f32), vm((8, conv), f32),
+           LineSum.sems(length, block), DMA((2, head_count)), DMA((4, seq)), DMA((2, head_count)),
+           DMA((2, seq)), DMA((2, head_count)), DMA((2,)), pltpu.SemaphoreType.REGULAR],
         compiler_params=pltpu.CompilerParams(
             dimension_semantics=("arbitrary",), collective_id=4, has_side_effects=True,
-            vmem_limit_bytes=LIMIT),
+            vmem_limit_bytes=LAYER_LIMIT),
         name="layer",
-    )(conv_out, conv_in, heads_in, gate, cot, out_proj, gains, entering, decay, conv_w, params, conv_halo)
-
-
-PACE = 2.9
-MIX, SWAP, GATE, SCAN, BACK = 2.7, 3.0, 2.0, 10.0, 6.6
-EARLY, LATE = -2.0, 5.0
-PROJECT, CUTS = 2.6, (17, 21)
-
-
-def tail_kernel(count, block, lag, plans, cuts, owners, last_rows, taps,
-                normed, d_gate, d_conv, d_step, zx, weights, gain, back_rows, tail_mask, gate_rows, conv_grads,
-                head_grads, line_out, zx_out, bc_out, small_out,
-                own, got, total, grad_zx, grad_low, zx_slots, zx_res, grad_bc, bc_part, bc_slots, bc_z, bc_res, small, small_slots,
-                small_own, small_z, landed,
-                line_sems, zx_sems, bc_sems, bcz_sems, small_sems, smallz_sems, row_sems):
-    at = pl.program_id(0)
-    rows, width = normed.shape
-    inner = d_gate.shape[1]
-    seq, heads = lax.axis_size("seq"), lax.axis_size("head")
-    me, my_head = lax.axis_index("seq"), lax.axis_index("head")
-    bc_width = bc_part.shape[0] * bc_part.shape[1]
-    line = LineSum(own, got, total, line_out, line_sems, block)
-    zx_sum = PlaneSum(grad_low, zx_slots, zx_res, zx_sems, owners[0])
-    small_swap = Swap("seq", small, small_slots, small_sems)
-    both_swap = Swap("head", small_own, small_z, smallz_sems)
-    row_copy = pltpu.make_async_remote_copy(
-        src_ref=back_rows, dst_ref=landed, send_sem=row_sems.at[0], recv_sem=row_sems.at[1],
-        device_id={"seq": lax.rem(me + seq - 1, seq)}, device_id_type=MESH)
-    served, sent = at_point(plans[0]), at_point(plans[1])
-
-    @pl.when(at == 0)
-    def _():
-        greet("head", "seq")
-        row_copy.start()
-        grad_zx[...] = jnp.zeros_like(grad_zx)
-        grad_bc[...] = jnp.zeros_like(grad_bc)
-        small[...] = jnp.zeros_like(small)
-        small[8 : 9 + taps, :inner] = conv_grads[: taps + 1, :inner]
-        small[8:10, inner : 2 * inner] = gate_rows[0:2]
-        small[10:12, inner : inner + 128] = head_grads[0:2]
-        small[17 : 18 + taps, :bc_width] = conv_grads[: taps + 1, inner:]
-
-    line.send(sent(at - 1), sent(at))
-    line.serve(served(at - 1), served(at), lag)
-
-    block_low = normed[...]
-    gate_low, conv_low, step_low = d_gate[...], d_conv[...], d_step[...]
-    rest_low = jnp.concatenate([conv_low[:, inner:], step_low], axis=1)
-    d_normed = (dot_nt(gate_low, zx[:, :inner]) + dot_nt(conv_low[:, :inner], zx[:, inner:])
-                + dot(rest_low, weights[...]))
-    grad_zx[:, :inner] += dot_tn(block_low, gate_low)
-    grad_zx[:, inner:] += dot_tn(block_low, conv_low[:, :inner])
-    grad_bc[...] += dot_tn(rest_low, block_low)
-    small[16:17] += jnp.sum(d_normed * block_low.astype(f32), axis=0, keepdims=True) / gain[...]
-    mine = pl.ds(pl.multiple_of(at * rows, rows), rows)
-    own[mine] = d_normed.astype(bf16)
-
-    @pl.when(at == count - 1)
-    def _():
-        row_copy.wait()
-        extra = jnp.where(me < seq - 1, landed[...] * tail_mask[8:, 0:1], 0.0)
-        extra = jnp.concatenate([jnp.zeros_like(extra), extra], axis=0).astype(bf16)
-        tail_low = normed[rows - 16 :]
-        more = dot_nt(extra[:, :inner], zx[:, inner:]) + dot(extra[:, inner:], weights[:bc_width])
-        grad_zx[:, inner:] += dot_tn(tail_low, extra[:, :inner])
-        grad_bc[:bc_width] += dot_tn(extra[:, inner:], tail_low)
-        small[16:17] += jnp.sum(more * tail_low.astype(f32), axis=0, keepdims=True) / gain[...]
-        own[last_rows:] = (own[last_rows:].astype(f32) + more).astype(bf16)
-
-    piece = bc_part.shape[1] // owners[1]
-
-    def bc_scatter(to, source):
-        return pltpu.make_async_remote_copy(
-            src_ref=bc_part.at[:, pl.ds(pl.multiple_of(to * piece, piece), piece)],
-            dst_ref=bc_slots.at[source], send_sem=bc_sems.at[0, to], recv_sem=bc_sems.at[1, source],
-            device_id={"seq": to}, device_id_type=MESH)
-
-    def bc_gather(owner, to):
-        rows = pl.ds(pl.multiple_of(owner * piece, piece), piece)
-        return pltpu.make_async_remote_copy(
-            src_ref=bc_res.at[rows], dst_ref=bc_res.at[rows],
-            send_sem=bc_sems.at[2, to], recv_sem=bc_sems.at[3, owner],
-            device_id={"seq": to}, device_id_type=MESH)
-
-    def bc_swap(to, source):
-        return pltpu.make_async_remote_copy(
-            src_ref=bc_slots.at[me, to], dst_ref=bc_z.at[source],
-            send_sem=bcz_sems.at[0, to], recv_sem=bcz_sems.at[1, source],
-            device_id={"head": to}, device_id_type=MESH)
-
-    @pl.when(at == count - 1)
-    def _():
-        grad_low[...] = grad_zx[...].astype(bf16)
-        zx_sum.scatter()
-        small[0:8] += grad_bc[bc_width : bc_width + 8]
-        small_swap.start()
-        for k in range(heads):
-            bc_part[k] = grad_bc[k * bc_part.shape[1] : (k + 1) * bc_part.shape[1]]
-
-        @pl.loop(1, seq)
-        def _(k):
-            to = other_of("seq", k)
-
-            @pl.when(to < owners[1])
-            def _():
-                bc_scatter(to, me).start()
-
-        last = count - 1
-
-        def go(first, until, sent_first, sent_until):
-            line.send(sent_first, sent_until)
-            line.serve(first, until, lag)
-        go(served(last), cuts[0], sent(last), cuts[0] + 2)
-        zx_sum.reduce()
-        small_swap.wait()
-        sums = small_swap.total()
-        lone = small.shape[0] - small_own.shape[0]
-        small_out[:lone] = sums[:lone]
-        small_own[...] = sums[lone:]
-        both_swap.start()
-
-        @pl.when(me < owners[1])
-        def _():
-            @pl.loop(1, seq)
-            def _(k):
-                bc_scatter(me, other_of("seq", k)).wait_recv()
-            bc_slots[me] = bc_part[:, pl.ds(pl.multiple_of(me * piece, piece), piece)]
-            sums = bc_slots[0]
-            for k in range(1, seq):
-                sums = sums + bc_slots[k]
-            bc_slots[me] = sums
-            bc_z[my_head] = bc_slots[me, my_head]
-
-            @pl.loop(1, heads)
-            def _(k):
-                bc_swap(other_of("head", k), my_head).start()
-
-        go(cuts[0], cuts[1], cuts[0] + 2, cuts[1] + 2)
-        both_swap.wait()
-        small_out[lone:] = both_swap.total()
-
-        @pl.when(me < owners[1])
-        def _():
-            @pl.loop(1, heads)
-            def _(k):
-                bc_swap(my_head, other_of("head", k)).wait_recv()
-            sums = bc_z[0]
-            for k in range(1, heads):
-                sums = sums + bc_z[k]
-            bc_res[pl.ds(pl.multiple_of(me * piece, piece), piece)] = sums
-
-            @pl.loop(1, seq)
-            def _(k):
-                bc_gather(me, other_of("seq", k)).start()
-
-        go(cuts[1], line.count + lag, cuts[1] + 2, line.count)
-        line.finish()
-        zx_sum.finish()
-        zx_out[...] = zx_res[...]
-        small_swap.finish()
-        both_swap.finish()
-
-        @pl.loop(1, seq)
-        def _(k):
-            other = other_of("seq", k)
-
-            @pl.when(other < owners[1])
-            def _():
-                bc_gather(other, me).wait_recv()
-                bc_scatter(other, me).wait_send()
-
-            @pl.when(me < owners[1])
-            def _():
-                bc_gather(me, other).wait_send()
-        bc_out[...] = bc_res[...]
-
-        @pl.when(me < owners[1])
-        def _():
-            @pl.loop(1, heads)
-            def _(k):
-                bc_swap(other_of("head", k), my_head).wait_send()
-
-
-def tail(normed, d_gate, d_conv, d_step, zx, weights, gain, back_rows, tail_mask, gate_rows, conv_grads,
-         head_grads, taps):
-    length, width = normed.shape
-    inner, conv = d_gate.shape[1], d_conv.shape[1]
-    count = length // GROUP
-    seq, heads = lax.axis_size("seq"), lax.axis_size("head")
-    bc_rows = (conv - inner) // heads
-    owners = (min(seq, width // 16), min(seq, bc_rows // 8))
-    piece = bc_rows // owners[1]
-    block = 64
-    blocks = length // block
-    lag = max(2, heads // 2)
-    made = [k * (GROUP // block) for k in range(count)]
-    times = [PROJECT * k for k in range(count)]
-    plans = (paced(times, PACE, LATE, blocks), [min(a, b) for a, b in zip(made, paced(times, PACE, EARLY, blocks))])
-    cuts = ((blocks * CUTS[0]) // 32, (blocks * CUTS[1]) // 32)
-
-    def by(cols):
-        return pl.BlockSpec((GROUP, cols), lambda g: (g, 0))
-    shape = jax.ShapeDtypeStruct
-    return pl.pallas_call(
-        functools.partial(tail_kernel, count, block, lag, plans, cuts, owners, length - 16, taps),
-        grid=(count,),
-        out_shape=(shape((length, width), bf16), shape((width, 2 * inner), bf16), shape((bc_rows, width), f32),
-                   shape((24, width), f32)),
-        in_specs=[by(width), by(inner), by(conv), by(128)] + [VMEM] * 8,
-        out_specs=(HBM, VMEM, VMEM, VMEM),
-        scratch_shapes=[pltpu.VMEM((length, width), bf16)] * 3 + [
-            pltpu.VMEM((width, 2 * inner), f32), pltpu.VMEM((width, 2 * inner), bf16),
-            pltpu.VMEM((seq, width // owners[0], 2 * inner), bf16), pltpu.VMEM((width, 2 * inner), bf16),
-            pltpu.VMEM((conv - inner + 128, width), f32), pltpu.VMEM((heads, bc_rows, width), f32),
-            pltpu.VMEM((seq, heads, piece, width), f32), pltpu.VMEM((heads, piece, width), f32),
-            pltpu.VMEM((bc_rows, width), f32), pltpu.VMEM((24, width), f32), pltpu.VMEM((seq, 24, width), f32),
-            pltpu.VMEM((8, width), f32), pltpu.VMEM((heads, 8, width), f32),
-            pltpu.VMEM(back_rows.shape, f32),
-            LineSum.sems(length, block), DMA((4, seq)), DMA((4, seq)), DMA((2, heads)), DMA((2, seq)),
-            DMA((2, heads)), DMA((2,))],
-        compiler_params=pltpu.CompilerParams(
-            dimension_semantics=("arbitrary",), collective_id=5, has_side_effects=True,
-            vmem_limit_bytes=LIMIT),
-        name="tail",
-    )(normed, d_gate, d_conv, d_step, zx, weights, gain, back_rows, tail_mask, gate_rows, conv_grads, head_grads)
+    )(conv_out, conv_in, heads_in, gate, cot, normed, normed, out_proj, gains, entering, decay, conv_w, params,
+      conv_halo, zx, weights, gain, tail_mask)
+
+
+PACE = 29
+MIX, SWAP, GATE, SCAN, BACK = 27, 30, 20, 100, 82
+MIX_POINTS, BACK_POINTS = 2, 4
+EARLY, LATE = 25, 60
+BLOCK = 64
+CUTS = (8, 13, 18, 23, 28, 31)
+LAYER_LIMIT = 63 * 2**20
 
 
 def finish_kernel(heads, head_dim, all_channels, taps,
@@ -1199,13 +1263,10 @@
     zx_out[:, 0, :] = sums_zx[:, :inner]
     zx_out[:, 1, :] = sums_zx[:, inner:]
     op_out[...] = op[...].astype(f32)
-    cols = bc.shape[1]
-    mine = pl.ds(pl.multiple_of(at * cols, cols), cols)
-    bc_out[...] = bc[...].T
-    dt_out[...] = small[0:8, mine].T[:, :heads]
-
     @pl.when(at == 0)
     def _():
+        bc_out[...] = bc[...]
+        dt_out[...] = small[0:heads]
         gain_out[...] = small[16:17]
         conv_w_out[...] = small[8 : 8 + taps, :inner]
         conv_b_out[...] = small[8 + taps : 9 + taps, :inner]
@@ -1243,12 +1304,12 @@
         functools.partial(finish_kernel, heads, head_dim, inner * lax.axis_size("head"), taps),
         grid=(count,),
         out_shape=(shape((length, width), bf16), shape((length, width), f32), shape((width, 2, inner), f32),
-                   shape((inner, width), f32), shape((width, part), f32), shape((width, heads), f32))
+                   shape((inner, width), f32), shape((part, width), f32), shape((heads, width), f32))
         + tuple(shape(each, f32) for each in lone),
         in_specs=[tall] * 4 + [VMEM, VMEM, by(cols, 2 * inner), by(inner // count, width),
-                               pl.BlockSpec((part, cols), lambda g: (0, g)), VMEM],
+                               VMEM, VMEM],
         out_specs=(tall, tall, pl.BlockSpec((cols, 2, inner), lambda g: (g, 0, 0)), by(inner // count, width),
-                   by(cols, part), by(cols, heads)) + (VMEM,) * len(lone),
+                   VMEM, VMEM) + (VMEM,) * len(lone),
         compiler_params=pltpu.CompilerParams(dimension_semantics=("arbitrary",), vmem_limit_bytes=LIMIT),
         name="finish",
     )(tokens, cot, mixed, d_normed, sums, gain, zx, op, bc, small)
@@ -1275,17 +1336,14 @@
         conv_x_bias[None], conv_bc_weight, conv_bc_bias[None], dt_bias[None], a_log[None], skip_scale[None],
         norm_gain[None], heads, head_dim, state_dim)
     all_channels = inner * head_count
-    mixed, d_gate, d_conv, d_step, op_sum, gate_rows, conv_grads, head_grads, back_rows, sums = layer(
-        conv_out, conv_in, info, gate, cotangent, out_proj, gains, entering, decay, conv_w, params,
-        conv_halo, heads, head_dim, state_dim, all_channels)
-    d_normed, zx_sum, bc_sum, small_sum = tail(
-        normed, d_gate, d_conv, d_step, zx, weights, gain, back_rows, tail_mask, gate_rows, conv_grads,
-        head_grads, taps)
+    mixed, d_normed, sums, zx_sum, op_sum, bc_sum, small_sum = layer(
+        conv_out, conv_in, info, gate, cotangent, normed, out_proj, gains, entering, decay, conv_w, params,
+        conv_halo, zx, weights, gain, tail_mask, heads, head_dim, state_dim, all_channels, taps)
     (mixed_out, grad_tokens, grad_zx, grad_op, grad_bc, grad_dt, grad_gain, grad_conv_w, grad_conv_b,
      grad_bc_w, grad_bc_b, grad_bias, grad_rate, grad_skip, grad_norm) = finish(
         tokens, cotangent, mixed, d_normed, sums, gain, zx_sum, op_sum, bc_sum, small_sum, heads, head_dim, taps)
     return (
-        mixed_out, grad_tokens, grad_gain[0], grad_zx, grad_bc, grad_dt, grad_conv_w, grad_conv_b[0],
+        mixed_out, grad_tokens, grad_gain[0], grad_zx, grad_bc.T, grad_dt.T, grad_conv_w, grad_conv_b[0],
         grad_bc_w, grad_bc_b[0], grad_bias[0], grad_rate[0], grad_skip[0], grad_norm[0], grad_op,
     )
 

time: 331 us -> 302 us (0.912); the launches traced: 326 us -> 301 us
  Pallas kernels: 318 us -> 297 us
  local copies, waits for them, and re-layouts: 7.23 us -> 3.48 us
    pallas_call x1 -> x0, Pallas kernels: 120 us -> none  [tail(): pl.pallas_call(functools.partial(tail_kernel, count, block, lag, plans, c...]
    pallas_call x1, Pallas kernels: 131 us -> 231 us  [layer(): pl.pallas_call(functools.partial(layer_kernel, heads, head_dim, state_dim...]
    unnamed x3 -> x1, local copies, waits for them, and re-layouts: 7.23 us -> 3.48 us
where the time goes in v5:
time: 302 us; the launch traced here: 301 us
  Pallas kernels  297 us (98%)
  local copies, waits for them, and re-layouts  3.48 us (1%)
    pallas_call x1, Pallas kernels, layer(): pl.pallas_call(functools.partial(layer_kernel, heads, head_dim, state_dim...  231 us
    pallas_call x1, Pallas kernels, front(): pl.pallas_call(functools.partial(front_kernel, heads, head_dim, state_dim...  47.9 us
    pallas_call x1, Pallas kernels, finish(): pl.pallas_call(functools.partial(finish_kernel, heads, head_dim, inner *...  17.8 us

profile of v5, /device:TPU:0, one launch (start us, length us, event | category | flops | bytes accessed | tf_op | source)
XLA Modules:
  0.0 301.2 jit_solution(3825166344992621436)
XLA Ops:
  0.6 3.5 %copy.31 = bf16[128,8,2,512]{3,1,2,0:T(8,128)(2,1)} copy(bf16[128,8,2,512]{3,2,1,0:T(2,128)(2,1)} %bitcast.23) | data formatting | bytes 4194304
  4.1 47.9 %front.1 = (bf16[2048,1024]{1,0:T(8,128)(2,1)}, f32[2048,512]{1,0:T(8,128)}, bf16[2048,768]{1,0:T(8,128)(2,1)}, f32[2048,768]{1,0:T(8,128)}, f32[2048,128]{1,0:T...) custom-call(bf16[2048,1024]{1,0:T(8,128)(2,1)} %tokens.3, ...), custom_call_target="tpu_custom_call" | custom-call | tf_op jit(solution)/shard_map/front/pallas_call | solution.py:594
  52.0 231.2 %layer.1 = (bf16[2048,1024]{1,0:T(8,128)(2,1)}, bf16[2048,1024]{1,0:T(8,128)(2,1)}, f32[2,8,256]{2,1,0:T(8,128)}, bf16[1024,1024]{1,0:T(8,128)(2,1)}, bf16[512,1...) custom-call(f32[2048,768]{1,0:T(8,128)} %get-tuple-element.50.conv_out, ...), custom_call_target="tpu_custom_call" | custom-call | tf_op jit(solution)/shard_map/layer/pallas_call | solution.py:1203
  283.2 17.8 %finish.1 = (bf16[2048,1024]{1,0:T(8,128)(2,1)}, f32[2048,1024]{1,0:T(8,128)}, f32[1024,2,512]{2,1,0:T(2,128)}, f32[512,1024]{1,0:T(8,128)}, f32[64,1024]{1,0:T(...) custom-call(bf16[2048,1024]{1,0:T(8,128)(2,1)} %tokens.3, ...), custom_call_target="tpu_custom_call" | custom-call | tf_op jit(solution)/shard_map/finish/pallas_call | solution.py:1303

commit v6 on v5

--- a/solution.py
+++ b/solution.py
@@ -112,7 +112,7 @@
     def inward(self, b):
         rows = self.slot(b)
         self.in_copy(b, self.outer).wait_recv()
-        self.own[rows] = (self.got[rows].astype(f32) + self.own[rows].astype(f32)).astype(bf16)
+        self.own[rows] = self.got[rows] + self.own[rows]
 
         @pl.when(self.mid)
         def _():
@@ -132,7 +132,7 @@
 
         @pl.when(self.mid)
         def _():
-            self.total[rows] = (self.own[self.slot(b)].astype(f32) + self.total[rows].astype(f32)).astype(bf16)
+            self.total[rows] = self.own[self.slot(b)] + self.total[rows]
 
         @pl.when(self.has_outer)
         def _():
@@ -448,10 +448,10 @@
 def front_kernel(heads, head_dim, state_dim, count,
                  tokens, last_tokens, zx, flags, gain, proj_bc, proj_dt, conv_x_weight, conv_x_bias,
                  conv_bc_weight, conv_bc_bias, dt_bias, a_log, skip, norm_gain,
-                 normed_out, gate_out, conv_in_out, conv_out_out, heads_out, entering, decay_out,
+                 normed_out, x_in_out, x_conv_out, bc_in_out, bc_conv_out, heads_out, entering, decay_out,
                  halo_out, weights_out, conv_w_out, params, gains_out, mask_out,
-                 normed, taken, tail_rows, landed, proj_all, conv_bc, conv_all, flag_cols, flag_ext,
-                 carry, ext, state, running, lead, fade,
+                 normed, x_active, tail_rows, landed, head_low, proj_all, conv_bc, conv_all, flag_cols, flag_ext,
+                 x_ext, bc_ext, state, running, lead, fade,
                  scan_got, scan_got_fade, scan_sent, scan_sent_fade, scan_sems, proj_sems, conv_sems, row_sems):
     at = pl.program_id(0)
     rows = tokens.shape[0]
@@ -490,21 +490,50 @@
         gains_out[1:2] = spread(head_lanes(skip[...], heads, lane_row), 0, heads, head_dim)
         flat = flags[...].astype(f32)
         turned = jnp.concatenate([flat, jnp.zeros((128 - flat.shape[0], 128), f32)], axis=0).T
+        conv_w_out[...] = jnp.zeros_like(conv_w_out)
+        conv_w_out[0:4, :inner] = conv_x_weight[...].astype(f32)
+        conv_w_out[4:5, :inner] = conv_x_bias[...]
         for k in range(flat.shape[0]):
             flag_cols[k * 128 : (k + 1) * 128] = jnp.broadcast_to(turned[:, k : k + 1], (128, 128))
+        flag_ext[0:8] = jnp.zeros((8, 128), f32)
+
+    def keeps(flag):
+        flag_ext[8:] = flag
+        one = 1.0 - flag
+        two = one * (1.0 - flag_ext[7 : 7 + rows])
+        three = two * (1.0 - flag_ext[6 : 6 + rows])
+        flag_ext[0:8] = flag_ext[rows:]
+        return one, two, three
+
+    def convolve(ext, current, keep, first, last):
+        ext[8:] = current
+        total = conv_w_out[4:5, first:last] + conv_w_out[0:1, first:last] * current
+        for j in range(1, 4):
+            total = total + conv_w_out[j : j + 1, first:last] * ext[pl.ds(8 - j, rows)] * keep[j - 1][:, 0:1]
+        ext[0:8] = ext[rows:]
+        return total
 
     @pl.when(at < count)
     def _():
         low = norm_rows(tokens[...], gain[...])
         normed[mine] = low
         normed_out[...] = low
-        raw = dot(low, zx[...])
-        gate_out[...] = raw[:, :inner]
-        taken[mine] = raw[:, inner:].astype(bf16)
+        x_in = dot(low, zx[:, inner:]).astype(bf16)
+        x_in_out[...] = x_in
+
+        @pl.when(at == 0)
+        def _():
+            row_copy.wait()
+            head_low[...] = norm_rows(landed[...], gain[...])
+            ahead = jnp.where(me > 0, dot(head_low[...], zx[:, inner:]), 0.0).astype(bf16)
+            halo_out[:, :inner] = ahead
+            x_ext[0:8] = ahead[8:].astype(f32)
+        total = convolve(x_ext, x_in.astype(f32), keeps(flag_cols[mine]), 0, inner)
+        x_conv_out[...] = total
+        x_active[mine] = total * sigmoid(total)
 
     @pl.when(at == count)
     def _():
-        row_copy.wait()
         for each in swaps:
             each.wait()
             each.finish()
@@ -514,15 +543,10 @@
         eight = jnp.concatenate([proj_dt[...].astype(f32)] + (
             [jnp.zeros((8 - heads, proj_dt.shape[1]), f32)] if heads < 8 else []), axis=0)
         weights_out[bc_width:] = jnp.concatenate([eight] * 16, axis=0).astype(bf16)
-        conv_w_out[...] = jnp.zeros_like(conv_w_out)
-        conv_w_out[0:4, :inner] = conv_x_weight[...].astype(f32)
-        conv_w_out[4:5, :inner] = conv_x_bias[...]
         conv_w_out[:, inner:] = jnp.concatenate([conv_all[k, :, :bc_part] for k in range(heads_there)], axis=1)
-        head_rows = norm_rows(landed[...], gain[...])
-        ahead = jnp.concatenate([dot(head_rows, zx[:, inner:]), dot_nt(head_rows, weights_out[:bc_width])], axis=1)
-        ahead = jnp.where(me > 0, ahead, 0.0).astype(bf16)
-        halo_out[...] = ahead
-        carry[...] = ahead[8:].astype(f32)
+        ahead = jnp.where(me > 0, dot_nt(head_low[...], weights_out[:bc_width]), 0.0).astype(bf16)
+        halo_out[:, inner:] = ahead
+        bc_ext[0:8] = ahead[8:].astype(f32)
         state[...] = jnp.zeros_like(state)
         running[...] = jnp.zeros_like(running)
         flag_ext[0:8] = jnp.zeros((8, 128), f32)
@@ -530,24 +554,13 @@
     @pl.when(at >= count)
     def _():
         raw = dot_nt(normed[mine], weights_out[...])
-        conv_in = jnp.concatenate([taken[mine], raw[:, :bc_width].astype(bf16)], axis=1)
-        conv_in_out[...] = conv_in
-        current = conv_in.astype(f32)
-        ext[0:8] = carry[...]
-        ext[8:] = current
-        carry[...] = ext[rows:]
+        bc_in = raw[:, :bc_width].astype(bf16)
+        bc_in_out[...] = bc_in
         flag = flag_cols[mine]
-        flag_ext[8:] = flag
-        keep1 = 1.0 - flag
-        keep2 = keep1 * (1.0 - flag_ext[7 : 7 + rows])
-        keep3 = keep2 * (1.0 - flag_ext[6 : 6 + rows])
-        flag_ext[0:8] = flag_ext[rows:]
-        keep = (None, keep1, keep2, keep3)
-        total = conv_w_out[4:5] + conv_w_out[0:1] * current
-        for j in range(1, 4):
-            total = total + conv_w_out[j : j + 1] * ext[pl.ds(8 - j, rows)] * keep[j][:, 0:1]
-        conv_out_out[...] = total
-        active = total * sigmoid(total)
+        keep = keeps(flag)
+        total = convolve(bc_ext, bc_in.astype(f32), keep, inner, inner + bc_width)
+        bc_conv_out[...] = total
+        b_proj = (total[:, :state_dim] * sigmoid(total[:, :state_dim])).astype(bf16)
 
         step_raw = raw[:, bc_width:]
         step = softplus(step_raw + params[0:1])
@@ -556,13 +569,12 @@
         order_c = lax.broadcasted_iota(jnp.int32, (rows, rows), 1)
         cum = exact_left((order_r >= order_c).astype(bf16), log_decay)
         lane = lax.broadcasted_iota(jnp.int32, (rows, 128), 1)
-        keeps = jnp.where(lane < KEEP + 1, keep1, jnp.where(lane < KEEP + 2, keep2, keep3))
-        heads_out[...] = lane_groups(rows, step_raw, step, cum, cum + running[0:1], keeps)
+        kept = jnp.where(lane < KEEP + 1, keep[0], jnp.where(lane < KEEP + 2, keep[1], keep[2]))
+        heads_out[...] = lane_groups(rows, step_raw, step, cum, cum + running[0:1], kept)
         end = cum[rows - 1 : rows]
         running[...] = running[...] + end
         weight = step * jnp.exp(end - cum)
-        scaled = (active[:, :inner] * spread(weight, 0, heads, head_dim)).astype(bf16)
-        b_proj = active[:, inner : inner + state_dim].astype(bf16)
+        scaled = (x_active[mine] * spread(weight, 0, heads, head_dim)).astype(bf16)
         state[...] = state[...] * spread(jnp.exp(end), 0, heads, head_dim) + dot_tn(b_proj, scaled)
 
     @pl.when(at == 2 * count - 1)
@@ -594,19 +606,21 @@
     return pl.pallas_call(
         functools.partial(front_kernel, heads, head_dim, state_dim, count),
         grid=(2 * count,),
-        out_shape=(shape((length, width), bf16), shape((length, inner), f32), shape((length, conv), bf16),
-                   shape((length, conv), f32), shape((length, 128), f32), shape(state, f32),
+        out_shape=(shape((length, width), bf16), shape((length, inner), bf16), shape((length, inner), f32),
+                   shape((length, conv - inner), bf16), shape((length, conv - inner), f32),
+                   shape((length, 128), f32), shape(state, f32),
                    shape(fade, f32), shape((16, conv), bf16), shape((rest, width), bf16),
                    shape((8, conv), f32), shape((8, 128), f32), shape((8, inner), f32), shape((16, 128), f32)),
         in_specs=[early(width), pl.BlockSpec((16, width), lambda g: (length // 16 - 1, 0))] + [VMEM] * 13,
-        out_specs=(early(width), early(inner), late(conv), late(conv), late(128)) + (VMEM,) * 8,
+        out_specs=(early(width), early(inner), early(inner), late(conv - inner), late(conv - inner), late(128))
+        + (VMEM,) * 8,
         scratch_shapes=[
-            pltpu.VMEM((length, width), bf16), pltpu.VMEM((length, inner), bf16),
-            pltpu.VMEM((16, width), bf16), pltpu.VMEM((16, width), bf16),
+            pltpu.VMEM((length, width), bf16), pltpu.VMEM((length, inner), f32),
+            pltpu.VMEM((16, width), bf16), pltpu.VMEM((16, width), bf16), pltpu.VMEM((16, width), bf16),
             pltpu.VMEM((head_count,) + proj_bc.shape, bf16), pltpu.VMEM((8, 128), f32),
             pltpu.VMEM((head_count, 8, 128), f32), pltpu.VMEM((length, 128), f32),
-            pltpu.VMEM((GROUP + 8, 128), f32), pltpu.VMEM((8, conv), f32),
-            pltpu.VMEM((GROUP + 8, conv), f32), pltpu.VMEM(state, f32), pltpu.VMEM((8, 128), f32)]
+            pltpu.VMEM((GROUP + 8, 128), f32), pltpu.VMEM((GROUP + 8, inner), f32),
+            pltpu.VMEM((GROUP + 8, conv - inner), f32), pltpu.VMEM(state, f32), pltpu.VMEM((8, 128), f32)]
         + DeviceScan.scratch(state, fade) + [DMA((2, head_count)), DMA((2, head_count)), DMA((2,))],
         compiler_params=pltpu.CompilerParams(
             dimension_semantics=("arbitrary",), collective_id=3, has_side_effects=True,
@@ -621,9 +635,9 @@
 
 
 def mix_step(heads, head_dim, state_dim, at,
-             conv_out, heads_in, gate, cot, out_proj, gains, entering,
+             x_conv, bc_conv, heads_in, normed, zx, cot, out_proj, gains, entering,
              ssm_out, d_normed_out, partial_out, sums_out, starts_out, state, between):
-    rows = conv_out.shape[0]
+    rows = x_conv.shape[0]
     inner = heads * head_dim
     per = 128 // head_dim
 
@@ -631,7 +645,7 @@
     def _():
         state[...] = entering[...]
 
-    values = conv_out[...]
+    values = jnp.concatenate([x_conv[...], bc_conv[...]], axis=1)
     active = values * sigmoid(values)
     x = active[:, :inner]
     b_proj = active[:, inner : inner + state_dim].astype(bf16)
@@ -673,7 +687,7 @@
     fade = spread(jnp.exp(end - info), CUM, heads, head_dim)
     state[...] = start * spread(jnp.exp(end), CUM, heads, head_dim) + dot_tn(b_proj, (stepped * fade).astype(bf16))
     ssm_out[...] = result
-    z = gate[...]
+    z = dot(normed[...], zx[:, :inner])
     gated = result * (z * sigmoid(z))
     d_normed = dot_nt(cot[...], out_proj[...])
     d_normed_out[...] = d_normed.astype(bf16)
@@ -687,7 +701,7 @@
 
 
 def gate_step(heads, head_dim, state_dim, all_channels, at,
-              ssm, gate, d_normed, sums, conv_out, heads_in, cot, gains,
+              ssm, d_normed, sums, x_conv, bc_conv, heads_in, normed, zx, cot, gains,
               d_ssm_out, d_gate_out, grad_out, rows_out, total_out):
     rows = ssm.shape[0]
     inner = heads * head_dim
@@ -701,7 +715,7 @@
     tall = jnp.concatenate([sums[0, pl.ds(at, 1)], sums[1, pl.ds(at, 1)], jnp.zeros((126, rows), f32)], axis=0).T
     inv = lax.rsqrt(tall[:, 0:1] / all_channels + epsilon)
     cross = tall[:, 1:2] / all_channels
-    z = gate[...]
+    z = dot(normed[...], zx[:, :inner])
     s = sigmoid(z)
     y = ssm[...]
     gated = y * (z * s)
@@ -713,17 +727,16 @@
     d_ssm = d_gated * (z * s)
     d_ssm_out[...] = d_ssm
     d_gate_out[...] = (d_gated * y * (s * (1.0 + z * (1.0 - s)))).astype(bf16)
-    values = conv_out[...]
-    active = values * sigmoid(values)
+    x_values, c_values = x_conv[...], bc_conv[:, state_dim:]
     rows_out[0:1] += jnp.sum(back * unit, axis=0, keepdims=True)
-    rows_out[1:2] += jnp.sum(d_ssm * active[:, :inner], axis=0, keepdims=True)
-    c_proj = active[:, inner + state_dim :].astype(bf16)
+    rows_out[1:2] += jnp.sum(d_ssm * (x_values * sigmoid(x_values)), axis=0, keepdims=True)
+    c_proj = (c_values * sigmoid(c_values)).astype(bf16)
     grown = spread(jnp.exp(heads_in[...]), DEV, heads, head_dim)
     total_out[...] += dot_tn(c_proj, (grown * d_ssm).astype(bf16))
 
 
 def back_step(heads, head_dim, state_dim, first_step, last_step,
-              d_ssm, conv_out, conv_in, heads_in, start, entering, conv_w, params, skip, conv_halo,
+              d_ssm, x_conv, bc_conv, x_in, bc_in, heads_in, start, entering, conv_w, params, skip, conv_halo,
               d_conv_in_out, d_step_out, conv_grads, head_grads, halo_out,
               lam, later, later_info, between):
     rows = d_ssm.shape[0]
@@ -738,7 +751,7 @@
         for each in (later, later_info):
             each[rows:] = jnp.zeros((8, each.shape[1]), f32)
 
-    values = conv_out[...]
+    values = jnp.concatenate([x_conv[...], bc_conv[...]], axis=1)
     gates = sigmoid(values)
     active = values * gates
     x = active[:, :inner]
@@ -792,8 +805,7 @@
             d_rows.append(row_total)
         dy_stack = jnp.concatenate([jnp.where(own, dy_tile, jnp.zeros_like(dy_tile)) for own in owns], axis=0)
         tiles.append(dot(jnp.concatenate(weights, axis=1), dy_stack))
-        if pair < BACK_POINTS - 1:
-            between(pair + 1)
+        between(pair + 1)
     d_stepped = jnp.concatenate(tiles, axis=1)
     d_cum = jnp.concatenate(d_cols, axis=0)
     d_cum = d_cum + jnp.concatenate(d_rows + [jnp.zeros((128 - heads, rows), f32)], axis=0).T
@@ -827,6 +839,7 @@
     lam[...] = end_grown * after + dot_tn(c_proj, grown_low)
     d_step = dot((d_stepped * x).astype(bf16), group_ones)
     d_x = step * d_stepped + skip[0:1] * dy
+    between(heads // per + 1)
 
     order_r = lax.broadcasted_iota(jnp.int32, (rows, rows), 0)
     order_c = lax.broadcasted_iota(jnp.int32, (rows, rows), 1)
@@ -842,7 +855,7 @@
 
     d_active = jnp.concatenate([d_x, d_b, d_c], axis=1)
     d_conv = d_active * (gates * (1.0 + values * (1.0 - gates)))
-    taken = conv_in[...].astype(f32)
+    taken = jnp.concatenate([x_in[...], bc_in[...]], axis=1).astype(f32)
     total = d_conv * conv_w[0:1]
     conv_grads[0:1] += jnp.sum(d_conv * taken, axis=0, keepdims=True)
     conv_grads[4:5] += jnp.sum(d_conv, axis=0, keepdims=True)
@@ -879,8 +892,8 @@
     return place
 
 
-def layer_kernel(heads, head_dim, state_dim, all_channels, count, block, lag, plans, cuts, owners, taps,
-                 conv_out, conv_in, heads_in, gate, cot, normed, last_normed, out_proj, gains, entering, decay,
+def layer_kernel(heads, head_dim, state_dim, all_channels, count, block, lag, plans, steps, owners, taps,
+                 x_conv, bc_conv, x_in, bc_in, heads_in, cot, normed, last_normed, out_proj, gains, entering, decay,
                  conv_w, params, conv_halo, zx, weights, gain, tail_mask,
                  mixed_out, d_normed_out, sums_out, zx_out, op_out, bc_out, small_out,
                  own, got, total, held, ssm, d_normed, starts, state, leaving, later, later_info,
@@ -912,6 +925,7 @@
         src_ref=halo_rows, dst_ref=landed, send_sem=row_sems.at[0], recv_sem=row_sems.at[1],
         device_id={"seq": lax.rem(me + seq - 1, seq)}, device_id_type=MESH)
     served, sent = plans
+    back_points = inner // 128 + 3
     back_at = at - 2 * count - 1
     last_step = back_at == count - 1
 
@@ -928,7 +942,7 @@
     def _():
         mine = pl.ds(pl.multiple_of(at * rows, rows), rows)
         serve(0, MIX_POINTS * at)
-        mix_step(heads, head_dim, state_dim, at, conv_out, heads_in, gate, cot, out_proj, gains, entering,
+        mix_step(heads, head_dim, state_dim, at, x_conv, bc_conv, heads_in, normed, zx, cot, out_proj, gains, entering,
                  ssm.at[mine], d_normed.at[mine], own.at[mine], sums, starts, state,
                  lambda: serve(0, MIX_POINTS * at + 1))
 
@@ -954,7 +968,7 @@
         here = at - count
         mine = pl.ds(pl.multiple_of(here * rows, rows), rows)
         gate_step(heads, head_dim, state_dim, all_channels, here,
-                  ssm.at[mine], gate, d_normed.at[mine], sums_out, conv_out, heads_in, cot, gains,
+                  ssm.at[mine], d_normed.at[mine], sums_out, x_conv, bc_conv, heads_in, normed, zx, cot, gains,
                   ssm.at[mine], d_normed.at[mine], grad.at[:inner], gate_rows, state)
 
     @pl.when(at == 2 * count)
@@ -984,15 +998,16 @@
     def _():
         here = 3 * count - at
         mine = pl.ds(pl.multiple_of(here * rows, rows), rows)
-        serve(3, BACK_POINTS * back_at)
+        serve(3, back_points * back_at)
         back_step(heads, head_dim, state_dim, back_at == 0, last_step,
-                  ssm.at[mine], conv_out, conv_in, heads_in, starts[here], leaving, conv_w, params,
+                  ssm.at[mine], x_conv, bc_conv, x_in, bc_in, heads_in, starts[here], leaving, conv_w, params,
                   gains[1:2], conv_halo, d_conv, d_step, conv_grads, head_grads, halo_rows,
-                  state, later, later_info, lambda k: serve(3, BACK_POINTS * back_at + k))
+                  state, later, later_info, lambda k: serve(3, back_points * back_at + k))
 
         @pl.when(last_step)
         def _():
             row_copy.start()
+        serve(3, back_points * back_at + back_points - 1)
         rest_low = jnp.concatenate([d_conv[:, inner:], d_step[...]], axis=1)
         d_rows = project(normed[...], d_normed[mine], d_conv[:, :inner], rest_low).astype(bf16)
 
@@ -1045,12 +1060,14 @@
         op_sum.release(free_sem)
         at_block = [served.count(3, plans[0].phases[3][0] - 1), sent.count(3, plans[0].phases[3][0] - 1)]
 
-        def go(until):
-            ahead = max(at_block[1], min(line.count, until + 2))
+        def go(more):
+            until = min(line.count + lag, at_block[0] + more)
+            ahead = max(at_block[1], min(line.count - (0 if filled else 1), until + 2))
             line.send(at_block[1], ahead)
             line.serve(at_block[0], until, lag)
             at_block[:] = [until, ahead]
-        go(cuts[0])
+        filled = False
+        go(steps[0])
         row_copy.wait()
         extra = jnp.where(me < seq - 1, landed[...] * tail_mask[8:, 0:1], 0.0)
         extra = jnp.concatenate([jnp.zeros_like(extra), extra], axis=0).astype(bf16)
@@ -1058,12 +1075,15 @@
         more = project(last_normed[...], None, extra[:, :inner], extra_rest)
         final = held[...].astype(f32) + jnp.concatenate([jnp.zeros((block - 16, width), f32), more], axis=0)
         own[count * rows - block :] = final.astype(bf16)
-
+        filled = True
+        go(steps[1])
+
+        pl.semaphore_wait(free_sem, 1)
         pair_rows = sum_own.shape[1]
         for k in range(sum_own.shape[0]):
             sum_own[k, :, : 2 * inner] = grad[k * pair_rows : (k + 1) * pair_rows, : 2 * inner].astype(bf16)
-        pl.semaphore_wait(free_sem, 1)
         zx_sum.swap()
+        go(steps[2])
         small[0:8] += grad_bc[head_count, 0:8]
         small[8 : 9 + taps, :inner] = conv_grads[: taps + 1, :inner]
         small[8:10, inner : 2 * inner] = gate_rows[0:2]
@@ -1079,15 +1099,16 @@
             def _():
                 bc_scatter(to, me).start()
 
-        go(cuts[1])
+        go(steps[3])
         zx_sum.scatter()
-        go(cuts[2])
+        go(steps[4])
         small_swap.wait()
         sums_small = small_swap.total()
         lone = small.shape[0] - small_own.shape[0]
         small_out[:lone] = sums_small[:lone]
         small_own[...] = sums_small[lone:]
         both_swap.start()
+        go(steps[5])
 
         @pl.when(me < owners)
         def _():
@@ -1105,8 +1126,9 @@
             def _(k):
                 bc_swap(other_of("head", k), my_head).start()
 
-        go(cuts[3])
+        go(steps[6])
         zx_sum.gather()
+        go(steps[7])
         both_swap.wait()
         small_out[lone:] = both_swap.total()
 
@@ -1124,9 +1146,9 @@
             def _(k):
                 bc_gather(me, other_of("seq", k)).start()
 
-        go(cuts[4])
+        go(steps[8])
         zx_sum.back()
-        go(cuts[5])
+        go(steps[9])
         zx_sum.finish(zx_out)
         go(line.count + lag)
         line.finish()
@@ -1154,11 +1176,11 @@
                 bc_swap(other_of("head", k), my_head).wait_send()
 
 
-def layer(conv_out, conv_in, heads_in, gate, cot, normed, out_proj, gains, entering, decay, conv_w, params,
+def layer(x_conv, bc_conv, x_in, bc_in, heads_in, cot, normed, out_proj, gains, entering, decay, conv_w, params,
           conv_halo, zx, weights, gain, tail_mask, heads, head_dim, state_dim, all_channels, taps):
-    length, conv = conv_out.shape
+    length, inner = x_conv.shape
+    conv = inner + bc_conv.shape[1]
     count = length // GROUP
-    inner = heads * head_dim
     width = cot.shape[1]
     seq, head_count = lax.axis_size("seq"), lax.axis_size("head")
     block = BLOCK
@@ -1166,7 +1188,7 @@
     blocks = length // block
     per = GROUP // block
     lag = max(2, head_count // 2)
-    back_points = min(BACK_POINTS, inner // 128)
+    back_points = inner // 128 + 3
     gate_at = MIX * count + SWAP
     scan_at = gate_at + GATE * count
     back_start = scan_at + SCAN
@@ -1181,7 +1203,7 @@
         assert sent.count(3, point) >= min(blocks, (k + 1) * per) + LineSum.AHEAD
         for each in (served, sent):
             assert each.count(3, point) <= blocks + max(0, k * per - 1)
-    cuts = [2 * blocks - (blocks * (32 - cut)) // 32 for cut in CUTS]
+    steps = [step * 64 // block for step in STEPS]
 
     def by(cols, first, step):
         def index(g):
@@ -1202,13 +1224,13 @@
     paired = PairedSum.scratch(width, max(width, 2 * inner))
     return pl.pallas_call(
         functools.partial(layer_kernel, heads, head_dim, state_dim, all_channels, count, block, lag,
-                          (served, sent), cuts, owners, taps),
+                          (served, sent), steps, owners, taps),
         grid=(3 * count + 1,),
         out_shape=(shape((length, width), bf16), shape((length, width), bf16), shape((2, count, GROUP), f32),
                    shape((width, 2 * inner), bf16), shape((inner, width), bf16), shape((bc_rows, width), f32),
                    shape((24, width), f32)),
-        in_specs=[by(conv, 0, 2), by(conv, 2, 2), by(128, 0, 2), by(inner, 0, 1), by(width, 0, 1),
-                  by(width, 2, 2), pl.BlockSpec((16, width), lambda g: (length // 16 - 1, 0))] + [VMEM] * 11,
+        in_specs=[by(inner, 0, 2), by(conv - inner, 0, 2), by(inner, 2, 2), by(conv - inner, 2, 2),
+                  by(128, 0, 2), by(width, 0, 1), by(width, 0, 2), pl.BlockSpec((16, width), lambda g: (length // 16 - 1, 0))] + [VMEM] * 11,
         out_specs=(HBM, HBM) + (VMEM,) * 5,
         scratch_shapes=[
             vm((length, width), bf16), vm((length, width), bf16), vm((2 * length, width), bf16),
@@ -1230,16 +1252,16 @@
             dimension_semantics=("arbitrary",), collective_id=4, has_side_effects=True,
             vmem_limit_bytes=LAYER_LIMIT),
         name="layer",
-    )(conv_out, conv_in, heads_in, gate, cot, normed, normed, out_proj, gains, entering, decay, conv_w, params,
+    )(x_conv, bc_conv, x_in, bc_in, heads_in, cot, normed, normed, out_proj, gains, entering, decay, conv_w, params,
       conv_halo, zx, weights, gain, tail_mask)
 
 
 PACE = 29
-MIX, SWAP, GATE, SCAN, BACK = 27, 30, 20, 100, 82
-MIX_POINTS, BACK_POINTS = 2, 4
-EARLY, LATE = 25, 60
+MIX, SWAP, GATE, SCAN, BACK = 27, 30, 20, 100, 94
+MIX_POINTS = 2
+EARLY, LATE = -14, 50
 BLOCK = 64
-CUTS = (8, 13, 18, 23, 28, 31)
+STEPS = (1, 1, 1, 1, 5, 1, 2, 1, 5, 1)
 LAYER_LIMIT = 63 * 2**20
 
 
@@ -1330,14 +1352,14 @@
     state_dim = bc_width // 2
     zx = proj_zx.reshape(width, 2 * inner)
     gain = in_gain[None]
-    (normed, gate, conv_in, conv_out, info, entering, decay, conv_halo, weights, conv_w, params, gains,
+    (normed, x_in, x_conv, bc_in, bc_conv, info, entering, decay, conv_halo, weights, conv_w, params, gains,
      tail_mask) = front(
         tokens, zx, start_flags.reshape(length // 128, 128), gain, proj_bc.T, proj_dt.T, conv_x_weight,
         conv_x_bias[None], conv_bc_weight, conv_bc_bias[None], dt_bias[None], a_log[None], skip_scale[None],
         norm_gain[None], heads, head_dim, state_dim)
     all_channels = inner * head_count
     mixed, d_normed, sums, zx_sum, op_sum, bc_sum, small_sum = layer(
-        conv_out, conv_in, info, gate, cotangent, normed, out_proj, gains, entering, decay, conv_w, params,
+        x_conv, bc_conv, x_in, bc_in, info, cotangent, normed, out_proj, gains, entering, decay, conv_w, params,
         conv_halo, zx, weights, gain, tail_mask, heads, head_dim, state_dim, all_channels, taps)
     (mixed_out, grad_tokens, grad_zx, grad_op, grad_bc, grad_dt, grad_gain, grad_conv_w, grad_conv_b,
      grad_bc_w, grad_bc_b, grad_bias, grad_rate, grad_skip, grad_norm) = finish(

time: 302 us -> 291 us (0.964)
  Pallas kernels: 297 us -> 286 us
    pallas_call x1, Pallas kernels: 231 us -> 222 us  [layer(): pl.pallas_call(functools.partial(layer_kernel, heads, head_dim, state_dim...]
where the time goes in v6:
time: 291 us
  Pallas kernels  286 us (98%)
  local copies, waits for them, and re-layouts  3.48 us (1%)
    pallas_call x1, Pallas kernels, layer(): pl.pallas_call(functools.partial(layer_kernel, heads, head_dim, state_dim...  222 us
    pallas_call x1, Pallas kernels, front(): pl.pallas_call(functools.partial(front_kernel, heads, head_dim, state_dim...  46.5 us
    pallas_call x1, Pallas kernels, finish(): pl.pallas_call(functools.partial(finish_kernel, heads, head_dim, inner *...  17.8 us

profile of v6, /device:TPU:0, one launch (start us, length us, event | category | flops | bytes accessed | tf_op | source)
XLA Modules:
  0.0 290.8 jit_solution(4558518800245595521)
XLA Ops:
  0.6 3.5 %copy.31 = bf16[128,8,2,512]{3,1,2,0:T(8,128)(2,1)} copy(bf16[128,8,2,512]{3,2,1,0:T(2,128)(2,1)} %bitcast.23) | data formatting | bytes 4194304
  4.1 46.5 %front.1 = (bf16[2048,1024]{1,0:T(8,128)(2,1)}, bf16[2048,512]{1,0:T(8,128)(2,1)}, f32[2048,512]{1,0:T(8,128)}, bf16[2048,256]{1,0:T(8,128)(2,1)}, f32[2048,256]...) custom-call(bf16[2048,1024]{1,0:T(8,128)(2,1)} %tokens.3, ...), custom_call_target="tpu_custom_call" | custom-call | tf_op jit(solution)/shard_map/front/pallas_call | solution.py:606
  50.7 222.2 %layer.1 = (bf16[2048,1024]{1,0:T(8,128)(2,1)}, bf16[2048,1024]{1,0:T(8,128)(2,1)}, f32[2,8,256]{2,1,0:T(8,128)}, bf16[1024,1024]{1,0:T(8,128)(2,1)}, bf16[512,1...) custom-call(f32[2048,512]{1,0:T(8,128)} %get-tuple-element.51.x_conv, ...), custom_call_target="tpu_custom_call" | custom-call | tf_op jit(solution)/shard_map/layer/pallas_call | solution.py:1225
  272.9 17.8 %finish.1 = (bf16[2048,1024]{1,0:T(8,128)(2,1)}, f32[2048,1024]{1,0:T(8,128)}, f32[1024,2,512]{2,1,0:T(2,128)}, f32[512,1024]{1,0:T(8,128)}, f32[64,1024]{1,0:T(...) custom-call(bf16[2048,1024]{1,0:T(8,128)(2,1)} %tokens.3, ...), custom_call_target="tpu_custom_call" | custom-call | tf_op jit(solution)/shard_map/finish/pallas_call | solution.py:1325

commit v7 on v6

--- a/solution.py
+++ b/solution.py
@@ -61,8 +61,8 @@
 class LineSum:
     AHEAD = 3
 
-    def __init__(self, own, got, total, outs, place, sems, block):
-        self.own, self.got, self.total, self.outs, self.place = own, got, total, outs, place
+    def __init__(self, own, got, total, out, place, sems, block):
+        self.own, self.got, self.total, self.out, self.place = own, got, total, out, place
         self.send1, self.got_in, self.got_total, self.send2, self.stored = (sems.at[i] for i in range(5))
         self.block = block
         self.half = own.shape[0] // block
@@ -101,13 +101,9 @@
             send_sem=self.send2.at[b], recv_sem=self.got_total.at[b],
             device_id={"head": to}, device_id_type=MESH)
 
-    def store(self, b, do):
-        for n, out in enumerate(self.outs):
-            @pl.when(b // self.half == n)
-            def _():
-                do(pltpu.make_async_copy(self.total.at[self.rows(b)],
-                                         out.at[self.rows(self.place(n, lax.rem(b, self.half)))],
-                                         self.stored.at[b]))
+    def store(self, b):
+        return pltpu.make_async_copy(
+            self.total.at[self.rows(b)], self.out.at[self.rows(self.place(b))], self.stored.at[b])
 
     def inward(self, b):
         rows = self.slot(b)
@@ -137,7 +133,7 @@
         @pl.when(self.has_outer)
         def _():
             self.out_copy(b, self.outer).start()
-        self.store(b, lambda copy: copy.start())
+        self.store(b).start()
 
     def serve(self, first, last, lag):
         @pl.when(self.has_outer)
@@ -177,7 +173,7 @@
 
         @pl.loop(0, self.count)
         def _(b):
-            self.store(b, lambda copy: copy.wait())
+            self.store(b).wait()
 
             @pl.when(self.has_outer)
             def _():
@@ -198,7 +194,7 @@
         seq = lax.axis_size("seq")
         piece = max(16, rows // seq)
         part = pltpu.VMEM((seq // 2, piece, width), bf16)
-        return [pltpu.VMEM((seq // 2, 2 * piece, width), bf16)] + [part] * 4 + [DMA((6, seq // 2))]
+        return [pltpu.VMEM((seq // 2, 2 * piece, width), bf16)] + [part] * 4 + [DMA((8, seq // 2))]
 
     def half(self, odd):
         return pl.ds(pl.multiple_of(odd * self.piece, self.piece), self.piece)
@@ -257,13 +253,22 @@
         self.others(lambda other: self.gather_copy(other, self.chip).wait_recv())
         self.back_copy().start()
 
+    def stores(self, out):
+        for k in range(min(self.chips, out.shape[0] // (2 * self.piece))):
+            for n, (odd, ref) in enumerate(((self.odd, self.pair), (1 - self.odd, self.theirs))):
+                start = pl.multiple_of((2 * k + odd) * self.piece, self.piece)
+                yield pltpu.make_async_copy(
+                    ref.at[k], out.at[pl.ds(start, self.piece)], self.sems.at[6 + n, k])
+
     def finish(self, out):
         self.back_copy().wait()
         self.others(lambda other: self.gather_copy(self.chip, other).wait_send())
-        for k in range(min(self.chips, out.shape[0] // (2 * self.piece))):
-            for odd, ref in ((self.odd, self.pair), (1 - self.odd, self.theirs)):
-                start = pl.multiple_of((2 * k + odd) * self.piece, self.piece)
-                out[pl.ds(start, self.piece)] = ref[k]
+        for copy in self.stores(out):
+            copy.start()
+
+    def stored(self, out):
+        for copy in self.stores(out):
+            copy.wait()
 
 
 class Swap:
@@ -445,14 +450,21 @@
     return out
 
 
+def loads_of(source, target, sems, first):
+    parts = sems.shape[0]
+    rows = source.shape[0] // parts
+    return [pltpu.make_async_copy(source.at[pl.ds(k * rows, rows), pl.ds(first, target.shape[1])],
+                                  target.at[pl.ds(k * rows, rows)], sems.at[k]) for k in range(parts)]
+
+
 def front_kernel(heads, head_dim, state_dim, count,
                  tokens, last_tokens, zx, flags, gain, proj_bc, proj_dt, conv_x_weight, conv_x_bias,
                  conv_bc_weight, conv_bc_bias, dt_bias, a_log, skip, norm_gain,
                  normed_out, x_in_out, x_conv_out, bc_in_out, bc_conv_out, heads_out, entering, decay_out,
                  halo_out, weights_out, conv_w_out, params, gains_out, mask_out,
                  normed, x_active, tail_rows, landed, head_low, proj_all, conv_bc, conv_all, flag_cols, flag_ext,
-                 x_ext, bc_ext, state, running, lead, fade,
-                 scan_got, scan_got_fade, scan_sent, scan_sent_fade, scan_sems, proj_sems, conv_sems, row_sems):
+                 x_ext, bc_ext, state, running, x_weights, lead, fade,
+                 scan_got, scan_got_fade, scan_sent, scan_sent_fade, scan_sems, proj_sems, conv_sems, row_sems, load_sems):
     at = pl.program_id(0)
     rows = tokens.shape[0]
     inner = heads * head_dim
@@ -466,9 +478,12 @@
         src_ref=tail_rows, dst_ref=landed, send_sem=row_sems.at[0], recv_sem=row_sems.at[1],
         device_id={"seq": lax.rem(me + 1, seq)}, device_id_type=MESH)
     lane_row = lax.broadcasted_iota(jnp.int32, (1, 128), 1)
+    loads = loads_of(zx, x_weights, load_sems, inner)
 
     @pl.when(at == 0)
     def _():
+        for copy in loads:
+            copy.start()
         final = 1.0 - flags[flags.shape[0] - 1 :].astype(f32)
         one, two = final[:, 127:128], final[:, 126:127]
         row = lax.broadcasted_iota(jnp.int32, (16, 128), 0)
@@ -518,14 +533,19 @@
         low = norm_rows(tokens[...], gain[...])
         normed[mine] = low
         normed_out[...] = low
-        x_in = dot(low, zx[:, inner:]).astype(bf16)
+
+        @pl.when(at == 0)
+        def _():
+            for copy in loads:
+                copy.wait()
+        x_in = dot(low, x_weights[...]).astype(bf16)
         x_in_out[...] = x_in
 
         @pl.when(at == 0)
         def _():
             row_copy.wait()
             head_low[...] = norm_rows(landed[...], gain[...])
-            ahead = jnp.where(me > 0, dot(head_low[...], zx[:, inner:]), 0.0).astype(bf16)
+            ahead = jnp.where(me > 0, dot(head_low[...], x_weights[...]), 0.0).astype(bf16)
             halo_out[:, :inner] = ahead
             x_ext[0:8] = ahead[8:].astype(f32)
         total = convolve(x_ext, x_in.astype(f32), keeps(flag_cols[mine]), 0, inner)
@@ -611,7 +631,7 @@
                    shape((length, 128), f32), shape(state, f32),
                    shape(fade, f32), shape((16, conv), bf16), shape((rest, width), bf16),
                    shape((8, conv), f32), shape((8, 128), f32), shape((8, inner), f32), shape((16, 128), f32)),
-        in_specs=[early(width), pl.BlockSpec((16, width), lambda g: (length // 16 - 1, 0))] + [VMEM] * 13,
+        in_specs=[early(width), pl.BlockSpec((16, width), lambda g: (length // 16 - 1, 0)), HBM] + [VMEM] * 12,
         out_specs=(early(width), early(inner), early(inner), late(conv - inner), late(conv - inner), late(128))
         + (VMEM,) * 8,
         scratch_shapes=[
@@ -620,8 +640,9 @@
             pltpu.VMEM((head_count,) + proj_bc.shape, bf16), pltpu.VMEM((8, 128), f32),
             pltpu.VMEM((head_count, 8, 128), f32), pltpu.VMEM((length, 128), f32),
             pltpu.VMEM((GROUP + 8, 128), f32), pltpu.VMEM((GROUP + 8, inner), f32),
-            pltpu.VMEM((GROUP + 8, conv - inner), f32), pltpu.VMEM(state, f32), pltpu.VMEM((8, 128), f32)]
-        + DeviceScan.scratch(state, fade) + [DMA((2, head_count)), DMA((2, head_count)), DMA((2,))],
+            pltpu.VMEM((GROUP + 8, conv - inner), f32), pltpu.VMEM(state, f32), pltpu.VMEM((8, 128), f32),
+            pltpu.VMEM((width, inner), bf16)]
+        + DeviceScan.scratch(state, fade) + [DMA((2, head_count)), DMA((2, head_count)), DMA((2,)), DMA((4,))],
         compiler_params=pltpu.CompilerParams(
             dimension_semantics=("arbitrary",), collective_id=3, has_side_effects=True,
             vmem_limit_bytes=LIMIT),
@@ -882,27 +903,26 @@
 
 
 def block_place(per, blocks):
-    def place(n, b):
-        if n == 0:
-            return b
-        late = b - (per - 1)
-        group = blocks // per - 2 - late // per
-        rest = jnp.where(b == blocks - 1, blocks - 1, group * per + lax.rem(late, per))
-        return jnp.where(b < per - 1, blocks - per + b, rest)
+    def place(b):
+        late = b - blocks - (per - 1)
+        group = 2 * blocks - 2 * per - late // per * per + late % per
+        second = jnp.where(b < blocks + per - 1, b + blocks - per, group)
+        return jnp.where((b < blocks) | (b == 2 * blocks - 1), b, second)
     return place
 
 
 def layer_kernel(heads, head_dim, state_dim, all_channels, count, block, lag, plans, steps, owners, taps,
                  x_conv, bc_conv, x_in, bc_in, heads_in, cot, normed, last_normed, out_proj, gains, entering, decay,
-                 conv_w, params, conv_halo, zx, weights, gain, tail_mask,
-                 mixed_out, d_normed_out, sums_out, zx_out, op_out, bc_out, small_out,
+                 conv_w, params, conv_halo, zx_hbm, weights, gain, tail_mask,
+                 totals_out, sums_out, zx_out, op_out, bc_out, small_out,
                  own, got, total, held, ssm, d_normed, starts, state, leaving, later, later_info,
                  sums, sum_slots, lead, fade,
                  scan_got, scan_got_fade, scan_sent, scan_sent_fade, scan_sems,
                  grad, sum_own, sum_pair, sum_mine, sum_slot, sum_theirs, sum_sems, grad_bc,
                  bc_slots, bc_z, bc_res, small, small_slots, small_own, small_z,
                  d_conv, d_step, gate_rows, conv_grads, head_grads, halo_rows, landed,
-                 line_sems, swap_sems, bc_sems, bcz_sems, small_sems, smallz_sems, row_sems, free_sem):
+                 line_sems, swap_sems, bc_sems, bcz_sems, small_sems, smallz_sems, row_sems, free_sem, zx,
+                 load_sems):
     at = pl.program_id(0)
     rows, width = cot.shape
     inner = heads * head_dim
@@ -910,7 +930,7 @@
     seq, head_count = lax.axis_size("seq"), lax.axis_size("head")
     me, my_head = lax.axis_index("seq"), lax.axis_index("head")
     per = rows // block
-    line = LineSum(own, got, total, (mixed_out, d_normed_out), block_place(per, count * per), line_sems, block)
+    line = LineSum(own, got, total, totals_out, block_place(per, count * per), line_sems, block)
     swap = Swap("head", sums, sum_slots, swap_sems)
     scan = DeviceScan(True, state, fade, lead, leaving, scan_got, scan_got_fade, scan_sent, scan_sent_fade,
                       scan_sems)
@@ -933,18 +953,29 @@
         line.send(*sent.span(phase, k))
         line.serve(*served.span(phase, k), lag)
 
+    def serve_mix(k):
+        @pl.when(at > 0)
+        def _():
+            serve(1, MIX_POINTS * (at - 1) + k)
+
+    loads = loads_of(zx_hbm, zx, load_sems, 0)
+
     @pl.when(at == 0)
     def _():
+        for copy in loads:
+            copy.start()
         greet("head", "seq")
         state[...] = entering[...]
+        for copy in loads:
+            copy.wait()
 
     @pl.when(at < count)
     def _():
         mine = pl.ds(pl.multiple_of(at * rows, rows), rows)
-        serve(0, MIX_POINTS * at)
+        serve_mix(0)
         mix_step(heads, head_dim, state_dim, at, x_conv, bc_conv, heads_in, normed, zx, cot, out_proj, gains, entering,
                  ssm.at[mine], d_normed.at[mine], own.at[mine], sums, starts, state,
-                 lambda: serve(0, MIX_POINTS * at + 1))
+                 lambda: serve_mix(1))
 
     @pl.when(at == count - 1)
     def _():
@@ -952,7 +983,7 @@
 
     @pl.when((at >= count) & (at < 2 * count))
     def _():
-        serve(1, at - count)
+        serve(2, at - count)
 
     @pl.when(at == count)
     def _():
@@ -978,7 +1009,7 @@
             if hi > lo:
                 sum_own[k, : hi - lo, :width] = grad[lo:hi, :width].astype(bf16)
         scan.begin(decay[...])
-        scan.run(lambda k: serve(2, k))
+        scan.run(lambda k: serve(3, k))
         op_sum.swap()
         grad[...] = jnp.zeros_like(grad)
         grad_bc[...] = jnp.zeros_like(grad_bc)
@@ -998,16 +1029,16 @@
     def _():
         here = 3 * count - at
         mine = pl.ds(pl.multiple_of(here * rows, rows), rows)
-        serve(3, back_points * back_at)
+        serve(4, back_points * back_at)
         back_step(heads, head_dim, state_dim, back_at == 0, last_step,
                   ssm.at[mine], x_conv, bc_conv, x_in, bc_in, heads_in, starts[here], leaving, conv_w, params,
                   gains[1:2], conv_halo, d_conv, d_step, conv_grads, head_grads, halo_rows,
-                  state, later, later_info, lambda k: serve(3, back_points * back_at + k))
+                  state, later, later_info, lambda k: serve(4, back_points * back_at + k))
 
         @pl.when(last_step)
         def _():
             row_copy.start()
-        serve(3, back_points * back_at + back_points - 1)
+        serve(4, back_points * back_at + back_points - 1)
         rest_low = jnp.concatenate([d_conv[:, inner:], d_step[...]], axis=1)
         d_rows = project(normed[...], d_normed[mine], d_conv[:, :inner], rest_low).astype(bf16)
 
@@ -1057,8 +1088,7 @@
     @pl.when(last_step)
     def _():
         op_sum.finish(op_out)
-        op_sum.release(free_sem)
-        at_block = [served.count(3, plans[0].phases[3][0] - 1), sent.count(3, plans[0].phases[3][0] - 1)]
+        at_block = [served.before[-1], sent.before[-1]]
 
         def go(more):
             until = min(line.count + lag, at_block[0] + more)
@@ -1078,10 +1108,12 @@
         filled = True
         go(steps[1])
 
-        pl.semaphore_wait(free_sem, 1)
+        op_sum.stored(op_out)
+        op_sum.release(free_sem)
         pair_rows = sum_own.shape[1]
         for k in range(sum_own.shape[0]):
             sum_own[k, :, : 2 * inner] = grad[k * pair_rows : (k + 1) * pair_rows, : 2 * inner].astype(bf16)
+        pl.semaphore_wait(free_sem, 1)
         zx_sum.swap()
         go(steps[2])
         small[0:8] += grad_bc[head_count, 0:8]
@@ -1152,6 +1184,7 @@
         zx_sum.finish(zx_out)
         go(line.count + lag)
         line.finish()
+        zx_sum.stored(zx_out)
         small_swap.finish()
         both_swap.finish()
 
@@ -1187,22 +1220,22 @@
     pace = PACE * block // 64
     blocks = length // block
     per = GROUP // block
-    lag = max(2, head_count // 2)
+    lag = max(LAG, head_count // 2 - 1)
     back_points = inner // 128 + 3
     gate_at = MIX * count + SWAP
     scan_at = gate_at + GATE * count
     back_start = scan_at + SCAN
     rounds = seq.bit_length() - 1
-    phases = [(MIX_POINTS * count, 0, MIX // MIX_POINTS), (count, gate_at, GATE),
+    phases = [(MIX_POINTS, -(10**6), 0), (MIX_POINTS * (count - 1), MIX, MIX // MIX_POINTS), (count, gate_at, GATE),
               (rounds, scan_at, SCAN // rounds), (back_points * count, back_start, BACK // back_points)]
     served = Pace(phases, pace, LATE, 2 * blocks + lag)
     sent = Pace(phases, pace, EARLY, 2 * blocks)
     for k in range(count):
         point = (k + 1) * back_points - 1
-        assert served.count(3, point) >= min(blocks, (k + 1) * per) + lag
-        assert sent.count(3, point) >= min(blocks, (k + 1) * per) + LineSum.AHEAD
+        assert served.count(4, point) >= min(blocks, (k + 1) * per) + lag
+        assert sent.count(4, point) >= min(blocks, (k + 1) * per) + LineSum.AHEAD
         for each in (served, sent):
-            assert each.count(3, point) <= blocks + max(0, k * per - 1)
+            assert each.count(4, point) <= blocks + max(0, k * per - 1)
     steps = [step * 64 // block for step in STEPS]
 
     def by(cols, first, step):
@@ -1226,12 +1259,13 @@
         functools.partial(layer_kernel, heads, head_dim, state_dim, all_channels, count, block, lag,
                           (served, sent), steps, owners, taps),
         grid=(3 * count + 1,),
-        out_shape=(shape((length, width), bf16), shape((length, width), bf16), shape((2, count, GROUP), f32),
+        out_shape=(shape((2 * length, width), bf16), shape((2, count, GROUP), f32),
                    shape((width, 2 * inner), bf16), shape((inner, width), bf16), shape((bc_rows, width), f32),
                    shape((24, width), f32)),
         in_specs=[by(inner, 0, 2), by(conv - inner, 0, 2), by(inner, 2, 2), by(conv - inner, 2, 2),
-                  by(128, 0, 2), by(width, 0, 1), by(width, 0, 2), pl.BlockSpec((16, width), lambda g: (length // 16 - 1, 0))] + [VMEM] * 11,
-        out_specs=(HBM, HBM) + (VMEM,) * 5,
+                  by(128, 0, 2), by(width, 0, 1), by(width, 0, 2), pl.BlockSpec((16, width), lambda g: (length // 16 - 1, 0))]
+        + [VMEM] * 7 + [HBM] + [VMEM] * 3,
+        out_specs=(HBM, VMEM, HBM, HBM, VMEM, VMEM),
         scratch_shapes=[
             vm((length, width), bf16), vm((length, width), bf16), vm((2 * length, width), bf16),
             vm((block, width), bf16), vm((length, inner), f32), vm((length, inner), bf16),
@@ -1239,7 +1273,7 @@
         + [vm((GROUP + 8, conv), f32), vm((GROUP + 8, 128), f32)]
         + [vm((2, count, GROUP), f32), vm((head_count, 2, count, GROUP), f32)]
         + DeviceScan.scratch(state, fade)
-        + [vm((grad_rows, max(width, 2 * inner)), f32)] + paired[:-1] + [DMA((2,) + (6, seq // 2))]
+        + [vm((grad_rows, max(width, 2 * inner)), f32)] + paired[:-1] + [DMA((2,) + (8, seq // 2))]
         + [vm(((conv - inner + 128) // bc_rows, bc_rows, width), f32),
            vm((seq, head_count, piece, width), f32), vm((head_count, piece, width), f32),
            vm((bc_rows, width), f32), vm((24, width), f32), vm((seq, 24, width), f32),
@@ -1247,7 +1281,8 @@
            vm((GROUP, conv), bf16), vm((GROUP, 128), bf16), vm((8, inner), f32), vm((8, conv), f32),
            vm((8, 128), f32), vm((8, conv), f32), vm((8, conv), f32),
            LineSum.sems(length, block), DMA((2, head_count)), DMA((4, seq)), DMA((2, head_count)),
-           DMA((2, seq)), DMA((2, head_count)), DMA((2,)), pltpu.SemaphoreType.REGULAR],
+           DMA((2, seq)), DMA((2, head_count)), DMA((2,)), pltpu.SemaphoreType.REGULAR,
+           vm((width, 2 * inner), bf16), DMA((4,))],
         compiler_params=pltpu.CompilerParams(
             dimension_semantics=("arbitrary",), collective_id=4, has_side_effects=True,
             vmem_limit_bytes=LAYER_LIMIT),
@@ -1256,21 +1291,34 @@
       conv_halo, zx, weights, gain, tail_mask)
 
 
-PACE = 29
+PACE = 28
 MIX, SWAP, GATE, SCAN, BACK = 27, 30, 20, 100, 94
 MIX_POINTS = 2
 EARLY, LATE = -14, 50
-BLOCK = 64
-STEPS = (1, 1, 1, 1, 5, 1, 2, 1, 5, 1)
+BLOCK, LAG = 64, 3
+STEPS = (2, 2, 2, 2, 6, 2, 3, 2, 6, 2)
 LAYER_LIMIT = 63 * 2**20
 
 
-def finish_kernel(heads, head_dim, all_channels, taps,
+def finish_kernel(heads, head_dim, all_channels, taps, count,
                   tokens, cot, mixed, d_normed, sums, gain, zx, op, bc, small,
                   mixed_out, tokens_out, zx_out, op_out, bc_out, dt_out, gain_out, conv_w_out, conv_b_out,
-                  bc_w_out, bc_b_out, bias_out, rate_out, skip_out, norm_out):
+                  bc_w_out, bc_b_out, bias_out, rate_out, skip_out, norm_out, held, sems):
     at = pl.program_id(0)
     rows = tokens.shape[0]
+    slot = lax.rem(at, 2)
+    part = rows // 4
+
+    def stores(step, slot):
+        return [pltpu.make_async_copy(
+            held.at[slot, pl.ds(k * part, part)],
+            tokens_out.at[pl.ds(pl.multiple_of(step * rows + k * part, part), part)], sems.at[slot, k])
+            for k in range(4)]
+
+    @pl.when(at >= 2)
+    def _():
+        for copy in stores(at - 2, slot):
+            copy.wait()
     inner = heads * head_dim
     value = tokens[...].astype(f32)
     tall = jnp.concatenate([sums[0, pl.ds(at, 1)], jnp.zeros((127, rows), f32)], axis=0).T
@@ -1279,8 +1327,16 @@
     inv = lax.rsqrt(jnp.mean(value * value, axis=1, keepdims=True) + epsilon)
     xhat = value * inv
     scaled = d_normed[...].astype(f32) * gain[...]
-    tokens_out[...] = cot[...].astype(f32) + inv * (
+    held[slot] = cot[...].astype(f32) + inv * (
         scaled - xhat * jnp.mean(scaled * xhat, axis=1, keepdims=True))
+    for copy in stores(at, slot):
+        copy.start()
+
+    @pl.when(at == count - 1)
+    def _():
+        for step in (count - 2, count - 1):
+            for copy in stores(step, step % 2):
+                copy.wait()
     sums_zx = zx[...].astype(f32)
     zx_out[:, 0, :] = sums_zx[:, :inner]
     zx_out[:, 1, :] = sums_zx[:, inner:]
@@ -1309,7 +1365,7 @@
         bc_b_out[...] = chosen[taps : taps + 1]
 
 
-def finish(tokens, cot, mixed, d_normed, sums, gain, zx, op, bc, small, heads, head_dim, taps):
+def finish(tokens, cot, totals, sums, gain, zx, op, bc, small, heads, head_dim, taps):
     length, width = tokens.shape
     count = length // GROUP
     inner = heads * head_dim
@@ -1323,18 +1379,19 @@
             (1, inner)]
     cols = width // count
     return pl.pallas_call(
-        functools.partial(finish_kernel, heads, head_dim, inner * lax.axis_size("head"), taps),
+        functools.partial(finish_kernel, heads, head_dim, inner * lax.axis_size("head"), taps, count),
         grid=(count,),
         out_shape=(shape((length, width), bf16), shape((length, width), f32), shape((width, 2, inner), f32),
                    shape((inner, width), f32), shape((part, width), f32), shape((heads, width), f32))
         + tuple(shape(each, f32) for each in lone),
-        in_specs=[tall] * 4 + [VMEM, VMEM, by(cols, 2 * inner), by(inner // count, width),
+        in_specs=[tall] * 3 + [pl.BlockSpec((GROUP, width), lambda g: (count + g, 0)), VMEM, VMEM, by(cols, 2 * inner), by(inner // count, width),
                                VMEM, VMEM],
-        out_specs=(tall, tall, pl.BlockSpec((cols, 2, inner), lambda g: (g, 0, 0)), by(inner // count, width),
+        out_specs=(tall, HBM, pl.BlockSpec((cols, 2, inner), lambda g: (g, 0, 0)), by(inner // count, width),
                    VMEM, VMEM) + (VMEM,) * len(lone),
+        scratch_shapes=[pltpu.VMEM((2, GROUP, width), f32), DMA((2, 4))],
         compiler_params=pltpu.CompilerParams(dimension_semantics=("arbitrary",), vmem_limit_bytes=LIMIT),
         name="finish",
-    )(tokens, cot, mixed, d_normed, sums, gain, zx, op, bc, small)
+    )(tokens, cot, totals, totals, sums, gain, zx, op, bc, small)
 
 
 def shards(
@@ -1358,12 +1415,12 @@
         conv_x_bias[None], conv_bc_weight, conv_bc_bias[None], dt_bias[None], a_log[None], skip_scale[None],
         norm_gain[None], heads, head_dim, state_dim)
     all_channels = inner * head_count
-    mixed, d_normed, sums, zx_sum, op_sum, bc_sum, small_sum = layer(
+    totals, sums, zx_sum, op_sum, bc_sum, small_sum = layer(
         x_conv, bc_conv, x_in, bc_in, info, cotangent, normed, out_proj, gains, entering, decay, conv_w, params,
         conv_halo, zx, weights, gain, tail_mask, heads, head_dim, state_dim, all_channels, taps)
     (mixed_out, grad_tokens, grad_zx, grad_op, grad_bc, grad_dt, grad_gain, grad_conv_w, grad_conv_b,
      grad_bc_w, grad_bc_b, grad_bias, grad_rate, grad_skip, grad_norm) = finish(
-        tokens, cotangent, mixed, d_normed, sums, gain, zx_sum, op_sum, bc_sum, small_sum, heads, head_dim, taps)
+        tokens, cotangent, totals, sums, gain, zx_sum, op_sum, bc_sum, small_sum, heads, head_dim, taps)
     return (
         mixed_out, grad_tokens, grad_gain[0], grad_zx, grad_bc.T, grad_dt.T, grad_conv_w, grad_conv_b[0],
         grad_bc_w, grad_bc_b[0], grad_bias[0], grad_rate[0], grad_skip[0], grad_norm[0], grad_op,

time: 291 us -> 286 us (0.983)
  Pallas kernels: 286 us -> 281 us
    pallas_call x1, Pallas kernels: 222 us -> 218 us  [layer(): pl.pallas_call(functools.partial(layer_kernel, heads, head_dim, state_dim...]
where the time goes in v7:
time: 286 us; the launch traced here: 285 us
  Pallas kernels  281 us (98%)
  local copies, waits for them, and re-layouts  3.48 us (1%)
    pallas_call x1, Pallas kernels, layer(): pl.pallas_call(functools.partial(layer_kernel, heads, head_dim, state_dim...  218 us
    pallas_call x1, Pallas kernels, front(): pl.pallas_call(functools.partial(front_kernel, heads, head_dim, state_dim...  45.8 us
    pallas_call x1, Pallas kernels, finish(): pl.pallas_call(functools.partial(finish_kernel, heads, head_dim, inner *...  17.5 us

profile of v7, /device:TPU:0, one launch (start us, length us, event | category | flops | bytes accessed | tf_op | source)
XLA Modules:
  0.0 285.4 jit_solution(12527801591402093705)
XLA Ops:
  0.6 3.5 %copy.31 = bf16[128,8,2,512]{3,1,2,0:T(8,128)(2,1)} copy(bf16[128,8,2,512]{3,2,1,0:T(2,128)(2,1)} %bitcast.23) | data formatting | bytes 4194304
  4.1 45.8 %front.1 = (bf16[2048,1024]{1,0:T(8,128)(2,1)}, bf16[2048,512]{1,0:T(8,128)(2,1)}, f32[2048,512]{1,0:T(8,128)}, bf16[2048,256]{1,0:T(8,128)(2,1)}, f32[2048,256]...) custom-call(bf16[2048,1024]{1,0:T(8,128)(2,1)} %tokens.3, ...), custom_call_target="tpu_custom_call" | custom-call | tf_op jit(solution)/shard_map/front/pallas_call | solution.py:626
  50.0 217.8 %layer.1 = (bf16[4096,1024]{1,0:T(8,128)(2,1)}, f32[2,8,256]{2,1,0:T(8,128)}, bf16[1024,1024]{1,0:T(8,128)(2,1)}, bf16[512,1024]{1,0:T(8,128)(2,1)}, f32[64,1024]{1,0:T(8,128)}, /*index=5*/f32[24,1024]{1,0:T(8,128)}) custom-call(f32[2048,512]{1,0:T(8,128)} %get-tuple-element.50.x_conv, f32[2048,256]{1,0:T(8,128)} %get-tuple-element.51.bc_conv, ...), custom_call_target="tpu_custom_call" | custom-call | tf_op jit(solution)/shard_map/layer/pallas_call | solution.py:1258
  267.8 17.5 %finish.1 = (bf16[2048,1024]{1,0:T(8,128)(2,1)}, f32[2048,1024]{1,0:T(8,128)}, f32[1024,2,512]{2,1,0:T(2,128)}, f32[512,1024]{1,0:T(8,128)}, f32[64,1024]{1,0:T(...) custom-call(bf16[2048,1024]{1,0:T(8,128)(2,1)} %tokens.3, ...), custom_call_target="tpu_custom_call" | custom-call | tf_op jit(solution)/shard_map/finish/pallas_call | solution.py:1381

commit v8 on v7

--- a/solution.py
+++ b/solution.py
@@ -440,6 +440,7 @@
     return out
 
 
+FRONT = 512
 RAW, STEP, CUM, DEV, KEEP = 0, 8, 16, 24, 32
 
 
@@ -461,10 +462,11 @@
                  tokens, last_tokens, zx, flags, gain, proj_bc, proj_dt, conv_x_weight, conv_x_bias,
                  conv_bc_weight, conv_bc_bias, dt_bias, a_log, skip, norm_gain,
                  normed_out, x_in_out, x_conv_out, bc_in_out, bc_conv_out, heads_out, entering, decay_out,
-                 halo_out, weights_out, conv_w_out, params, gains_out, mask_out,
+                 halo_out, weights_hbm, conv_w_out, params, gains_out, mask_out,
                  normed, x_active, tail_rows, landed, head_low, proj_all, conv_bc, conv_all, flag_cols, flag_ext,
-                 x_ext, bc_ext, state, running, x_weights, lead, fade,
-                 scan_got, scan_got_fade, scan_sent, scan_sent_fade, scan_sems, proj_sems, conv_sems, row_sems, load_sems):
+                 x_ext, bc_ext, state, running, x_weights, weights_out, lead, fade,
+                 scan_got, scan_got_fade, scan_sent, scan_sent_fade, scan_sems, proj_sems, conv_sems, row_sems, load_sems,
+                 store_sem):
     at = pl.program_id(0)
     rows = tokens.shape[0]
     inner = heads * head_dim
@@ -479,6 +481,7 @@
         device_id={"seq": lax.rem(me + 1, seq)}, device_id_type=MESH)
     lane_row = lax.broadcasted_iota(jnp.int32, (1, 128), 1)
     loads = loads_of(zx, x_weights, load_sems, inner)
+    weights_store = pltpu.make_async_copy(weights_out, weights_hbm, store_sem.at[0])
 
     @pl.when(at == 0)
     def _():
@@ -564,6 +567,7 @@
             [jnp.zeros((8 - heads, proj_dt.shape[1]), f32)] if heads < 8 else []), axis=0)
         weights_out[bc_width:] = jnp.concatenate([eight] * 16, axis=0).astype(bf16)
         conv_w_out[:, inner:] = jnp.concatenate([conv_all[k, :, :bc_part] for k in range(heads_there)], axis=1)
+        weights_store.start()
         ahead = jnp.where(me > 0, dot_nt(head_low[...], weights_out[:bc_width]), 0.0).astype(bf16)
         halo_out[:, inner:] = ahead
         bc_ext[0:8] = ahead[8:].astype(f32)
@@ -582,20 +586,24 @@
         bc_conv_out[...] = total
         b_proj = (total[:, :state_dim] * sigmoid(total[:, :state_dim])).astype(bf16)
 
-        step_raw = raw[:, bc_width:]
-        step = softplus(step_raw + params[0:1])
-        log_decay = step * params[1:2] - GAP * flag
-        order_r = lax.broadcasted_iota(jnp.int32, (rows, rows), 0)
-        order_c = lax.broadcasted_iota(jnp.int32, (rows, rows), 1)
-        cum = exact_left((order_r >= order_c).astype(bf16), log_decay)
-        lane = lax.broadcasted_iota(jnp.int32, (rows, 128), 1)
-        kept = jnp.where(lane < KEEP + 1, keep[0], jnp.where(lane < KEEP + 2, keep[1], keep[2]))
-        heads_out[...] = lane_groups(rows, step_raw, step, cum, cum + running[0:1], kept)
-        end = cum[rows - 1 : rows]
-        running[...] = running[...] + end
-        weight = step * jnp.exp(end - cum)
-        scaled = (x_active[mine] * spread(weight, 0, heads, head_dim)).astype(bf16)
-        state[...] = state[...] * spread(jnp.exp(end), 0, heads, head_dim) + dot_tn(b_proj, scaled)
+        order_r = lax.broadcasted_iota(jnp.int32, (GROUP, GROUP), 0)
+        order_c = lax.broadcasted_iota(jnp.int32, (GROUP, GROUP), 1)
+        lower = (order_r >= order_c).astype(bf16)
+        lane = lax.broadcasted_iota(jnp.int32, (GROUP, 128), 1)
+        for lo in range(0, rows, GROUP):
+            part = slice(lo, lo + GROUP)
+            step_raw = raw[part, bc_width:]
+            step = softplus(step_raw + params[0:1])
+            log_decay = step * params[1:2] - GAP * flag[part]
+            cum = exact_left(lower, log_decay)
+            kept = jnp.where(lane < KEEP + 1, keep[0][part], jnp.where(lane < KEEP + 2, keep[1][part], keep[2][part]))
+            heads_out[part] = lane_groups(GROUP, step_raw, step, cum, cum + running[0:1], kept)
+            end = cum[GROUP - 1 :]
+            running[...] = running[...] + end
+            weight = step * jnp.exp(end - cum)
+            x_part = x_active[pl.ds(pl.multiple_of(block * rows + lo, GROUP), GROUP)]
+            scaled = (x_part * spread(weight, 0, heads, head_dim)).astype(bf16)
+            state[...] = state[...] * spread(jnp.exp(end), 0, heads, head_dim) + dot_tn(b_proj[part], scaled)
 
     @pl.when(at == 2 * count - 1)
     def _():
@@ -605,21 +613,23 @@
                           scan_sent_fade, scan_sems)
         scan.begin(decay)
         scan.run()
+        weights_store.wait()
 
 
 def front(tokens, zx, flags, gain, proj_bc, proj_dt, conv_x_weight, conv_x_bias, conv_bc_weight, conv_bc_bias,
           dt_bias, a_log, skip, norm_gain, heads, head_dim, state_dim):
     length, width = tokens.shape
-    count = length // GROUP
+    block = FRONT
+    count = length // block
     inner = heads * head_dim
     conv = inner + 2 * state_dim
     head_count = lax.axis_size("head")
 
     def early(cols):
-        return pl.BlockSpec((GROUP, cols), lambda g: (jnp.minimum(g, count - 1), 0))
+        return pl.BlockSpec((block, cols), lambda g: (jnp.minimum(g, count - 1), 0))
 
     def late(cols):
-        return pl.BlockSpec((GROUP, cols), lambda g: (jnp.maximum(g - count, 0), 0))
+        return pl.BlockSpec((block, cols), lambda g: (jnp.maximum(g - count, 0), 0))
     shape = jax.ShapeDtypeStruct
     state, fade = (state_dim, inner), (8, inner)
     rest = 2 * state_dim + 128
@@ -633,16 +643,16 @@
                    shape((8, conv), f32), shape((8, 128), f32), shape((8, inner), f32), shape((16, 128), f32)),
         in_specs=[early(width), pl.BlockSpec((16, width), lambda g: (length // 16 - 1, 0)), HBM] + [VMEM] * 12,
         out_specs=(early(width), early(inner), early(inner), late(conv - inner), late(conv - inner), late(128))
-        + (VMEM,) * 8,
+        + (VMEM,) * 3 + (HBM,) + (VMEM,) * 4,
         scratch_shapes=[
             pltpu.VMEM((length, width), bf16), pltpu.VMEM((length, inner), f32),
             pltpu.VMEM((16, width), bf16), pltpu.VMEM((16, width), bf16), pltpu.VMEM((16, width), bf16),
             pltpu.VMEM((head_count,) + proj_bc.shape, bf16), pltpu.VMEM((8, 128), f32),
             pltpu.VMEM((head_count, 8, 128), f32), pltpu.VMEM((length, 128), f32),
-            pltpu.VMEM((GROUP + 8, 128), f32), pltpu.VMEM((GROUP + 8, inner), f32),
-            pltpu.VMEM((GROUP + 8, conv - inner), f32), pltpu.VMEM(state, f32), pltpu.VMEM((8, 128), f32),
-            pltpu.VMEM((width, inner), bf16)]
-        + DeviceScan.scratch(state, fade) + [DMA((2, head_count)), DMA((2, head_count)), DMA((2,)), DMA((4,))],
+            pltpu.VMEM((block + 8, 128), f32), pltpu.VMEM((block + 8, inner), f32),
+            pltpu.VMEM((block + 8, conv - inner), f32), pltpu.VMEM(state, f32), pltpu.VMEM((8, 128), f32),
+            pltpu.VMEM((width, inner), bf16), pltpu.VMEM((rest, width), bf16)]
+        + DeviceScan.scratch(state, fade) + [DMA((2, head_count)), DMA((2, head_count)), DMA((2,)), DMA((4,)), DMA((1,))],
         compiler_params=pltpu.CompilerParams(
             dimension_semantics=("arbitrary",), collective_id=3, has_side_effects=True,
             vmem_limit_bytes=LIMIT),
@@ -912,7 +922,7 @@
 
 
 def layer_kernel(heads, head_dim, state_dim, all_channels, count, block, lag, plans, steps, owners, taps,
-                 x_conv, bc_conv, x_in, bc_in, heads_in, cot, normed, last_normed, out_proj, gains, entering, decay,
+                 x_conv, bc_conv, x_in, bc_in, heads_in, cot, normed, last_normed, op_hbm, gains, entering, decay,
                  conv_w, params, conv_halo, zx_hbm, weights, gain, tail_mask,
                  totals_out, sums_out, zx_out, op_out, bc_out, small_out,
                  own, got, total, held, ssm, d_normed, starts, state, leaving, later, later_info,
@@ -922,7 +932,7 @@
                  bc_slots, bc_z, bc_res, small, small_slots, small_own, small_z,
                  d_conv, d_step, gate_rows, conv_grads, head_grads, halo_rows, landed,
                  line_sems, swap_sems, bc_sems, bcz_sems, small_sems, smallz_sems, row_sems, free_sem, zx,
-                 load_sems):
+                 out_proj, load_sems, op_load_sems):
     at = pl.program_id(0)
     rows, width = cot.shape
     inner = heads * head_dim
@@ -958,7 +968,7 @@
         def _():
             serve(1, MIX_POINTS * (at - 1) + k)
 
-    loads = loads_of(zx_hbm, zx, load_sems, 0)
+    loads = loads_of(zx_hbm, zx, load_sems, 0) + loads_of(op_hbm, out_proj, op_load_sems, 0)
 
     @pl.when(at == 0)
     def _():
@@ -1264,7 +1274,7 @@
                    shape((24, width), f32)),
         in_specs=[by(inner, 0, 2), by(conv - inner, 0, 2), by(inner, 2, 2), by(conv - inner, 2, 2),
                   by(128, 0, 2), by(width, 0, 1), by(width, 0, 2), pl.BlockSpec((16, width), lambda g: (length // 16 - 1, 0))]
-        + [VMEM] * 7 + [HBM] + [VMEM] * 3,
+        + [HBM] + [VMEM] * 6 + [HBM] + [VMEM] * 3,
         out_specs=(HBM, VMEM, HBM, HBM, VMEM, VMEM),
         scratch_shapes=[
             vm((length, width), bf16), vm((length, width), bf16), vm((2 * length, width), bf16),
@@ -1282,7 +1292,7 @@
            vm((8, 128), f32), vm((8, conv), f32), vm((8, conv), f32),
            LineSum.sems(length, block), DMA((2, head_count)), DMA((4, seq)), DMA((2, head_count)),
            DMA((2, seq)), DMA((2, head_count)), DMA((2,)), pltpu.SemaphoreType.REGULAR,
-           vm((width, 2 * inner), bf16), DMA((4,))],
+           vm((width, 2 * inner), bf16), vm((inner, width), bf16), DMA((4,)), DMA((4,))],
         compiler_params=pltpu.CompilerParams(
             dimension_semantics=("arbitrary",), collective_id=4, has_side_effects=True,
             vmem_limit_bytes=LAYER_LIMIT),

time: 286 us -> 284 us (level)
  no operation moved by 1% of the time
where the time goes in v8:
time: 284 us
  Pallas kernels  280 us (99%)
  local copies, waits for them, and re-layouts  3.48 us (1%)
    pallas_call x1, Pallas kernels, layer(): pl.pallas_call(functools.partial(layer_kernel, heads, head_dim, state_dim...  218 us
    pallas_call x1, Pallas kernels, front(): pl.pallas_call(functools.partial(front_kernel, heads, head_dim, state_dim...  44.3 us
    pallas_call x1, Pallas kernels, finish(): pl.pallas_call(functools.partial(finish_kernel, heads, head_dim, inner *...  17.5 us

profile of v8, /device:TPU:0, one launch (start us, length us, event | category | flops | bytes accessed | tf_op | source)
XLA Modules:
  0.0 283.8 jit_solution(15018007044744111567)
XLA Ops:
  0.6 3.5 %copy.31 = bf16[128,8,2,512]{3,1,2,0:T(8,128)(2,1)} copy(bf16[128,8,2,512]{3,2,1,0:T(2,128)(2,1)} %bitcast.23) | data formatting | bytes 4194304
  4.1 44.3 %front.1 = (bf16[2048,1024]{1,0:T(8,128)(2,1)}, bf16[2048,512]{1,0:T(8,128)(2,1)}, f32[2048,512]{1,0:T(8,128)}, bf16[2048,256]{1,0:T(8,128)(2,1)}, f32[2048,256]...) custom-call(bf16[2048,1024]{1,0:T(8,128)(2,1)} %tokens.3, ...), custom_call_target="tpu_custom_call" | custom-call | tf_op jit(solution)/shard_map/front/pallas_call | solution.py:636
  48.4 217.8 %layer.1 = (bf16[4096,1024]{1,0:T(8,128)(2,1)}, f32[2,8,256]{2,1,0:T(8,128)}, bf16[1024,1024]{1,0:T(8,128)(2,1)}, bf16[512,1024]{1,0:T(8,128)(2,1)}, f32[64,1024]{1,0:T(8,128)}, /*index=5*/f32[24,1024]{1,0:T(8,128)}) custom-call(f32[2048,512]{1,0:T(8,128)} %get-tuple-element.50.x_conv, f32[2048,256]{1,0:T(8,128)} %get-tuple-element.51.bc_conv, ...), custom_call_target="tpu_custom_call" | custom-call | tf_op jit(solution)/shard_map/layer/pallas_call | solution.py:1268
  266.2 17.5 %finish.1 = (bf16[2048,1024]{1,0:T(8,128)(2,1)}, f32[2048,1024]{1,0:T(8,128)}, f32[1024,2,512]{2,1,0:T(2,128)}, f32[512,1024]{1,0:T(8,128)}, f32[64,1024]{1,0:T(...) custom-call(bf16[2048,1024]{1,0:T(8,128)(2,1)} %tokens.3, ...), custom_call_target="tpu_custom_call" | custom-call | tf_op jit(solution)/shard_map/finish/pallas_call | solution.py:1391

commit v9 on v8

--- a/solution.py
+++ b/solution.py
@@ -459,12 +459,12 @@
 
 
 def front_kernel(heads, head_dim, state_dim, count,
-                 tokens, last_tokens, zx, flags, gain, proj_bc, proj_dt, conv_x_weight, conv_x_bias,
+                 tokens, last_tokens, pairs_hbm, flags, gain, proj_bc, proj_dt, conv_x_weight, conv_x_bias,
                  conv_bc_weight, conv_bc_bias, dt_bias, a_log, skip, norm_gain,
                  normed_out, x_in_out, x_conv_out, bc_in_out, bc_conv_out, heads_out, entering, decay_out,
-                 halo_out, weights_hbm, conv_w_out, params, gains_out, mask_out,
+                 halo_out, weights_hbm, zx_hbm, conv_w_out, params, gains_out, mask_out,
                  normed, x_active, tail_rows, landed, head_low, proj_all, conv_bc, conv_all, flag_cols, flag_ext,
-                 x_ext, bc_ext, state, running, x_weights, weights_out, lead, fade,
+                 x_ext, bc_ext, state, running, pairs, zx, weights_out, lead, fade,
                  scan_got, scan_got_fade, scan_sent, scan_sent_fade, scan_sems, proj_sems, conv_sems, row_sems, load_sems,
                  store_sem):
     at = pl.program_id(0)
@@ -480,7 +480,12 @@
         src_ref=tail_rows, dst_ref=landed, send_sem=row_sems.at[0], recv_sem=row_sems.at[1],
         device_id={"seq": lax.rem(me + 1, seq)}, device_id_type=MESH)
     lane_row = lax.broadcasted_iota(jnp.int32, (1, 128), 1)
-    loads = loads_of(zx, x_weights, load_sems, inner)
+    quarter = pairs.shape[0] // 4
+    quarters = [pl.ds(k * quarter, quarter) for k in range(4)]
+    loads = [pltpu.make_async_copy(pairs_hbm.at[each], pairs.at[each], load_sems.at[k])
+             for k, each in enumerate(quarters)]
+    zx_stores = [pltpu.make_async_copy(zx.at[each], zx_hbm.at[each], store_sem.at[1 + k])
+                 for k, each in enumerate(quarters)]
     weights_store = pltpu.make_async_copy(weights_out, weights_hbm, store_sem.at[0])
 
     @pl.when(at == 0)
@@ -541,14 +546,18 @@
         def _():
             for copy in loads:
                 copy.wait()
-        x_in = dot(low, x_weights[...]).astype(bf16)
+            zx[:, :inner] = pairs[:, 0, :]
+            zx[:, inner:] = pairs[:, 1, :]
+            for copy in zx_stores:
+                copy.start()
+        x_in = dot(low, zx[:, inner:]).astype(bf16)
         x_in_out[...] = x_in
 
         @pl.when(at == 0)
         def _():
             row_copy.wait()
             head_low[...] = norm_rows(landed[...], gain[...])
-            ahead = jnp.where(me > 0, dot(head_low[...], x_weights[...]), 0.0).astype(bf16)
+            ahead = jnp.where(me > 0, dot(head_low[...], zx[:, inner:]), 0.0).astype(bf16)
             halo_out[:, :inner] = ahead
             x_ext[0:8] = ahead[8:].astype(f32)
         total = convolve(x_ext, x_in.astype(f32), keeps(flag_cols[mine]), 0, inner)
@@ -613,10 +622,11 @@
                           scan_sent_fade, scan_sems)
         scan.begin(decay)
         scan.run()
-        weights_store.wait()
-
-
-def front(tokens, zx, flags, gain, proj_bc, proj_dt, conv_x_weight, conv_x_bias, conv_bc_weight, conv_bc_bias,
+        for copy in [weights_store] + zx_stores:
+            copy.wait()
+
+
+def front(tokens, proj_zx, flags, gain, proj_bc, proj_dt, conv_x_weight, conv_x_bias, conv_bc_weight, conv_bc_bias,
           dt_bias, a_log, skip, norm_gain, heads, head_dim, state_dim):
     length, width = tokens.shape
     block = FRONT
@@ -639,11 +649,11 @@
         out_shape=(shape((length, width), bf16), shape((length, inner), bf16), shape((length, inner), f32),
                    shape((length, conv - inner), bf16), shape((length, conv - inner), f32),
                    shape((length, 128), f32), shape(state, f32),
-                   shape(fade, f32), shape((16, conv), bf16), shape((rest, width), bf16),
+                   shape(fade, f32), shape((16, conv), bf16), shape((rest, width), bf16), shape((width, 2 * inner), bf16),
                    shape((8, conv), f32), shape((8, 128), f32), shape((8, inner), f32), shape((16, 128), f32)),
         in_specs=[early(width), pl.BlockSpec((16, width), lambda g: (length // 16 - 1, 0)), HBM] + [VMEM] * 12,
         out_specs=(early(width), early(inner), early(inner), late(conv - inner), late(conv - inner), late(128))
-        + (VMEM,) * 3 + (HBM,) + (VMEM,) * 4,
+        + (VMEM,) * 3 + (HBM,) * 2 + (VMEM,) * 4,
         scratch_shapes=[
             pltpu.VMEM((length, width), bf16), pltpu.VMEM((length, inner), f32),
             pltpu.VMEM((16, width), bf16), pltpu.VMEM((16, width), bf16), pltpu.VMEM((16, width), bf16),
@@ -651,13 +661,13 @@
             pltpu.VMEM((head_count, 8, 128), f32), pltpu.VMEM((length, 128), f32),
             pltpu.VMEM((block + 8, 128), f32), pltpu.VMEM((block + 8, inner), f32),
             pltpu.VMEM((block + 8, conv - inner), f32), pltpu.VMEM(state, f32), pltpu.VMEM((8, 128), f32),
-            pltpu.VMEM((width, inner), bf16), pltpu.VMEM((rest, width), bf16)]
-        + DeviceScan.scratch(state, fade) + [DMA((2, head_count)), DMA((2, head_count)), DMA((2,)), DMA((4,)), DMA((1,))],
+            pltpu.VMEM(proj_zx.shape, bf16), pltpu.VMEM((width, 2 * inner), bf16), pltpu.VMEM((rest, width), bf16)]
+        + DeviceScan.scratch(state, fade) + [DMA((2, head_count)), DMA((2, head_count)), DMA((2,)), DMA((4,)), DMA((5,))],
         compiler_params=pltpu.CompilerParams(
             dimension_semantics=("arbitrary",), collective_id=3, has_side_effects=True,
             vmem_limit_bytes=LIMIT),
         name="front",
-    )(tokens, tokens, zx, flags, gain, proj_bc, proj_dt, conv_x_weight, conv_x_bias, conv_bc_weight,
+    )(tokens, tokens, proj_zx, flags, gain, proj_bc, proj_dt, conv_x_weight, conv_x_bias, conv_bc_weight,
       conv_bc_bias, dt_bias, a_log, skip, norm_gain)
 
 
@@ -1417,11 +1427,10 @@
     bc_part = conv_bc_bias.shape[0]
     bc_width = bc_part * head_count
     state_dim = bc_width // 2
-    zx = proj_zx.reshape(width, 2 * inner)
     gain = in_gain[None]
-    (normed, x_in, x_conv, bc_in, bc_conv, info, entering, decay, conv_halo, weights, conv_w, params, gains,
+    (normed, x_in, x_conv, bc_in, bc_conv, info, entering, decay, conv_halo, weights, zx, conv_w, params, gains,
      tail_mask) = front(
-        tokens, zx, start_flags.reshape(length // 128, 128), gain, proj_bc.T, proj_dt.T, conv_x_weight,
+        tokens, proj_zx, start_flags.reshape(length // 128, 128), gain, proj_bc.T, proj_dt.T, conv_x_weight,
         conv_x_bias[None], conv_bc_weight, conv_bc_bias[None], dt_bias[None], a_log[None], skip_scale[None],
         norm_gain[None], heads, head_dim, state_dim)
     all_channels = inner * head_count

time: 284 us -> 282 us (level)
  local copies, waits for them, and re-layouts: 3.48 us -> 0 us
    unnamed x1 -> x0, local copies, waits for them, and re-layouts: 3.48 us -> none
where the time goes in v9:
time: 282 us
  Pallas kernels  281 us (100%)
    pallas_call x1, Pallas kernels, layer(): pl.pallas_call(functools.partial(layer_kernel, heads, head_dim, state_dim...  217 us
    pallas_call x1, Pallas kernels, front(): pl.pallas_call(functools.partial(front_kernel, heads, head_dim, state_dim...  46.6 us
    pallas_call x1, Pallas kernels, finish(): pl.pallas_call(functools.partial(finish_kernel, heads, head_dim, inner *...  17.5 us

profile of v9, /device:TPU:0, one launch (start us, length us, event | category | flops | bytes accessed | tf_op | source)
XLA Modules:
  0.0 282.0 jit_solution(10395542817859193544)
XLA Ops:
  0.7 46.6 %front.1 = (bf16[2048,1024]{1,0:T(8,128)(2,1)}, bf16[2048,512]{1,0:T(8,128)(2,1)}, f32[2048,512]{1,0:T(8,128)}, bf16[2048,256]{1,0:T(8,128)(2,1)}, f32[2048,256]...) custom-call(bf16[2048,1024]{1,0:T(8,128)(2,1)} %tokens.3, ...), custom_call_target="tpu_custom_call" | custom-call | tf_op jit(solution)/shard_map/front/pallas_call | solution.py:646
  47.3 217.0 %layer.1 = (bf16[4096,1024]{1,0:T(8,128)(2,1)}, f32[2,8,256]{2,1,0:T(8,128)}, bf16[1024,1024]{1,0:T(8,128)(2,1)}, bf16[512,1024]{1,0:T(8,128)(2,1)}, f32[64,1024]{1,0:T(8,128)}, /*index=5*/f32[24,1024]{1,0:T(8,128)}) custom-call(f32[2048,512]{1,0:T(8,128)} %get-tuple-element.51.x_conv, f32[2048,256]{1,0:T(8,128)} %get-tuple-element.52.bc_conv, ...), custom_call_target="tpu_custom_call" | custom-call | tf_op jit(solution)/shard_map/layer/pallas_call | solution.py:1278
  264.3 17.5 %finish.1 = (bf16[2048,1024]{1,0:T(8,128)(2,1)}, f32[2048,1024]{1,0:T(8,128)}, f32[1024,2,512]{2,1,0:T(2,128)}, f32[512,1024]{1,0:T(8,128)}, f32[64,1024]{1,0:T(...) custom-call(bf16[2048,1024]{1,0:T(8,128)(2,1)} %tokens.3, ...), custom_call_target="tpu_custom_call" | custom-call | tf_op jit(solution)/shard_map/finish/pallas_call | solution.py:1401

commit v10 on v9

--- a/solution.py
+++ b/solution.py
@@ -162,22 +162,32 @@
                     self.outward(b - self.half)
                 self.in_copy(b, self.inner).start()
 
+    def drain(self, first, last):
+        @pl.loop(first, last)
+        def _(b):
+            self.store(b).wait()
+
+            @pl.when(self.has_outer)
+            def _():
+                self.out_copy(b, self.outer).wait_send()
+
     def finish(self):
+        last = self.count - 4
+
         @pl.when(jnp.logical_not(self.has_outer))
         def _():
-            pl.loop(self.half, self.count)(self.outward)
+            pl.loop(self.half, last)(self.outward)
 
             @pl.loop(self.count - self.AHEAD, self.count)
             def _(b):
                 self.in_copy(b, self.inner).wait_send()
-
-        @pl.loop(0, self.count)
-        def _(b):
-            self.store(b).wait()
-
-            @pl.when(self.has_outer)
-            def _():
-                self.out_copy(b, self.outer).wait_send()
+            self.drain(0, last)
+            pl.loop(last, self.count)(self.outward)
+            self.drain(last, self.count)
+
+        @pl.when(self.has_outer)
+        def _():
+            self.drain(0, self.count)
 
 
 class PairedSum:
@@ -1311,7 +1321,7 @@
       conv_halo, zx, weights, gain, tail_mask)
 
 
-PACE = 28
+PACE = 27
 MIX, SWAP, GATE, SCAN, BACK = 27, 30, 20, 100, 94
 MIX_POINTS = 2
 EARLY, LATE = -14, 50

time: 282 us -> 281 us (level)
  no operation moved by 1% of the time
where the time goes in v10:
time: 281 us
  Pallas kernels  280 us (100%)
    pallas_call x1, Pallas kernels, layer(): pl.pallas_call(functools.partial(layer_kernel, heads, head_dim, state_dim...  216 us
    pallas_call x1, Pallas kernels, front(): pl.pallas_call(functools.partial(front_kernel, heads, head_dim, state_dim...  46.6 us
    pallas_call x1, Pallas kernels, finish(): pl.pallas_call(functools.partial(finish_kernel, heads, head_dim, inner *...  17.5 us

profile of v10, /device:TPU:0, one launch (start us, length us, event | category | flops | bytes accessed | tf_op | source)
XLA Modules:
  0.0 281.1 jit_solution(3336605977832453901)
XLA Ops:
  0.7 46.6 %front.1 = (bf16[2048,1024]{1,0:T(8,128)(2,1)}, bf16[2048,512]{1,0:T(8,128)(2,1)}, f32[2048,512]{1,0:T(8,128)}, bf16[2048,256]{1,0:T(8,128)(2,1)}, f32[2048,256]...) custom-call(bf16[2048,1024]{1,0:T(8,128)(2,1)} %tokens.3, ...), custom_call_target="tpu_custom_call" | custom-call | tf_op jit(solution)/shard_map/front/pallas_call | solution.py:656
  47.3 216.2 %layer.1 = (bf16[4096,1024]{1,0:T(8,128)(2,1)}, f32[2,8,256]{2,1,0:T(8,128)}, bf16[1024,1024]{1,0:T(8,128)(2,1)}, bf16[512,1024]{1,0:T(8,128)(2,1)}, f32[64,1024]{1,0:T(8,128)}, /*index=5*/f32[24,1024]{1,0:T(8,128)}) custom-call(f32[2048,512]{1,0:T(8,128)} %get-tuple-element.51.x_conv, f32[2048,256]{1,0:T(8,128)} %get-tuple-element.52.bc_conv, ...), custom_call_target="tpu_custom_call" | custom-call | tf_op jit(solution)/shard_map/layer/pallas_call | solution.py:1288
  263.5 17.5 %finish.1 = (bf16[2048,1024]{1,0:T(8,128)(2,1)}, f32[2048,1024]{1,0:T(8,128)}, f32[1024,2,512]{2,1,0:T(2,128)}, f32[512,1024]{1,0:T(8,128)}, f32[64,1024]{1,0:T(...) custom-call(bf16[2048,1024]{1,0:T(8,128)(2,1)} %tokens.3, ...), custom_call_target="tpu_custom_call" | custom-call | tf_op jit(solution)/shard_map/finish/pallas_call | solution.py:1411
